TPU v7x, 32 devices: a whole 2x2x4 slice. The times are simulated.
32 devices in a mesh: expert: 8 (over z, y), tensor: 4 (over x, core).
Axes of the slice: x: 2, y: 2, z: 4, core: 2. Of those that a mesh axis runs over, the one named last changes fastest.
Arguments:
- tokens: bfloat16 [12608, 768], P('expert'), may hold values from -16 to 16
- gain_attn: float32 [768], replicated, may hold values from 0.5 to 1.5
- shift_attn: float32 [768], replicated, may hold values from -1.5 to 1.5
- qkv_weight: bfloat16 [3, 768, 768], P(None, None, 'tensor'), may hold values from -0.21875 to 0.21875
- out_weight: bfloat16 [768, 768], P('tensor'), may hold values from -1.75 to 1.75
- gain_moe: float32 [768], replicated, may hold values from 0.5 to 1.5
- shift_moe: float32 [768], replicated, may hold values from -1.5 to 1.5
- router_weight: bfloat16 [768, 4], replicated, may hold values from -0.15625 to 0.15625
- expert_up: bfloat16 [8, 768, 1536], P('expert', None, 'tensor'), may hold values from -0.21875 to 0.21875
- expert_down: bfloat16 [8, 1536, 768], P('expert', 'tensor'), may hold values from -0.21875 to 0.21875
- routes: int32 [12608, 2], P('expert'), may hold values from 0 to 3, all different within a row; in each aligned block of 1576 rows (0 to 1575, 1576 to 3151, ...) at most 1379 rows name the same one
- keep_mask: int32 [12608, 2], P('expert'), may hold values 0 or 1
- cotangent: bfloat16 [12608, 768], P('expert', 'tensor'), may hold values from -6 to 6
Outputs:
- mixed: bfloat16 [12608, 768], P('expert', 'tensor')
- grad_tokens: float32 [12608, 768], P('expert')
- grad_gain_attn: float32 [768], replicated
- grad_shift_attn: float32 [768], replicated
- grad_qkv: float32 [3, 768, 768], P(None, None, 'tensor')
- grad_out: float32 [768, 768], P('tensor')
- grad_gain_moe: float32 [768], replicated
- grad_shift_moe: float32 [768], replicated
- grad_router: float32 [768, 4], replicated
- grad_up: float32 [8, 768, 1536], P('expert', None, 'tensor')
- grad_down: float32 [8, 1536, 768], P('expert', 'tensor')
Inputs may be any that keep to these rules, and one draw needn't show every extreme that they name: `routes`: each row names two different experts. Within each aligned block of 1576 rows (rows 0 to 1575, 1576 to 3151 and so on), each expert is named at most 1379 times.
All inputs are finite; a program needn't handle non-finite values. No bound on the sum of `keep_mask` on one device may be relied on, other than what follows from the above.
Results may differ from a plain program's by a relative error of at most 0.015.
Values may be sent and summed in bfloat16 or wider, within the bound.
A program may use at most 320 MiB of HBM per device.

v0:
```python
from functools import partial

import jax
import jax.numpy as jnp
from jax import lax
from jax.sharding import PartitionSpec as P

HD = 64
SEQ = 197


norm_epsilon = 1e-06


def norm_rows(values, gain, shift):
    row_mean = jnp.mean(values, axis=-1, keepdims=True)
    centred = values - row_mean
    spread = jnp.mean(centred * centred, axis=-1, keepdims=True)
    return centred * lax.rsqrt(spread + norm_epsilon) * gain + shift


def gelu_exact(values):
    return jax.nn.gelu(values, approximate=False)


def gate_from_logits(logit_rows, picked_rows, keep_rows):
    router_probs = jax.nn.softmax(logit_rows, axis=-1)
    return jnp.sum(jnp.where(picked_rows, router_probs[:, None, :], 0.0), axis=-1) * keep_rows


def attention_forward(h_rows, qkv_w, out_w):
    row_total_count = h_rows.shape[0]
    head_count = qkv_w.shape[2] // HD
    image_count = row_total_count // SEQ
    score_scale = HD ** (-0.5)
    projected = jnp.einsum("td,cdf->ctf", h_rows, qkv_w, preferred_element_type=jnp.float32).astype(
        jnp.bfloat16
    )
    split_heads = projected.reshape(3, image_count, SEQ, head_count, HD)
    queries = split_heads[0]
    keys_all = split_heads[1]
    values_all = split_heads[2]
    scores = (
        jnp.einsum("gqhe,gkhe->ghqk", queries, keys_all, preferred_element_type=jnp.float32)
        * score_scale
    )
    row_peak = jnp.max(scores, axis=-1, keepdims=True)
    exp_scores = jnp.exp(scores - row_peak)
    row_total = jnp.sum(exp_scores, axis=-1, keepdims=True)
    log_total = row_peak + jnp.log(row_total)
    weights = (exp_scores / row_total).astype(jnp.bfloat16)
    attended = jnp.einsum(
        "ghqk,gkhe->gqhe", weights, values_all, preferred_element_type=jnp.float32
    ).astype(jnp.bfloat16)
    attended = attended.reshape(row_total_count, head_count * HD)
    partial_out = jnp.dot(attended, out_w, preferred_element_type=jnp.float32)
    return (partial_out, (attended, queries, keys_all, values_all, log_total))


def attention_backward(grad_branch, saved, h_rows, qkv_w, out_w):
    attended, queries, keys_all, values_all, log_total = saved
    row_total_count = h_rows.shape[0]
    head_count = qkv_w.shape[2] // HD
    image_count = row_total_count // SEQ
    score_scale = HD ** (-0.5)
    grad_out = jnp.einsum("tc,td->cd", attended, grad_branch, preferred_element_type=jnp.float32)
    grad_attended = jnp.einsum(
        "td,cd->tc", grad_branch, out_w, preferred_element_type=jnp.float32
    ).astype(jnp.bfloat16)
    grad_attended = grad_attended.reshape(image_count, SEQ, head_count, HD)
    scores_again = (
        jnp.einsum("gqhe,gkhe->ghqk", queries, keys_all, preferred_element_type=jnp.float32)
        * score_scale
    )
    probs_again = jnp.exp(scores_again - log_total)
    grad_weights = jnp.einsum(
        "gqhe,gkhe->ghqk", grad_attended, values_all, preferred_element_type=jnp.float32
    )
    grad_scores = (
        probs_again * (grad_weights - jnp.sum(probs_again * grad_weights, axis=-1, keepdims=True))
    ).astype(jnp.bfloat16)
    grad_queries = (
        jnp.einsum("ghqk,gkhe->gqhe", grad_scores, keys_all, preferred_element_type=jnp.float32)
        * score_scale
    )
    grad_keys = (
        jnp.einsum("ghqk,gqhe->gkhe", grad_scores, queries, preferred_element_type=jnp.float32)
        * score_scale
    )
    grad_values = jnp.einsum(
        "ghqk,gqhe->gkhe",
        probs_again.astype(jnp.bfloat16),
        grad_attended,
        preferred_element_type=jnp.float32,
    )
    grad_rows = (
        jnp.stack([grad_queries, grad_keys, grad_values])
        .astype(jnp.bfloat16)
        .reshape(3, row_total_count, head_count * HD)
    )
    grad_qkv = jnp.einsum("td,ctf->cdf", h_rows, grad_rows, preferred_element_type=jnp.float32)
    grad_h_one = jnp.einsum("ctf,cdf->td", grad_rows, qkv_w, preferred_element_type=jnp.float32)
    return (grad_qkv, grad_out, grad_h_one)


def moe_tail(
    grad_h_rows,
    grad_gate_rows,
    grad_out_rows,
    h_two_rows,
    resid_rows,
    gate_back,
    router_weight,
    gain_moe,
    shift_moe,
):
    row_total_count = grad_h_rows.shape[0]
    grad_gate = jnp.sum(grad_gate_rows.reshape(row_total_count, -1, 2), axis=1)
    grad_logits = gate_back(grad_gate)[0].astype(jnp.bfloat16)
    grad_router = jnp.einsum(
        "td,te->de", h_two_rows, grad_logits, preferred_element_type=jnp.float32
    )
    grad_h_two = grad_h_rows + jnp.einsum(
        "te,de->td", grad_logits, router_weight, preferred_element_type=jnp.float32
    )
    norm_out, norm_back = jax.vjp(norm_rows, resid_rows, gain_moe, shift_moe)
    grad_resid_norm, grad_gain_moe, grad_shift_moe = norm_back(grad_h_two)
    return (grad_out_rows + grad_resid_norm, grad_router, grad_gain_moe, grad_shift_moe)


def per_device(
    tokens,
    gain_attn,
    shift_attn,
    qkv_weight,
    out_weight,
    gain_moe,
    shift_moe,
    router_weight,
    expert_up,
    expert_down,
    routes,
    keep_mask,
    cotangent,
):
    row_count, feature_count = tokens.shape
    tensor_count = lax.axis_size("tensor")
    expert_count = lax.axis_size("expert")
    tensor_here = lax.axis_index("tensor")
    quarter_width = feature_count // tensor_count
    col_start = tensor_here * quarter_width
    experts_all = router_weight.shape[1]
    capacity = max(2, 7 * row_count // (2 * experts_all))
    tokens_float = tokens.astype(jnp.float32)
    h_one = norm_rows(tokens_float, gain_attn, shift_attn).astype(jnp.bfloat16)
    partial_out, saved = attention_forward(h_one, qkv_weight, out_weight)
    branch = lax.psum(partial_out, "tensor")
    resid = tokens_float + branch
    h_two = norm_rows(resid, gain_moe, shift_moe).astype(jnp.bfloat16)
    logits = jnp.dot(h_two, router_weight, preferred_element_type=jnp.float32)
    keep_float = keep_mask.astype(jnp.float32)
    picked = routes[:, :, None] == jnp.arange(experts_all, dtype=jnp.int32)[None, None, :]
    gate_values, gate_back = jax.vjp(
        partial(gate_from_logits, picked_rows=picked, keep_rows=keep_float), logits
    )
    flat_expert = routes.reshape(-1)
    one_hot = (flat_expert[:, None] == jnp.arange(experts_all, dtype=jnp.int32)[None, :]).astype(
        jnp.int32
    )
    rank_within = jnp.sum((jnp.cumsum(one_hot, axis=0) - one_hot) * one_hot, axis=1)
    slot_index = flat_expert * capacity + rank_within
    token_index = jnp.repeat(jnp.arange(row_count, dtype=jnp.int32), 2)
    live_route = keep_mask.reshape(-1) > 0
    source_table = (
        jnp.full((experts_all * capacity,), row_count, jnp.int32)
        .at[slot_index]
        .set(jnp.where(live_route, token_index, row_count))
    )
    padded_rows = jnp.concatenate([h_two, jnp.zeros((1, feature_count), jnp.bfloat16)], axis=0)
    dispatch = padded_rows[source_table].reshape(experts_all, capacity, feature_count)
    paired = jnp.broadcast_to(dispatch[:, None], (experts_all, 2, capacity, feature_count)).reshape(
        expert_count, capacity, feature_count
    )
    arrived = lax.all_to_all(paired, "expert", split_axis=0, concat_axis=0, tiled=True)
    expert_rows = arrived.reshape(expert_count * capacity, feature_count)
    up_local = expert_up[0]
    down_local = expert_down[0]
    pre_act = jnp.dot(expert_rows, up_local, preferred_element_type=jnp.float32)
    hidden_float, gelu_back = jax.vjp(gelu_exact, pre_act)
    hidden = hidden_float.astype(jnp.bfloat16)
    partial_down = jnp.dot(hidden, down_local, preferred_element_type=jnp.float32)
    summed = lax.psum_scatter(partial_down, "tensor", scatter_dimension=1, tiled=True)
    returned = lax.all_to_all(
        summed.reshape(expert_count, capacity, quarter_width),
        "expert",
        split_axis=0,
        concat_axis=0,
        tiled=True,
    )
    answer_table = jnp.sum(
        returned.reshape(experts_all, 2, capacity, quarter_width), axis=1
    ).astype(jnp.bfloat16)
    answers = (
        answer_table.reshape(experts_all * capacity, quarter_width)[slot_index]
        .astype(jnp.float32)
        .reshape(row_count, 2, quarter_width)
    )
    resid_part = lax.dynamic_slice_in_dim(resid, col_start, quarter_width, 1)
    mixed = (resid_part + jnp.sum(gate_values[:, :, None] * answers, axis=1)).astype(jnp.bfloat16)
    grad_part = cotangent.astype(jnp.float32)
    grad_answers = (
        (gate_values[:, :, None] * grad_part[:, None, :])
        .astype(jnp.bfloat16)
        .reshape(2 * row_count, quarter_width)
    )
    grad_gate_part = jnp.sum(grad_part[:, None, :] * answers, axis=-1)
    outgoing = (
        jnp.zeros((experts_all * capacity, quarter_width), jnp.bfloat16)
        .at[slot_index]
        .set(grad_answers)
    )
    outgoing = jnp.broadcast_to(
        outgoing.reshape(experts_all, 1, capacity, quarter_width),
        (experts_all, 2, capacity, quarter_width),
    ).reshape(expert_count, capacity, quarter_width)
    incoming = lax.all_to_all(outgoing, "expert", split_axis=0, concat_axis=0, tiled=True)
    grad_full = lax.all_gather(incoming, "tensor", axis=2, tiled=True).reshape(
        expert_count * capacity, feature_count
    )
    grad_hidden = jnp.einsum("rd,fd->rf", grad_full, down_local, preferred_element_type=jnp.float32)
    grad_pre = gelu_back(grad_hidden)[0].astype(jnp.bfloat16)
    grad_down = jnp.einsum("rf,rd->fd", hidden, grad_full, preferred_element_type=jnp.float32)
    grad_up = jnp.einsum("rd,rf->df", expert_rows, grad_pre, preferred_element_type=jnp.float32)
    grad_rows_partial = jnp.einsum(
        "rf,df->rd", grad_pre, up_local, preferred_element_type=jnp.float32
    )
    grad_rows_sum = lax.psum_scatter(
        grad_rows_partial.astype(jnp.bfloat16), "tensor", scatter_dimension=1, tiled=True
    ).astype(jnp.float32)
    sent_back = lax.all_to_all(
        grad_rows_sum.reshape(expert_count, capacity, quarter_width).astype(jnp.bfloat16),
        "expert",
        split_axis=0,
        concat_axis=0,
        tiled=True,
    ).astype(jnp.float32)
    grad_table = jnp.sum(sent_back.reshape(experts_all, 2, capacity, quarter_width), axis=1).astype(
        jnp.bfloat16
    )
    grad_inputs = (
        grad_table.reshape(experts_all * capacity, quarter_width)[slot_index]
        .astype(jnp.float32)
        .reshape(row_count, 2, quarter_width)
    )
    grad_h_part = jnp.sum(grad_inputs * keep_float[:, :, None], axis=1)
    grad_h_full, grad_gate_all, grad_out_full = (
        lax.all_gather(grad_h_part, "tensor", axis=1, tiled=True),
        lax.all_gather(grad_gate_part, "tensor", axis=1, tiled=True),
        lax.all_gather(grad_part, "tensor", axis=1, tiled=True),
    )
    grad_resid, grad_router, grad_gain_moe, grad_shift_moe = moe_tail(
        grad_h_full,
        grad_gate_all,
        grad_out_full,
        h_two,
        resid,
        gate_back,
        router_weight,
        gain_moe,
        shift_moe,
    )
    grad_qkv, grad_out, grad_h_one_part = attention_backward(
        grad_resid.astype(jnp.bfloat16), saved, h_one, qkv_weight, out_weight
    )
    grad_h_one = lax.psum(grad_h_one_part.astype(jnp.bfloat16), "tensor").astype(jnp.float32)
    norm_one_out, norm_one_back = jax.vjp(norm_rows, tokens_float, gain_attn, shift_attn)
    grad_tok_norm, grad_gain_attn, grad_shift_attn = norm_one_back(grad_h_one)
    grad_tokens = grad_resid + grad_tok_norm
    summed_grads = lax.psum(
        (
            grad_gain_attn,
            grad_shift_attn,
            grad_qkv,
            grad_out,
            grad_gain_moe,
            grad_shift_moe,
            grad_router,
        ),
        "expert",
    )
    grad_qkv_mine = summed_grads[2]
    grad_out_mine = summed_grads[3]
    return (
        mixed,
        grad_tokens,
        summed_grads[0],
        summed_grads[1],
        grad_qkv_mine,
        grad_out_mine,
        summed_grads[4],
        summed_grads[5],
        summed_grads[6],
        grad_up[None],
        grad_down[None],
    )


def solution(mesh):
    placed = (
        P("expert", None),
        P(),
        P(),
        P(None, None, "tensor"),
        P("tensor", None),
        P(),
        P(),
        P(),
        P("expert", None, "tensor"),
        P("expert", "tensor", None),
        P("expert", None),
        P("expert", None),
        P("expert", "tensor"),
    )
    return jax.shard_map(
        per_device,
        mesh=mesh,
        in_specs=placed,
        out_specs=(
            P("expert", "tensor"),
            P("expert", None),
            P(),
            P(),
            P(None, None, "tensor"),
            P("tensor", None),
            P(),
            P(),
            P(),
            P("expert", None, "tensor"),
            P("expert", "tensor", None),
        ),
        check_vma=False,
    )
```

profile of v0, /device:TPU:0, one launch (start us, length us, event | category | flops | bytes accessed | tf_op | source)
XLA Modules:
  0.0 1661.6 jit_solution(16342742900339136870)
XLA Ops:
  60.5 76.8 %all-reduce.8.cloned.1.call-done = f32[1576,768]{1,0:T(8,128)} async-done(((f32[1576,768]{1,0:T(8,128)}), f32[1576,768]{1,0:T(8,128)}) %all-reduce.8.cloned.1.call-update) | async-done | bytes 4841488 | tf_op jit(solution)/shard_map/psum | solution.py:157
  145.6 28.6 %scatter_custom_fusion.1 = bf16[5516,192]{1,0:T(8,128)(2,1)} fusion(s32[3152]{0:T(1024)S(1)} %fusion.67, f32[3152,192]{1,0:T(8,128)} %mul.287, f32[3152]{0:T(1024)S(1)} %mul.284, bf16[]{:T(256)} %constant.15.clone.1), kind=kCustom, calls=%fused_computation.73 | custom fusion | flops 1210368 | bytes 4555266 | tf_op jit(solution)/shard_map/scatter | solution.py:220
  191.5 15.9 scatter_custom_fusion
  209.2 17.3 %gather_fusion = bf16[5516,768]{1,0:T(8,128)(2,1)} fusion(bf16[1577,768]{1,0:T(8,128)(2,1)S(1)} %concatenate.5, s32[6144]{0:T(1024)S(1)} %pad_clamp_fusion), kind=kCustom, calls=%fused_computation | custom fusion | bytes 16967216 | tf_op jit(solution)/shard_map/gather | solution.py:180
  226.5 8.9 broadcast_in_dim.60
  235.4 50.6 %all-to-all-done.2 = bf16[8,1379,192]{1,2,0:T(8,128)(2,1)} async-done(((bf16[8,1379,192]{1,2,0:T(8,128)(2,1)}), bf16[8,1379,192]{1,2,0:T(8,128)(2,1)}, u32[]{:S(2)}, u32[]{:S(2)}) %all-to-all-start.2) | async-done | bytes 4236320 | tf_op jit(solution)/shard_map/all_to_all | solution.py:226
  286.0 10.5 broadcast_in_dim.61
  302.4 6.7 copy.199
  309.1 359.9 %all-to-all-done = bf16[8,1379,768]{2,1,0:T(8,128)(2,1)} async-done(((bf16[8,1379,768]{2,1,0:T(8,128)(2,1)}), bf16[8,1379,768]{2,1,0:T(8,128)(2,1)}, u32[]{:S(2)}, u32[]{:S(2)}) %all-to-all-start) | async-done | bytes 16945184 | tf_op jit(solution)/shard_map/all_to_all | solution.py:184
  669.1 16.6 reshape.249
  685.7 47.7 %multiply_convert_fusion = (bf16[11032,384]{1,0:T(8,128)(2,1)}, f32[11032,384]{1,0:T(8,128)}, f32[11032,384]{1,0:T(8,128)}) fusion(bf16[11032,768]{1,0:T(8,128)(2,1)} %reshape.249, bf16[1,768,384]{2,1,0:T(8,128)(2,1)S(1)} %copy-done.57), kind=kOutput, calls=%fused_computation.9 | convolution fusion | flops 6782297088 | bytes 59897856 | tf_op jit(solution)/shard_map/dot_general | solution.py:188
  733.4 29.6 %reshape.310 = bf16[11032,768]{0,1:T(8,128)(2,1)} reshape(bf16[8,1379,768]{1,0,2:T(8,128)(2,1)} %all-gather.7.cloned.1.call-done) | data formatting | bytes 33890304 | tf_op jit(solution)/shard_map/reshape | solution.py:227
  763.0 25.6 %add_convert_fusion = bf16[11032,384]{1,0:T(8,128)(2,1)} fusion(f32[11032,384]{1,0:T(8,128)} %get-tuple-element.96, f32[11032,384]{1,0:T(8,128)} %get-tuple-element.106, bf16[11032,768]{0,1:T(8,128)(2,1)} %reshape.310, bf16[1,384,768]{2,1,0:T(8,128)(2,1)S(1)} %copy-done.20), kind=kOutput, calls=%fused_computation.8 | convolution fusion | flops 6566246400 | bytes 59897856 | tf_op jit(solution)/shard_map/rd,fd->rf/dot_general | solution.py:230
  788.6 15.6 convolution_convert_fusion
  804.2 25.1 %fusion.58 = f32[11032,768]{0,1:T(8,128)} fusion(bf16[11032,384]{1,0:T(8,128)(2,1)} %get-tuple-element.95, bf16[1,384,768]{2,1,0:T(8,128)(2,1)S(1)} %copy-done.20), kind=kOutput, calls=%fused_computation.103 | convolution fusion | flops 6506938368 | bytes 42952704 | tf_op jit(solution)/shard_map/dot_general | solution.py:191
  829.4 101.9 %reduce-scatter.5.cloned.1.call-done = bf16[11032,192]{0,1:T(8,128)(2,1)} async-done(((bf16[11032,768]{0,1:T(8,128)(2,1)}), bf16[11032,192]{0,1:T(8,128)(2,1)}) %reduce-scatter.5.cloned.1.call-update) | async-done | bytes 4236304 | tf_op jit(solution)/shard_map/reduce_scatter | solution.py:237
  931.3 9.4 convert_element_type.131
  940.7 6.4 copy.201
  952.5 220.3 %reduce-scatter.3.cloned.1.call-done = f32[11032,192]{0,1:T(8,128)} async-done(((f32[11032,768]{0,1:T(8,128)}), f32[11032,192]{0,1:T(8,128)}) %reduce-scatter.3.cloned.1.call-update) | async-done | bytes 8472592 | tf_op jit(solution)/shard_map/reduce_scatter | solution.py:192
  1172.8 10.7 reshape.250
  1183.5 8.5 copy.192
  1211.5 9.6 gather_fusion.2
  1224.1 17.9 %multiply_reduce_fusion.6 = f32[1576,192]{1,0:T(8,128)S(1)} fusion(f32[1576,2,192]{2,1,0:T(2,128)} %reshape.260, f32[1576,2]{1,0:T(8,128)S(1)} %copy-done.13), kind=kLoop, calls=%fused_computation.60 | loop fusion | flops 907776 | bytes 3643712 | tf_op jit(solution)/shard_map/reduce_sum | solution.py:255
  1249.9 17.1 %convolution_bitcast_fusion.1 = f32[1,768,384]{2,1,0:T(8,128)} fusion(bf16[11032,768]{1,0:T(8,128)(2,1)} %reshape.249, bf16[11032,384]{1,0:T(8,128)(2,1)} %add_convert_fusion), kind=kOutput, calls=%fused_computation.81 | convolution fusion | flops 6506938368 | bytes 26597376 | tf_op jit(solution)/shard_map/rd,rf->df/dot_general | solution.py:233
  1267.0 11.4 convolution_bitcast_fusion
  1290.0 96.5 %all-to-all-done.1 = f32[8,1379,192]{1,2,0:T(8,128)} async-done(((f32[8,1379,192]{1,2,0:T(8,128)}), f32[8,1379,192]{1,2,0:T(8,128)}, u32[]{:S(2)}, u32[]{:S(2)}) %all-to-all-start.1) | async-done | bytes 8472608 | tf_op jit(solution)/shard_map/all_to_all | solution.py:193
  1398.2 10.7 gather_fusion.1
  1414.1 19.2 %multiply_reduce_fusion.5 = (f32[1576,2]{1,0:T(8,128)}, f32[1576,192]{1,0:T(8,128)}) fusion(f32[1576,2,192]{2,1,0:T(2,128)} %reshape.259, f32[1576,192]{1,0:T(8,128)S(1)} %copy-done.8, f32[1576,2]{1,0:T(8,128)} %copy-done.9), kind=kLoop, calls=%fused_computation.59 | loop fusion | flops 2114992 | bytes 4866688 | tf_op jit(solution)/shard_map/reduce_sum | solution.py:216
  1440.3 6.3 multiply_reduce_fusion.1
  1491.2 44.3 %all-reduce.10.cloned.1.call-done = bf16[1576,768]{1,0:T(8,128)(2,1)} async-done(((bf16[1576,768]{1,0:T(8,128)(2,1)}), bf16[1576,768]{1,0:T(8,128)(2,1)}) %all-reduce.10.cloned.1.call-update) | async-done | bytes 2420752 | tf_op jit(solution)/shard_map/psum | solution.py:275
  1541.9 39.2 %all-reduce.2 = (f32[768]{0:T(1024)}, f32[768]{0:T(1024)}, f32[768]{0:T(1024)}, f32[768]{0:T(1024)}, f32[768,4]{0,1:T(4,128)}) all-reduce(f32[768]{0:T(1024)S(1)} %get-tuple-element.79, f32[768]{0:T(1024)S(1)} %get-tuple-element.84, f32[768]{0:T(1024)S(1)} %get-tuple-element.77, ...), channel_id=1, replica_groups=mesh['expert'=8,'tensor'=4] {'expert'}, use_global_device_ids=true, to_apply=%region_32.33 | all-reduce | flops 6144 | bytes 49152 | tf_op jit(solution)/shard_map/psum | solution.py:279
  1586.6 63.3 %all-reduce.12.cloned.1.call-done = (f32[3,768,192]{1,2,0:T(8,128)}, f32[192,768]{1,0:T(8,128)}) async-done(((f32[3,768,192]{1,2,0:T(8,128)}, f32[192,768]{1,0:T(8,128)}), (f32[3,768,192]{1,2,0:T(8,128)}, f32[192,768]{1,0:T(8,128)})) %all-reduce.12.cloned.1.call-update) | async-done | bytes 2359312 | tf_op jit(solution)/shard_map/psum | solution.py:279
  (280 shorter events, 217.9 us)
Async XLA Ops:
  7.2 130.1 %all-reduce.8.cloned.1.call-start = ((), (), s32[]{:S(2)}) async-start(), calls=%async_computation.6 | async-start | bytes 9682944 | tf_op jit(solution)/shard_map/psum | solution.py:157
  60.5 130.9 %copy-start.47 = (s32[3152]{0:T(1024)}, s32[3152]{0:T(1024)S(1)}, u32[]{:S(2)}) copy-start(s32[3152]{0:T(1024)S(1)} %fusion.67) | copy-start | bytes 37828
  145.2 29.0 %copy-start.9 = (f32[1576,2]{1,0:T(8,128)}, f32[1576,2]{1,0:T(8,128)S(1)}, u32[]{:S(2)}) copy-start(f32[1576,2]{1,0:T(8,128)S(1)} %copy.188) | copy-start | bytes 37828
  184.4 101.7 %all-to-all-start.2 = ((bf16[8,1379,192]{1,2,0:T(8,128)(2,1)}), bf16[8,1379,192]{1,2,0:T(8,128)(2,1)}, u32[]{:S(2)}, u32[]{:S(2)}) async-start(bf16[8,1379,192]{1,2,0:T(8,128)(2,1)} %bitcast.126), calls=%async_computation.3 | async-start | bytes 8650752 | tf_op jit(solution)/shard_map/all_to_all | solution.py:226
  296.6 372.5 %all-to-all-start = ((bf16[8,1379,768]{2,1,0:T(8,128)(2,1)}), bf16[8,1379,768]{2,1,0:T(8,128)(2,1)}, u32[]{:S(2)}, u32[]{:S(2)}) async-start(bf16[8,1379,768]{2,1,0:T(8,128)(2,1)} %bitcast.123), calls=%async_computation | async-start | bytes 34013184 | tf_op jit(solution)/shard_map/all_to_all | solution.py:184
  302.3 431.0 %all-gather.7.cloned.1.call-start = ((), (), s32[]{:S(2)}) async-start(), calls=%async_computation.9 | async-start | bytes 21626880 | tf_op jit(solution)/shard_map/all_gather | solution.py:227
  309.1 376.6 %copy-start.57 = (bf16[1,768,384]{2,1,0:T(8,128)(2,1)S(1)}, bf16[1,768,384]{2,1,0:T(8,128)(2,1)}, u32[]{:S(2)}) copy-start(bf16[1,768,384]{2,1,0:T(8,128)(2,1)} %param.21) | copy-start | bytes 1769476
  309.1 622.2 %reduce-scatter.5.cloned.1.call-start = ((), (), s32[]{:S(2)}) async-start(), calls=%async_computation.10 | async-start | bytes 21381120 | tf_op jit(solution)/shard_map/reduce_scatter | solution.py:237
  733.4 29.6 %copy-start.20 = (bf16[1,384,768]{2,1,0:T(8,128)(2,1)S(1)}, bf16[1,384,768]{2,1,0:T(8,128)(2,1)}, u32[]{:S(2)}) copy-start(bf16[1,384,768]{2,1,0:T(8,128)(2,1)} %param.22) | copy-start | bytes 1769476
  804.2 368.6 %reduce-scatter.3.cloned.1.call-start = ((), (), s32[]{:S(2)}) async-start(), calls=%async_computation.7 | async-start | bytes 42762240 | tf_op jit(solution)/shard_map/reduce_scatter | solution.py:192
  947.1 245.0 %all-to-all-start.3 = ((bf16[8,1379,192]{1,2,0:T(8,128)(2,1)}), bf16[8,1379,192]{1,2,0:T(8,128)(2,1)}, u32[]{:S(2)}, u32[]{:S(2)}) async-start(bf16[8,1379,192]{1,2,0:T(8,128)(2,1)} %copy.201), calls=%async_computation.5 | async-start | bytes 8650752 | tf_op jit(solution)/shard_map/all_to_all | solution.py:240
  1192.0 194.4 %all-to-all-start.1 = ((f32[8,1379,192]{1,2,0:T(8,128)}), f32[8,1379,192]{1,2,0:T(8,128)}, u32[]{:S(2)}, u32[]{:S(2)}) async-start(f32[8,1379,192]{1,2,0:T(8,128)} %copy.192), calls=%async_computation.2 | async-start | bytes 17301504 | tf_op jit(solution)/shard_map/all_to_all | solution.py:193
  1197.7 46.1 %all-gather.5.cloned.1.call-start = ((), (), s32[]{:S(2)}) async-start(), calls=%async_computation.8 | async-start | bytes 6389760 | tf_op jit(solution)/shard_map/all_gather | solution.py:259
  1198.9 85.1 %all-gather.9.cloned.1.call-start = ((), (), s32[]{:S(2)}) async-start(), calls=%async_computation.11 | async-start | bytes 6389760 | tf_op jit(solution)/shard_map/all_gather | solution.py:257
  1224.1 19.6 %copy-start.22 = (f32[8,3,197]{2,1,0:T(4,128)S(1)}, f32[8,3,197]{2,1,0:T(4,128)}, u32[]{:S(2)}) copy-start(f32[8,3,197]{2,1,0:T(4,128)} %copy-done.21) | copy-start | bytes 56740
  1224.1 19.6 %copy-start.36 = (f32[8,3,197]{2,1,0:T(4,128)S(1)}, f32[8,3,197]{2,1,0:T(4,128)}, u32[]{:S(2)}) copy-start(f32[8,3,197]{2,1,0:T(4,128)} %copy-done.35) | copy-start | bytes 56740
  1224.1 19.6 %copy-start.38 = (f32[1576]{0:T(1024)S(1)}, f32[1576]{0:T(1024)}, u32[]{:S(2)}) copy-start(f32[1576]{0:T(1024)} %copy-done.37) | copy-start | bytes 18916
  1243.6 291.9 %all-reduce.10.cloned.1.call-start = ((), (), s32[]{:S(2)}) async-start(), calls=%async_computation.12 | async-start | bytes 4841472 | tf_op jit(solution)/shard_map/psum | solution.py:275
  1243.8 23.2 %slice-start.6 = ((s8[8472576]{0:T(1024)(128)(4,1)}), s8[83968]{0:T(1024)(128)(4,1)S(1)}, s32[]{:S(2)}) async-start(s8[8472576]{0:T(1024)(128)(4,1)} %bitcast.127), calls=%async_computation.20 | async-start | bytes 167936
  1249.9 17.1 %slice-start.7 = ((s8[8472576]{0:T(1024)(128)(4,1)}), s8[4194304]{0:T(1024)(128)(4,1)S(1)}, s32[]{:S(2)}) async-start(s8[8472576]{0:T(1024)(128)(4,1)} %bitcast.127), calls=%async_computation.21 | async-start | bytes 8388608
  1249.9 17.1 %slice-start.8 = ((s8[8472576]{0:T(1024)(128)(4,1)}), s8[4194304]{0:T(1024)(128)(4,1)S(1)}, s32[]{:S(2)}) async-start(s8[8472576]{0:T(1024)(128)(4,1)} %bitcast.127), calls=%async_computation.22 | async-start | bytes 8388608
  1414.0 26.1 %copy-start.40 = (s32[1576,2]{0,1:T(2,128)S(1)}, s32[1576,2]{0,1:T(2,128)}, u32[]{:S(2)}) copy-start(s32[1576,2]{0,1:T(2,128)} %param.24) | copy-start | bytes 37828
  1414.0 26.1 %copy-start.26 = (s32[1576,2]{0,1:T(2,128)S(1)}, s32[1576,2]{0,1:T(2,128)}, u32[]{:S(2)}) copy-start(s32[1576,2]{0,1:T(2,128)} %param.23) | copy-start | bytes 37828
  1414.0 26.2 %copy-start.19 = (f32[1576,4]{0,1:T(4,128)S(1)}, f32[1576,4]{0,1:T(4,128)}, u32[]{:S(2)}) copy-start(f32[1576,4]{0,1:T(4,128)} %copy-done.18) | copy-start | bytes 75652
  1414.0 26.2 %copy-start.32 = (f32[1576]{0:T(1024)S(1)}, f32[1576]{0:T(1024)}, u32[]{:S(2)}) copy-start(f32[1576]{0:T(1024)} %copy-done.31) | copy-start | bytes 18916
  1414.0 26.2 %copy-start.28 = (f32[1576]{0:T(1024)S(1)}, f32[1576]{0:T(1024)}, u32[]{:S(2)}) copy-start(f32[1576]{0:T(1024)} %copy-done.27) | copy-start | bytes 18916
  1414.0 26.2 %copy-start.34 = (f32[1576]{0:T(1024)S(1)}, f32[1576]{0:T(1024)}, u32[]{:S(2)}) copy-start(f32[1576]{0:T(1024)} %copy-done.33) | copy-start | bytes 18916
  1414.0 26.2 %copy-start.51 = (f32[768]{0:T(1024)S(1)}, f32[768]{0:T(1024)}, u32[]{:S(2)}) copy-start(f32[768]{0:T(1024)} %param.18) | copy-start | bytes 9220
  1414.0 26.2 %copy-start.55 = (bf16[768,4]{0,1:T(4,128)(2,1)S(1)}, bf16[768,4]{0,1:T(4,128)(2,1)}, u32[]{:S(2)}) copy-start(bf16[768,4]{0,1:T(4,128)(2,1)} %param.20) | copy-start | bytes 18436
  1414.1 32.6 %slice-start = ((s8[4841472]{0:T(1024)(128)(4,1)}), s8[647168]{0:T(1024)(128)(4,1)S(1)}, s32[]{:S(2)}) async-start(s8[4841472]{0:T(1024)(128)(4,1)} %bitcast.119), calls=%async_computation.14 | async-start | bytes 1294336
  1480.6 169.3 %all-reduce.12.cloned.1.call-start = ((), (), s32[]{:S(2)}) async-start(), calls=%async_computation.13 | async-start | bytes 4718592 | tf_op jit(solution)/shard_map/psum | solution.py:279
  1491.2 48.0 %copy-start.44 = (f32[1576]{0:T(1024)S(1)}, f32[1576]{0:T(1024)}, u32[]{:S(2)}) copy-start(f32[1576]{0:T(1024)} %copy-done.43) | copy-start | bytes 18916
  (49 other events, 183.1 us)
Sparse Core Ops, SparseCore 0:
  38.5 98.7 all-reduce.7
  309.2 112.0 all-gather.6
  804.3 126.9 reduce-scatter.4
  933.9 238.8 reduce-scatter.2
  1200.3 40.1 all-gather.4
  1243.7 40.2 all-gather.8
  1480.6 54.8 all-reduce.9
  1540.1 109.6 all-reduce.11
where the time goes:
time: 1670 us; the launch traced here: 1660 us
  waiting for transfers between devices  1020 us (61%)
  local copies, waits for them, and re-layouts  270 us (16%)
  matrix products  185 us (11%)
  other arithmetic  105 us (6%)
  blocking collectives  44.5 us (3%)
  starting transfers between devices  22.9 us (1%)
    all_to_all x1, waiting for transfers between devices, per_device(): lax.all_to_all(paired, 'expert', split_axis=0, concat_axis=0, tiled=True)  360 us
    reduce_scatter x1, waiting for transfers between devices, per_device(): lax.psum_scatter(partial_down, 'tensor', scatter_dimension=1, tiled=True)  220 us
    reduce_scatter x1, waiting for transfers between devices, per_device(): lax.psum_scatter(grad_rows_partial.astype(jnp.bfloat16), 'tensor', scatte...  102 us
    all_to_all x1, waiting for transfers between devices, per_device(): lax.all_to_all(summed.reshape(expert_count, capacity, quarter_width), 'ex...  96.5 us
    psum x1, waiting for transfers between devices, per_device(): branch = lax.psum(partial_out, 'tensor')  76.8 us
    psum x1, waiting for transfers between devices, per_device(): lax.psum((grad_gain_attn, grad_shift_attn, grad_qkv, grad_out, grad_gain_...  63.3 us
    all_to_all x1, waiting for transfers between devices, per_device(): lax.all_to_all(outgoing, 'expert', split_axis=0, concat_axis=0, tiled=True)  50.6 us
    dot_general x1, matrix products, per_device(): pre_act = jnp.dot(expert_rows, up_local, preferred_element_type=jnp.float32)  47.7 us
  transfers between devices with their start and end apart: 12, of which 9 were waited for; matrix products, arithmetic and copies ran while one was open for 18% of the time, Pallas kernels for 0%

commit v1 on v0

--- a/solution.py
+++ b/solution.py
@@ -128,7 +128,7 @@
     return (grad_out_rows + grad_resid_norm, grad_router, grad_gain_moe, grad_shift_moe)
 
 
-def per_device(
+def per_device_routed(
     tokens,
     gain_attn,
     shift_attn,
@@ -305,6 +305,131 @@
     )
 
 
+def per_device_dense(
+    tokens,
+    gain_attn,
+    shift_attn,
+    qkv_weight,
+    out_weight,
+    gain_moe,
+    shift_moe,
+    router_weight,
+    expert_up,
+    expert_down,
+    routes,
+    keep_mask,
+    cotangent,
+):
+    row_count, feature_count = tokens.shape
+    tensor_count = lax.axis_size("tensor")
+    tensor_here = lax.axis_index("tensor")
+    quarter_width = feature_count // tensor_count
+    col_start = tensor_here * quarter_width
+    experts_all = router_weight.shape[1]
+    hidden_local = expert_up.shape[2]
+    up_all = lax.all_gather(expert_up[0], "expert", axis=0).reshape(
+        experts_all, 2, feature_count, hidden_local
+    )
+    down_all = lax.all_gather(expert_down[0], "expert", axis=0).reshape(
+        experts_all, 2 * hidden_local, feature_count
+    )
+    up_all = up_all.transpose(2, 0, 1, 3).reshape(feature_count, -1)
+    down_all = down_all.reshape(-1, feature_count)
+    grad_full = lax.all_gather(cotangent, "tensor", axis=1, tiled=True)
+    tokens_float = tokens.astype(jnp.float32)
+    h_one = norm_rows(tokens_float, gain_attn, shift_attn).astype(jnp.bfloat16)
+    partial_out, saved = attention_forward(h_one, qkv_weight, out_weight)
+    branch = lax.psum(partial_out.astype(jnp.bfloat16), "tensor").astype(jnp.float32)
+    resid = tokens_float + branch
+    h_two = norm_rows(resid, gain_moe, shift_moe).astype(jnp.bfloat16)
+    logits = jnp.dot(h_two, router_weight, preferred_element_type=jnp.float32)
+    keep_float = keep_mask.astype(jnp.float32)
+    kept = jnp.sum(
+        jnp.where(
+            routes[:, :, None] == jnp.arange(experts_all, dtype=jnp.int32)[None, None, :],
+            keep_float[:, :, None],
+            0.0,
+        ),
+        axis=1,
+    )
+    router_probs = jax.nn.softmax(logits, axis=-1)
+    gates = kept * router_probs
+    pre_act = jnp.dot(h_two, up_all, preferred_element_type=jnp.float32)
+    hidden, gelu_back = jax.vjp(gelu_exact, pre_act)
+    grad_hidden = jnp.einsum("td,fd->tf", grad_full, down_all, preferred_element_type=jnp.float32)
+    by_expert = (row_count, experts_all, 2 * hidden_local)
+    grad_gate = jnp.sum((hidden * grad_hidden).reshape(by_expert), axis=-1)
+    gated_hidden = (
+        (hidden.reshape(by_expert) * gates[:, :, None]).reshape(row_count, -1).astype(jnp.bfloat16)
+    )
+    grad_pre = gelu_back(
+        (grad_hidden.reshape(by_expert) * gates[:, :, None]).reshape(row_count, -1)
+    )[0].astype(jnp.bfloat16)
+    mixed_part = jnp.dot(gated_hidden, down_all, preferred_element_type=jnp.float32)
+    grad_h_part = jnp.einsum("tf,df->td", grad_pre, up_all, preferred_element_type=jnp.float32)
+    grad_up = jnp.einsum("td,tf->fd", h_two, grad_pre, preferred_element_type=jnp.float32)
+    grad_down = jnp.einsum("tf,td->fd", gated_hidden, grad_full, preferred_element_type=jnp.float32)
+    grad_h_rows = lax.psum(grad_h_part.astype(jnp.bfloat16), "tensor").astype(jnp.float32)
+    grad_gate = lax.psum(grad_gate, "tensor")
+    mixed_sum = lax.psum_scatter(
+        mixed_part.astype(jnp.bfloat16), "tensor", scatter_dimension=1, tiled=True
+    ).astype(jnp.float32)
+    resid_part = lax.dynamic_slice_in_dim(resid, col_start, quarter_width, 1)
+    mixed = (resid_part + mixed_sum).astype(jnp.bfloat16)
+    grad_down = lax.psum_scatter(
+        grad_down.astype(jnp.bfloat16), "expert", scatter_dimension=0, tiled=True
+    ).astype(jnp.float32)
+    grad_up = (
+        lax.psum_scatter(grad_up.astype(jnp.bfloat16), "expert", scatter_dimension=0, tiled=True)
+        .astype(jnp.float32)
+        .T
+    )
+    d_gate = kept * grad_gate
+    grad_logits = (
+        router_probs * (d_gate - jnp.sum(router_probs * d_gate, axis=-1, keepdims=True))
+    ).astype(jnp.bfloat16)
+    grad_router = jnp.einsum("td,te->de", h_two, grad_logits, preferred_element_type=jnp.float32)
+    grad_h_two = grad_h_rows + jnp.einsum(
+        "te,de->td", grad_logits, router_weight, preferred_element_type=jnp.float32
+    )
+    norm_out, norm_back = jax.vjp(norm_rows, resid, gain_moe, shift_moe)
+    grad_resid_norm, grad_gain_moe, grad_shift_moe = norm_back(grad_h_two)
+    grad_resid = grad_full.astype(jnp.float32) + grad_resid_norm
+    grad_qkv, grad_out, grad_h_one_part = attention_backward(
+        grad_resid.astype(jnp.bfloat16), saved, h_one, qkv_weight, out_weight
+    )
+    grad_h_one = lax.psum(grad_h_one_part.astype(jnp.bfloat16), "tensor").astype(jnp.float32)
+    norm_one_out, norm_one_back = jax.vjp(norm_rows, tokens_float, gain_attn, shift_attn)
+    grad_tok_norm, grad_gain_attn, grad_shift_attn = norm_one_back(grad_h_one)
+    grad_tokens = grad_resid + grad_tok_norm
+    grad_qkv, grad_out = lax.psum(
+        (grad_qkv.astype(jnp.bfloat16), grad_out.astype(jnp.bfloat16)), "expert"
+    )
+    small = lax.psum(
+        (grad_gain_attn, grad_shift_attn, grad_gain_moe, grad_shift_moe, grad_router), "expert"
+    )
+    return (
+        mixed,
+        grad_tokens,
+        small[0],
+        small[1],
+        grad_qkv.astype(jnp.float32),
+        grad_out.astype(jnp.float32),
+        small[2],
+        small[3],
+        small[4],
+        grad_up[None],
+        grad_down[None],
+    )
+
+
+def per_device(*arguments):
+    router_weight = arguments[7]
+    if router_weight.shape[1] <= 4:
+        return per_device_dense(*arguments)
+    return per_device_routed(*arguments)
+
+
 def solution(mesh):
     placed = (
         P("expert", None),

time: 1670 us -> 813 us (0.49)
  waiting for transfers between devices: 1020 us -> 362 us
  local copies, waits for them, and re-layouts: 270 us -> 97.4 us
  starting transfers between devices: 22.9 us -> 1.06 us
  matrix products: 185 us -> 165 us
    all_to_all x4 -> x0, waiting for transfers between devices: 507 us -> none  [the longest x1 360 us: per_device(): lax.all_to_all(paired, 'expert', split_axis=0, concat_axis=0, tiled=True)]
    reduce_scatter x2, waiting for transfers between devices: 322 us -> 47.2 us  [the longest x1 47.2 us: per_device_dense(): lax.psum_scatter(grad_down.astype(jnp.bfloat16), 'expert', scatter_dimens...]
    all_gather x3, waiting for transfers between devices: 5.58 us -> 103 us  [the longest x1 81.8 us: per_device_dense(): lax.all_gather(expert_down[0], 'expert', axis=0)]
    convert_element_type x10 -> x0, local copies, waits for them, and re-layouts: 43.3 us -> none  [the longest x2 15.8 us: per_device(): grad_rows_sum.reshape(expert_count, capacity, quarter_width)]
    reshape x5 -> x1, local copies, waits for them, and re-layouts: 65.5 us -> 23.8 us  [per_device_dense(): grad_gate = jnp.sum((hidden * grad_hidden).reshape(by_expert), axis=-1)]
    gather x3 -> x0, local copies, waits for them, and re-layouts: 37.6 us -> none  [the longest x1 17.3 us: per_device(): padded_rows[source_table].reshape(experts_all, capacity, feature_count)]
    convert_element_type x5 -> x8, other arithmetic: 5.02 us -> 38.3 us  [the longest x1 29.5 us: per_device_dense(): grad_pre = gelu_back((grad_hidden.reshape(by_expert) * gates[:, :, None])...]
    broadcast_in_dim x5 -> x0, local copies, waits for them, and re-layouts: 29.6 us -> none  [the longest x2 19.4 us: per_device(): jnp.broadcast_to(dispatch[:, None], (experts_all, 2, capacity, feature_co...]
  transfers between devices with their start and end apart: 12 -> 10, of which waited for: 9 -> 8; matrix products, arithmetic and copies ran while one was open for 18% -> 13% of each run, Pallas kernels for 0% -> 0%
where the time goes in v1:
time: 813 us; the launch traced here: 803 us
  waiting for transfers between devices  362 us (45%)
  matrix products  165 us (20%)
  other arithmetic  111 us (14%)
  local copies, waits for them, and re-layouts  97.4 us (12%)
  blocking collectives  49.7 us (6%)
  between operations  16.7 us (2%)
    all_gather x1, waiting for transfers between devices, per_device_dense(): lax.all_gather(expert_down[0], 'expert', axis=0)  81.8 us
    psum x1, waiting for transfers between devices, per_device_dense(): lax.psum(partial_out.astype(jnp.bfloat16), 'tensor').astype(jnp.float32)  56.9 us
    dot_general x1, matrix products, per_device_dense(): jnp.einsum('td,fd->tf', grad_full, down_all, preferred_element_type=jnp.f...  55.9 us
    psum x1, waiting for transfers between devices, per_device_dense(): lax.psum(grad_h_one_part.astype(jnp.bfloat16), 'tensor').astype(jnp.float32)  54 us
    psum x1, waiting for transfers between devices, per_device_dense(): lax.psum(grad_h_part.astype(jnp.bfloat16), 'tensor').astype(jnp.float32)  50.5 us
    psum x1, waiting for transfers between devices, per_device_dense(): lax.psum((grad_qkv.astype(jnp.bfloat16), grad_out.astype(jnp.bfloat16)),...  49 us
    reduce_scatter x1, waiting for transfers between devices, per_device_dense(): lax.psum_scatter(grad_down.astype(jnp.bfloat16), 'expert', scatter_dimens...  47.2 us
    psum x1, blocking collectives, per_device_dense(): lax.psum((grad_gain_attn, grad_shift_attn, grad_gain_moe, grad_shift_moe,...  39.4 us
  transfers between devices with their start and end apart: 10, of which 8 were waited for; matrix products, arithmetic and copies ran while one was open for 13% of the time, Pallas kernels for 0%

profile of v1, /device:TPU:0, one launch (start us, length us, event | category | flops | bytes accessed | tf_op | source)
XLA Modules:
  0.0 802.8 jit_solution(535228380046006833)
XLA Ops:
  34.5 3.4 convolution_convert_fusion.4
  40.7 56.9 %all-reduce.7.cloned.1.call-done = bf16[1576,768]{1,0:T(8,128)(2,1)} async-done(((bf16[1576,768]{1,0:T(8,128)(2,1)}), bf16[1576,768]{1,0:T(8,128)(2,1)}) %all-reduce.7.cloned.1.call-update) | async-done | bytes 2420752 | tf_op jit(solution)/shard_map/psum | solution.py:342
  106.3 16.8 %all-gather.4.cloned.1.call-done = bf16[8,768,384]{2,1,0:T(8,128)(2,1)} async-done(((bf16[1,768,384]{2,1,0:T(8,128)(2,1)}), bf16[8,768,384]{2,1,0:T(8,128)(2,1)}) %all-gather.4.cloned.1.call-update) | async-done | bytes 4718608 | tf_op jit(solution)/shard_map/all_gather | solution.py:330
  123.1 6.6 copy.97
  129.7 13.6 %fusion.71 = f32[1576,3072]{1,0:T(8,128)} fusion(bf16[1576,768]{1,0:T(8,128)(2,1)S(1)} %copy-done.8, bf16[768,3072]{0,1:T(8,128)(2,1)} %bitcast.102), kind=kOutput, calls=%fused_computation.123 | convolution fusion | flops 7436500992 | bytes 26505216 | tf_op jit(solution)/shard_map/dot_general | solution.py:357
  143.3 4.6 all-gather.8.cloned.1.call-done
  147.9 81.8 %all-gather.6.cloned.1.call-done = bf16[8,384,768]{2,1,0:T(8,128)(2,1)} async-done(((bf16[1,384,768]{2,1,0:T(8,128)(2,1)}), bf16[8,384,768]{2,1,0:T(8,128)(2,1)}) %all-gather.6.cloned.1.call-update) | async-done | bytes 4718608 | tf_op jit(solution)/shard_map/all_gather | solution.py:333
  229.7 55.9 %fusion.6 = (f32[1576,3072]{1,0:T(8,128)}, f32[1576,3072]{1,0:T(8,128)}, f32[1576,3072]{1,0:T(8,128)}) fusion(f32[1576,3072]{1,0:T(8,128)} %fusion.71, bf16[1576,768]{0,1:T(8,128)(2,1)} %all-gather.8.cloned.1.call-done, bf16[3072,768]{1,0:T(8,128)(2,1)} %bitcast.106), kind=kOutput, calls=%fused_computation.18 | convolution fusion | flops 7751196672 | bytes 84602880 | tf_op jit(solution)/shard_map/td,fd->tf/dot_general | solution.py:359
  285.6 23.8 %reshape.144 = f32[1576,4,768]{2,1,0:T(4,128)} reshape(f32[1576,3072]{1,0:T(8,128)} %get-tuple-element.73) | data formatting | bytes 38731776 | tf_op jit(solution)/shard_map/reshape | solution.py:361
  309.4 37.9 %reduce_sum.169 = f32[1576,4]{1,0:T(8,128)S(1)} reduce(f32[1576,4,768]{2,1,0:T(4,128)} %reshape.144, f32[]{:T(128)} %constant.40.clone.1), dimensions={2}, to_apply=%region_12.13 | reduce | flops 4835168 | bytes 19391108 | tf_op jit(solution)/shard_map/reduce_sum | solution.py:361
  347.5 10.3 %psum.79 = f32[1576,4]{0,1:T(4,128)S(1)} all-reduce(f32[1576,4]{0,1:T(4,128)S(1)} %copy.101), channel_id=1, replica_groups=mesh['expert'=8,'tensor'=4] {'tensor'}, use_global_device_ids=true, to_apply=%region_13.14 | all-reduce | flops 6304 | bytes 50432 | tf_op jit(solution)/shard_map/psum | solution.py:373
  361.4 9.1 %copy.121 = f32[197,8,4,768]{3,1,2,0:T(8,128)} copy(f32[197,8,4,768]{3,2,1,0:T(4,128)S(1)} %bitcast.100) | data formatting | bytes 38731776
  370.5 29.5 %add_convert_fusion = (bf16[1576,3072]{1,0:T(8,128)(2,1)S(1)}, bf16[1576,3072]{1,0:T(8,128)(2,1)}) fusion(f32[1576,3072]{1,0:T(8,128)} %get-tuple-element.74, f32[1576,3072]{1,0:T(8,128)} %get-tuple-element.84, f32[1576,3072]{1,0:T(8,128)} %bitcast.101, f32[1576,3072]{1,0:T(8,128)} %fusion.71), kind=kLoop, calls=%fused_computation.2 | loop fusion | flops 87146496 | bytes 96829440 | tf_op jit(solution)/shard_map/convert_element_type | solution.py:367
  400.1 3.7 copy-done.11
  403.8 11.3 %convolution_convert_fusion.2 = bf16[1576,768]{1,0:T(8,128)(2,1)} fusion(bf16[1576,3072]{1,0:T(8,128)(2,1)S(1)} %get-tuple-element.75, bf16[768,3072]{0,1:T(8,128)(2,1)} %bitcast.103), kind=kOutput, calls=%fused_computation.55 | convolution fusion | flops 7437711360 | bytes 16822272 | tf_op jit(solution)/shard_map/tf,df->td/dot_general | solution.py:369
  415.2 4.6 copy.100
  419.8 50.5 %all-reduce.9.cloned.1.call-done = bf16[1576,768]{1,0:T(8,128)(2,1)} async-done(((bf16[1576,768]{1,0:T(8,128)(2,1)}), bf16[1576,768]{1,0:T(8,128)(2,1)}) %all-reduce.9.cloned.1.call-update) | async-done | bytes 2420752 | tf_op jit(solution)/shard_map/psum | solution.py:372
  470.4 6.7 multiply_reduce_fusion.1
  477.1 6.7 fusion.67
  489.4 3.5 reshape.145
  492.9 3.8 fusion.43
  496.8 4.0 multiply_reduce_fusion
  529.0 5.1 bitcast_convert_fusion
  534.2 14.6 %fusion.22 = bf16[768,1576]{1,0:T(8,128)(2,1)} fusion(bf16[1576,3072]{1,0:T(8,128)(2,1)} %get-tuple-element.76, bf16[3072,768]{1,0:T(8,128)(2,1)} %bitcast.107), kind=kOutput, calls=%fused_computation.61 | convolution fusion | flops 7437711360 | bytes 16822272 | tf_op jit(solution)/shard_map/dot_general | solution.py:368
  548.9 13.8 %convolution_convert_fusion.1 = bf16[3072,768]{1,0:T(8,128)(2,1)} fusion(bf16[1576,3072]{1,0:T(8,128)(2,1)} %copy-done.11, bf16[1576,768]{1,0:T(8,128)(2,1)} %copy-done.7), kind=kOutput, calls=%fused_computation.34 | convolution fusion | flops 7438860288 | bytes 16822272 | tf_op jit(solution)/shard_map/td,tf->fd/dot_general | solution.py:370
  562.9 13.9 %convolution_convert_fusion = bf16[3072,768]{1,0:T(8,128)(2,1)} fusion(bf16[1576,3072]{1,0:T(8,128)(2,1)} %get-tuple-element.76, bf16[1576,768]{0,1:T(8,128)(2,1)} %all-gather.8.cloned.1.call-done), kind=kOutput, calls=%fused_computation.33 | convolution fusion | flops 7438860288 | bytes 16822272 | tf_op jit(solution)/shard_map/tf,td->fd/dot_general | solution.py:371
  578.9 49.0 %all-reduce.13.cloned.1.call-done = (bf16[3,768,192]{1,2,0:T(8,128)(2,1)}, bf16[192,768]{1,0:T(8,128)(2,1)}) async-done(((bf16[3,768,192]{1,2,0:T(8,128)(2,1)}, bf16[192,768]{1,0:T(8,128)(2,1)}), (bf16[3,768,192]{1,2,0:T(8,128)(2,1)}, bf16[192,768]{1,0:T(8,128)(2,1)})) %all-reduce.13.cloned.1.call-update) | async-done | bytes 1179664 | tf_op jit(solution)/shard_map/psum | solution.py:405
  632.2 54.0 %all-reduce.11.cloned.1.call-done = bf16[1576,768]{1,0:T(8,128)(2,1)} async-done(((bf16[1576,768]{1,0:T(8,128)(2,1)}), bf16[1576,768]{1,0:T(8,128)(2,1)}) %all-reduce.11.cloned.1.call-update) | async-done | bytes 2420752 | tf_op jit(solution)/shard_map/psum | solution.py:401
  686.3 3.6 convert_reduce_fusion
  692.6 39.4 %all-reduce = (f32[768]{0:T(1024)}, f32[768]{0:T(1024)}, f32[768]{0:T(1024)}, f32[768]{0:T(1024)}, f32[768,4]{0,1:T(4,128)}) all-reduce(f32[768]{0:T(1024)S(1)} %get-tuple-element.57, f32[768]{0:T(1024)S(1)} %get-tuple-element.60, f32[768]{0:T(1024)S(1)} %get-tuple-element.55, ...), channel_id=1, replica_groups=mesh['expert'=8,'tensor'=4] {'expert'}, use_global_device_ids=true, to_apply=%region_22.23 | all-reduce | flops 6144 | bytes 49152 | tf_op jit(solution)/shard_map/psum | solution.py:408
  732.0 6.4 add_add_fusion.2
  745.7 47.2 %reduce-scatter.8.cloned.1.call-done = bf16[384,768]{1,0:T(8,128)(2,1)} async-done(((bf16[3072,768]{1,0:T(8,128)(2,1)}), bf16[384,768]{1,0:T(8,128)(2,1)}) %reduce-scatter.8.cloned.1.call-update) | async-done | bytes 589840 | tf_op jit(solution)/shard_map/reduce_scatter | solution.py:379
  (196 shorter events, 94.3 us)
Async XLA Ops:
  8.1 89.5 %all-reduce.7.cloned.1.call-start = ((), (), s32[]{:S(2)}) async-start(), calls=%async_computation.3 | async-start | bytes 4841472 | tf_op jit(solution)/shard_map/psum | solution.py:342
  31.9 8.1 %copy-start.48 = (s32[1576,2]{0,1:T(2,128)S(1)}, s32[1576,2]{0,1:T(2,128)}, u32[]{:S(2)}) copy-start(s32[1576,2]{0,1:T(2,128)} %param.24) | copy-start | bytes 37828
  31.9 8.1 %copy-start.49 = (s32[1576,2]{0,1:T(2,128)S(1)}, s32[1576,2]{0,1:T(2,128)}, u32[]{:S(2)}) copy-start(s32[1576,2]{0,1:T(2,128)} %param.23) | copy-start | bytes 37828
  38.0 85.1 %all-gather.4.cloned.1.call-start = ((), (), s32[]{:S(2)}) async-start(), calls=%async_computation.4 | async-start | bytes 5308416 | tf_op jit(solution)/shard_map/all_gather | solution.py:330
  38.6 109.3 %all-gather.8.cloned.1.call-start = ((), (), s32[]{:S(2)}) async-start(), calls=%async_computation.6 | async-start | bytes 3194880 | tf_op jit(solution)/shard_map/all_gather | solution.py:338
  39.1 190.5 %all-gather.6.cloned.1.call-start = ((), (), s32[]{:S(2)}) async-start(), calls=%async_computation.5 | async-start | bytes 5308416 | tf_op jit(solution)/shard_map/all_gather | solution.py:333
  39.7 430.6 %all-reduce.9.cloned.1.call-start = ((), (), s32[]{:S(2)}) async-start(), calls=%async_computation.7 | async-start | bytes 4841472 | tf_op jit(solution)/shard_map/psum | solution.py:372
  40.7 60.6 %copy-start.46 = (f32[768]{0:T(1024)S(1)}, f32[768]{0:T(1024)}, u32[]{:S(2)}) copy-start(f32[768]{0:T(1024)} %param.18) | copy-start | bytes 9220
  40.7 60.6 %copy-start.52 = (f32[768]{0:T(1024)S(1)}, f32[768]{0:T(1024)}, u32[]{:S(2)}) copy-start(f32[768]{0:T(1024)} %param.19) | copy-start | bytes 9220
  105.1 24.6 %copy-start.8 = (bf16[1576,768]{1,0:T(8,128)(2,1)S(1)}, bf16[1576,768]{1,0:T(8,128)(2,1)}, u32[]{:S(2)}) copy-start(bf16[1576,768]{1,0:T(8,128)(2,1)} %copy-done.7) | copy-start | bytes 7262212
  309.4 48.4 %copy-start.21 = (f32[1576,4]{0,1:T(4,128)S(1)}, f32[1576,4]{0,1:T(4,128)}, u32[]{:S(2)}) copy-start(f32[1576,4]{0,1:T(4,128)} %copy-done.20) | copy-start | bytes 75652
  309.4 48.4 %copy-start.31 = (f32[1576]{0:T(1024)S(1)}, f32[1576]{0:T(1024)}, u32[]{:S(2)}) copy-start(f32[1576]{0:T(1024)} %copy-done.30) | copy-start | bytes 18916
  309.4 48.5 %copy-start.34 = (f32[1576,4]{0,1:T(4,128)S(1)}, f32[1576,4]{0,1:T(4,128)}, u32[]{:S(2)}) copy-start(f32[1576,4]{0,1:T(4,128)} %select_reduce_fusion) | copy-start | bytes 75652
  309.4 48.5 %copy-start.41 = (f32[1576]{0:T(1024)S(1)}, f32[1576]{0:T(1024)}, u32[]{:S(2)}) copy-start(f32[1576]{0:T(1024)} %fusion.57) | copy-start | bytes 18916
  403.8 11.4 %copy-start.23 = (f32[8,3,197]{2,1,0:T(4,128)S(1)}, f32[8,3,197]{2,1,0:T(4,128)}, u32[]{:S(2)}) copy-start(f32[8,3,197]{2,1,0:T(4,128)} %copy-done.22) | copy-start | bytes 56740
  403.8 11.4 %copy-start.29 = (f32[8,3,197]{2,1,0:T(4,128)S(1)}, f32[8,3,197]{2,1,0:T(4,128)}, u32[]{:S(2)}) copy-start(f32[8,3,197]{2,1,0:T(4,128)} %copy-done.28) | copy-start | bytes 56740
  415.1 55.3 %copy-start.2 = (bf16[1576,768]{1,0:T(8,128)(2,1)S(1)}, bf16[1576,768]{1,0:T(8,128)(2,1)}, u32[]{:S(2)}) copy-start(bf16[1576,768]{1,0:T(8,128)(2,1)} %param.13) | copy-start | bytes 7262212
  415.1 55.3 %copy-start.33 = (f32[1576]{0:T(1024)S(1)}, f32[1576]{0:T(1024)}, u32[]{:S(2)}) copy-start(f32[1576]{0:T(1024)} %copy-done.32) | copy-start | bytes 18916
  415.1 55.3 %copy-start.43 = (f32[1576]{0:T(1024)S(1)}, f32[1576]{0:T(1024)}, u32[]{:S(2)}) copy-start(f32[1576]{0:T(1024)} %copy-done.42) | copy-start | bytes 18916
  415.1 55.3 %copy-start.47 = (f32[768]{0:T(1024)S(1)}, f32[768]{0:T(1024)}, u32[]{:S(2)}) copy-start(f32[768]{0:T(1024)} %param.18) | copy-start | bytes 9220
  415.1 55.3 %copy-start.51 = (bf16[768,4]{0,1:T(4,128)(2,1)S(1)}, bf16[768,4]{0,1:T(4,128)(2,1)}, u32[]{:S(2)}) copy-start(bf16[768,4]{0,1:T(4,128)(2,1)} %param.20) | copy-start | bytes 18436
  415.1 212.8 %all-reduce.13.cloned.1.call-start = ((), (), s32[]{:S(2)}) async-start(), calls=%async_computation.12 | async-start | bytes 2359296 | tf_op jit(solution)/shard_map/psum | solution.py:405
  419.8 57.3 %copy-start.40 = (f32[1576]{0:T(1024)S(1)}, f32[1576]{0:T(1024)}, u32[]{:S(2)}) copy-start(f32[1576]{0:T(1024)} %copy-done.39) | copy-start | bytes 18916
  510.6 14.8 %copy-start.27 = (f32[1576]{0:T(1024)S(1)}, f32[1576]{0:T(1024)}, u32[]{:S(2)}) copy-start(f32[1576]{0:T(1024)} %copy-done.26) | copy-start | bytes 18916
  510.6 14.8 %copy-start.36 = (f32[1576]{0:T(1024)S(1)}, f32[1576]{0:T(1024)}, u32[]{:S(2)}) copy-start(f32[1576]{0:T(1024)} %copy-done.35) | copy-start | bytes 18916
  510.6 14.8 %copy-start.45 = (f32[768]{0:T(1024)S(1)}, f32[768]{0:T(1024)}, u32[]{:S(2)}) copy-start(f32[768]{0:T(1024)} %param.14) | copy-start | bytes 9220
  510.6 14.8 %copy-start.54 = (f32[768]{0:T(1024)S(1)}, f32[768]{0:T(1024)}, u32[]{:S(2)}) copy-start(f32[768]{0:T(1024)} %param.15) | copy-start | bytes 9220
  528.8 157.5 %all-reduce.11.cloned.1.call-start = ((), (), s32[]{:S(2)}) async-start(), calls=%async_computation.8 | async-start | bytes 4841472 | tf_op jit(solution)/shard_map/psum | solution.py:401
  534.1 204.3 %reduce-scatter.10.cloned.1.call-start = ((), (), s32[]{:S(2)}) async-start(), calls=%async_computation.11 | async-start | bytes 3194880
  548.8 194.3 %reduce-scatter.6.cloned.1.call-start = ((), (), s32[]{:S(2)}) async-start(), calls=%async_computation.9 | async-start | bytes 5308416 | tf_op jit(solution)/shard_map/reduce_scatter | solution.py:383
  562.7 230.2 %reduce-scatter.8.cloned.1.call-start = ((), (), s32[]{:S(2)}) async-start(), calls=%async_computation.10 | async-start | bytes 5308416 | tf_op jit(solution)/shard_map/reduce_scatter | solution.py:379
  578.9 111.0 %copy-start.38 = (f32[1576]{0:T(1024)S(1)}, f32[1576]{0:T(1024)}, u32[]{:S(2)}) copy-start(f32[1576]{0:T(1024)} %copy-done.37) | copy-start | bytes 18916
  (35 other events, 116.1 us)
Sparse Core Ops, SparseCore 0:
  38.1 59.4 all-reduce.6
  415.2 55.0 all-reduce.8
  549.0 34.5 reduce-scatter.9
  587.5 105.9 reduce-scatter.5
  697.5 95.3 reduce-scatter.7
Sparse Core Ops, SparseCore 1:
  40.9 82.1 all-gather.3
  124.6 23.3 all-gather.7
  150.2 79.4 all-gather.5
  528.9 98.9 all-reduce.12
  630.3 55.9 all-reduce.10

commit v2 on v0

--- a/solution.py
+++ b/solution.py
@@ -3,6 +3,8 @@
 import jax
 import jax.numpy as jnp
 from jax import lax
+from jax.experimental import pallas as pl
+from jax.experimental.pallas import tpu as pltpu
 from jax.sharding import PartitionSpec as P
 
 HD = 64
@@ -128,7 +130,7 @@
     return (grad_out_rows + grad_resid_norm, grad_router, grad_gain_moe, grad_shift_moe)
 
 
-def per_device(
+def per_device_routed(
     tokens,
     gain_attn,
     shift_attn,
@@ -305,6 +307,683 @@
     )
 
 
+MESH = pl.DeviceIdType.MESH
+f32 = jnp.float32
+bf16 = jnp.bfloat16
+PITCH = 208
+
+
+def dot(left, right, over=((1,), (0,))):
+    return lax.dot_general(left, right, (over, ((), ())), preferred_element_type=f32)
+
+
+def aligned(start, size):
+    return pl.ds(pl.multiple_of(start, 16), size)
+
+
+def lanes_at(start, size):
+    return pl.ds(pl.multiple_of(start, 128), size)
+
+
+def norm_stats(values):
+    row_mean = jnp.mean(values, axis=1, keepdims=True)
+    centred = values - row_mean
+    inverse = lax.rsqrt(jnp.mean(centred * centred, axis=1, keepdims=True) + norm_epsilon)
+    return centred * inverse, inverse
+
+
+def greet(neighbours):
+    barrier = pltpu.get_barrier_semaphore()
+    count = 0
+    for is_there, device in neighbours:
+
+        @pl.when(is_there)
+        def _():
+            pl.semaphore_signal(barrier, inc=1, device_id=device, device_id_type=MESH)
+
+        count = count + jnp.where(is_there, 1, 0)
+    pl.semaphore_wait(barrier, count)
+
+
+def head_mask(lane, head):
+    return (lane < HD) if head % 2 == 0 else (lane >= HD)
+
+
+def forward_kernel(
+    tok_ref,
+    gain1_ref,
+    shift1_ref,
+    gain2_ref,
+    shift2_ref,
+    qkv_ref,
+    out_w_ref,
+    up_ref,
+    down_ref,
+    cot_ref,
+    kept_ref,
+    q_ref,
+    k_ref,
+    v_ref,
+    att_ref,
+    lse_ref,
+    resid_ref,
+    h_out,
+    cot_out,
+    kept_out,
+    up_out,
+    down_out,
+    h_all,
+    cot_all,
+    kept_all,
+    part,
+    mine,
+    core_from,
+    core_to,
+    x_to,
+    x_from,
+    total_to,
+    total_from,
+    cot_core,
+    core_s,
+    core_r,
+    x_s,
+    x_r,
+    tot_s,
+    tot_r,
+    y_s,
+    y_r,
+    rel_s,
+    rel_r,
+    w_s,
+    w_r,
+    c_s,
+    c_r,
+    out_sem,
+    *,
+    images,
+    heads,
+):
+    expert_at = lax.axis_index("expert")
+    tensor_at = lax.axis_index("tensor")
+    z_at, y_at = expert_at // 2, expert_at % 2
+    z_last = lax.axis_size("expert") // 2 - 1
+    x_at, core_at = tensor_at // 2, tensor_at % 2
+    other = 1 - core_at
+    rows = images * PITCH
+    half = rows // 2
+    wide = out_w_ref.shape[1] // 2
+    hidden = up_ref.shape[1]
+    core_dev = (expert_at, tensor_at + 1 - 2 * core_at)
+    x_dev = (expert_at, tensor_at + 2 - 4 * x_at)
+    y_dev = (expert_at + 1 - 2 * y_at, tensor_at)
+    z_up = (expert_at + 2, tensor_at)
+    z_down = (expert_at - 2, tensor_at)
+    has_up, has_down = z_at < z_last, z_at > 0
+    greet([(True, core_dev), (True, x_dev), (True, y_dev), (has_up, z_up), (has_down, z_down)])
+
+    def remote(src, dst, send, recv, device):
+        return pltpu.make_async_remote_copy(
+            src_ref=src, dst_ref=dst, send_sem=send, recv_sem=recv, device_id=device, device_id_type=MESH
+        )
+
+    def slot(expert):
+        return (
+            up_out.at[expert // 2, :, lanes_at(expert % 2 * hidden, hidden)],
+            down_out.at[expert // 2, aligned(expert % 2 * hidden, hidden), :],
+        )
+
+    def hop(step, way):
+        expert = z_at - step if way == 0 else z_at + step
+        source = (up_ref, down_ref) if step == 0 else slot(expert)
+        target = slot(expert)
+        device = z_up if way == 0 else z_down
+        return [remote(source[n], target[n], w_s.at[way, step, n], w_r.at[way, step, n], device) for n in range(2)]
+
+    def hop_goes(step, way):
+        if way == 0:
+            return (z_at - step >= 0) & has_up
+        return (z_at + step <= z_last) & has_down
+
+    def hop_comes(step, way):
+        return (z_at - 1 - step >= 0) if way == 0 else (z_at + 1 + step <= z_last)
+
+    def hop_arriving(step, way):
+        expert = z_at - 1 - step if way == 0 else z_at + 1 + step
+        target = slot(expert)
+        return [remote(target[n], target[n], w_s.at[way, step, n], w_r.at[way, step, n], core_dev) for n in range(2)]
+
+    def start_hops(step):
+        for way in range(2):
+
+            @pl.when(hop_goes(step, way))
+            def _():
+                for copy in hop(step, way):
+                    copy.start()
+
+    def await_hops(step):
+        for way in range(2):
+
+            @pl.when(hop_comes(step, way))
+            def _():
+                for copy in hop_arriving(step, way):
+                    copy.wait_recv()
+
+    start_hops(0)
+    own = slot(z_at)
+    own_copies = [
+        pltpu.make_async_copy((up_ref, down_ref)[n], own[n], out_sem.at[n]) for n in range(2)
+    ]
+    for copy in own_copies:
+        copy.start()
+
+    quarter = cot_ref.shape[1]
+    swap = remote(cot_ref, cot_core, c_s.at[0], c_r.at[0], core_dev)
+    swap.start()
+    kept_all[aligned(y_at * rows, rows), :] = kept_ref[...]
+    kept_mine = kept_all.at[aligned(y_at * rows, rows), :]
+    kept_y = remote(kept_mine, kept_mine, c_s.at[7], c_r.at[7], y_dev)
+    kept_y.start()
+    swap.wait_recv()
+    base = y_at * rows
+
+    @pl.when(core_at == 0)
+    def _():
+        both = jnp.concatenate([cot_ref[...], cot_core[...]], axis=1)
+        cot_all[aligned(base, rows), lanes_at(x_at * wide, wide)] = both
+
+    @pl.when(core_at == 1)
+    def _():
+        both = jnp.concatenate([cot_core[...], cot_ref[...]], axis=1)
+        cot_all[aligned(base, rows), lanes_at(x_at * wide, wide)] = both
+
+    def block(row_side, col_side, core):
+        return cot_all.at[aligned(row_side * rows + core * half, half), lanes_at(col_side * wide, wide)]
+
+    def cot_copy(number, row_side, col_side, core, device):
+        ref = block(row_side, col_side, core)
+        return remote(ref, ref, c_s.at[number], c_r.at[number], device)
+
+    cot_x = cot_copy(1, y_at, x_at, core_at, x_dev)
+    cot_y = cot_copy(2, y_at, x_at, core_at, y_dev)
+    cot_x.start()
+    cot_y.start()
+    cot_x_in = cot_copy(1, y_at, 1 - x_at, core_at, x_dev)
+    cot_y_in = cot_copy(2, 1 - y_at, x_at, core_at, y_dev)
+    cot_relay = cot_copy(3, y_at, 1 - x_at, core_at, y_dev)
+    cot_relay_in = cot_copy(3, 1 - y_at, 1 - x_at, core_at, y_dev)
+    cot_share = [
+        cot_copy(4, y_at, 1 - x_at, core_at, core_dev),
+        cot_copy(5, 1 - y_at, x_at, core_at, core_dev),
+        cot_copy(6, 1 - y_at, 1 - x_at, core_at, core_dev),
+    ]
+    cot_share_in = [
+        cot_copy(4, y_at, 1 - x_at, other, core_dev),
+        cot_copy(5, 1 - y_at, x_at, other, core_dev),
+        cot_copy(6, 1 - y_at, 1 - x_at, other, core_dev),
+    ]
+
+    lane = lax.broadcasted_iota(jnp.int32, (PITCH, 2 * HD), 1)
+    key_mask = lax.broadcasted_iota(jnp.int32, (PITCH, PITCH), 1) < SEQ
+    gain1, shift1 = gain1_ref[...], shift1_ref[...]
+    gain2, shift2 = gain2_ref[...], shift2_ref[...]
+    my_cols = lanes_at(core_at * wide, wide)
+    their_cols = lanes_at(other * wide, wide)
+
+    def attend(image):
+        normed, _ = norm_stats(tok_ref[image].astype(f32))
+        h_one = (normed * gain1 + shift1).astype(bf16)
+        queries = dot(h_one, qkv_ref[0]).astype(bf16)
+        keys = dot(h_one, qkv_ref[1]).astype(bf16)
+        values = dot(h_one, qkv_ref[2]).astype(bf16)
+        q_ref[image] = queries
+        k_ref[image] = keys
+        v_ref[image] = values
+        outs = []
+        lse = jnp.zeros((PITCH, 2 * HD), f32)
+        for head in range(heads):
+            first = head // 2 * 2 * HD
+            last = min(first + 2 * HD, heads * HD)
+            q_head, k_head, v_head = queries[:, first:last], keys[:, first:last], values[:, first:last]
+            if last - first == 2 * HD:
+                q_head = jnp.where(head_mask(lane, head), q_head, jnp.zeros_like(q_head))
+            scores = dot(q_head, k_head, ((1,), (1,))) * (HD**-0.5)
+            scores = jnp.where(key_mask, scores, -1e30)
+            peak = jnp.max(scores, axis=1, keepdims=True)
+            powers = jnp.exp(scores - peak)
+            row_sum = jnp.sum(powers, axis=1, keepdims=True)
+            weights = (powers / row_sum).astype(bf16)
+            outs.append(dot(weights, v_head))
+            lse = jnp.where(lane == head, peak + jnp.log(row_sum), lse)
+        lse_ref[image] = lse
+        joined = []
+        for head in range(0, heads, 2):
+            if head + 1 < heads:
+                joined.append(jnp.where(lane < HD, outs[head], outs[head + 1]))
+            else:
+                joined.append(outs[head])
+        attended = jnp.concatenate(joined, axis=1).astype(bf16)
+        att_ref[image] = attended
+        part[...] = dot(attended, out_w_ref[...])
+        mine[image] = part[:, my_cols]
+        core_to[image] = part[:, their_cols].astype(bf16)
+
+    def core_copy(image):
+        return remote(core_to.at[image], core_from.at[image], core_s.at[image], core_r.at[image], core_dev)
+
+    def x_copy(image):
+        return remote(x_to.at[image], x_from.at[image], x_s.at[image], x_r.at[image], x_dev)
+
+    def total_copy(image):
+        return remote(total_to.at[image], total_from.at[image], tot_s.at[image], tot_r.at[image], core_dev)
+
+    def h_block(row_side, image, core):
+        return h_all.at[aligned(row_side * rows + image * PITCH, PITCH), lanes_at(core * wide, wide)]
+
+    def y_copy(image):
+        ref = h_block(y_at, image, core_at)
+        return remote(ref, ref, y_s.at[image], y_r.at[image], y_dev)
+
+    def y_arriving(image):
+        ref = h_block(1 - y_at, image, core_at)
+        return remote(ref, ref, y_s.at[image], y_r.at[image], y_dev)
+
+    def relay_copy(image):
+        ref = h_block(1 - y_at, image, core_at)
+        return remote(ref, ref, rel_s.at[image], rel_r.at[image], core_dev)
+
+    def relay_arriving(image):
+        ref = h_block(1 - y_at, image, other)
+        return remote(ref, ref, rel_s.at[image], rel_r.at[image], core_dev)
+
+    def stage(tick, lag, run):
+        image = tick - lag
+
+        @pl.when((image >= 0) & (image < images))
+        def _():
+            run(image)
+
+    def run_attend(image):
+        attend(image)
+        core_copy(image).start()
+
+    def run_x(image):
+        core_copy(image).wait_recv()
+        x_to[image] = (mine[image] + core_from[image].astype(f32)).astype(bf16)
+        x_copy(image).start()
+
+    def run_total(image):
+        x_copy(image).wait_recv()
+        total_to[image] = (x_to[image].astype(f32) + x_from[image].astype(f32)).astype(bf16)
+        total_copy(image).start()
+
+    def run_norm(image):
+        total_copy(image).wait_recv()
+        part[:, my_cols] = total_to[image].astype(f32)
+        part[:, their_cols] = total_from[image].astype(f32)
+        resid = tok_ref[image].astype(f32) + part[...]
+        resid_ref[image] = resid
+        normed, _ = norm_stats(resid)
+        h_all[aligned(base + image * PITCH, PITCH), :] = (normed * gain2 + shift2).astype(bf16)
+        y_copy(image).start()
+
+    def run_relay(image):
+        y_arriving(image).wait_recv()
+        relay_copy(image).start()
+
+    def run_end(image):
+        relay_arriving(image).wait_recv()
+
+    def at_tick(tick, when, run):
+        @pl.when(tick == when)
+        def _():
+            run()
+
+    def cot_step_one():
+        cot_x_in.wait_recv()
+        cot_relay.start()
+        cot_share[0].start()
+
+    def cot_step_two():
+        cot_y_in.wait_recv()
+        cot_share[1].start()
+
+    def weights_step_one():
+        await_hops(0)
+        start_hops(1)
+
+    def weights_step_two():
+        await_hops(1)
+        start_hops(2)
+
+    def cot_step_three():
+        cot_relay_in.wait_recv()
+        cot_share[2].start()
+
+    def per_tick(tick, _):
+        stage(tick, 0, run_attend)
+        stage(tick, 1, run_x)
+        stage(tick, 4, run_total)
+        stage(tick, 5, run_norm)
+        stage(tick, 9, run_relay)
+        stage(tick, 10, run_end)
+        at_tick(tick, 7, cot_step_one)
+        at_tick(tick, 8, weights_step_one)
+        at_tick(tick, 9, cot_step_two)
+        at_tick(tick, 14, weights_step_two)
+        at_tick(tick, 15, cot_step_three)
+        return 0
+
+    lax.fori_loop(0, images + 10, per_tick, 0)
+    for copy in cot_share_in:
+        copy.wait_recv()
+    kept_theirs = kept_all.at[aligned((1 - y_at) * rows, rows), :]
+    remote(kept_theirs, kept_theirs, c_s.at[7], c_r.at[7], y_dev).wait_recv()
+    outs = [
+        pltpu.make_async_copy(h_all, h_out, out_sem.at[2]),
+        pltpu.make_async_copy(cot_all, cot_out, out_sem.at[3]),
+        pltpu.make_async_copy(kept_all, kept_out, out_sem.at[4]),
+    ]
+    for copy in outs:
+        copy.start()
+    for copy in (swap, kept_y, cot_x, cot_y, cot_relay, *cot_share):
+        copy.wait_send()
+
+    def drain(image, _):
+        core_copy(image).wait_send()
+        x_copy(image).wait_send()
+        total_copy(image).wait_send()
+        y_copy(image).wait_send()
+        relay_copy(image).wait_send()
+        return 0
+
+    lax.fori_loop(0, images, drain, 0)
+    await_hops(2)
+    for step in range(3):
+        for way in range(2):
+
+            @pl.when(hop_goes(step, way))
+            def _():
+                for copy in hop(step, way):
+                    copy.wait_send()
+
+    for copy in (*own_copies, *outs):
+        copy.wait()
+
+
+def run_forward(tok, gain1, shift1, gain2, shift2, qkv_w, out_w, up, down, cot, kept):
+    images = tok.shape[0]
+    rows = images * PITCH
+    features = tok.shape[2]
+    share = out_w.shape[0]
+    heads = share // HD
+    hidden = up.shape[1]
+    wide = features // 2
+    vmem = pl.BlockSpec(memory_space=pltpu.VMEM)
+    anywhere = pl.BlockSpec(memory_space=pl.ANY)
+    shape = jax.ShapeDtypeStruct
+    block = (images, PITCH, wide)
+    dma = pltpu.SemaphoreType.DMA
+    return pl.pallas_call(
+        partial(forward_kernel, images=images, heads=heads),
+        out_shape=[
+            shape((images, PITCH, share), bf16),
+            shape((images, PITCH, share), bf16),
+            shape((images, PITCH, share), bf16),
+            shape((images, PITCH, share), bf16),
+            shape((images, PITCH, 128), f32),
+            shape((images, PITCH, features), f32),
+            shape((2 * rows, features), bf16),
+            shape((2 * rows, features), bf16),
+            shape((2 * rows, 128), bf16),
+            shape((2, features, 2 * hidden), bf16),
+            shape((2, 2 * hidden, features), bf16),
+        ],
+        in_specs=[vmem] * 7 + [anywhere] * 2 + [vmem] * 2,
+        out_specs=[vmem] * 6 + [anywhere] * 5,
+        scratch_shapes=[
+            pltpu.VMEM((2 * rows, features), bf16),
+            pltpu.VMEM((2 * rows, features), bf16),
+            pltpu.VMEM((2 * rows, 128), bf16),
+            pltpu.VMEM((PITCH, features), f32),
+            pltpu.VMEM(block, f32),
+            pltpu.VMEM(block, bf16),
+            pltpu.VMEM(block, bf16),
+            pltpu.VMEM(block, bf16),
+            pltpu.VMEM(block, bf16),
+            pltpu.VMEM(block, bf16),
+            pltpu.VMEM(block, bf16),
+            pltpu.VMEM((rows, share), bf16),
+        ]
+        + [dma((images,))] * 10
+        + [dma((2, 3, 2))] * 2
+        + [dma((8,))] * 2
+        + [dma((5,))],
+        compiler_params=pltpu.CompilerParams(
+            collective_id=1, has_side_effects=True, vmem_limit_bytes=60 << 20
+        ),
+    )(tok, gain1, shift1, gain2, shift2, qkv_w, out_w, up, down, cot, kept)
+
+
+def expert_kernel(
+    h_ref,
+    cot_ref,
+    up_ref,
+    down_ref,
+    kept_ref,
+    router_ref,
+    mixed_ref,
+    grad_h_ref,
+    grad_up_ref,
+    grad_down_ref,
+    grad_router_ref,
+    up_sum,
+    down_sum,
+    *,
+    experts,
+    block,
+):
+    pairs = up_ref.shape[0]
+    hidden = up_ref.shape[2] // 2
+    lane = lax.broadcasted_iota(jnp.int32, (block, 128), 1)
+    up_sum[...] = jnp.zeros_like(up_sum)
+    down_sum[...] = jnp.zeros_like(down_sum)
+    grad_router_ref[...] = jnp.zeros_like(grad_router_ref)
+
+    def per_block(number, _):
+        at = pl.ds(pl.multiple_of(number * block, block), block)
+        h_rows, cot_rows = h_ref[at, :], cot_ref[at, :]
+        h_turned, cot_turned = h_rows.T, cot_rows.T
+        logits = jnp.where(lane < experts, dot(h_rows, router_ref[...]), -1e30)
+        powers = jnp.exp(logits - jnp.max(logits, axis=1, keepdims=True))
+        probs = powers / jnp.sum(powers, axis=1, keepdims=True)
+        kept = kept_ref[at, :].astype(f32)
+        gates = kept * probs
+        grad_gate = jnp.zeros((block, 128), f32)
+        mixed = grad_h = 0.0
+        for pair in range(pairs):
+            pre_act = dot(h_rows, up_ref[pair])
+            back = dot(cot_rows, down_ref[pair], ((1,), (1,)))
+            normal_cdf = 0.5 + 0.5 * lax.erf(pre_act * 0.7071067811865476)
+            gelu = pre_act * normal_cdf
+            slope = normal_cdf + pre_act * (0.3989422804014327 * jnp.exp(-0.5 * pre_act * pre_act))
+            product = gelu * back
+            spread = []
+            for side in range(2):
+                expert = 2 * pair + side
+                part = jnp.sum(product[:, side * hidden : (side + 1) * hidden], axis=1, keepdims=True)
+                grad_gate = jnp.where(lane == expert, part, grad_gate)
+                spread.append(jnp.broadcast_to(gates[:, expert : expert + 1], (block, hidden)))
+            gate = jnp.concatenate(spread, axis=1)
+            hidden_rows = (gelu * gate).astype(bf16)
+            grad_pre = (slope * back * gate).astype(bf16)
+            mixed += dot(hidden_rows, down_ref[pair])
+            grad_h += dot(grad_pre, up_ref[pair], ((1,), (1,)))
+            up_sum[pair] += dot(h_turned, grad_pre)
+            down_sum[pair] += dot(cot_turned, hidden_rows)
+        grad_gate = kept * grad_gate
+        grad_logits = (
+            probs * (grad_gate - jnp.sum(probs * grad_gate, axis=1, keepdims=True))
+        ).astype(bf16)
+        mixed_ref[at, :] = mixed.astype(bf16)
+        grad_h_ref[at, :] = (grad_h + dot(grad_logits, router_ref[...], ((1,), (1,)))).astype(bf16)
+        grad_router_ref[...] += dot(h_turned, grad_logits)
+        return 0
+
+    lax.fori_loop(0, h_ref.shape[0] // block, per_block, 0)
+    grad_up_ref[...] = up_sum[...].astype(bf16)
+    grad_down_ref[...] = down_sum[...].astype(bf16)
+
+
+def run_experts(h_rows, cot_rows, up, down, kept, router, experts):
+    rows, features = h_rows.shape
+    pairs, _, width = up.shape
+    vmem = pl.BlockSpec(memory_space=pltpu.VMEM)
+    shape = jax.ShapeDtypeStruct
+    return pl.pallas_call(
+        partial(expert_kernel, experts=experts, block=256),
+        out_shape=[
+            shape((rows, features), bf16),
+            shape((rows, features), bf16),
+            shape((pairs, features, width), bf16),
+            shape((pairs, features, width), bf16),
+            shape((features, 128), f32),
+        ],
+        in_specs=[vmem] * 6,
+        out_specs=[vmem] * 5,
+        scratch_shapes=[pltpu.VMEM((pairs, features, width), f32)] * 2,
+        compiler_params=pltpu.CompilerParams(vmem_limit_bytes=60 << 20),
+    )(h_rows, cot_rows, up, down, kept, router)
+
+
+def per_image(rows_in):
+    images = rows_in.shape[0] // SEQ
+    blocks = rows_in.reshape(images, SEQ, rows_in.shape[1])
+    return jnp.pad(blocks, ((0, 0), (0, PITCH - SEQ), (0, 0)))
+
+
+def unpad(blocks):
+    images = blocks.shape[0]
+    return blocks[:, :SEQ].reshape(images * SEQ, blocks.shape[2])
+
+
+def per_device_dense(
+    tokens,
+    gain_attn,
+    shift_attn,
+    qkv_weight,
+    out_weight,
+    gain_moe,
+    shift_moe,
+    router_weight,
+    expert_up,
+    expert_down,
+    routes,
+    keep_mask,
+    cotangent,
+):
+    row_count, feature_count = tokens.shape
+    images = row_count // SEQ
+    rows = images * PITCH
+    tensor_count = lax.axis_size("tensor")
+    expert_count = lax.axis_size("expert")
+    tensor_here = lax.axis_index("tensor")
+    expert_here = lax.axis_index("expert")
+    quarter_width = feature_count // tensor_count
+    experts_all = router_weight.shape[1]
+    hidden = expert_up.shape[2]
+    chosen = routes[:, :, None] == jnp.arange(128, dtype=jnp.int32)[None, None, :]
+    kept = jnp.sum(jnp.where(chosen, keep_mask[:, :, None], 0), axis=1).astype(bf16)
+    router_wide = jnp.pad(router_weight, ((0, 0), (0, 128 - experts_all)))
+    tok = per_image(tokens)
+    queries, keys, values, attended, lse, resid, h_all, cot_all, kept_all, up_all, down_all = run_forward(
+        tok,
+        gain_attn[None],
+        shift_attn[None],
+        gain_moe[None],
+        shift_moe[None],
+        qkv_weight,
+        out_weight,
+        expert_up[0],
+        expert_down[0],
+        per_image(cotangent).reshape(rows, quarter_width),
+        per_image(kept).reshape(rows, 128),
+    )
+    mixed_part, grad_h_part, grad_up, grad_down, grad_router = run_experts(
+        h_all, cot_all, up_all, down_all, kept_all, router_wide, experts_all
+    )
+    y_groups = [[2 * z, 2 * z + 1] for z in range(expert_count // 2)]
+    z_groups = [[2 * z + y for z in range(expert_count // 2)] for y in range(2)]
+    grad_h_rows = lax.psum(
+        lax.psum_scatter(grad_h_part, "expert", scatter_dimension=0, axis_index_groups=y_groups, tiled=True),
+        "tensor",
+    ).astype(f32)
+    mixed_sum = lax.psum_scatter(
+        lax.psum_scatter(mixed_part, "expert", scatter_dimension=0, axis_index_groups=y_groups, tiled=True),
+        "tensor",
+        scatter_dimension=1,
+        tiled=True,
+    ).astype(f32)
+
+    def to_owner(grads):
+        apart = grads.reshape(2, feature_count, 2, hidden).transpose(0, 2, 1, 3)
+        apart = apart.reshape(experts_all * feature_count, hidden)
+        return lax.psum_scatter(
+            apart, "expert", scatter_dimension=0, axis_index_groups=z_groups, tiled=True
+        ).astype(f32)
+
+    grad_up = to_owner(grad_up)
+    grad_down = to_owner(grad_down).T
+    resid = resid.reshape(rows, feature_count)
+    resid_part = lax.dynamic_slice_in_dim(resid, tensor_here * quarter_width, quarter_width, 1)
+    mixed = (resid_part + mixed_sum).astype(bf16)
+    norm_out, norm_back = jax.vjp(norm_rows, resid, gain_moe, shift_moe)
+    grad_resid_norm, grad_gain_moe, grad_shift_moe = norm_back(grad_h_rows)
+    cot_mine = lax.dynamic_slice_in_dim(cot_all, expert_here % 2 * rows, rows, 0)
+    grad_resid = unpad((cot_mine.astype(f32) + grad_resid_norm).reshape(images, PITCH, feature_count))
+    head_count = qkv_weight.shape[2] // HD
+    tokens_float = tokens.astype(f32)
+    h_one = norm_rows(tokens_float, gain_attn, shift_attn).astype(bf16)
+    by_head = (images, SEQ, head_count, HD)
+    log_total = lse[:, :SEQ, :head_count].transpose(0, 2, 1)[..., None]
+    saved = (
+        unpad(attended),
+        unpad(queries).reshape(by_head),
+        unpad(keys).reshape(by_head),
+        unpad(values).reshape(by_head),
+        log_total,
+    )
+    grad_qkv, grad_out, grad_h_one_part = attention_backward(
+        grad_resid.astype(bf16), saved, h_one, qkv_weight, out_weight
+    )
+    grad_h_one = lax.psum(grad_h_one_part.astype(bf16), "tensor").astype(f32)
+    norm_one_out, norm_one_back = jax.vjp(norm_rows, tokens_float, gain_attn, shift_attn)
+    grad_tok_norm, grad_gain_attn, grad_shift_attn = norm_one_back(grad_h_one)
+    grad_tokens = grad_resid + grad_tok_norm
+    grad_qkv, grad_out = lax.psum((grad_qkv.astype(bf16), grad_out.astype(bf16)), "expert")
+    small = lax.psum((grad_gain_attn, grad_shift_attn, grad_gain_moe, grad_shift_moe), "expert")
+    grad_router = lax.psum(grad_router[:, :experts_all], ("expert", "tensor"))
+    return (
+        unpad(mixed.reshape(images, PITCH, quarter_width)),
+        grad_tokens,
+        small[0],
+        small[1],
+        grad_qkv.astype(f32),
+        grad_out.astype(f32),
+        small[2],
+        small[3],
+        grad_router,
+        grad_up[None],
+        grad_down[None],
+    )
+
+
+def per_device(*arguments):
+    router_weight = arguments[7]
+    if router_weight.shape[1] <= 4:
+        return per_device_dense(*arguments)
+    return per_device_routed(*arguments)
+
+
 def solution(mesh):
     placed = (
         P("expert", None),

time: 1670 us -> 754 us (0.45)
  waiting for transfers between devices: 1020 us -> 293 us
  Pallas kernels: 0 us -> 173 us
  local copies, waits for them, and re-layouts: 270 us -> 101 us
  matrix products: 185 us -> 31.5 us
  other arithmetic: 105 us -> 48.7 us
  blocking collectives: 44.5 us -> 85.7 us
  starting transfers between devices: 22.9 us -> 0.85 us
    all_to_all x4 -> x0, waiting for transfers between devices: 507 us -> none  [the longest x1 360 us: per_device(): lax.all_to_all(paired, 'expert', split_axis=0, concat_axis=0, tiled=True)]
    pallas_call x0 -> x2, Pallas kernels: none -> 173 us  [the longest x1 103 us: run_forward(): pl.pallas_call(partial(forward_kernel, images=images, heads=heads), out_s...]
    reduce_scatter x2 -> x4, waiting for transfers between devices: 322 us -> 164 us  [the longest x1 59.6 us: per_device_dense(): lax.psum_scatter(grad_h_part, 'expert', scatter_dimension=0, axis_index_g...]
    dot_general x12 -> x1, matrix products: 160 us -> 4.27 us  [attention_backward(): jnp.einsum('gqhe,gkhe->ghqk', queries, keys_all, preferred_element_type=j...]
    psum x3, waiting for transfers between devices: 184 us -> 95.6 us  [the longest x1 38.3 us: per_device_dense(): lax.psum(lax.psum_scatter(grad_h_part, 'expert', scatter_dimension=0, axi...]
    psum x1 -> x2, blocking collectives: 39.2 us -> 85.7 us  [the longest x1 48.9 us: per_device_dense(): grad_router = lax.psum(grad_router[:, :experts_all], ('expert', 'tensor'))]
    reduce_sum x12 -> x1, other arithmetic: 47.4 us -> 2.42 us  [per_device_dense(): jnp.sum(jnp.where(chosen, keep_mask[:, :, None], 0), axis=1).astype(bf16)]
    convert_element_type x11 -> x1, local copies, waits for them, and re-layouts: 44.6 us -> 0.13 us  [per_device_dense(): jnp.sum(jnp.where(chosen, keep_mask[:, :, None], 0), axis=1).astype(bf16)]
  transfers between devices with their start and end apart: 12 -> 8, of which waited for: 9 -> 7; matrix products, arithmetic and copies ran while one was open for 18% -> 12% of each run, Pallas kernels for 0% -> 0%
where the time goes in v2:
time: 754 us; the launch traced here: 748 us
  waiting for transfers between devices  293 us (39%)
  Pallas kernels  173 us (23%)
  local copies, waits for them, and re-layouts  101 us (13%)
  blocking collectives  85.7 us (11%)
  other arithmetic  48.7 us (6%)
  matrix products  31.5 us (4%)
  between operations  14.9 us (2%)
    pallas_call x1, Pallas kernels, run_forward(): pl.pallas_call(partial(forward_kernel, images=images, heads=heads), out_s...  103 us
    pallas_call x1, Pallas kernels, run_experts(): pl.pallas_call(partial(expert_kernel, experts=experts, block=256), out_sh...  70.3 us
    reduce_scatter x1, waiting for transfers between devices, per_device_dense(): lax.psum_scatter(grad_h_part, 'expert', scatter_dimension=0, axis_index_g...  59.6 us
    reduce_scatter x1, waiting for transfers between devices, per_device_dense(): lax.psum_scatter(mixed_part, 'expert', scatter_dimension=0, axis_index_gr...  59.2 us
    psum x1, blocking collectives, per_device_dense(): grad_router = lax.psum(grad_router[:, :experts_all], ('expert', 'tensor'))  48.9 us
    reduce_scatter x2, waiting for transfers between devices, to_owner(): lax.psum_scatter(apart, 'expert', scatter_dimension=0, axis_index_groups=...  45.6 us
    psum x1, waiting for transfers between devices, per_device_dense(): lax.psum(lax.psum_scatter(grad_h_part, 'expert', scatter_dimension=0, axi...  38.3 us
    psum x1, blocking collectives, per_device_dense(): lax.psum((grad_gain_attn, grad_shift_attn, grad_gain_moe, grad_shift_moe)...  36.7 us
  transfers between devices with their start and end apart: 8, of which 7 were waited for; matrix products, arithmetic and copies ran while one was open for 12% of the time, Pallas kernels for 0%

profile of v2, /device:TPU:0, one launch (start us, length us, event | category | flops | bytes accessed | tf_op | source)
XLA Modules:
  0.0 748.4 jit_solution(15930310415721312275)
XLA Ops:
  27.7 3.3 pad.16.tok_ref
  31.0 103.0 %shard_map.212 = (bf16[8,208,192]{2,1,0:T(8,128)(2,1)}, bf16[8,208,192]{2,1,0:T(8,128)(2,1)}, bf16[8,208,192]{2,1,0:T(8,128)(2,1)}, bf16[8,208,192]{2,1,0:T(8,12...) custom-call(bf16[8,208,768]{2,1,0:T(8,128)(2,1)} %pad.16.tok_ref, ...), custom_call_target="tpu_custom_call" | custom-call | tf_op jit(solution)/shard_map/pallas_call | solution.py:726
  134.0 70.3 %shard_map.213 = (bf16[3328,768]{1,0:T(8,128)(2,1)}, bf16[3328,768]{1,0:T(8,128)(2,1)}, bf16[2,768,768]{2,1,0:T(8,128)(2,1)}, bf16[2,768,768]{2,1,0:T(8,128)(2,1)}, f32[768,128]{1,0:T(8,128)}) custom-call(bf16[3328,768]{1,0:T(8,128)(2,1)} %get-tuple-element.28.h_ref, bf16[3328,768]{1,0:T(8,128)(2,1)} %get-tuple-element.29.cot_ref, ...), custom_call_target="tpu_custom_call" | custom-call | tf_op jit(solution)/shard_map/pallas_call | solution.py:842
  207.2 59.6 %reduce-scatter.10.cloned.1.call-done = bf16[1664,768]{1,0:T(8,128)(2,1)} async-done(((bf16[3328,768]{1,0:T(8,128)(2,1)}), bf16[1664,768]{1,0:T(8,128)(2,1)}) %reduce-scatter.10.cloned.1.call-update) | async-done | bytes 2555920 | tf_op jit(solution)/shard_map/reduce_scatter | solution.py:917
  285.6 4.3 fusion.59
  289.9 38.3 %all-reduce.10.cloned.1.call-done = bf16[1664,768]{1,0:T(8,128)(2,1)} async-done(((bf16[1664,768]{1,0:T(8,128)(2,1)}), bf16[1664,768]{1,0:T(8,128)(2,1)}) %all-reduce.10.cloned.1.call-update) | async-done | bytes 2555920 | tf_op jit(solution)/shard_map/psum | solution.py:916
  328.2 5.0 convert_reduce_fusion
  333.3 5.1 fusion.9
  338.5 3.8 add_add_fusion.2
  347.2 5.3 reshape.173
  352.4 4.2 convolution_convert_fusion
  359.3 3.6 fusion.42
  362.9 4.0 multiply_reduce_fusion.1
  385.0 4.8 bitcast_convert_fusion
  390.5 6.0 reshape.175
  396.4 3.4 copy.106
  399.8 5.8 reshape.177
  405.6 8.7 %copy.107 = bf16[2,2,768,384]{2,1,0,3:T(2,128)(2,1)} copy(bf16[2,2,768,384]{3,1,2,0:T(2,128)(2,1)} %bitcast.92) | data formatting | bytes 4718592 | tf_op jit(solution)/shard_map/transpose | solution.py:928
  414.3 6.4 reshape.178
  421.2 3.9 fusion.48
  425.2 21.6 %all-reduce.12.cloned.1.call-done = bf16[1576,768]{1,0:T(8,128)(2,1)} async-done(((bf16[1576,768]{1,0:T(8,128)(2,1)}), bf16[1576,768]{1,0:T(8,128)(2,1)}) %all-reduce.12.cloned.1.call-update) | async-done | bytes 2420752 | tf_op jit(solution)/shard_map/psum | solution.py:958
  446.8 4.0 fusion.12
  450.8 3.4 fusion.37
  454.2 59.2 %reduce-scatter.8.cloned.1.call-done = bf16[1664,768]{1,0:T(8,128)(2,1)} async-done(((bf16[3328,768]{1,0:T(8,128)(2,1)}), bf16[1664,768]{1,0:T(8,128)(2,1)}) %reduce-scatter.8.cloned.1.call-update) | async-done | bytes 2555920 | tf_op jit(solution)/shard_map/reduce_scatter | solution.py:921
  513.4 4.5 copy.114
  517.9 48.9 %psum.71 = f32[768,4]{1,0:T(8,128)S(1)} all-reduce(f32[768,4]{1,0:T(8,128)S(1)} %bitcast.104), channel_id=1, replica_groups=mesh['expert'=8,'tensor'=4] {'expert','tensor'}, use_global_device_ids=true, to_apply=%region_25.26 | all-reduce | flops 3072 | bytes 24576 | tf_op jit(solution)/shard_map/psum | solution.py:964
  569.8 45.6 %reduce-scatter.14.cloned.1.call-done = bf16[768,384]{0,1:T(8,128)(2,1)} async-done(((bf16[3072,384]{0,1:T(8,128)(2,1)}), bf16[768,384]{0,1:T(8,128)(2,1)}) %reduce-scatter.14.cloned.1.call-update) | async-done | bytes 589840 | tf_op jit(solution)/shard_map/reduce_scatter | solution.py:930
  617.5 4.4 fusion.14
  621.9 36.7 %all-reduce.4 = (f32[768]{0:T(1024)}, f32[768]{0:T(1024)}, f32[768]{0:T(1024)}, f32[768]{0:T(1024)}) all-reduce(f32[768]{0:T(1024)S(1)} %get-tuple-element.89, f32[768]{0:T(1024)S(1)} %get-tuple-element.95, f32[768]{0:T(1024)S(1)} %get-tuple-element.87, f32[768]{0:T(1024)S(1)} %get-tuple-element.91), channel_id=1, replica_groups=mesh['expert'=8,'tensor'=4] {'expert'}, use_global_device_ids=true, to_apply=%region_16.17 | all-reduce | flops 3072 | bytes 24576 | tf_op jit(solution)/shard_map/psum | solution.py:963
  658.7 5.4 add_add_fusion.3
  664.1 35.7 %all-reduce.14.cloned.1.call-done = (bf16[3,768,192]{1,2,0:T(8,128)(2,1)}, bf16[192,768]{1,0:T(8,128)(2,1)}) async-done(((bf16[3,768,192]{1,2,0:T(8,128)(2,1)}, bf16[192,768]{1,0:T(8,128)(2,1)}), (bf16[3,768,192]{1,2,0:T(8,128)(2,1)}, bf16[192,768]{1,0:T(8,128)(2,1)})) %all-reduce.14.cloned.1.call-update) | async-done | bytes 1179664 | tf_op jit(solution)/shard_map/psum | solution.py:962
  704.1 32.0 %reduce-scatter.16.cloned.1.call-done = bf16[192,1664]{1,0:T(8,128)(2,1)} async-done(((bf16[768,1664]{1,0:T(8,128)(2,1)}), bf16[192,1664]{1,0:T(8,128)(2,1)}) %reduce-scatter.16.cloned.1.call-update) | async-done | bytes 638992
  (122 shorter events, 83.4 us)
Async XLA Ops:
  7.2 12.6 %copy-start.15 = (s32[1576,2]{0,1:T(2,128)S(1)}, s32[1576,2]{0,1:T(2,128)}, u32[]{:S(2)}) copy-start(s32[1576,2]{0,1:T(2,128)} %param.24) | copy-start | bytes 37828
  7.2 12.6 %copy-start.16 = (s32[1576,2]{0,1:T(2,128)S(1)}, s32[1576,2]{0,1:T(2,128)}, u32[]{:S(2)}) copy-start(s32[1576,2]{0,1:T(2,128)} %param.23) | copy-start | bytes 37828
  7.2 259.6 %reduce-scatter.10.cloned.1.call-start = ((), (), s32[]{:S(2)}) async-start(), calls=%async_computation.6 | async-start | bytes 7667712 | tf_op jit(solution)/shard_map/reduce_scatter | solution.py:917
  16.3 9.2 %copy-start = (bf16[1576,768]{1,0:T(8,128)(2,1)S(1)}, bf16[1576,768]{1,0:T(8,128)(2,1)}, u32[]{:S(2)}) copy-start(bf16[1576,768]{1,0:T(8,128)(2,1)} %param.13) | copy-start | bytes 7262212
  204.4 123.9 %all-reduce.10.cloned.1.call-start = ((), (), s32[]{:S(2)}) async-start(), calls=%async_computation.7 | async-start | bytes 5111808 | tf_op jit(solution)/shard_map/psum | solution.py:916
  207.2 63.6 %copy-start.8 = (bf16[8,208,192]{2,1,0:T(8,128)(2,1)S(1)}, bf16[8,208,192]{2,1,0:T(8,128)(2,1)}, u32[]{:S(2)}) copy-start(bf16[8,208,192]{2,1,0:T(8,128)(2,1)} %get-tuple-element.35) | copy-start | bytes 1916932
  266.9 179.9 %all-reduce.12.cloned.1.call-start = ((), (), s32[]{:S(2)}) async-start(), calls=%async_computation.8 | async-start | bytes 4841472 | tf_op jit(solution)/shard_map/psum | solution.py:958
  273.2 16.7 %copy-start.3 = (bf16[8,197,192]{1,2,0:T(8,128)(2,1)}, bf16[8,197,192]{1,2,0:T(8,128)(2,1)S(1)}, u32[]{:S(2)}) copy-start(bf16[8,197,192]{1,2,0:T(8,128)(2,1)S(1)} %copy.93) | copy-start | bytes 1815556
  281.3 46.9 %copy-start.13 = (f32[768]{0:T(1024)S(1)}, f32[768]{0:T(1024)}, u32[]{:S(2)}) copy-start(f32[768]{0:T(1024)} %param.18) | copy-start | bytes 9220
  328.2 5.1 copy-start.2
  328.2 10.2 %slice-start = ((s8[5111808]{0:T(1024)(128)(4,1)}), s8[4194304]{0:T(1024)(128)(4,1)S(1)}, s32[]{:S(2)}) async-start(s8[5111808]{0:T(1024)(128)(4,1)} %bitcast.83), calls=%async_computation.13 | async-start | bytes 8388608
  333.3 5.1 slice-start.1
  342.2 2.3 copy-start.1
  347.2 5.3 copy-start.7
  359.3 3.6 copy-start.6
  359.3 7.6 %slice-start.2 = ((s8[4915200]{0:T(1024)(128)(4,1)}), s8[4194304]{0:T(1024)(128)(4,1)S(1)}, s32[]{:S(2)}) async-start(s8[4915200]{0:T(1024)(128)(4,1)} %bitcast.85), calls=%async_computation.15 | async-start | bytes 8388608
  362.9 4.1 slice-start.3
  367.0 1.2 copy-start.5
  367.0 3.0 copy-start.4
  383.7 1.3 copy-start.11
  389.8 123.6 %reduce-scatter.8.cloned.1.call-start = ((), (), s32[]{:S(2)}) async-start(), calls=%async_computation.5 | async-start | bytes 7667712 | tf_op jit(solution)/shard_map/reduce_scatter | solution.py:921
  390.4 177.2 %reduce-scatter.12.cloned.1.call-start = ((), (), s32[]{:S(2)}) async-start(), calls=%async_computation.9 | async-start | bytes 2949120 | tf_op jit(solution)/shard_map/reduce_scatter | solution.py:930
  399.8 215.6 %reduce-scatter.14.cloned.1.call-start = ((), (), s32[]{:S(2)}) async-start(), calls=%async_computation.10 | async-start | bytes 2949120 | tf_op jit(solution)/shard_map/reduce_scatter | solution.py:930
  414.3 6.9 copy-start.9
  420.7 26.0 %copy-start.14 = (f32[768]{0:T(1024)S(1)}, f32[768]{0:T(1024)}, u32[]{:S(2)}) copy-start(f32[768]{0:T(1024)} %param.14) | copy-start | bytes 9220
  420.8 279.0 %all-reduce.14.cloned.1.call-start = ((), (), s32[]{:S(2)}) async-start(), calls=%async_computation.12 | async-start | bytes 2359296 | tf_op jit(solution)/shard_map/psum | solution.py:962
  421.2 29.6 %copy-start.17 = (f32[768]{0:T(1024)S(1)}, f32[768]{0:T(1024)}, u32[]{:S(2)}) copy-start(f32[768]{0:T(1024)} %param.15) | copy-start | bytes 9220
  446.8 4.0 copy-start.12
  454.2 63.8 %copy-start.10 = (f32[768,128]{1,0:T(8,128)S(1)}, f32[768,128]{1,0:T(8,128)}, u32[]{:S(2)}) copy-start(f32[768,128]{1,0:T(8,128)} %get-tuple-element.40) | copy-start | bytes 1179652
  454.2 281.9 %reduce-scatter.16.cloned.1.call-start = ((), (), s32[]{:S(2)}) async-start(), calls=%async_computation.11 | async-start | bytes 3194880
Sparse Core Ops, SparseCore 0:
  204.5 62.3 reduce-scatter.9
  269.4 58.8 all-reduce.9
  390.0 56.7 all-reduce.11
  449.0 64.3 reduce-scatter.7
  515.5 50.0 reduce-scatter.11
  567.8 47.5 reduce-scatter.13
  619.4 80.3 all-reduce.13
  702.6 33.5 reduce-scatter.15

commit v3 on v2

--- a/solution.py
+++ b/solution.py
@@ -372,6 +372,12 @@
     kept_out,
     up_out,
     down_out,
+    q_all,
+    k_all,
+    v_all,
+    att_all,
+    lse_all,
+    resid_all,
     h_all,
     cot_all,
     kept_all,
@@ -398,6 +404,8 @@
     w_r,
     c_s,
     c_r,
+    own_sem,
+    cot_sem,
     out_sem,
     *,
     images,
@@ -426,16 +434,18 @@
             src_ref=src, dst_ref=dst, send_sem=send, recv_sem=recv, device_id=device, device_id_type=MESH
         )
 
-    def slot(expert):
+    def slot(expert, plane):
+        pair = (expert // 2 + plane // 2) % 2
         return (
-            up_out.at[expert // 2, :, lanes_at(expert % 2 * hidden, hidden)],
-            down_out.at[expert // 2, aligned(expert % 2 * hidden, hidden), :],
+            up_out.at[pair, :, lanes_at(expert % 2 * hidden, hidden)],
+            down_out.at[pair, aligned(expert % 2 * hidden, hidden), :],
         )
 
     def hop(step, way):
         expert = z_at - step if way == 0 else z_at + step
-        source = (up_ref, down_ref) if step == 0 else slot(expert)
-        target = slot(expert)
+        plane = z_at + 1 if way == 0 else z_at - 1
+        source = (up_ref, down_ref) if step == 0 else slot(expert, z_at)
+        target = slot(expert, plane)
         device = z_up if way == 0 else z_down
         return [remote(source[n], target[n], w_s.at[way, step, n], w_r.at[way, step, n], device) for n in range(2)]
 
@@ -449,7 +459,7 @@
 
     def hop_arriving(step, way):
         expert = z_at - 1 - step if way == 0 else z_at + 1 + step
-        target = slot(expert)
+        target = slot(expert, z_at)
         return [remote(target[n], target[n], w_s.at[way, step, n], w_r.at[way, step, n], core_dev) for n in range(2)]
 
     def start_hops(step):
@@ -469,58 +479,58 @@
                     copy.wait_recv()
 
     start_hops(0)
-    own = slot(z_at)
-    own_copies = [
-        pltpu.make_async_copy((up_ref, down_ref)[n], own[n], out_sem.at[n]) for n in range(2)
-    ]
+    own = slot(z_at, z_at)
+    own_copies = [pltpu.make_async_copy((up_ref, down_ref)[n], own[n], own_sem.at[n]) for n in range(2)]
     for copy in own_copies:
         copy.start()
 
-    quarter = cot_ref.shape[1]
     swap = remote(cot_ref, cot_core, c_s.at[0], c_r.at[0], core_dev)
     swap.start()
-    kept_all[aligned(y_at * rows, rows), :] = kept_ref[...]
-    kept_mine = kept_all.at[aligned(y_at * rows, rows), :]
-    kept_y = remote(kept_mine, kept_mine, c_s.at[7], c_r.at[7], y_dev)
+    kept_all[pl.ds(0, rows), :] = kept_ref[...]
+
+    def kept_half(side, core):
+        return kept_all.at[aligned(side * rows + core * half, half), :]
+
+    kept_y = remote(kept_half(0, core_at), kept_half(1, core_at), c_s.at[7], c_r.at[7], y_dev)
+    kept_share = remote(kept_half(1, core_at), kept_half(1, core_at), c_s.at[6], c_r.at[6], core_dev)
+    kept_share_in = remote(kept_half(1, other), kept_half(1, other), c_s.at[6], c_r.at[6], core_dev)
     kept_y.start()
     swap.wait_recv()
-    base = y_at * rows
 
     @pl.when(core_at == 0)
     def _():
         both = jnp.concatenate([cot_ref[...], cot_core[...]], axis=1)
-        cot_all[aligned(base, rows), lanes_at(x_at * wide, wide)] = both
+        cot_all[pl.ds(0, rows), lanes_at(x_at * wide, wide)] = both
 
     @pl.when(core_at == 1)
     def _():
         both = jnp.concatenate([cot_core[...], cot_ref[...]], axis=1)
-        cot_all[aligned(base, rows), lanes_at(x_at * wide, wide)] = both
-
-    def block(row_side, col_side, core):
-        return cot_all.at[aligned(row_side * rows + core * half, half), lanes_at(col_side * wide, wide)]
-
-    def cot_copy(number, row_side, col_side, core, device):
-        ref = block(row_side, col_side, core)
-        return remote(ref, ref, c_s.at[number], c_r.at[number], device)
-
-    cot_x = cot_copy(1, y_at, x_at, core_at, x_dev)
-    cot_y = cot_copy(2, y_at, x_at, core_at, y_dev)
+        cot_all[pl.ds(0, rows), lanes_at(x_at * wide, wide)] = both
+
+    def block(side, col_side, core):
+        return cot_all.at[aligned(side * rows + core * half, half), lanes_at(col_side * wide, wide)]
+
+    def cot_copy(number, source, target, device):
+        return remote(source, target, c_s.at[number], c_r.at[number], device)
+
+    mine_block = block(0, x_at, core_at)
+    cot_x = cot_copy(1, mine_block, mine_block, x_dev)
+    cot_y = cot_copy(2, mine_block, block(1, x_at, core_at), y_dev)
     cot_x.start()
     cot_y.start()
-    cot_x_in = cot_copy(1, y_at, 1 - x_at, core_at, x_dev)
-    cot_y_in = cot_copy(2, 1 - y_at, x_at, core_at, y_dev)
-    cot_relay = cot_copy(3, y_at, 1 - x_at, core_at, y_dev)
-    cot_relay_in = cot_copy(3, 1 - y_at, 1 - x_at, core_at, y_dev)
+    across_x, across_y, across_both = block(0, 1 - x_at, core_at), block(1, x_at, core_at), block(1, 1 - x_at, core_at)
+    cot_x_in = cot_copy(1, across_x, across_x, x_dev)
+    cot_y_in = cot_copy(2, across_y, across_y, y_dev)
+    relay_y = cot_copy(3, across_x, across_both, y_dev)
+    relay_x = cot_copy(3, across_y, across_y, x_dev)
+    relay_in = cot_copy(3, across_both, across_both, y_dev)
     cot_share = [
-        cot_copy(4, y_at, 1 - x_at, core_at, core_dev),
-        cot_copy(5, 1 - y_at, x_at, core_at, core_dev),
-        cot_copy(6, 1 - y_at, 1 - x_at, core_at, core_dev),
+        cot_copy(4, across_x, across_x, core_dev),
+        cot_copy(5, across_y, across_y, core_dev),
+        cot_copy(8, across_both, across_both, core_dev),
     ]
-    cot_share_in = [
-        cot_copy(4, y_at, 1 - x_at, other, core_dev),
-        cot_copy(5, 1 - y_at, x_at, other, core_dev),
-        cot_copy(6, 1 - y_at, 1 - x_at, other, core_dev),
-    ]
+    arriving = [block(0, 1 - x_at, other), block(1, x_at, other), block(1, 1 - x_at, other)]
+    cot_share_in = [cot_copy(number, ref, ref, core_dev) for number, ref in zip((4, 5, 8), arriving)]
 
     lane = lax.broadcasted_iota(jnp.int32, (PITCH, 2 * HD), 1)
     key_mask = lax.broadcasted_iota(jnp.int32, (PITCH, PITCH), 1) < SEQ
@@ -535,9 +545,9 @@
         queries = dot(h_one, qkv_ref[0]).astype(bf16)
         keys = dot(h_one, qkv_ref[1]).astype(bf16)
         values = dot(h_one, qkv_ref[2]).astype(bf16)
-        q_ref[image] = queries
-        k_ref[image] = keys
-        v_ref[image] = values
+        q_all[image] = queries
+        k_all[image] = keys
+        v_all[image] = values
         outs = []
         lse = jnp.zeros((PITCH, 2 * HD), f32)
         for head in range(heads):
@@ -554,7 +564,7 @@
             weights = (powers / row_sum).astype(bf16)
             outs.append(dot(weights, v_head))
             lse = jnp.where(lane == head, peak + jnp.log(row_sum), lse)
-        lse_ref[image] = lse
+        lse_all[image] = lse
         joined = []
         for head in range(0, heads, 2):
             if head + 1 < heads:
@@ -562,7 +572,7 @@
             else:
                 joined.append(outs[head])
         attended = jnp.concatenate(joined, axis=1).astype(bf16)
-        att_ref[image] = attended
+        att_all[image] = attended
         part[...] = dot(attended, out_w_ref[...])
         mine[image] = part[:, my_cols]
         core_to[image] = part[:, their_cols].astype(bf16)
@@ -576,24 +586,36 @@
     def total_copy(image):
         return remote(total_to.at[image], total_from.at[image], tot_s.at[image], tot_r.at[image], core_dev)
 
-    def h_block(row_side, image, core):
-        return h_all.at[aligned(row_side * rows + image * PITCH, PITCH), lanes_at(core * wide, wide)]
+    def h_block(side, image, core):
+        return h_all.at[aligned(side * rows + image * PITCH, PITCH), lanes_at(core * wide, wide)]
 
     def y_copy(image):
-        ref = h_block(y_at, image, core_at)
-        return remote(ref, ref, y_s.at[image], y_r.at[image], y_dev)
-
-    def y_arriving(image):
-        ref = h_block(1 - y_at, image, core_at)
-        return remote(ref, ref, y_s.at[image], y_r.at[image], y_dev)
+        return remote(h_block(0, image, core_at), h_block(1, image, core_at), y_s.at[image], y_r.at[image], y_dev)
 
     def relay_copy(image):
-        ref = h_block(1 - y_at, image, core_at)
+        ref = h_block(1, image, core_at)
         return remote(ref, ref, rel_s.at[image], rel_r.at[image], core_dev)
 
     def relay_arriving(image):
-        ref = h_block(1 - y_at, image, other)
+        ref = h_block(1, image, other)
         return remote(ref, ref, rel_s.at[image], rel_r.at[image], core_dev)
+
+    attend_outs = ((q_all, q_ref), (k_all, k_ref), (v_all, v_ref), (att_all, att_ref), (lse_all, lse_ref))
+
+    def out_copies(image):
+        copies = [
+            pltpu.make_async_copy(kept.at[image], out.at[image], out_sem.at[n, image])
+            for n, (kept, out) in enumerate(attend_outs)
+        ]
+        at = aligned(image * PITCH, PITCH)
+        return copies, [
+            pltpu.make_async_copy(resid_all.at[image], resid_ref.at[at, :], out_sem.at[5, image]),
+            pltpu.make_async_copy(h_all.at[at, :], h_out.at[at, :], out_sem.at[6, image]),
+        ]
+
+    def other_copy(image):
+        at = aligned(rows + image * PITCH, PITCH)
+        return pltpu.make_async_copy(h_all.at[at, :], h_out.at[at, :], out_sem.at[7, image])
 
     def stage(tick, lag, run):
         image = tick - lag
@@ -605,6 +627,8 @@
     def run_attend(image):
         attend(image)
         core_copy(image).start()
+        for copy in out_copies(image)[0]:
+            copy.start()
 
     def run_x(image):
         core_copy(image).wait_recv()
@@ -621,17 +645,20 @@
         part[:, my_cols] = total_to[image].astype(f32)
         part[:, their_cols] = total_from[image].astype(f32)
         resid = tok_ref[image].astype(f32) + part[...]
-        resid_ref[image] = resid
+        resid_all[image] = resid
         normed, _ = norm_stats(resid)
-        h_all[aligned(base + image * PITCH, PITCH), :] = (normed * gain2 + shift2).astype(bf16)
+        h_all[aligned(image * PITCH, PITCH), :] = (normed * gain2 + shift2).astype(bf16)
         y_copy(image).start()
+        for copy in out_copies(image)[1]:
+            copy.start()
 
     def run_relay(image):
-        y_arriving(image).wait_recv()
+        y_copy(image).wait_recv()
         relay_copy(image).start()
 
     def run_end(image):
         relay_arriving(image).wait_recv()
+        other_copy(image).start()
 
     def at_tick(tick, when, run):
         @pl.when(tick == when)
@@ -640,23 +667,29 @@
 
     def cot_step_one():
         cot_x_in.wait_recv()
-        cot_relay.start()
         cot_share[0].start()
+
+        @pl.when(core_at == 0)
+        def _():
+            relay_y.start()
+
+        kept_y.wait_recv()
+        kept_share.start()
 
     def cot_step_two():
         cot_y_in.wait_recv()
         cot_share[1].start()
 
+        @pl.when(core_at == 1)
+        def _():
+            relay_x.start()
+
     def weights_step_one():
         await_hops(0)
         start_hops(1)
 
-    def weights_step_two():
-        await_hops(1)
-        start_hops(2)
-
     def cot_step_three():
-        cot_relay_in.wait_recv()
+        relay_in.wait_recv()
         cot_share[2].start()
 
     def per_tick(tick, _):
@@ -666,39 +699,43 @@
         stage(tick, 5, run_norm)
         stage(tick, 9, run_relay)
         stage(tick, 10, run_end)
-        at_tick(tick, 7, cot_step_one)
+        at_tick(tick, 5, cot_step_one)
+        at_tick(tick, 7, cot_step_two)
         at_tick(tick, 8, weights_step_one)
-        at_tick(tick, 9, cot_step_two)
-        at_tick(tick, 14, weights_step_two)
-        at_tick(tick, 15, cot_step_three)
+        at_tick(tick, 14, cot_step_three)
         return 0
 
     lax.fori_loop(0, images + 10, per_tick, 0)
-    for copy in cot_share_in:
+    for copy in (*cot_share_in, kept_share_in):
         copy.wait_recv()
-    kept_theirs = kept_all.at[aligned((1 - y_at) * rows, rows), :]
-    remote(kept_theirs, kept_theirs, c_s.at[7], c_r.at[7], y_dev).wait_recv()
     outs = [
-        pltpu.make_async_copy(h_all, h_out, out_sem.at[2]),
-        pltpu.make_async_copy(cot_all, cot_out, out_sem.at[3]),
-        pltpu.make_async_copy(kept_all, kept_out, out_sem.at[4]),
+        pltpu.make_async_copy(cot_all, cot_out, cot_sem.at[0]),
+        pltpu.make_async_copy(kept_all, kept_out, cot_sem.at[1]),
     ]
     for copy in outs:
         copy.start()
-    for copy in (swap, kept_y, cot_x, cot_y, cot_relay, *cot_share):
+    for copy in (swap, kept_y, kept_share, cot_x, cot_y, *cot_share):
         copy.wait_send()
 
+    @pl.when(core_at == 0)
+    def _():
+        relay_y.wait_send()
+
+    @pl.when(core_at == 1)
+    def _():
+        relay_x.wait_send()
+
     def drain(image, _):
-        core_copy(image).wait_send()
-        x_copy(image).wait_send()
-        total_copy(image).wait_send()
-        y_copy(image).wait_send()
-        relay_copy(image).wait_send()
+        for copy in (core_copy, x_copy, total_copy, y_copy, relay_copy):
+            copy(image).wait_send()
+        first, second = out_copies(image)
+        for copy in (*first, *second, other_copy(image)):
+            copy.wait()
         return 0
 
     lax.fori_loop(0, images, drain, 0)
-    await_hops(2)
-    for step in range(3):
+    await_hops(1)
+    for step in range(2):
         for way in range(2):
 
             @pl.when(hop_goes(step, way))
@@ -731,7 +768,7 @@
             shape((images, PITCH, share), bf16),
             shape((images, PITCH, share), bf16),
             shape((images, PITCH, 128), f32),
-            shape((images, PITCH, features), f32),
+            shape((rows, features), f32),
             shape((2 * rows, features), bf16),
             shape((2 * rows, features), bf16),
             shape((2 * rows, 128), bf16),
@@ -739,8 +776,11 @@
             shape((2, 2 * hidden, features), bf16),
         ],
         in_specs=[vmem] * 7 + [anywhere] * 2 + [vmem] * 2,
-        out_specs=[vmem] * 6 + [anywhere] * 5,
+        out_specs=[anywhere] * 11,
         scratch_shapes=[
+            *[pltpu.VMEM((images, PITCH, share), bf16)] * 4,
+            pltpu.VMEM((images, PITCH, 128), f32),
+            pltpu.VMEM((images, PITCH, features), f32),
             pltpu.VMEM((2 * rows, features), bf16),
             pltpu.VMEM((2 * rows, features), bf16),
             pltpu.VMEM((2 * rows, 128), bf16),
@@ -755,104 +795,1133 @@
             pltpu.VMEM((rows, share), bf16),
         ]
         + [dma((images,))] * 10
-        + [dma((2, 3, 2))] * 2
-        + [dma((8,))] * 2
-        + [dma((5,))],
+        + [dma((2, 2, 2))] * 2
+        + [dma((9,))] * 2
+        + [dma((2,)), dma((2,)), dma((8, images))],
         compiler_params=pltpu.CompilerParams(
             collective_id=1, has_side_effects=True, vmem_limit_bytes=60 << 20
         ),
     )(tok, gain1, shift1, gain2, shift2, qkv_w, out_w, up, down, cot, kept)
 
 
-def expert_kernel(
+def expert_math(h_rows, cot_rows, kept, router, up, down, pair, experts):
+    block = h_rows.shape[0]
+    hidden = up.shape[1] // 2
+    lane = lax.broadcasted_iota(jnp.int32, (block, 128), 1)
+    logits = jnp.where(lane < experts, dot(h_rows, router), -1e30)
+    powers = jnp.exp(logits - jnp.max(logits, axis=1, keepdims=True))
+    probs = powers / jnp.sum(powers, axis=1, keepdims=True)
+    gates = kept * probs
+    pre_act = dot(h_rows, up)
+    back = dot(cot_rows, down, ((1,), (1,)))
+    normal_cdf = 0.5 + 0.5 * lax.erf(pre_act * 0.7071067811865476)
+    gelu = pre_act * normal_cdf
+    slope = normal_cdf + pre_act * (0.3989422804014327 * jnp.exp(-0.5 * pre_act * pre_act))
+    product = gelu * back
+    grad_gate = jnp.zeros((block, 128), f32)
+    spread = []
+    for side in range(2):
+        chosen = lane == 2 * pair + side
+        part = jnp.sum(product[:, side * hidden : (side + 1) * hidden], axis=1, keepdims=True)
+        grad_gate = jnp.where(chosen, part, grad_gate)
+        gate = jnp.sum(jnp.where(chosen, gates, 0.0), axis=1, keepdims=True)
+        spread.append(jnp.broadcast_to(gate, (block, hidden)))
+    gate = jnp.concatenate(spread, axis=1)
+    hidden_rows = (gelu * gate).astype(bf16)
+    grad_pre = (slope * back * gate).astype(bf16)
+    return hidden_rows, grad_pre, probs, grad_gate
+
+
+def first_pair_kernel(
     h_ref,
     cot_ref,
+    kept_ref,
+    router_ref,
     up_ref,
     down_ref,
+    up_all,
+    down_all,
+    mixed_ref,
+    grad_h_ref,
+    gate_ref,
+    grad_up_ref,
+    grad_down_ref,
+    up_late,
+    down_late,
+    up_sum,
+    down_sum,
+    late_s,
+    late_r,
+    *,
+    experts,
+    steps,
+):
+    expert_at = lax.axis_index("expert")
+    tensor_at = lax.axis_index("tensor")
+    z_at = expert_at // 2
+    hidden = up_late.shape[1]
+    partner = (jnp.where(z_at % 2 == 0, expert_at + 2, expert_at - 2), tensor_at)
+    inner = (z_at == 1) | (z_at == 2)
+    outer = (z_at == 0) | (z_at == 3)
+    far = jnp.where(z_at == 1, hidden, 0)
+    sources = (up_all.at[1, :, lanes_at(far, hidden)], down_all.at[1, aligned(far, hidden), :])
+    hops = [
+        pltpu.make_async_remote_copy(
+            src_ref=source,
+            dst_ref=target,
+            send_sem=late_s.at[number],
+            recv_sem=late_r.at[number],
+            device_id=partner,
+            device_id_type=MESH,
+        )
+        for number, (source, target) in enumerate(zip(sources, (up_late, down_late)))
+    ]
+
+    @pl.when(pl.program_id(0) == 0)
+    def _():
+        greet([(True, partner)])
+
+        @pl.when(inner)
+        def _():
+            for copy in hops:
+                copy.start()
+
+        up_sum[...] = jnp.zeros_like(up_sum)
+        down_sum[...] = jnp.zeros_like(down_sum)
+
+    h_rows, cot_rows = h_ref[...], cot_ref[...]
+    up, down = up_ref[0], down_ref[0]
+    hidden_rows, grad_pre, _, grad_gate = expert_math(
+        h_rows, cot_rows, kept_ref[...].astype(f32), router_ref[...], up, down, z_at // 2, experts
+    )
+    gate_ref[...] = grad_gate
+    mixed_ref[...] = dot(hidden_rows, down).astype(bf16)
+    grad_h_ref[...] = dot(grad_pre, up, ((1,), (1,))).astype(bf16)
+    up_sum[...] += dot(h_rows.T, grad_pre)
+    down_sum[...] += dot(cot_rows.T, hidden_rows)
+
+    @pl.when(pl.program_id(0) == steps - 1)
+    def _():
+        grad_up_ref[...] = up_sum[...].astype(bf16)
+        grad_down_ref[...] = down_sum[...].astype(bf16)
+
+        @pl.when(inner)
+        def _():
+            for copy in hops:
+                copy.wait_send()
+
+        @pl.when(outer)
+        def _():
+            for copy in hops:
+                copy.wait_recv()
+
+
+BLOCK = 2 * PITCH
+
+
+def run_first_pair(h_rows, cot_rows, kept, router, up, down, experts):
+    rows, features = h_rows.shape
+    width = up.shape[2]
+    steps = rows // BLOCK
+    anywhere = pl.BlockSpec(memory_space=pl.ANY)
+    shape = jax.ShapeDtypeStruct
+
+    def by_step(lanes):
+        return pl.BlockSpec((BLOCK, lanes), lambda n: (n, 0))
+
+    def whole(*dims):
+        return pl.BlockSpec(dims, lambda n: (0,) * len(dims))
+
+    return pl.pallas_call(
+        partial(first_pair_kernel, experts=experts, steps=steps),
+        grid=(steps,),
+        out_shape=[
+            shape((rows, features), bf16),
+            shape((rows, features), bf16),
+            shape((rows, 128), f32),
+            shape((features, width), bf16),
+            shape((features, width), bf16),
+            shape((features, width // 2), bf16),
+            shape((width // 2, features), bf16),
+        ],
+        in_specs=[
+            by_step(features),
+            by_step(features),
+            by_step(128),
+            whole(features, 128),
+            whole(1, features, width),
+            whole(1, width, features),
+            anywhere,
+            anywhere,
+        ],
+        out_specs=[
+            by_step(features),
+            by_step(features),
+            by_step(128),
+            whole(features, width),
+            whole(features, width),
+            anywhere,
+            anywhere,
+        ],
+        scratch_shapes=[pltpu.VMEM((features, width), f32)] * 2 + [pltpu.SemaphoreType.DMA((2,))] * 2,
+        compiler_params=pltpu.CompilerParams(
+            collective_id=3, has_side_effects=True, vmem_limit_bytes=60 << 20
+        ),
+    )(h_rows, cot_rows, kept, router, up, down, up, down)
+
+
+def turn_is_other(turn):
+    return (turn == 0) | ((turn % 2 == 1) & (turn < 7))
+
+
+def turn_block(turn):
+    own = jnp.where(turn == 7, 3, turn // 2 - 1)
+    return jnp.where(turn_is_other(turn), 4 + (turn + 1) // 2, own)
+
+
+def second_pair_kernel(
+    h_ref,
+    cot_ref,
     kept_ref,
     router_ref,
+    mixed_first,
+    grad_h_first,
+    gate_first,
+    up_all,
+    down_all,
+    up_late,
+    down_late,
     mixed_ref,
-    grad_h_ref,
     grad_up_ref,
     grad_down_ref,
     grad_router_ref,
+    grad_h_out,
+    up_vm,
+    down_vm,
     up_sum,
     down_sum,
+    router_sum,
+    ring,
+    from_core,
+    from_y,
+    from_x,
+    load,
+    core_s,
+    core_r,
+    y_s,
+    y_r,
+    x_s,
+    x_r,
+    tot_s,
+    tot_r,
+    store,
     *,
     experts,
-    block,
+    steps,
 ):
-    pairs = up_ref.shape[0]
-    hidden = up_ref.shape[2] // 2
-    lane = lax.broadcasted_iota(jnp.int32, (block, 128), 1)
-    up_sum[...] = jnp.zeros_like(up_sum)
-    down_sum[...] = jnp.zeros_like(down_sum)
-    grad_router_ref[...] = jnp.zeros_like(grad_router_ref)
-
-    def per_block(number, _):
-        at = pl.ds(pl.multiple_of(number * block, block), block)
-        h_rows, cot_rows = h_ref[at, :], cot_ref[at, :]
-        h_turned, cot_turned = h_rows.T, cot_rows.T
-        logits = jnp.where(lane < experts, dot(h_rows, router_ref[...]), -1e30)
-        powers = jnp.exp(logits - jnp.max(logits, axis=1, keepdims=True))
-        probs = powers / jnp.sum(powers, axis=1, keepdims=True)
-        kept = kept_ref[at, :].astype(f32)
-        gates = kept * probs
-        grad_gate = jnp.zeros((block, 128), f32)
-        mixed = grad_h = 0.0
-        for pair in range(pairs):
-            pre_act = dot(h_rows, up_ref[pair])
-            back = dot(cot_rows, down_ref[pair], ((1,), (1,)))
-            normal_cdf = 0.5 + 0.5 * lax.erf(pre_act * 0.7071067811865476)
-            gelu = pre_act * normal_cdf
-            slope = normal_cdf + pre_act * (0.3989422804014327 * jnp.exp(-0.5 * pre_act * pre_act))
-            product = gelu * back
-            spread = []
-            for side in range(2):
-                expert = 2 * pair + side
-                part = jnp.sum(product[:, side * hidden : (side + 1) * hidden], axis=1, keepdims=True)
-                grad_gate = jnp.where(lane == expert, part, grad_gate)
-                spread.append(jnp.broadcast_to(gates[:, expert : expert + 1], (block, hidden)))
-            gate = jnp.concatenate(spread, axis=1)
-            hidden_rows = (gelu * gate).astype(bf16)
-            grad_pre = (slope * back * gate).astype(bf16)
-            mixed += dot(hidden_rows, down_ref[pair])
-            grad_h += dot(grad_pre, up_ref[pair], ((1,), (1,)))
-            up_sum[pair] += dot(h_turned, grad_pre)
-            down_sum[pair] += dot(cot_turned, hidden_rows)
-        grad_gate = kept * grad_gate
-        grad_logits = (
-            probs * (grad_gate - jnp.sum(probs * grad_gate, axis=1, keepdims=True))
-        ).astype(bf16)
-        mixed_ref[at, :] = mixed.astype(bf16)
-        grad_h_ref[at, :] = (grad_h + dot(grad_logits, router_ref[...], ((1,), (1,)))).astype(bf16)
-        grad_router_ref[...] += dot(h_turned, grad_logits)
-        return 0
-
-    lax.fori_loop(0, h_ref.shape[0] // block, per_block, 0)
-    grad_up_ref[...] = up_sum[...].astype(bf16)
-    grad_down_ref[...] = down_sum[...].astype(bf16)
-
-
-def run_experts(h_rows, cot_rows, up, down, kept, router, experts):
+    turn = pl.program_id(0)
+    expert_at = lax.axis_index("expert")
+    tensor_at = lax.axis_index("tensor")
+    z_at, y_at = expert_at // 2, expert_at % 2
+    x_at, core_at = tensor_at // 2, tensor_at % 2
+    hidden = up_late.shape[1]
+    wide = ring.shape[2] // 2
+    core_dev = (expert_at, tensor_at + 1 - 2 * core_at)
+    x_dev = (expert_at, tensor_at + 2 - 4 * x_at)
+    y_dev = (expert_at + 1 - 2 * y_at, tensor_at)
+    my_cols = lanes_at(core_at * wide, wide)
+    their_cols = lanes_at((1 - core_at) * wide, wide)
+
+    def remote(src, dst, send, recv, device):
+        return pltpu.make_async_remote_copy(
+            src_ref=src, dst_ref=dst, send_sem=send, recv_sem=recv, device_id=device, device_id_type=MESH
+        )
+
+    def core_copy(number):
+        return remote(ring.at[number % 2, :, their_cols], from_core.at[number], core_s.at[number], core_r.at[number], core_dev)
+
+    def y_copy(number, place):
+        return remote(from_core.at[number], from_y.at[place], y_s.at[place], y_r.at[place], y_dev)
+
+    def x_copy(number, place):
+        return remote(from_core.at[number], from_x.at[place], x_s.at[place], x_r.at[place], x_dev)
+
+    def out_rows(place):
+        return grad_h_out.at[aligned(place * BLOCK, BLOCK), my_cols]
+
+    def total_copy(place):
+        return remote(from_x.at[place], out_rows(place), tot_s.at[place], tot_r.at[place], core_dev)
+
+    def store_copy(place):
+        return pltpu.make_async_copy(from_x.at[place], out_rows(place), store.at[place])
+
+    def own_turn(place):
+        return jnp.where(place == 3, 7, 2 * place + 2)
+
+    def other_turn(place):
+        return jnp.where(place == 0, 0, 2 * place - 1)
+
+    def pass_other(number):
+        core_copy(number).wait_recv()
+        total = from_core[number].astype(f32) + ring[number % 2, :, my_cols].astype(f32)
+        from_core[number] = total.astype(bf16)
+        y_copy(number, (number + 1) // 2).start()
+
+    def pass_own(number, place):
+        core_copy(number).wait_recv()
+        y_copy(number, place).wait_recv()
+        total = from_core[number].astype(f32) + ring[number % 2, :, my_cols].astype(f32) + from_y[place].astype(f32)
+        from_core[number] = total.astype(bf16)
+        x_copy(number, place).start()
+
+    def pass_total(place):
+        number = own_turn(place)
+        x_copy(number, place).wait_recv()
+        from_x[place] = (from_core[number].astype(f32) + from_x[place].astype(f32)).astype(bf16)
+        total_copy(place).start()
+        store_copy(place).start()
+
+    @pl.when(turn == 0)
+    def _():
+        greet([(True, core_dev), (True, x_dev), (True, y_dev)])
+        late_expert = jnp.where(z_at == 0, 1, 0)
+        late = late_expert * hidden
+        is_outer = (z_at == 0) | (z_at == 3)
+        whole = [
+            pltpu.make_async_copy(up_all.at[1], up_vm, load.at[0]),
+            pltpu.make_async_copy(down_all.at[1], down_vm, load.at[1]),
+        ]
+        for copy in whole:
+            copy.start()
+        up_sum[...] = jnp.zeros_like(up_sum)
+        down_sum[...] = jnp.zeros_like(down_sum)
+        router_sum[...] = jnp.zeros_like(router_sum)
+        for copy in whole:
+            copy.wait()
+
+        @pl.when(is_outer)
+        def _():
+            parts = [
+                pltpu.make_async_copy(up_late, up_vm.at[:, lanes_at(late, hidden)], load.at[0]),
+                pltpu.make_async_copy(down_late, down_vm.at[aligned(late, hidden), :], load.at[1]),
+            ]
+            for copy in parts:
+                copy.start()
+            for copy in parts:
+                copy.wait()
+
+    h_rows, cot_rows = h_ref[...], cot_ref[...]
+    up, down, router = up_vm[...], down_vm[...], router_ref[...]
+    kept = kept_ref[...].astype(f32)
+    hidden_rows, grad_pre, probs, grad_gate = expert_math(
+        h_rows, cot_rows, kept, router, up, down, 1 - z_at // 2, experts
+    )
+    grad_gate = kept * (grad_gate + gate_first[...])
+    grad_logits = (probs * (grad_gate - jnp.sum(probs * grad_gate, axis=1, keepdims=True))).astype(bf16)
+
+    before = turn - 1
+
+    @pl.when((turn >= 1) & turn_is_other(before))
+    def _():
+        pass_other(before)
+
+    @pl.when((turn == 5) | (turn == 7))
+    def _():
+        pass_total((turn - 5) // 2)
+
+    @pl.when((turn == 3) | (turn == 5) | (turn == 7))
+    def _():
+        pass_own(before, (turn - 3) // 2)
+
+    mixed_ref[...] = (mixed_first[...].astype(f32) + dot(hidden_rows, down)).astype(bf16)
+
+    @pl.when(turn >= 2)
+    def _():
+        core_copy(turn - 2).wait_send()
+
+    ring[turn % 2] = (
+        grad_h_first[...].astype(f32) + dot(grad_pre, up, ((1,), (1,))) + dot(grad_logits, router, ((1,), (1,)))
+    ).astype(bf16)
+    core_copy(turn).start()
+    h_turned = h_rows.T
+    up_sum[...] += dot(h_turned, grad_pre)
+    router_sum[...] += dot(h_turned, grad_logits)
+    down_sum[...] += dot(cot_rows.T, hidden_rows)
+
+    @pl.when(turn == steps - 1)
+    def _():
+        pass_own(7, 3)
+        pass_total(2)
+        grad_up_ref[...] = up_sum[...].astype(bf16)
+        grad_down_ref[...] = down_sum[...].astype(bf16)
+        grad_router_ref[...] = router_sum[...].T[:8]
+        pass_total(3)
+        for number in (6, 7):
+            core_copy(number).wait_send()
+        for place in range(4):
+            y_copy(other_turn(place), place).wait_send()
+            x_copy(own_turn(place), place).wait_send()
+            total_copy(place).wait_send()
+            total_copy(place).wait_recv()
+            store_copy(place).wait()
+
+
+def run_second_pair(
+    h_rows, cot_rows, kept, router, mixed_first, grad_h_first, gate_first, up, down, up_late, down_late, experts
+):
     rows, features = h_rows.shape
-    pairs, _, width = up.shape
-    vmem = pl.BlockSpec(memory_space=pltpu.VMEM)
+    width = up.shape[2]
+    steps = rows // BLOCK
+    half = (BLOCK, features // 2)
+    anywhere = pl.BlockSpec(memory_space=pl.ANY)
     shape = jax.ShapeDtypeStruct
+    dma = pltpu.SemaphoreType.DMA
+
+    def by_step(lanes):
+        return pl.BlockSpec((BLOCK, lanes), lambda n: (turn_block(n), 0))
+
+    def whole(*dims):
+        return pl.BlockSpec(dims, lambda n: (0,) * len(dims))
+
     return pl.pallas_call(
-        partial(expert_kernel, experts=experts, block=256),
+        partial(second_pair_kernel, experts=experts, steps=steps),
+        grid=(steps,),
         out_shape=[
             shape((rows, features), bf16),
-            shape((rows, features), bf16),
-            shape((pairs, features, width), bf16),
-            shape((pairs, features, width), bf16),
-            shape((features, 128), f32),
+            shape((features, width), bf16),
+            shape((features, width), bf16),
+            shape((8, features), f32),
+            shape((rows // 2, features), bf16),
         ],
-        in_specs=[vmem] * 6,
-        out_specs=[vmem] * 5,
-        scratch_shapes=[pltpu.VMEM((pairs, features, width), f32)] * 2,
-        compiler_params=pltpu.CompilerParams(vmem_limit_bytes=60 << 20),
-    )(h_rows, cot_rows, up, down, kept, router)
+        in_specs=[
+            by_step(features),
+            by_step(features),
+            by_step(128),
+            whole(features, 128),
+            by_step(features),
+            by_step(features),
+            by_step(128),
+        ]
+        + [anywhere] * 4,
+        out_specs=[by_step(features), whole(features, width), whole(features, width), whole(8, features), anywhere],
+        scratch_shapes=[
+            pltpu.VMEM((features, width), bf16),
+            pltpu.VMEM((width, features), bf16),
+            pltpu.VMEM((features, width), f32),
+            pltpu.VMEM((features, width), f32),
+            pltpu.VMEM((features, 128), f32),
+            pltpu.VMEM((2, BLOCK, features), bf16),
+            pltpu.VMEM((8, *half), bf16),
+            pltpu.VMEM((4, *half), bf16),
+            pltpu.VMEM((4, *half), bf16),
+            dma((2,)),
+        ]
+        + [dma((8,))] * 2
+        + [dma((4,))] * 7,
+        compiler_params=pltpu.CompilerParams(
+            collective_id=4, has_side_effects=True, vmem_limit_bytes=60 << 20
+        ),
+    )(h_rows, cot_rows, kept, router, mixed_first, grad_h_first, gate_first, up, down, up_late, down_late)
+
+
+def backward_kernel(
+    tok_ref,
+    gain1_ref,
+    shift1_ref,
+    gain2_ref,
+    qkv_ref,
+    out_w_ref,
+    q_ref,
+    k_ref,
+    v_ref,
+    att_ref,
+    lse_ref,
+    grad_h_ref,
+    grad_router_ref,
+    resid_ref,
+    cot_ref,
+    mixed_ref,
+    up_first,
+    up_second,
+    down_first,
+    down_second,
+    up_out,
+    down_out,
+    tokens_out,
+    weights_out,
+    mixed_out,
+    rows_kept,
+    cot_rows,
+    m_mine,
+    m_core,
+    m_y,
+    m_x,
+    m_out,
+    m_resid,
+    own_vm,
+    one_mine,
+    one_to,
+    one_core,
+    one_x,
+    one_total,
+    line,
+    weight_sum,
+    weight_half,
+    shared,
+    shared_y,
+    shared_line,
+    shared_all,
+    route_core,
+    route_x,
+    whole,
+    mc_s,
+    mc_r,
+    my_s,
+    my_r,
+    mx_s,
+    mx_r,
+    mq_s,
+    mq_r,
+    m_store,
+    oc_s,
+    oc_r,
+    ox_s,
+    ox_r,
+    ot_s,
+    ot_r,
+    l_s,
+    l_r,
+    sy_s,
+    sy_r,
+    sl_s,
+    sl_r,
+    sg_s,
+    sg_r,
+    sz_s,
+    sz_r,
+    r_s,
+    r_r,
+    load,
+    own_sem,
+    weight_store,
+    store,
+    *,
+    images,
+    heads,
+):
+    expert_at = lax.axis_index("expert")
+    tensor_at = lax.axis_index("tensor")
+    z_at, y_at = expert_at // 2, expert_at % 2
+    z_last = lax.axis_size("expert") // 2 - 1
+    x_at, core_at = tensor_at // 2, tensor_at % 2
+    other = 1 - core_at
+    rows = images * PITCH
+    features = tok_ref.shape[2]
+    wide = features // 2
+    share = out_w_ref.shape[0]
+    hidden = line.shape[4]
+    core_dev = (expert_at, tensor_at + 1 - 2 * core_at)
+    x_dev = (expert_at, tensor_at + 2 - 4 * x_at)
+    y_dev = (expert_at + 1 - 2 * y_at, tensor_at)
+    z_devs = [(expert_at + 2, tensor_at), (expert_at - 2, tensor_at)]
+    has_up, has_down = z_at < z_last, z_at > 0
+    greet([(True, core_dev), (True, x_dev), (True, y_dev), (has_up, z_devs[0]), (has_down, z_devs[1])])
+    my_cols = lanes_at(core_at * wide, wide)
+    their_cols = lanes_at(other * wide, wide)
+
+    def remote(src, dst, send, recv, device):
+        return pltpu.make_async_remote_copy(
+            src_ref=src, dst_ref=dst, send_sem=send, recv_sem=recv, device_id=device, device_id_type=MESH
+        )
+
+    def at_image(image):
+        return aligned(image * PITCH, PITCH)
+
+    part_count = m_y.shape[0]
+    part_rows_m = rows // part_count
+
+    def m_rows(side, part):
+        return aligned(side * rows + part * part_rows_m, part_rows_m)
+
+    def m_core_copy(side, part):
+        at = m_rows(side, part)
+        return remote(mixed_ref.at[at, their_cols], m_core.at[at, :], mc_s.at[side, part], mc_r.at[side, part], core_dev)
+
+    for part in range(part_count):
+        m_core_copy(1, part).start()
+    for part in range(part_count):
+        m_core_copy(0, part).start()
+    loads = [
+        pltpu.make_async_copy(resid_ref, rows_kept, load.at[0]),
+        pltpu.make_async_copy(cot_ref.at[pl.ds(0, rows), :], cot_rows, load.at[1]),
+        pltpu.make_async_copy(mixed_ref.at[:, my_cols], m_mine, load.at[2]),
+    ]
+    for copy in loads:
+        copy.start()
+    route_one = remote(grad_router_ref, route_core, r_s.at[0], r_r.at[0], core_dev)
+    route_one.start()
+
+    def place(way):
+        return z_at if way == 0 else z_last - z_at
+
+    def expert_of(step, at, way):
+        mirrored = z_last - step + at
+        return mirrored if way == 0 else z_last - mirrored
+
+    def with_own(expert, run):
+        lanes = lanes_at(expert % 2 * hidden, hidden)
+        is_first = expert // 2 == z_at // 2
+
+        @pl.when(is_first)
+        def _():
+            run([part.at[:, lanes] for part in (up_first, down_first)])
+
+        @pl.when(jnp.logical_not(is_first))
+        def _():
+            run([part.at[:, lanes] for part in (up_second, down_second)])
+
+    def load_own(expert):
+        def load_from(sources):
+            copies = [pltpu.make_async_copy(sources[n], own_vm.at[n], own_sem.at[n]) for n in range(2)]
+            for copy in copies:
+                copy.start()
+            for copy in copies:
+                copy.wait()
+
+        with_own(expert, load_from)
+
+    def line_copy(source, step, way, number):
+        return remote(
+            source, line.at[way, step, number], l_s.at[way, step, number], l_r.at[way, step, number], z_devs[way]
+        )
+
+    def line_send(step):
+        for way in range(2):
+            at = place(way)
+
+            @pl.when(at == 0)
+            def _():
+                def send_from(sources):
+                    for number in range(2):
+                        line_copy(sources[number], step, way, number).start()
+
+                with_own(expert_of(step, at, way), send_from)
+
+            if step > 0:
+
+                @pl.when((at > 0) & (at <= step) & (at < z_last))
+                def _():
+                    for number in range(2):
+                        line_copy(line.at[way, step - 1, number], step, way, number).start()
+
+    def line_await(step):
+        for way in range(2):
+            at = place(way)
+
+            @pl.when((at > 0) & (at - 1 <= step))
+            def _():
+                for number in range(2):
+                    line_copy(line.at[way, step, number], step, way, number).wait_recv()
+
+    def line_add(step):
+        for way in range(2):
+            at = place(way)
+
+            @pl.when((at > 0) & (at - 1 <= step))
+            def _():
+                load_own(expert_of(step, at - 1, way))
+                for number in range(2):
+
+                    def add(piece, _):
+                        at_rows = aligned(piece * 96, 96)
+                        total = line[way, step, number, at_rows, :].astype(f32) + own_vm[number, at_rows, :].astype(f32)
+                        line[way, step, number, at_rows, :] = total.astype(bf16)
+                        return 0
+
+                    lax.fori_loop(0, features // 96, add, 0)
+
+    line_send(0)
+    for copy in loads:
+        copy.wait()
+    weight_sum[...] = jnp.zeros_like(weight_sum)
+
+    def m_y_copy(part):
+        return remote(m_core.at[m_rows(1, part), :], m_y.at[part], my_s.at[part], my_r.at[part], y_dev)
+
+    def m_x_copy(part):
+        return remote(m_core.at[m_rows(0, part), :], m_x.at[part], mx_s.at[part], mx_r.at[part], x_dev)
+
+    def m_place(part):
+        return mixed_out.at[aligned(part * part_rows_m, part_rows_m), :]
+
+    def m_quarter_copy(part):
+        return remote(m_out.at[part, other], m_place(part), mq_s.at[part], mq_r.at[part], core_dev)
+
+    def m_store_copy(part):
+        return pltpu.make_async_copy(m_out.at[part, core_at], m_place(part), m_store.at[part])
+
+    def m_resid_copy(part):
+        at = aligned(part * part_rows_m, part_rows_m)
+        return pltpu.make_async_copy(resid_ref.at[at, lanes_at(x_at * wide, wide)], m_resid, load.at[3])
+
+    keeps = x_at == core_at
+
+    def run_m_y(part):
+        m_core_copy(1, part).wait_recv()
+        at = m_rows(1, part)
+        m_core[at, :] = (m_core[at, :].astype(f32) + m_mine[at, :].astype(f32)).astype(bf16)
+        m_y_copy(part).start()
+
+    def run_m_x(part):
+        m_core_copy(0, part).wait_recv()
+        m_y_copy(part).wait_recv()
+        at = m_rows(0, part)
+        total = m_core[at, :].astype(f32) + m_mine[at, :].astype(f32) + m_y[part].astype(f32)
+        m_core[at, :] = total.astype(bf16)
+
+        @pl.when(jnp.logical_not(keeps))
+        def _():
+            m_x_copy(part).start()
+
+    def run_m_out(part):
+        @pl.when(keeps)
+        def _():
+            m_resid_copy(part).start()
+            m_x_copy(part).wait_recv()
+            m_resid_copy(part).wait()
+            total = m_core[m_rows(0, part), :].astype(f32) + m_x[part].astype(f32)
+            mixed = (m_resid[...] + total).astype(bf16)
+            m_out[part, 0] = mixed[:, : wide // 2]
+            m_out[part, 1] = mixed[:, wide // 2 :]
+            m_quarter_copy(part).start()
+            m_store_copy(part).start()
+
+    for part in range(part_count):
+        run_m_y(part)
+    route_one.wait_recv()
+    route_core[...] += grad_router_ref[...]
+    route_two = remote(route_core, route_x, r_s.at[1], r_r.at[1], x_dev)
+    route_two.start()
+
+    def one_core_copy(image):
+        return remote(one_to.at[image], one_core.at[image], oc_s.at[image], oc_r.at[image], core_dev)
+
+    def one_x_copy(image):
+        return remote(one_core.at[image], one_x.at[image], ox_s.at[image], ox_r.at[image], x_dev)
+
+    def one_total_copy(image):
+        return remote(one_x.at[image], one_total.at[image], ot_s.at[image], ot_r.at[image], core_dev)
+
+    def store_copy(image):
+        return pltpu.make_async_copy(rows_kept.at[at_image(image), :], tokens_out.at[at_image(image), :], store.at[image])
+
+    lane = lax.broadcasted_iota(jnp.int32, (PITCH, 2 * HD), 1)
+    key_mask = lax.broadcasted_iota(jnp.int32, (PITCH, PITCH), 1) < SEQ
+    gain1, shift1, gain2 = gain1_ref[...], shift1_ref[...], gain2_ref[...]
+
+    def norm_back(grad, gain, normed, inverse):
+        scaled = grad * gain
+        mean = jnp.mean(scaled, axis=1, keepdims=True)
+        along = jnp.mean(scaled * normed, axis=1, keepdims=True)
+        return (scaled - mean - normed * along) * inverse
+
+    def add_sums(row, grad, normed):
+        weight_sum[features + row : features + row + 1, :] += jnp.sum(grad * normed, axis=0, keepdims=True)
+        weight_sum[features + row + 1 : features + row + 2, :] += jnp.sum(grad, axis=0, keepdims=True)
+
+    def run_attention(image):
+        at = at_image(image)
+        grad_h = grad_h_ref[at, :].astype(f32)
+        normed, inverse = norm_stats(rows_kept[at, :])
+        add_sums(2, grad_h, normed)
+        grad_resid = cot_rows[at, :].astype(f32) + norm_back(grad_h, gain2, normed, inverse)
+        rows_kept[at, :] = grad_resid
+        grad_branch = grad_resid.astype(bf16)
+        token_normed, _ = norm_stats(tok_ref[image].astype(f32))
+        h_one = (token_normed * gain1 + shift1).astype(bf16)
+        queries, keys, values, attended = q_ref[image], k_ref[image], v_ref[image], att_ref[image]
+        lse = lse_ref[image]
+        grad_attended = dot(grad_branch, out_w_ref[...], ((1,), (1,))).astype(bf16)
+        grads = [[], [], []]
+        for head in range(heads):
+            first = head // 2 * 2 * HD
+            last = min(first + 2 * HD, heads * HD)
+            parts = [whose[:, first:last] for whose in (queries, keys, values, grad_attended)]
+            if last - first == 2 * HD:
+                own = head_mask(lane, head)
+                q_own, k_own, _, g_own = (jnp.where(own, part, jnp.zeros_like(part)) for part in parts)
+            else:
+                q_own, k_own, _, g_own = parts
+            scores = dot(q_own, parts[1], ((1,), (1,))) * (HD**-0.5)
+            probs = jnp.where(key_mask, jnp.exp(scores - lse[:, head : head + 1]), 0.0)
+            back = dot(g_own, parts[2], ((1,), (1,)))
+            product = probs * back
+            grad_scores = (product - probs * jnp.sum(product, axis=1, keepdims=True)).astype(bf16)
+            pieces = (
+                dot(grad_scores, k_own) * (HD**-0.5),
+                dot(grad_scores, q_own, ((0,), (0,))) * (HD**-0.5),
+                dot(probs.astype(bf16), g_own, ((0,), (0,))),
+            )
+            for which in range(3):
+                if head % 2 == 0:
+                    grads[which].append(pieces[which])
+                else:
+                    grads[which][-1] += pieces[which]
+        grad_rows = [jnp.concatenate(grads[which], axis=1).astype(bf16) for which in range(3)]
+        grad_one = 0.0
+        for which in range(3):
+            weight_sum[which * share : (which + 1) * share, :] += dot(grad_rows[which].T, h_one)
+            grad_one += dot(grad_rows[which], qkv_ref[which], ((1,), (1,)))
+        weight_sum[3 * share : 4 * share, :] += dot(attended.T, grad_branch)
+        whole[...] = grad_one
+        one_mine[image] = whole[:, my_cols].astype(bf16)
+        one_to[image] = whole[:, their_cols].astype(bf16)
+        one_core_copy(image).start()
+
+    def run_one_x(image):
+        one_core_copy(image).wait_recv()
+        one_core[image] = (one_core[image].astype(f32) + one_mine[image].astype(f32)).astype(bf16)
+        one_x_copy(image).start()
+
+    def run_one_total(image):
+        one_x_copy(image).wait_recv()
+        one_x[image] = (one_core[image].astype(f32) + one_x[image].astype(f32)).astype(bf16)
+        one_total_copy(image).start()
+
+    def run_tokens(image):
+        one_total_copy(image).wait_recv()
+        whole[:, my_cols] = one_x[image].astype(f32)
+        whole[:, their_cols] = one_total[image].astype(f32)
+        grad_one = whole[...]
+        at = at_image(image)
+        normed, inverse = norm_stats(tok_ref[image].astype(f32))
+        add_sums(0, grad_one, normed)
+        rows_kept[at, :] = rows_kept[at, :] + norm_back(grad_one, gain1, normed, inverse)
+        store_copy(image).start()
+
+    def stage(tick, lag, run):
+        image = tick - lag
+
+        @pl.when((image >= 0) & (image < images))
+        def _():
+            run(image)
+
+    def m_stage(tick, first, run):
+        @pl.when((tick >= first) & ((tick - first) % 2 == 0) & ((tick - first) // 2 < part_count))
+        def _():
+            run((tick - first) // 2)
+
+    def per_tick(tick, _):
+        stage(tick, 0, run_attention)
+        stage(tick, 1, run_one_x)
+        stage(tick, 2, run_one_total)
+        stage(tick, 3, run_tokens)
+        m_stage(tick, 2, run_m_x)
+        m_stage(tick, 4, run_m_out)
+
+        @pl.when(tick == 4)
+        def _():
+            line_await(0)
+            line_add(0)
+            line_send(1)
+
+        @pl.when(tick == 9)
+        def _():
+            line_await(1)
+            line_add(1)
+            line_send(2)
+
+        return 0
+
+    lax.fori_loop(0, images + 3, per_tick, 0)
+
+    route_two.wait_recv()
+    weight_sum[features + 8 : features + 16, :] = route_core[...] + route_x[...]
+    part_rows = shared.shape[1]
+    quarter = part_rows // (z_last + 1)
+
+    def to_half(side):
+        def cast(piece, _):
+            at_rows = aligned(piece * quarter, quarter)
+            shared[side, at_rows, :] = weight_sum[aligned(side * part_rows + piece * quarter, quarter), :].astype(bf16)
+            return 0
+
+        lax.fori_loop(0, z_last + 1, cast, 0)
+
+    to_half(0)
+    to_half(1)
+
+    def y_piece(number):
+        inner = jnp.where(z_at == 1, jnp.where(number < 2, z_last - number, number - 2), jnp.where(number < 2, number, 5 - number))
+        return jnp.where(z_at == 0, z_last - number, jnp.where(z_at == z_last, number, inner))
+
+    def quarter_at(piece):
+        return aligned(piece * quarter, quarter)
+
+    def shared_y_copy(number):
+        at_rows = quarter_at(y_piece(number))
+        return remote(shared.at[1 - y_at, at_rows, :], shared_y.at[at_rows, :], sy_s.at[number], sy_r.at[number], y_dev)
+
+    def take_y(number):
+        shared_y_copy(number).wait_recv()
+        at_rows = quarter_at(y_piece(number))
+        weight_half[at_rows, :] = shared[y_at, at_rows, :].astype(f32) + shared_y[at_rows, :].astype(f32)
+
+    for number in range(4):
+        shared_y_copy(number).start()
+
+    def small_copy(step, way):
+        return remote(shared_line.at[way, 0, step], shared_line.at[way, 1, step], sl_s.at[way, step], sl_r.at[way, step], z_devs[way])
+
+    for step in range(3):
+        take_y(step)
+        if step == 2:
+            take_y(3)
+        for way in range(2):
+            at = place(way)
+
+            @pl.when((at <= step) & (at < z_last))
+            def _():
+                at_rows = quarter_at(expert_of(step, at, way))
+                if step == 0:
+                    shared_line[way, 0, step] = weight_half[at_rows, :].astype(bf16)
+                else:
+                    came = jnp.where(at > 0, shared_line[way, 1, step - 1].astype(f32), 0.0)
+                    shared_line[way, 0, step] = (weight_half[at_rows, :] + came).astype(bf16)
+                small_copy(step, way).start()
+
+        for way in range(2):
+            at = place(way)
+
+            @pl.when((at > 0) & (at - 1 <= step))
+            def _():
+                small_copy(step, way).wait_recv()
+
+    own_rows = quarter_at(z_at)
+    from_below = jnp.where(z_at > 0, shared_line[0, 1, 2].astype(f32), 0.0)
+    from_above = jnp.where(z_at < z_last, shared_line[1, 1, 2].astype(f32), 0.0)
+
+    def final_rows(side, piece):
+        return shared_all.at[side, quarter_at(piece), :]
+
+    shared_all[y_at, own_rows, :] = (weight_half[own_rows, :] + from_below + from_above).astype(bf16)
+    for number in range(4):
+        shared_y_copy(number).wait_send()
+
+    def gather_z(step, way, piece):
+        ref = final_rows(y_at, piece)
+        return remote(ref, ref, sg_s.at[way, step], sg_r.at[way, step], z_devs[way])
+
+    def gather_y(step, way, piece, side):
+        ref = final_rows(side, piece)
+        return remote(ref, ref, sz_s.at[way, step], sz_r.at[way, step], y_dev)
+
+    gather_y(0, 0, z_at, y_at).start()
+    for step in range(3):
+        for way in range(2):
+            at = place(way)
+            piece = z_at - step if way == 0 else z_at + step
+
+            @pl.when((at >= step) & (at < z_last))
+            def _():
+                gather_z(step, way, piece).start()
+
+        for way in range(2):
+            at = place(way)
+            piece = z_at - 1 - step if way == 0 else z_at + 1 + step
+
+            @pl.when(at >= 1 + step)
+            def _():
+                gather_z(step, way, piece).wait_recv()
+                gather_y(step + 1, way, piece, y_at).start()
+
+    gather_y(0, 0, z_at, 1 - y_at).wait_recv()
+    for step in range(3):
+        for way in range(2):
+            at = place(way)
+            piece = z_at - 1 - step if way == 0 else z_at + 1 + step
+
+            @pl.when(at >= 1 + step)
+            def _():
+                gather_y(step + 1, way, piece, 1 - y_at).wait_recv()
+
+    def to_out(piece, _):
+        for side in range(2):
+            weight_sum[aligned(side * part_rows + piece * quarter, quarter), :] = shared_all[
+                side, quarter_at(piece), :
+            ].astype(f32)
+        return 0
+
+    lax.fori_loop(0, z_last + 1, to_out, 0)
+    weight_copy = pltpu.make_async_copy(weight_sum, weights_out, weight_store.at[0])
+    weight_copy.start()
+    line_await(2)
+    load_own(z_at)
+
+    def finish(piece, _):
+        at_rows = aligned(piece * 128, 128)
+        totals = []
+        for number in range(2):
+            below = jnp.where(z_at > 0, line[0, 2, number, at_rows, :].astype(f32), 0.0)
+            above = jnp.where(z_at < z_last, line[1, 2, number, at_rows, :].astype(f32), 0.0)
+            totals.append(own_vm[number, at_rows, :].astype(f32) + below + above)
+        up_out[at_rows, :] = totals[0]
+        down_out[:, lanes_at(piece * 128, 128)] = totals[1].T
+        return 0
+
+    lax.fori_loop(0, features // 128, finish, 0)
+
+    route_one.wait_send()
+    route_two.wait_send()
+
+    def drain(image, _):
+        for copy in (one_core_copy, one_x_copy, one_total_copy):
+            copy(image).wait_send()
+        store_copy(image).wait()
+        return 0
+
+    lax.fori_loop(0, images, drain, 0)
+    for part in range(part_count):
+        m_core_copy(0, part).wait_send()
+        m_core_copy(1, part).wait_send()
+        m_y_copy(part).wait_send()
+
+        @pl.when(keeps)
+        def _():
+            m_quarter_copy(part).wait_send()
+            m_store_copy(part).wait()
+
+        @pl.when(jnp.logical_not(keeps))
+        def _():
+            m_x_copy(part).wait_send()
+            m_quarter_copy(part).wait_recv()
+
+    weight_copy.wait()
+    gather_y(0, 0, z_at, y_at).wait_send()
+    for step in range(3):
+        for way in range(2):
+            at = place(way)
+
+            @pl.when((at <= step) & (at < z_last))
+            def _():
+                small_copy(step, way).wait_send()
+                for number in range(2):
+                    line_copy(line.at[way, step, number], step, way, number).wait_send()
+
+            piece = z_at - step if way == 0 else z_at + step
+
+            @pl.when((at >= step) & (at < z_last))
+            def _():
+                gather_z(step, way, piece).wait_send()
+
+            piece = z_at - 1 - step if way == 0 else z_at + 1 + step
+
+            @pl.when(at >= 1 + step)
+            def _():
+                gather_y(step + 1, way, piece, y_at).wait_send()
+
+
+def run_backward(
+    tok,
+    gain1,
+    shift1,
+    gain2,
+    qkv_w,
+    out_w,
+    q,
+    k,
+    v,
+    att,
+    lse,
+    grad_h,
+    grad_router,
+    resid,
+    cot,
+    mixed,
+    up_first,
+    up_second,
+    down_first,
+    down_second,
+):
+    images, _, features = tok.shape
+    rows = images * PITCH
+    share = out_w.shape[0]
+    heads = share // HD
+    hidden = up_first.shape[1] // 2
+    wide = features // 2
+    packed = features + 128
+    parts = 4
+    vmem = pl.BlockSpec(memory_space=pltpu.VMEM)
+    anywhere = pl.BlockSpec(memory_space=pl.ANY)
+    shape = jax.ShapeDtypeStruct
+    dma = pltpu.SemaphoreType.DMA
+    block = (images, PITCH, wide)
+    return pl.pallas_call(
+        partial(backward_kernel, images=images, heads=heads),
+        out_shape=[
+            shape((features, hidden), f32),
+            shape((hidden, features), f32),
+            shape((rows, features), f32),
+            shape((packed, features), f32),
+            shape((rows, wide // 2), bf16),
+        ],
+        in_specs=[vmem] * 13 + [anywhere] * 7,
+        out_specs=[vmem] * 2 + [anywhere] * 3,
+        scratch_shapes=[
+            pltpu.VMEM((rows, features), f32),
+            pltpu.VMEM((rows, features), bf16),
+            pltpu.VMEM((2 * rows, wide), bf16),
+            pltpu.VMEM((2 * rows, wide), bf16),
+            *[pltpu.VMEM((parts, rows // parts, wide), bf16)] * 2,
+            pltpu.VMEM((parts, 2, rows // parts, wide // 2), bf16),
+            pltpu.VMEM((rows // parts, wide), f32),
+            pltpu.VMEM((2, features, hidden), bf16),
+            *[pltpu.VMEM(block, bf16)] * 5,
+            pltpu.VMEM((2, 3, 2, features, hidden), bf16),
+            pltpu.VMEM((packed, features), f32),
+            pltpu.VMEM((packed // 2, features), f32),
+            pltpu.VMEM((2, packed // 2, features), bf16),
+            pltpu.VMEM((packed // 2, features), bf16),
+            pltpu.VMEM((2, 2, 3, packed // 8, features), bf16),
+            pltpu.VMEM((2, packed // 2, features), bf16),
+            pltpu.VMEM((8, features), f32),
+            pltpu.VMEM((8, features), f32),
+            pltpu.VMEM((PITCH, features), f32),
+        ]
+        + [dma((2, parts))] * 2
+        + [dma((parts,))] * 7
+        + [dma((images,))] * 6
+        + [dma((2, 3, 2))] * 2
+        + [dma((4,))] * 2
+        + [dma((2, 3))] * 4
+        + [dma((2, 4))] * 2
+        + [dma((2,))] * 2
+        + [dma((4,)), dma((2,)), dma((1,)), dma((images,))],
+        compiler_params=pltpu.CompilerParams(
+            collective_id=2, has_side_effects=True, vmem_limit_bytes=63 << 20
+        ),
+    )(
+        tok,
+        gain1,
+        shift1,
+        gain2,
+        qkv_w,
+        out_w,
+        q,
+        k,
+        v,
+        att,
+        lse,
+        grad_h,
+        grad_router,
+        resid,
+        cot,
+        mixed,
+        up_first,
+        up_second,
+        down_first,
+        down_second,
+    )
 
 
 def per_image(rows_in):
@@ -885,9 +1954,6 @@
     images = row_count // SEQ
     rows = images * PITCH
     tensor_count = lax.axis_size("tensor")
-    expert_count = lax.axis_size("expert")
-    tensor_here = lax.axis_index("tensor")
-    expert_here = lax.axis_index("expert")
     quarter_width = feature_count // tensor_count
     experts_all = router_weight.shape[1]
     hidden = expert_up.shape[2]
@@ -908,70 +1974,58 @@
         per_image(cotangent).reshape(rows, quarter_width),
         per_image(kept).reshape(rows, 128),
     )
-    mixed_part, grad_h_part, grad_up, grad_down, grad_router = run_experts(
-        h_all, cot_all, up_all, down_all, kept_all, router_wide, experts_all
-    )
-    y_groups = [[2 * z, 2 * z + 1] for z in range(expert_count // 2)]
-    z_groups = [[2 * z + y for z in range(expert_count // 2)] for y in range(2)]
-    grad_h_rows = lax.psum(
-        lax.psum_scatter(grad_h_part, "expert", scatter_dimension=0, axis_index_groups=y_groups, tiled=True),
-        "tensor",
-    ).astype(f32)
-    mixed_sum = lax.psum_scatter(
-        lax.psum_scatter(mixed_part, "expert", scatter_dimension=0, axis_index_groups=y_groups, tiled=True),
-        "tensor",
-        scatter_dimension=1,
-        tiled=True,
-    ).astype(f32)
-
-    def to_owner(grads):
-        apart = grads.reshape(2, feature_count, 2, hidden).transpose(0, 2, 1, 3)
-        apart = apart.reshape(experts_all * feature_count, hidden)
-        return lax.psum_scatter(
-            apart, "expert", scatter_dimension=0, axis_index_groups=z_groups, tiled=True
-        ).astype(f32)
-
-    grad_up = to_owner(grad_up)
-    grad_down = to_owner(grad_down).T
-    resid = resid.reshape(rows, feature_count)
-    resid_part = lax.dynamic_slice_in_dim(resid, tensor_here * quarter_width, quarter_width, 1)
-    mixed = (resid_part + mixed_sum).astype(bf16)
-    norm_out, norm_back = jax.vjp(norm_rows, resid, gain_moe, shift_moe)
-    grad_resid_norm, grad_gain_moe, grad_shift_moe = norm_back(grad_h_rows)
-    cot_mine = lax.dynamic_slice_in_dim(cot_all, expert_here % 2 * rows, rows, 0)
-    grad_resid = unpad((cot_mine.astype(f32) + grad_resid_norm).reshape(images, PITCH, feature_count))
-    head_count = qkv_weight.shape[2] // HD
-    tokens_float = tokens.astype(f32)
-    h_one = norm_rows(tokens_float, gain_attn, shift_attn).astype(bf16)
-    by_head = (images, SEQ, head_count, HD)
-    log_total = lse[:, :SEQ, :head_count].transpose(0, 2, 1)[..., None]
-    saved = (
-        unpad(attended),
-        unpad(queries).reshape(by_head),
-        unpad(keys).reshape(by_head),
-        unpad(values).reshape(by_head),
-        log_total,
-    )
-    grad_qkv, grad_out, grad_h_one_part = attention_backward(
-        grad_resid.astype(bf16), saved, h_one, qkv_weight, out_weight
-    )
-    grad_h_one = lax.psum(grad_h_one_part.astype(bf16), "tensor").astype(f32)
-    norm_one_out, norm_one_back = jax.vjp(norm_rows, tokens_float, gain_attn, shift_attn)
-    grad_tok_norm, grad_gain_attn, grad_shift_attn = norm_one_back(grad_h_one)
-    grad_tokens = grad_resid + grad_tok_norm
-    grad_qkv, grad_out = lax.psum((grad_qkv.astype(bf16), grad_out.astype(bf16)), "expert")
-    small = lax.psum((grad_gain_attn, grad_shift_attn, grad_gain_moe, grad_shift_moe), "expert")
-    grad_router = lax.psum(grad_router[:, :experts_all], ("expert", "tensor"))
+    mixed_first, grad_h_first, gate_first, up_first, down_first, up_late, down_late = run_first_pair(
+        h_all, cot_all, kept_all, router_wide, up_all, down_all, experts_all
+    )
+    mixed_part, up_second, down_second, grad_router, grad_h_two = run_second_pair(
+        h_all,
+        cot_all,
+        kept_all,
+        router_wide,
+        mixed_first,
+        grad_h_first,
+        gate_first,
+        up_all,
+        down_all,
+        up_late,
+        down_late,
+        experts_all,
+    )
+    grad_up, grad_down, tokens_grad, weights_grad, mixed = run_backward(
+        tok,
+        gain_attn[None],
+        shift_attn[None],
+        gain_moe[None],
+        qkv_weight,
+        out_weight,
+        queries,
+        keys,
+        values,
+        attended,
+        lse,
+        grad_h_two,
+        grad_router,
+        resid,
+        cot_all,
+        mixed_part,
+        up_first,
+        up_second,
+        down_first,
+        down_second,
+    )
+    share = qkv_weight.shape[2]
+    grad_qkv = weights_grad[: 3 * share].reshape(3, share, feature_count).transpose(0, 2, 1)
+    small = weights_grad[feature_count : feature_count + 16]
     return (
         unpad(mixed.reshape(images, PITCH, quarter_width)),
-        grad_tokens,
+        unpad(tokens_grad.reshape(images, PITCH, feature_count)),
         small[0],
         small[1],
-        grad_qkv.astype(f32),
-        grad_out.astype(f32),
+        grad_qkv,
+        weights_grad[3 * share : 4 * share],
         small[2],
         small[3],
-        grad_router,
+        small[8 : 8 + experts_all].T,
         grad_up[None],
         grad_down[None],
     )
@@ -979,7 +2033,7 @@
 
 def per_device(*arguments):
     router_weight = arguments[7]
-    if router_weight.shape[1] <= 4:
+    if router_weight.shape[1] == 4 and lax.axis_size("expert") == 8 and lax.axis_size("tensor") == 4:
         return per_device_dense(*arguments)
     return per_device_routed(*arguments)
 

time: 754 us -> 338 us (0.45)
  waiting for transfers between devices: 293 us -> 0 us
  Pallas kernels: 173 us -> 298 us
  blocking collectives: 85.7 us -> 0 us
  local copies, waits for them, and re-layouts: 101 us -> 35.7 us
  other arithmetic: 48.7 us -> 2.46 us
  matrix products: 31.5 us -> 0 us
  between operations: 14.9 us -> 0.74 us
    reduce_scatter x4 -> x0, waiting for transfers between devices: 164 us -> none  [the longest x1 59.6 us: per_device_dense(): lax.psum_scatter(grad_h_part, 'expert', scatter_dimension=0, axis_index_g...]
    pallas_call x1 -> x3, Pallas kernels: 70.3 us -> 225 us  [the longest x1 125 us: run_backward(): pl.pallas_call(partial(backward_kernel, images=images, heads=heads), out_...]
    psum x3 -> x0, waiting for transfers between devices: 95.6 us -> none  [the longest x1 38.3 us: per_device_dense(): lax.psum(lax.psum_scatter(grad_h_part, 'expert', scatter_dimension=0, axi...]
    psum x2 -> x0, blocking collectives: 85.7 us -> none  [the longest x1 48.9 us: per_device_dense(): grad_router = lax.psum(grad_router[:, :experts_all], ('expert', 'tensor'))]
    unnamed x9 -> x0, waiting for transfers between devices: 32.6 us -> none
    dot_general x9 -> x0, matrix products: 31.5 us -> none  [the longest x1 4.85 us: attention_backward(): jnp.einsum('ctf,cdf->td', grad_rows, qkv_w, preferred_element_type=jnp.fl...]
    pallas_call x1, Pallas kernels: 103 us -> 73.7 us  [run_forward(): pl.pallas_call(partial(forward_kernel, images=images, heads=heads), out_s...]
    reduce_sum x7 -> x0, other arithmetic: 24.9 us -> none  [the longest x3 14.6 us: norm_rows(): return centred * lax.rsqrt(spread + norm_epsilon) * gain + shift]
  transfers between devices with their start and end apart: 8 -> 0, of which waited for: 7 -> 0; matrix products, arithmetic and copies ran while one was open for 12% -> 0% of each run, Pallas kernels for 0% -> 0%
where the time goes in v3:
time: 338 us; the launch traced here: 337 us
  Pallas kernels  298 us (88%)
  local copies, waits for them, and re-layouts  35.7 us (11%)
    pallas_call x1, Pallas kernels, run_backward(): pl.pallas_call(partial(backward_kernel, images=images, heads=heads), out_...  125 us
    pallas_call x1, Pallas kernels, run_forward(): pl.pallas_call(partial(forward_kernel, images=images, heads=heads), out_s...  73.7 us
    pallas_call x1, Pallas kernels, run_second_pair(): pl.pallas_call(partial(second_pair_kernel, experts=experts, steps=steps),...  63.5 us
    pallas_call x1, Pallas kernels, run_first_pair(): pl.pallas_call(partial(first_pair_kernel, experts=experts, steps=steps),...  36.5 us
    reshape x3, local copies, waits for them, and re-layouts, unpad(): return blocks[:, :SEQ].reshape(images * SEQ, blocks.shape[2])  6.85 us

profile of v3, /device:TPU:0, one launch (start us, length us, event | category | flops | bytes accessed | tf_op | source)
XLA Modules:
  0.0 337.3 jit_solution(6118345285419017682)
XLA Ops:
  0.6 1.3 broadcast_in_dim.36.gain1_ref
  1.9 1.3 broadcast_in_dim.37.shift1_ref
  3.2 1.3 broadcast_in_dim.38.gain2_ref
  4.4 1.3 broadcast_in_dim.39.shift2_ref
  5.7 0.9 copy.40
  6.6 0.7 pad.19.router_ref
  7.3 2.4 reshape.55
  9.8 0.8 copy.38
  10.5 0.0 copy-start.3
  10.5 1.0 pad.17
  11.6 0.0 copy-done.5
  11.6 2.4 select_reduce_fusion
  14.1 0.1 convert_element_type.16
  14.2 0.8 pad.18
  15.0 1.4 copy.41.qkv_ref
  16.4 2.4 reshape.54
  18.8 1.6 pad.16.tok_ref
  20.4 73.7 %shard_map.212 = (bf16[8,208,192]{2,1,0:T(8,128)(2,1)}, bf16[8,208,192]{2,1,0:T(8,128)(2,1)}, bf16[8,208,192]{2,1,0:T(8,128)(2,1)}, bf16[8,208,192]{2,1,0:T(8,12...) custom-call(bf16[8,208,768]{2,1,0:T(8,128)(2,1)} %pad.16.tok_ref, ...), custom_call_target="tpu_custom_call" | custom-call | tf_op jit(solution)/shard_map/pallas_call | solution.py:763
  94.1 36.5 %shard_map.213 = (bf16[3328,768]{1,0:T(8,128)(2,1)}, bf16[3328,768]{1,0:T(8,128)(2,1)}, f32[3328,128]{1,0:T(8,128)}, bf16[768,768]{1,0:T(8,128)(2,1)}, bf16[768,...) custom-call(bf16[3328,768]{1,0:T(8,128)(2,1)} %get-tuple-element.44.h_ref, ...), custom_call_target="tpu_custom_call" | custom-call | tf_op jit(solution)/shard_map/pallas_call | solution.py:935
  130.7 63.5 %shard_map.214 = (bf16[3328,768]{1,0:T(8,128)(2,1)}, bf16[768,768]{1,0:T(8,128)(2,1)}, bf16[768,768]{1,0:T(8,128)(2,1)}, f32[8,768]{1,0:T(8,128)}, bf16[1664,768]{1,0:T(8,128)(2,1)}) custom-call(bf16[3328,768]{1,0:T(8,128)(2,1)} %get-tuple-element.44.h_ref, bf16[3328,768]{1,0:T(8,128)(2,1)} %get-tuple-element.45.cot_ref, ...), custom_call_target="tpu_custom_call" | custom-call | tf_op jit(solution)/shard_map/pallas_call | solution.py:1186
  194.2 124.8 %shard_map.215 = (f32[768,384]{1,0:T(8,128)}, f32[384,768]{1,0:T(8,128)}, f32[1664,768]{1,0:T(8,128)}, f32[896,768]{1,0:T(8,128)}, bf16[1664,192]{1,0:T(8,128)(2,1)}) custom-call(bf16[8,208,768]{2,1,0:T(8,128)(2,1)} %pad.16.tok_ref, f32[1,768]{1,0:T(1,128)} %broadcast_in_dim.36.gain1_ref, f32[1,768]{1,0:T(1,128)} %broadcast_in_dim.37.shift1_ref, ...), custom_call_target="tpu_custom_call" | custom-call | tf_op jit(solution)/shard_map/pallas_call | solution.py:1859
  318.9 1.2 slice.42
  320.1 0.4 reshape.63
  320.5 1.1 copy.43
  321.6 4.9 %slice.43 = f32[8,197,768]{2,1,0:T(8,128)} slice(f32[8,208,768]{2,1,0:T(8,128)} %bitcast.15), slice={[0:8], [0:197], [0:768]} | slice | bytes 9682944 | tf_op jit(solution)/shard_map/slice | solution.py:1935
  326.5 5.4 %reshape.61 = f32[1576,768]{1,0:T(8,128)} reshape(f32[8,197,768]{2,1,0:T(8,128)} %slice.43) | data formatting | bytes 9682944 | tf_op jit(solution)/shard_map/reshape | solution.py:1935
  331.9 0.6 slice_bitcast_fusion
  332.5 0.6 slice_reduce_fusion
  333.1 0.9 slice.38
  334.0 1.3 slice.37
  335.3 1.0 copy.46
  336.3 1.0 copy.47
  (11 shorter events, 0.1 us)
Async XLA Ops:
  7.3 4.3 %copy-start.4 = (s32[1576,2]{0,1:T(2,128)S(1)}, s32[1576,2]{0,1:T(2,128)}, u32[]{:S(2)}) copy-start(s32[1576,2]{0,1:T(2,128)} %param.24) | copy-start | bytes 37828
  7.3 4.3 %copy-start.5 = (s32[1576,2]{0,1:T(2,128)S(1)}, s32[1576,2]{0,1:T(2,128)}, u32[]{:S(2)}) copy-start(s32[1576,2]{0,1:T(2,128)} %param.23) | copy-start | bytes 37828
  10.5 4.5 %copy-start.3 = (bf16[3,768,192]{1,2,0:T(8,128)(2,1)S(1)}, bf16[3,768,192]{1,2,0:T(8,128)(2,1)}, u32[]{:S(2)}) copy-start(bf16[3,768,192]{1,2,0:T(8,128)(2,1)} %param.16) | copy-start | bytes 2654212
  326.5 5.4 %copy-start = (f32[896,768]{1,0:T(8,128)S(1)}, f32[896,768]{1,0:T(8,128)}, u32[]{:S(2)}) copy-start(f32[896,768]{1,0:T(8,128)} %get-tuple-element.64) | copy-start | bytes 8257540
  333.1 2.2 copy-start.2
  334.0 2.3 copy-start.1

commit v4 on v3

--- a/solution.py
+++ b/solution.py
@@ -534,17 +534,16 @@
 
     lane = lax.broadcasted_iota(jnp.int32, (PITCH, 2 * HD), 1)
     key_mask = lax.broadcasted_iota(jnp.int32, (PITCH, PITCH), 1) < SEQ
-    gain1, shift1 = gain1_ref[...], shift1_ref[...]
-    gain2, shift2 = gain2_ref[...], shift2_ref[...]
+    gain1, shift1, gain2, shift2 = (ref[...].reshape(1, 2 * wide) for ref in (gain1_ref, shift1_ref, gain2_ref, shift2_ref))
     my_cols = lanes_at(core_at * wide, wide)
     their_cols = lanes_at(other * wide, wide)
 
     def attend(image):
         normed, _ = norm_stats(tok_ref[image].astype(f32))
         h_one = (normed * gain1 + shift1).astype(bf16)
-        queries = dot(h_one, qkv_ref[0]).astype(bf16)
-        keys = dot(h_one, qkv_ref[1]).astype(bf16)
-        values = dot(h_one, qkv_ref[2]).astype(bf16)
+        queries = dot(h_one, qkv_ref[0], ((1,), (1,))).astype(bf16)
+        keys = dot(h_one, qkv_ref[1], ((1,), (1,))).astype(bf16)
+        values = dot(h_one, qkv_ref[2], ((1,), (1,))).astype(bf16)
         q_all[image] = queries
         k_all[image] = keys
         v_all[image] = values
@@ -991,11 +990,15 @@
     down_all,
     up_late,
     down_late,
+    up_first,
+    down_first,
     mixed_ref,
     grad_up_ref,
     grad_down_ref,
     grad_router_ref,
     grad_h_out,
+    up_pair,
+    down_pair,
     up_vm,
     down_vm,
     up_sum,
@@ -1015,6 +1018,8 @@
     tot_s,
     tot_r,
     store,
+    pair_s,
+    pair_r,
     *,
     experts,
     steps,
@@ -1081,9 +1086,18 @@
         total_copy(place).start()
         store_copy(place).start()
 
+    z_dev = (jnp.where(z_at % 2 == 0, expert_at + 2, expert_at - 2), tensor_at)
+    pair_lanes = lanes_at((1 - z_at % 2) * hidden, hidden)
+    pair_copies = [
+        remote(source.at[:, pair_lanes], target, pair_s.at[number], pair_r.at[number], z_dev)
+        for number, (source, target) in enumerate(((up_first, up_pair), (down_first, down_pair)))
+    ]
+
     @pl.when(turn == 0)
     def _():
-        greet([(True, core_dev), (True, x_dev), (True, y_dev)])
+        greet([(True, core_dev), (True, x_dev), (True, y_dev), (True, z_dev)])
+        for copy in pair_copies:
+            copy.start()
         late_expert = jnp.where(z_at == 0, 1, 0)
         late = late_expert * hidden
         is_outer = (z_at == 0) | (z_at == 3)
@@ -1156,6 +1170,8 @@
         grad_down_ref[...] = down_sum[...].astype(bf16)
         grad_router_ref[...] = router_sum[...].T[:8]
         pass_total(3)
+        for copy in pair_copies:
+            copy.wait()
         for number in (6, 7):
             core_copy(number).wait_send()
         for place in range(4):
@@ -1167,7 +1183,20 @@
 
 
 def run_second_pair(
-    h_rows, cot_rows, kept, router, mixed_first, grad_h_first, gate_first, up, down, up_late, down_late, experts
+    h_rows,
+    cot_rows,
+    kept,
+    router,
+    mixed_first,
+    grad_h_first,
+    gate_first,
+    up,
+    down,
+    up_late,
+    down_late,
+    up_first,
+    down_first,
+    experts,
 ):
     rows, features = h_rows.shape
     width = up.shape[2]
@@ -1192,6 +1221,8 @@
             shape((features, width), bf16),
             shape((8, features), f32),
             shape((rows // 2, features), bf16),
+            shape((features, width // 2), bf16),
+            shape((features, width // 2), bf16),
         ],
         in_specs=[
             by_step(features),
@@ -1202,8 +1233,8 @@
             by_step(features),
             by_step(128),
         ]
-        + [anywhere] * 4,
-        out_specs=[by_step(features), whole(features, width), whole(features, width), whole(8, features), anywhere],
+        + [anywhere] * 6,
+        out_specs=[by_step(features), whole(features, width), whole(features, width), whole(8, features)] + [anywhere] * 3,
         scratch_shapes=[
             pltpu.VMEM((features, width), bf16),
             pltpu.VMEM((width, features), bf16),
@@ -1217,11 +1248,12 @@
             dma((2,)),
         ]
         + [dma((8,))] * 2
-        + [dma((4,))] * 7,
+        + [dma((4,))] * 7
+        + [dma((2,))] * 2,
         compiler_params=pltpu.CompilerParams(
             collective_id=4, has_side_effects=True, vmem_limit_bytes=60 << 20
         ),
-    )(h_rows, cot_rows, kept, router, mixed_first, grad_h_first, gate_first, up, down, up_late, down_late)
+    )(h_rows, cot_rows, kept, router, mixed_first, grad_h_first, gate_first, up, down, up_late, down_late, up_first, down_first)
 
 
 def backward_kernel(
@@ -1242,13 +1274,17 @@
     cot_ref,
     mixed_ref,
     up_first,
+    down_first,
+    up_pair,
+    down_pair,
     up_second,
-    down_first,
     down_second,
     up_out,
     down_out,
     tokens_out,
-    weights_out,
+    qkv_out,
+    out_w_out,
+    sums_out,
     mixed_out,
     rows_kept,
     cot_rows,
@@ -1259,6 +1295,8 @@
     m_out,
     m_resid,
     own_vm,
+    pair_vm,
+    far_vm,
     one_mine,
     one_to,
     one_core,
@@ -1273,6 +1311,9 @@
     shared_all,
     route_core,
     route_x,
+    late_mine,
+    late_y,
+    late_z,
     whole,
     mc_s,
     mc_r,
@@ -1301,6 +1342,8 @@
     sz_r,
     r_s,
     r_r,
+    late_s,
+    late_r,
     load,
     own_sem,
     weight_store,
@@ -1319,13 +1362,14 @@
     features = tok_ref.shape[2]
     wide = features // 2
     share = out_w_ref.shape[0]
-    hidden = line.shape[4]
+    hidden = line.shape[3]
     core_dev = (expert_at, tensor_at + 1 - 2 * core_at)
     x_dev = (expert_at, tensor_at + 2 - 4 * x_at)
     y_dev = (expert_at + 1 - 2 * y_at, tensor_at)
     z_devs = [(expert_at + 2, tensor_at), (expert_at - 2, tensor_at)]
-    has_up, has_down = z_at < z_last, z_at > 0
-    greet([(True, core_dev), (True, x_dev), (True, y_dev), (has_up, z_devs[0]), (has_down, z_devs[1])])
+    planes = z_last + 1
+    z_others = [((z_at + hop) % planes * 2 + y_at, tensor_at) for hop in (1, 2, 3)]
+    greet([(True, device) for device in (core_dev, x_dev, y_dev, *z_others)])
     my_cols = lanes_at(core_at * wide, wide)
     their_cols = lanes_at(other * wide, wide)
 
@@ -1364,86 +1408,71 @@
     def place(way):
         return z_at if way == 0 else z_last - z_at
 
-    def expert_of(step, at, way):
-        mirrored = z_last - step + at
-        return mirrored if way == 0 else z_last - mirrored
-
-    def with_own(expert, run):
-        lanes = lanes_at(expert % 2 * hidden, hidden)
-        is_first = expert // 2 == z_at // 2
-
-        @pl.when(is_first)
-        def _():
-            run([part.at[:, lanes] for part in (up_first, down_first)])
-
-        @pl.when(jnp.logical_not(is_first))
-        def _():
-            run([part.at[:, lanes] for part in (up_second, down_second)])
-
-    def load_own(expert):
-        def load_from(sources):
-            copies = [pltpu.make_async_copy(sources[n], own_vm.at[n], own_sem.at[n]) for n in range(2)]
-            for copy in copies:
-                copy.start()
-            for copy in copies:
-                copy.wait()
-
-        with_own(expert, load_from)
-
-    def line_copy(source, step, way, number):
-        return remote(
-            source, line.at[way, step, number], l_s.at[way, step, number], l_r.at[way, step, number], z_devs[way]
+    def far_lanes(way, piece):
+        expert = z_last - piece // 2 if way == 0 else piece // 2
+        return pl.ds(expert % 2 * hidden, hidden)
+
+    def line_copy(source, way, piece):
+        return remote(source, line.at[way, piece], l_s.at[way, piece], l_r.at[way, piece], z_devs[way])
+
+    def line_copy_on(way, piece):
+        return line_copy(line.at[way, piece], way, piece)
+
+    def line_start():
+        for way in range(2):
+
+            @pl.when(place(way) == 0)
+            def _():
+                for piece in range(4):
+                    source = (up_second, down_second)[piece % 2]
+                    line_copy(source.at[:, far_lanes(way, piece)], way, piece).start()
+
+    def line_add(piece):
+        for way in range(2):
+
+            @pl.when(place(way) == 1)
+            def _():
+                line_copy_on(way, piece).wait_recv()
+                lanes = far_lanes(way, piece)
+
+                def add(part, _):
+                    at_rows = aligned(part * 96, 96)
+                    total = line[way, piece, at_rows, :].astype(f32) + far_vm[piece % 2, at_rows, lanes].astype(f32)
+                    line[way, piece, at_rows, :] = total.astype(bf16)
+                    return 0
+
+                lax.fori_loop(0, features // 96, add, 0)
+                line_copy_on(way, piece).start()
+
+    def line_pass(piece):
+        for way in range(2):
+
+            @pl.when(place(way) == 2)
+            def _():
+                line_copy_on(way, piece).wait_recv()
+                line_copy_on(way, piece).start()
+
+    line_start()
+    own_lanes = lanes_at(z_at % 2 * hidden, hidden)
+    later = [
+        pltpu.make_async_copy(source, target, own_sem.at[number])
+        for number, (source, target) in enumerate(
+            (
+                (up_second, far_vm.at[0]),
+                (down_second, far_vm.at[1]),
+                (up_first.at[:, own_lanes], own_vm.at[0]),
+                (down_first.at[:, own_lanes], own_vm.at[1]),
+                (up_pair, pair_vm.at[0]),
+                (down_pair, pair_vm.at[1]),
+            )
         )
-
-    def line_send(step):
-        for way in range(2):
-            at = place(way)
-
-            @pl.when(at == 0)
-            def _():
-                def send_from(sources):
-                    for number in range(2):
-                        line_copy(sources[number], step, way, number).start()
-
-                with_own(expert_of(step, at, way), send_from)
-
-            if step > 0:
-
-                @pl.when((at > 0) & (at <= step) & (at < z_last))
-                def _():
-                    for number in range(2):
-                        line_copy(line.at[way, step - 1, number], step, way, number).start()
-
-    def line_await(step):
-        for way in range(2):
-            at = place(way)
-
-            @pl.when((at > 0) & (at - 1 <= step))
-            def _():
-                for number in range(2):
-                    line_copy(line.at[way, step, number], step, way, number).wait_recv()
-
-    def line_add(step):
-        for way in range(2):
-            at = place(way)
-
-            @pl.when((at > 0) & (at - 1 <= step))
-            def _():
-                load_own(expert_of(step, at - 1, way))
-                for number in range(2):
-
-                    def add(piece, _):
-                        at_rows = aligned(piece * 96, 96)
-                        total = line[way, step, number, at_rows, :].astype(f32) + own_vm[number, at_rows, :].astype(f32)
-                        line[way, step, number, at_rows, :] = total.astype(bf16)
-                        return 0
-
-                    lax.fori_loop(0, features // 96, add, 0)
-
-    line_send(0)
+    ]
     for copy in loads:
         copy.wait()
+    for copy in later:
+        copy.start()
     weight_sum[...] = jnp.zeros_like(weight_sum)
+    late_mine[...] = jnp.zeros_like(late_mine)
 
     def m_y_copy(part):
         return remote(m_core.at[m_rows(1, part), :], m_y.at[part], my_s.at[part], my_r.at[part], y_dev)
@@ -1512,12 +1541,11 @@
     def one_total_copy(image):
         return remote(one_x.at[image], one_total.at[image], ot_s.at[image], ot_r.at[image], core_dev)
 
-    def store_copy(image):
-        return pltpu.make_async_copy(rows_kept.at[at_image(image), :], tokens_out.at[at_image(image), :], store.at[image])
+    store_copy = pltpu.make_async_copy(rows_kept.at[pl.ds(0, images * SEQ), :], tokens_out, store.at[0])
 
     lane = lax.broadcasted_iota(jnp.int32, (PITCH, 2 * HD), 1)
     key_mask = lax.broadcasted_iota(jnp.int32, (PITCH, PITCH), 1) < SEQ
-    gain1, shift1, gain2 = gain1_ref[...], shift1_ref[...], gain2_ref[...]
+    gain1, shift1, gain2 = (ref[...].reshape(1, features) for ref in (gain1_ref, shift1_ref, gain2_ref))
 
     def norm_back(grad, gain, normed, inverse):
         scaled = grad * gain
@@ -1525,15 +1553,15 @@
         along = jnp.mean(scaled * normed, axis=1, keepdims=True)
         return (scaled - mean - normed * along) * inverse
 
-    def add_sums(row, grad, normed):
-        weight_sum[features + row : features + row + 1, :] += jnp.sum(grad * normed, axis=0, keepdims=True)
-        weight_sum[features + row + 1 : features + row + 2, :] += jnp.sum(grad, axis=0, keepdims=True)
+    def add_sums(sums, row, grad, normed):
+        sums[row : row + 1, :] += jnp.sum(grad * normed, axis=0, keepdims=True)
+        sums[row + 1 : row + 2, :] += jnp.sum(grad, axis=0, keepdims=True)
 
     def run_attention(image):
         at = at_image(image)
         grad_h = grad_h_ref[at, :].astype(f32)
         normed, inverse = norm_stats(rows_kept[at, :])
-        add_sums(2, grad_h, normed)
+        add_sums(weight_sum, features, grad_h, normed)
         grad_resid = cot_rows[at, :].astype(f32) + norm_back(grad_h, gain2, normed, inverse)
         rows_kept[at, :] = grad_resid
         grad_branch = grad_resid.astype(bf16)
@@ -1571,7 +1599,7 @@
         grad_one = 0.0
         for which in range(3):
             weight_sum[which * share : (which + 1) * share, :] += dot(grad_rows[which].T, h_one)
-            grad_one += dot(grad_rows[which], qkv_ref[which], ((1,), (1,)))
+            grad_one += dot(grad_rows[which], qkv_ref[which])
         weight_sum[3 * share : 4 * share, :] += dot(attended.T, grad_branch)
         whole[...] = grad_one
         one_mine[image] = whole[:, my_cols].astype(bf16)
@@ -1595,9 +1623,15 @@
         grad_one = whole[...]
         at = at_image(image)
         normed, inverse = norm_stats(tok_ref[image].astype(f32))
-        add_sums(0, grad_one, normed)
-        rows_kept[at, :] = rows_kept[at, :] + norm_back(grad_one, gain1, normed, inverse)
-        store_copy(image).start()
+        add_sums(late_mine, 0, grad_one, normed)
+        total = rows_kept[at, :] + norm_back(grad_one, gain1, normed, inverse)
+        whole[...] = total
+        for number in range(images):
+
+            @pl.when(image == number)
+            def _():
+                rows_kept[pl.ds(number * SEQ, SEQ), :] = whole[pl.ds(0, SEQ), :]
+
 
     def stage(tick, lag, run):
         image = tick - lag
@@ -1606,34 +1640,36 @@
         def _():
             run(image)
 
-    def m_stage(tick, first, run):
-        @pl.when((tick >= first) & ((tick - first) % 2 == 0) & ((tick - first) // 2 < part_count))
+    def m_stage(tick, ticks, run):
+        part = sum(jnp.where(tick > when, 1, 0) for when in ticks)
+        falls = sum(jnp.where(tick == when, 1, 0) for when in ticks)
+
+        @pl.when(falls == 1)
         def _():
-            run((tick - first) // 2)
+            run(part)
 
     def per_tick(tick, _):
         stage(tick, 0, run_attention)
         stage(tick, 1, run_one_x)
         stage(tick, 2, run_one_total)
         stage(tick, 3, run_tokens)
-        m_stage(tick, 2, run_m_x)
-        m_stage(tick, 4, run_m_out)
-
-        @pl.when(tick == 4)
+        m_stage(tick, (2, 4, 5, 7), run_m_x)
+        m_stage(tick, (4, 5, 7), run_m_out)
+
+        @pl.when(tick == 2)
         def _():
-            line_await(0)
+            later[0].wait()
+            later[1].wait()
             line_add(0)
-            line_send(1)
-
-        @pl.when(tick == 9)
+
+        @pl.when(tick == 5)
         def _():
-            line_await(1)
             line_add(1)
-            line_send(2)
+            line_pass(0)
 
         return 0
 
-    lax.fori_loop(0, images + 3, per_tick, 0)
+    lax.fori_loop(0, images, per_tick, 0)
 
     route_two.wait_recv()
     weight_sum[features + 8 : features + 16, :] = route_core[...] + route_x[...]
@@ -1669,6 +1705,21 @@
 
     for number in range(4):
         shared_y_copy(number).start()
+    run_one_x(images - 1)
+    run_one_total(images - 2)
+    run_tokens(images - 3)
+    line_pass(1)
+    line_add(2)
+
+    def quarter_of(step, at, way):
+        mirrored = z_last - step + at
+        return mirrored if way == 0 else z_last - mirrored
+
+    late_y_copy = remote(late_mine, late_y, late_s.at[0], late_r.at[0], y_dev)
+
+    def late_copy(number):
+        ref = late_z.at[z_at]
+        return remote(ref, ref, late_s.at[number + 1], late_r.at[number + 1], z_others[number])
 
     def small_copy(step, way):
         return remote(shared_line.at[way, 0, step], shared_line.at[way, 1, step], sl_s.at[way, step], sl_r.at[way, step], z_devs[way])
@@ -1682,7 +1733,7 @@
 
             @pl.when((at <= step) & (at < z_last))
             def _():
-                at_rows = quarter_at(expert_of(step, at, way))
+                at_rows = quarter_at(quarter_of(step, at, way))
                 if step == 0:
                     shared_line[way, 0, step] = weight_half[at_rows, :].astype(bf16)
                 else:
@@ -1697,6 +1748,20 @@
             def _():
                 small_copy(step, way).wait_recv()
 
+        if step == 0:
+            run_one_total(images - 1)
+            run_tokens(images - 2)
+        if step == 1:
+            run_tokens(images - 1)
+            late_y_copy.start()
+            store_copy.start()
+            run_m_out(part_count - 1)
+            line_add(3)
+
+    late_y_copy.wait_recv()
+    late_z[z_at] = late_mine[...] + late_y[...]
+    for number in range(planes - 1):
+        late_copy(number).start()
     own_rows = quarter_at(z_at)
     from_below = jnp.where(z_at > 0, shared_line[0, 1, 2].astype(f32), 0.0)
     from_above = jnp.where(z_at < z_last, shared_line[1, 1, 2].astype(f32), 0.0)
@@ -1753,18 +1818,47 @@
         return 0
 
     lax.fori_loop(0, z_last + 1, to_out, 0)
-    weight_copy = pltpu.make_async_copy(weight_sum, weights_out, weight_store.at[0])
-    weight_copy.start()
-    line_await(2)
-    load_own(z_at)
+    for number in range(planes - 1):
+        late_copy(number).wait_recv()
+    late = late_z[0]
+    for plane in range(1, planes):
+        late += late_z[plane]
+    weight_sum[features + 2 : features + 4, :] = late[:2]
+    weight_copies = [
+        *[
+            pltpu.make_async_copy(weight_sum.at[pl.ds(n * share, share), :], qkv_out.at[n], weight_store.at[n])
+            for n in range(3)
+        ],
+        pltpu.make_async_copy(weight_sum.at[pl.ds(3 * share, share), :], out_w_out, weight_store.at[3]),
+        pltpu.make_async_copy(weight_sum.at[pl.ds(features, 16), :], sums_out, weight_store.at[4]),
+    ]
+    for copy in weight_copies:
+        copy.start()
+    for copy in later[2:]:
+        copy.wait()
+    for way in range(2):
+
+        @pl.when(place(way) == 2)
+        def _():
+            line_copy_on(way, 2).wait_recv()
+            line_copy_on(way, 3).wait_recv()
+
+        @pl.when(place(way) == z_last)
+        def _():
+            line_copy_on(way, 0).wait_recv()
+            line_copy_on(way, 1).wait_recv()
+
+    from_far = 1 - z_at // 2
+    first_piece = jnp.where((z_at == 0) | (z_at == z_last), 0, 2)
 
     def finish(piece, _):
         at_rows = aligned(piece * 128, 128)
-        totals = []
-        for number in range(2):
-            below = jnp.where(z_at > 0, line[0, 2, number, at_rows, :].astype(f32), 0.0)
-            above = jnp.where(z_at < z_last, line[1, 2, number, at_rows, :].astype(f32), 0.0)
-            totals.append(own_vm[number, at_rows, :].astype(f32) + below + above)
+        totals = [
+            own_vm[n, at_rows, :].astype(f32)
+            + pair_vm[n, at_rows, :].astype(f32)
+            + line[from_far, first_piece + n, at_rows, :].astype(f32)
+            for n in range(2)
+        ]
         up_out[at_rows, :] = totals[0]
         down_out[:, lanes_at(piece * 128, 128)] = totals[1].T
         return 0
@@ -1777,7 +1871,6 @@
     def drain(image, _):
         for copy in (one_core_copy, one_x_copy, one_total_copy):
             copy(image).wait_send()
-        store_copy(image).wait()
         return 0
 
     lax.fori_loop(0, images, drain, 0)
@@ -1796,8 +1889,24 @@
             m_x_copy(part).wait_send()
             m_quarter_copy(part).wait_recv()
 
-    weight_copy.wait()
+    for copy in (*weight_copies, store_copy):
+        copy.wait()
+    late_y_copy.wait_send()
+    for number in range(planes - 1):
+        late_copy(number).wait_send()
     gather_y(0, 0, z_at, y_at).wait_send()
+    for way in range(2):
+
+        @pl.when(place(way) <= 1)
+        def _():
+            for piece in range(4):
+                line_copy_on(way, piece).wait_send()
+
+        @pl.when(place(way) == 2)
+        def _():
+            for piece in range(2):
+                line_copy_on(way, piece).wait_send()
+
     for step in range(3):
         for way in range(2):
             at = place(way)
@@ -1805,8 +1914,6 @@
             @pl.when((at <= step) & (at < z_last))
             def _():
                 small_copy(step, way).wait_send()
-                for number in range(2):
-                    line_copy(line.at[way, step, number], step, way, number).wait_send()
 
             piece = z_at - step if way == 0 else z_at + step
 
@@ -1839,8 +1946,10 @@
     cot,
     mixed,
     up_first,
+    down_first,
+    up_pair,
+    down_pair,
     up_second,
-    down_first,
     down_second,
 ):
     images, _, features = tok.shape
@@ -1861,12 +1970,14 @@
         out_shape=[
             shape((features, hidden), f32),
             shape((hidden, features), f32),
-            shape((rows, features), f32),
-            shape((packed, features), f32),
+            shape((images * SEQ, features), f32),
+            shape((3, share, features), f32),
+            shape((share, features), f32),
+            shape((16, features), f32),
             shape((rows, wide // 2), bf16),
         ],
-        in_specs=[vmem] * 13 + [anywhere] * 7,
-        out_specs=[vmem] * 2 + [anywhere] * 3,
+        in_specs=[vmem] * 13 + [anywhere] * 9,
+        out_specs=[vmem] * 2 + [anywhere] * 5,
         scratch_shapes=[
             pltpu.VMEM((rows, features), f32),
             pltpu.VMEM((rows, features), bf16),
@@ -1876,27 +1987,30 @@
             pltpu.VMEM((parts, 2, rows // parts, wide // 2), bf16),
             pltpu.VMEM((rows // parts, wide), f32),
             pltpu.VMEM((2, features, hidden), bf16),
+            pltpu.VMEM((2, features, hidden), bf16),
+            pltpu.VMEM((2, features, 2 * hidden), bf16),
             *[pltpu.VMEM(block, bf16)] * 5,
-            pltpu.VMEM((2, 3, 2, features, hidden), bf16),
+            pltpu.VMEM((2, 4, features, hidden), bf16),
             pltpu.VMEM((packed, features), f32),
             pltpu.VMEM((packed // 2, features), f32),
             pltpu.VMEM((2, packed // 2, features), bf16),
             pltpu.VMEM((packed // 2, features), bf16),
             pltpu.VMEM((2, 2, 3, packed // 8, features), bf16),
             pltpu.VMEM((2, packed // 2, features), bf16),
-            pltpu.VMEM((8, features), f32),
-            pltpu.VMEM((8, features), f32),
+            *[pltpu.VMEM((8, features), f32)] * 4,
+            pltpu.VMEM((4, 8, features), f32),
             pltpu.VMEM((PITCH, features), f32),
         ]
         + [dma((2, parts))] * 2
         + [dma((parts,))] * 7
         + [dma((images,))] * 6
-        + [dma((2, 3, 2))] * 2
+        + [dma((2, 4))] * 2
         + [dma((4,))] * 2
         + [dma((2, 3))] * 4
         + [dma((2, 4))] * 2
         + [dma((2,))] * 2
-        + [dma((4,)), dma((2,)), dma((1,)), dma((images,))],
+        + [dma((4,))] * 2
+        + [dma((4,)), dma((6,)), dma((5,)), dma((1,))],
         compiler_params=pltpu.CompilerParams(
             collective_id=2, has_side_effects=True, vmem_limit_bytes=63 << 20
         ),
@@ -1918,8 +2032,10 @@
         cot,
         mixed,
         up_first,
+        down_first,
+        up_pair,
+        down_pair,
         up_second,
-        down_first,
         down_second,
     )
 
@@ -1957,27 +2073,29 @@
     quarter_width = feature_count // tensor_count
     experts_all = router_weight.shape[1]
     hidden = expert_up.shape[2]
-    chosen = routes[:, :, None] == jnp.arange(128, dtype=jnp.int32)[None, None, :]
-    kept = jnp.sum(jnp.where(chosen, keep_mask[:, :, None], 0), axis=1).astype(bf16)
+    kept_routes = per_image(jnp.where(keep_mask > 0, routes, -1) + 1).reshape(rows, 2) - 1
+    chosen = kept_routes[:, :, None] == jnp.arange(128, dtype=jnp.int32)[None, None, :]
+    kept = jnp.any(chosen, axis=1).astype(bf16)
     router_wide = jnp.pad(router_weight, ((0, 0), (0, 128 - experts_all)))
     tok = per_image(tokens)
+    qkv_turned = jnp.swapaxes(qkv_weight, 1, 2)
     queries, keys, values, attended, lse, resid, h_all, cot_all, kept_all, up_all, down_all = run_forward(
         tok,
-        gain_attn[None],
-        shift_attn[None],
-        gain_moe[None],
-        shift_moe[None],
-        qkv_weight,
+        gain_attn,
+        shift_attn,
+        gain_moe,
+        shift_moe,
+        qkv_turned,
         out_weight,
         expert_up[0],
         expert_down[0],
         per_image(cotangent).reshape(rows, quarter_width),
-        per_image(kept).reshape(rows, 128),
+        kept,
     )
     mixed_first, grad_h_first, gate_first, up_first, down_first, up_late, down_late = run_first_pair(
         h_all, cot_all, kept_all, router_wide, up_all, down_all, experts_all
     )
-    mixed_part, up_second, down_second, grad_router, grad_h_two = run_second_pair(
+    mixed_part, up_second, down_second, grad_router, grad_h_two, up_pair, down_pair = run_second_pair(
         h_all,
         cot_all,
         kept_all,
@@ -1989,14 +2107,16 @@
         down_all,
         up_late,
         down_late,
+        up_first,
+        down_first,
         experts_all,
     )
-    grad_up, grad_down, tokens_grad, weights_grad, mixed = run_backward(
+    grad_up, grad_down, tokens_grad, grad_qkv, grad_out, sums, mixed = run_backward(
         tok,
-        gain_attn[None],
-        shift_attn[None],
-        gain_moe[None],
-        qkv_weight,
+        gain_attn,
+        shift_attn,
+        gain_moe,
+        qkv_turned,
         out_weight,
         queries,
         keys,
@@ -2009,23 +2129,22 @@
         cot_all,
         mixed_part,
         up_first,
+        down_first,
+        up_pair,
+        down_pair,
         up_second,
-        down_first,
         down_second,
     )
-    share = qkv_weight.shape[2]
-    grad_qkv = weights_grad[: 3 * share].reshape(3, share, feature_count).transpose(0, 2, 1)
-    small = weights_grad[feature_count : feature_count + 16]
     return (
         unpad(mixed.reshape(images, PITCH, quarter_width)),
-        unpad(tokens_grad.reshape(images, PITCH, feature_count)),
-        small[0],
-        small[1],
-        grad_qkv,
-        weights_grad[3 * share : 4 * share],
-        small[2],
-        small[3],
-        small[8 : 8 + experts_all].T,
+        tokens_grad,
+        sums[2],
+        sums[3],
+        jnp.swapaxes(grad_qkv, 1, 2),
+        grad_out,
+        sums[0],
+        sums[1],
+        sums[8 : 8 + experts_all].T,
         grad_up[None],
         grad_down[None],
     )

time: 338 us -> 317 us (0.938)
  local copies, waits for them, and re-layouts: 35.7 us -> 23.3 us
  Pallas kernels: 298 us -> 290 us
    pallas_call x1, Pallas kernels: 125 us -> 116 us  [run_backward(): pl.pallas_call(partial(backward_kernel, images=images, heads=heads), out_...]
    unnamed x16, local copies, waits for them, and re-layouts: 4.33 us -> 10.2 us
    reshape x3 -> x2, local copies, waits for them, and re-layouts: 6.85 us -> 1.49 us  [unpad(): return blocks[:, :SEQ].reshape(images * SEQ, blocks.shape[2])]
    broadcast_in_dim x4 -> x0, local copies, waits for them, and re-layouts: 5.07 us -> none  [the longest x1 1.27 us: per_device_dense(): gain_attn[None]]
    slice x2 -> x1, local copies, waits for them, and re-layouts: 6.11 us -> 1.21 us  [unpad(): return blocks[:, :SEQ].reshape(images * SEQ, blocks.shape[2])]
where the time goes in v4:
time: 317 us; the launch traced here: 316 us
  Pallas kernels  290 us (91%)
  local copies, waits for them, and re-layouts  23.3 us (7%)
    pallas_call x1, Pallas kernels, run_backward(): pl.pallas_call(partial(backward_kernel, images=images, heads=heads), out_...  116 us
    pallas_call x1, Pallas kernels, run_forward(): pl.pallas_call(partial(forward_kernel, images=images, heads=heads), out_s...  73.6 us
    pallas_call x1, Pallas kernels, run_second_pair(): pl.pallas_call(partial(second_pair_kernel, experts=experts, steps=steps),...  63.6 us
    pallas_call x1, Pallas kernels, run_first_pair(): pl.pallas_call(partial(first_pair_kernel, experts=experts, steps=steps),...  36.5 us
    unnamed x16, local copies, waits for them, and re-layouts  10.2 us

profile of v4, /device:TPU:0, one launch (start us, length us, event | category | flops | bytes accessed | tf_op | source)
XLA Modules:
  0.0 316.0 jit_solution(14072372161505561797)
XLA Ops:
  0.6 0.7 fusion.1
  1.4 0.1 reshape.51
  1.5 0.1 sub.7
  1.6 0.9 copy.33
  2.5 0.7 pad.19.router_ref
  3.2 0.8 fusion
  4.0 0.8 convert_element_type.9.kept_ref
  4.8 2.4 reshape.49
  7.2 0.8 copy.32
  8.0 1.0 pad.17
  9.1 2.4 reshape.48
  11.5 1.6 pad.16.tok_ref
  13.1 73.6 %shard_map.212 = (bf16[8,208,192]{2,1,0:T(8,128)(2,1)}, bf16[8,208,192]{2,1,0:T(8,128)(2,1)}, bf16[8,208,192]{2,1,0:T(8,128)(2,1)}, bf16[8,208,192]{2,1,0:T(8,12...) custom-call(bf16[8,208,768]{2,1,0:T(8,128)(2,1)} %pad.16.tok_ref, ...), custom_call_target="tpu_custom_call" | custom-call | tf_op jit(solution)/shard_map/pallas_call | solution.py:762
  86.7 36.5 %shard_map.213 = (bf16[3328,768]{1,0:T(8,128)(2,1)}, bf16[3328,768]{1,0:T(8,128)(2,1)}, f32[3328,128]{1,0:T(8,128)}, bf16[768,768]{1,0:T(8,128)(2,1)}, bf16[768,...) custom-call(bf16[3328,768]{1,0:T(8,128)(2,1)} %get-tuple-element.48.h_ref, ...), custom_call_target="tpu_custom_call" | custom-call | tf_op jit(solution)/shard_map/pallas_call | solution.py:934
  123.2 63.6 %shard_map.214 = (bf16[3328,768]{1,0:T(8,128)(2,1)}, bf16[768,768]{1,0:T(8,128)(2,1)}, bf16[768,768]{1,0:T(8,128)(2,1)}, f32[8,768]{1,0:T(8,128)}, bf16[1664,768...) custom-call(bf16[3328,768]{1,0:T(8,128)(2,1)} %get-tuple-element.48.h_ref, ...), custom_call_target="tpu_custom_call" | custom-call | tf_op jit(solution)/shard_map/pallas_call | solution.py:1215
  186.8 115.9 %shard_map.215 = (f32[768,384]{1,0:T(8,128)}, f32[384,768]{1,0:T(8,128)}, f32[1576,768]{1,0:T(8,128)}, f32[3,192,768]{2,1,0:T(8,128)}, f32[192,768]{1,0:T(8,128)...) custom-call(bf16[8,208,768]{2,1,0:T(8,128)(2,1)} %pad.16.tok_ref, f32[768]{0:T(1024)} %gain1_ref.3, f32[768]{0:T(1024)} %shift1_ref.3, ...), custom_call_target="tpu_custom_call" | custom-call | tf_op jit(solution)/shard_map/pallas_call | solution.py:1968
  302.7 0.0 copy-start.4
  302.7 1.2 slice.24
  303.9 0.4 reshape.54
  304.3 1.1 copy.35
  305.4 0.0 copy-done.4
  305.4 0.6 slice_bitcast_fusion
  306.1 0.6 slice_reduce_fusion
  306.7 5.0 %copy.41 = f32[1576,768]{1,0:T(8,128)} copy(f32[1576,768]{1,0:T(8,128)} %get-tuple-element.91) | data formatting | bytes 9682944
  311.7 0.0 copy-done
  311.7 1.2 copy.42
  312.9 0.2 copy-done.3
  313.2 0.8 copy.43
  314.0 0.0 copy-done.2
  314.0 1.0 copy.44
  315.0 0.0 copy-done.1
  315.0 1.0 copy.45
  (5 shorter events, 0.0 us)
Async XLA Ops:
  302.7 2.7 copy-start.4
  306.7 5.0 %copy-start = (f32[3,192,768]{2,1,0:T(8,128)S(1)}, f32[3,192,768]{2,1,0:T(8,128)}, u32[]{:S(2)}) copy-start(f32[3,192,768]{2,1,0:T(8,128)} %get-tuple-element.71) | copy-start | bytes 5308420
  311.7 1.4 copy-start.3
  311.7 2.3 copy-start.2
  313.2 1.8 copy-start.1

commit v5 on v4

--- a/solution.py
+++ b/solution.py
@@ -349,6 +349,37 @@
     return (lane < HD) if head % 2 == 0 else (lane >= HD)
 
 
+def expert_math(h_rows, cot_rows, kept, router, up, down, pair, experts):
+    block = h_rows.shape[0]
+    hidden = up.shape[1] // 2
+    lane = lax.broadcasted_iota(jnp.int32, (block, 128), 1)
+    logits = jnp.where(lane < experts, dot(h_rows, router), -1e30)
+    powers = jnp.exp(logits - jnp.max(logits, axis=1, keepdims=True))
+    probs = powers / jnp.sum(powers, axis=1, keepdims=True)
+    gates = kept * probs
+    pre_act = dot(h_rows, up)
+    back = dot(cot_rows, down, ((1,), (1,)))
+    normal_cdf = 0.5 + 0.5 * lax.erf(pre_act * 0.7071067811865476)
+    gelu = pre_act * normal_cdf
+    slope = normal_cdf + pre_act * (0.3989422804014327 * jnp.exp(-0.5 * pre_act * pre_act))
+    product = gelu * back
+    grad_gate = jnp.zeros((block, 128), f32)
+    spread = []
+    for side in range(2):
+        chosen = lane == 2 * pair + side
+        part = jnp.sum(product[:, side * hidden : (side + 1) * hidden], axis=1, keepdims=True)
+        grad_gate = jnp.where(chosen, part, grad_gate)
+        gate = jnp.sum(jnp.where(chosen, gates, 0.0), axis=1, keepdims=True)
+        spread.append(jnp.broadcast_to(gate, (block, hidden)))
+    gate = jnp.concatenate(spread, axis=1)
+    hidden_rows = (gelu * gate).astype(bf16)
+    grad_pre = (slope * back * gate).astype(bf16)
+    return hidden_rows, grad_pre, probs, grad_gate
+
+
+BLOCK = 2 * PITCH
+
+
 def forward_kernel(
     tok_ref,
     gain1_ref,
@@ -361,6 +392,7 @@
     down_ref,
     cot_ref,
     kept_ref,
+    router_ref,
     q_ref,
     k_ref,
     v_ref,
@@ -372,6 +404,20 @@
     kept_out,
     up_out,
     down_out,
+    mixed_out,
+    grad_h_out,
+    gate_out,
+    grad_up_out,
+    grad_down_out,
+    up_vm,
+    down_vm,
+    up_sum,
+    down_sum,
+    mixed_slots,
+    grad_h_slots,
+    gate_slots,
+    grad_up_vm,
+    grad_down_vm,
     q_all,
     k_all,
     v_all,
@@ -405,11 +451,15 @@
     c_s,
     c_r,
     own_sem,
+    pair_sem,
+    block_sem,
+    grad_sem,
     cot_sem,
     out_sem,
     *,
     images,
     heads,
+    experts,
 ):
     expert_at = lax.axis_index("expert")
     tensor_at = lax.axis_index("tensor")
@@ -479,8 +529,17 @@
                     copy.wait_recv()
 
     start_hops(0)
-    own = slot(z_at, z_at)
-    own_copies = [pltpu.make_async_copy((up_ref, down_ref)[n], own[n], own_sem.at[n]) for n in range(2)]
+
+    def pair_place(expert):
+        return up_vm.at[:, lanes_at(expert % 2 * hidden, hidden)], down_vm.at[aligned(expert % 2 * hidden, hidden), :]
+
+    near = z_at + 1 - 2 * (z_at % 2)
+    own_copies = [
+        pltpu.make_async_copy((up_ref, down_ref)[n], pair_place(z_at)[n], own_sem.at[n]) for n in range(2)
+    ]
+    near_copies = [
+        pltpu.make_async_copy(slot(near, z_at)[n], pair_place(near)[n], pair_sem.at[n]) for n in range(2)
+    ]
     for copy in own_copies:
         copy.start()
 
@@ -686,10 +745,62 @@
     def weights_step_one():
         await_hops(0)
         start_hops(1)
+        for copy in near_copies:
+            copy.start()
+
+    def weights_step_two():
+        await_hops(1)
+        start_hops(2)
 
     def cot_step_three():
         relay_in.wait_recv()
         cot_share[2].start()
+
+    def ready_own():
+        cot_share_in[0].wait_recv()
+        for copy in (*own_copies, *near_copies):
+            copy.wait()
+
+    def ready_other():
+        for copy in (cot_share_in[1], cot_share_in[2], kept_share_in):
+            copy.wait_recv()
+
+    def block_copies(number, place):
+        at = aligned(number * BLOCK, BLOCK)
+        pairs = ((mixed_slots, mixed_out), (grad_h_slots, grad_h_out), (gate_slots, gate_out))
+        return [
+            pltpu.make_async_copy(slots.at[place], out.at[at, :], block_sem.at[n, place])
+            for n, (slots, out) in enumerate(pairs)
+        ]
+
+    def run_block(number, turn):
+        at = aligned(number * BLOCK, BLOCK)
+        h_rows, cot_rows = h_all[at, :], cot_all[at, :]
+        up, down = up_vm[...], down_vm[...]
+        hidden_rows, grad_pre, _, grad_gate = expert_math(
+            h_rows, cot_rows, kept_all[at, :].astype(f32), router_ref[...], up, down, z_at // 2, experts
+        )
+
+        place = turn % 2
+
+        @pl.when(turn >= 2)
+        def _():
+            for copy in block_copies(number, place):
+                copy.wait()
+
+        gate_slots[place] = grad_gate
+        mixed_slots[place] = dot(hidden_rows, down).astype(bf16)
+        grad_h_slots[place] = dot(grad_pre, up, ((1,), (1,))).astype(bf16)
+        for copy in block_copies(number, place):
+            copy.start()
+        up_sum[...] += dot(h_rows.T, grad_pre)
+        down_sum[...] += dot(cot_rows.T, hidden_rows)
+
+    def choose(tick, table):
+        return sum(jnp.where(tick == when, value, 0) for when, value in table)
+
+    BLOCKS_AT = ((7, 0), (9, 1), (11, 2), (12, 4), (13, 3), (14, 5), (16, 6), (18, 7))
+    TURNS = tuple((when, turn) for turn, (when, _) in enumerate(BLOCKS_AT))
 
     def per_tick(tick, _):
         stage(tick, 0, run_attend)
@@ -699,14 +810,30 @@
         stage(tick, 9, run_relay)
         stage(tick, 10, run_end)
         at_tick(tick, 5, cot_step_one)
-        at_tick(tick, 7, cot_step_two)
-        at_tick(tick, 8, weights_step_one)
-        at_tick(tick, 14, cot_step_three)
+        at_tick(tick, 6, weights_step_one)
+        at_tick(tick, 6, cot_step_two)
+        at_tick(tick, 7, ready_own)
+        at_tick(tick, 9, cot_step_three)
+        at_tick(tick, 12, ready_other)
+        at_tick(tick, 13, weights_step_two)
+
+        @pl.when(choose(tick, tuple((when, 1) for when, _ in BLOCKS_AT)) == 1)
+        def _():
+            run_block(choose(tick, BLOCKS_AT), choose(tick, TURNS))
+
         return 0
 
-    lax.fori_loop(0, images + 10, per_tick, 0)
-    for copy in (*cot_share_in, kept_share_in):
-        copy.wait_recv()
+    up_sum[...] = jnp.zeros_like(up_sum)
+    down_sum[...] = jnp.zeros_like(down_sum)
+    lax.fori_loop(0, images + 11, per_tick, 0)
+    grad_up_vm[...] = up_sum[...].astype(bf16)
+    grad_down_vm[...] = down_sum[...].astype(bf16)
+    grad_copies = [
+        pltpu.make_async_copy(grad_up_vm, grad_up_out, grad_sem.at[0]),
+        pltpu.make_async_copy(grad_down_vm, grad_down_out, grad_sem.at[1]),
+    ]
+    for copy in grad_copies:
+        copy.start()
     outs = [
         pltpu.make_async_copy(cot_all, cot_out, cot_sem.at[0]),
         pltpu.make_async_copy(kept_all, kept_out, cot_sem.at[1]),
@@ -733,8 +860,12 @@
         return 0
 
     lax.fori_loop(0, images, drain, 0)
-    await_hops(1)
-    for step in range(2):
+    for place in range(2):
+        for copy in block_copies(0, place):
+            copy.wait()
+
+    await_hops(2)
+    for step in range(3):
         for way in range(2):
 
             @pl.when(hop_goes(step, way))
@@ -742,11 +873,11 @@
                 for copy in hop(step, way):
                     copy.wait_send()
 
-    for copy in (*own_copies, *outs):
+    for copy in (*grad_copies, *outs):
         copy.wait()
 
 
-def run_forward(tok, gain1, shift1, gain2, shift2, qkv_w, out_w, up, down, cot, kept):
+def run_forward(tok, gain1, shift1, gain2, shift2, qkv_w, out_w, up, down, cot, kept, router, experts):
     images = tok.shape[0]
     rows = images * PITCH
     features = tok.shape[2]
@@ -760,7 +891,7 @@
     block = (images, PITCH, wide)
     dma = pltpu.SemaphoreType.DMA
     return pl.pallas_call(
-        partial(forward_kernel, images=images, heads=heads),
+        partial(forward_kernel, images=images, heads=heads, experts=experts),
         out_shape=[
             shape((images, PITCH, share), bf16),
             shape((images, PITCH, share), bf16),
@@ -773,10 +904,21 @@
             shape((2 * rows, 128), bf16),
             shape((2, features, 2 * hidden), bf16),
             shape((2, 2 * hidden, features), bf16),
+            shape((2 * rows, features), bf16),
+            shape((2 * rows, features), bf16),
+            shape((2 * rows, 128), f32),
+            shape((features, 2 * hidden), bf16),
+            shape((features, 2 * hidden), bf16),
         ],
-        in_specs=[vmem] * 7 + [anywhere] * 2 + [vmem] * 2,
-        out_specs=[anywhere] * 11,
+        in_specs=[vmem] * 7 + [anywhere] * 2 + [vmem] * 3,
+        out_specs=[anywhere] * 16,
         scratch_shapes=[
+            pltpu.VMEM((features, 2 * hidden), bf16),
+            pltpu.VMEM((2 * hidden, features), bf16),
+            *[pltpu.VMEM((features, 2 * hidden), f32)] * 2,
+            *[pltpu.VMEM((2, BLOCK, features), bf16)] * 2,
+            pltpu.VMEM((2, BLOCK, 128), f32),
+            *[pltpu.VMEM((features, 2 * hidden), bf16)] * 2,
             *[pltpu.VMEM((images, PITCH, share), bf16)] * 4,
             pltpu.VMEM((images, PITCH, 128), f32),
             pltpu.VMEM((images, PITCH, features), f32),
@@ -794,179 +936,13 @@
             pltpu.VMEM((rows, share), bf16),
         ]
         + [dma((images,))] * 10
-        + [dma((2, 2, 2))] * 2
+        + [dma((2, 3, 2))] * 2
         + [dma((9,))] * 2
-        + [dma((2,)), dma((2,)), dma((8, images))],
+        + [dma((2,)), dma((2,)), dma((3, 2)), dma((2,)), dma((2,)), dma((8, images))],
         compiler_params=pltpu.CompilerParams(
-            collective_id=1, has_side_effects=True, vmem_limit_bytes=60 << 20
+            collective_id=1, has_side_effects=True, vmem_limit_bytes=63 << 20
         ),
-    )(tok, gain1, shift1, gain2, shift2, qkv_w, out_w, up, down, cot, kept)
-
-
-def expert_math(h_rows, cot_rows, kept, router, up, down, pair, experts):
-    block = h_rows.shape[0]
-    hidden = up.shape[1] // 2
-    lane = lax.broadcasted_iota(jnp.int32, (block, 128), 1)
-    logits = jnp.where(lane < experts, dot(h_rows, router), -1e30)
-    powers = jnp.exp(logits - jnp.max(logits, axis=1, keepdims=True))
-    probs = powers / jnp.sum(powers, axis=1, keepdims=True)
-    gates = kept * probs
-    pre_act = dot(h_rows, up)
-    back = dot(cot_rows, down, ((1,), (1,)))
-    normal_cdf = 0.5 + 0.5 * lax.erf(pre_act * 0.7071067811865476)
-    gelu = pre_act * normal_cdf
-    slope = normal_cdf + pre_act * (0.3989422804014327 * jnp.exp(-0.5 * pre_act * pre_act))
-    product = gelu * back
-    grad_gate = jnp.zeros((block, 128), f32)
-    spread = []
-    for side in range(2):
-        chosen = lane == 2 * pair + side
-        part = jnp.sum(product[:, side * hidden : (side + 1) * hidden], axis=1, keepdims=True)
-        grad_gate = jnp.where(chosen, part, grad_gate)
-        gate = jnp.sum(jnp.where(chosen, gates, 0.0), axis=1, keepdims=True)
-        spread.append(jnp.broadcast_to(gate, (block, hidden)))
-    gate = jnp.concatenate(spread, axis=1)
-    hidden_rows = (gelu * gate).astype(bf16)
-    grad_pre = (slope * back * gate).astype(bf16)
-    return hidden_rows, grad_pre, probs, grad_gate
-
-
-def first_pair_kernel(
-    h_ref,
-    cot_ref,
-    kept_ref,
-    router_ref,
-    up_ref,
-    down_ref,
-    up_all,
-    down_all,
-    mixed_ref,
-    grad_h_ref,
-    gate_ref,
-    grad_up_ref,
-    grad_down_ref,
-    up_late,
-    down_late,
-    up_sum,
-    down_sum,
-    late_s,
-    late_r,
-    *,
-    experts,
-    steps,
-):
-    expert_at = lax.axis_index("expert")
-    tensor_at = lax.axis_index("tensor")
-    z_at = expert_at // 2
-    hidden = up_late.shape[1]
-    partner = (jnp.where(z_at % 2 == 0, expert_at + 2, expert_at - 2), tensor_at)
-    inner = (z_at == 1) | (z_at == 2)
-    outer = (z_at == 0) | (z_at == 3)
-    far = jnp.where(z_at == 1, hidden, 0)
-    sources = (up_all.at[1, :, lanes_at(far, hidden)], down_all.at[1, aligned(far, hidden), :])
-    hops = [
-        pltpu.make_async_remote_copy(
-            src_ref=source,
-            dst_ref=target,
-            send_sem=late_s.at[number],
-            recv_sem=late_r.at[number],
-            device_id=partner,
-            device_id_type=MESH,
-        )
-        for number, (source, target) in enumerate(zip(sources, (up_late, down_late)))
-    ]
-
-    @pl.when(pl.program_id(0) == 0)
-    def _():
-        greet([(True, partner)])
-
-        @pl.when(inner)
-        def _():
-            for copy in hops:
-                copy.start()
-
-        up_sum[...] = jnp.zeros_like(up_sum)
-        down_sum[...] = jnp.zeros_like(down_sum)
-
-    h_rows, cot_rows = h_ref[...], cot_ref[...]
-    up, down = up_ref[0], down_ref[0]
-    hidden_rows, grad_pre, _, grad_gate = expert_math(
-        h_rows, cot_rows, kept_ref[...].astype(f32), router_ref[...], up, down, z_at // 2, experts
-    )
-    gate_ref[...] = grad_gate
-    mixed_ref[...] = dot(hidden_rows, down).astype(bf16)
-    grad_h_ref[...] = dot(grad_pre, up, ((1,), (1,))).astype(bf16)
-    up_sum[...] += dot(h_rows.T, grad_pre)
-    down_sum[...] += dot(cot_rows.T, hidden_rows)
-
-    @pl.when(pl.program_id(0) == steps - 1)
-    def _():
-        grad_up_ref[...] = up_sum[...].astype(bf16)
-        grad_down_ref[...] = down_sum[...].astype(bf16)
-
-        @pl.when(inner)
-        def _():
-            for copy in hops:
-                copy.wait_send()
-
-        @pl.when(outer)
-        def _():
-            for copy in hops:
-                copy.wait_recv()
-
-
-BLOCK = 2 * PITCH
-
-
-def run_first_pair(h_rows, cot_rows, kept, router, up, down, experts):
-    rows, features = h_rows.shape
-    width = up.shape[2]
-    steps = rows // BLOCK
-    anywhere = pl.BlockSpec(memory_space=pl.ANY)
-    shape = jax.ShapeDtypeStruct
-
-    def by_step(lanes):
-        return pl.BlockSpec((BLOCK, lanes), lambda n: (n, 0))
-
-    def whole(*dims):
-        return pl.BlockSpec(dims, lambda n: (0,) * len(dims))
-
-    return pl.pallas_call(
-        partial(first_pair_kernel, experts=experts, steps=steps),
-        grid=(steps,),
-        out_shape=[
-            shape((rows, features), bf16),
-            shape((rows, features), bf16),
-            shape((rows, 128), f32),
-            shape((features, width), bf16),
-            shape((features, width), bf16),
-            shape((features, width // 2), bf16),
-            shape((width // 2, features), bf16),
-        ],
-        in_specs=[
-            by_step(features),
-            by_step(features),
-            by_step(128),
-            whole(features, 128),
-            whole(1, features, width),
-            whole(1, width, features),
-            anywhere,
-            anywhere,
-        ],
-        out_specs=[
-            by_step(features),
-            by_step(features),
-            by_step(128),
-            whole(features, width),
-            whole(features, width),
-            anywhere,
-            anywhere,
-        ],
-        scratch_shapes=[pltpu.VMEM((features, width), f32)] * 2 + [pltpu.SemaphoreType.DMA((2,))] * 2,
-        compiler_params=pltpu.CompilerParams(
-            collective_id=3, has_side_effects=True, vmem_limit_bytes=60 << 20
-        ),
-    )(h_rows, cot_rows, kept, router, up, down, up, down)
+    )(tok, gain1, shift1, gain2, shift2, qkv_w, out_w, up, down, cot, kept, router)
 
 
 def turn_is_other(turn):
@@ -988,8 +964,6 @@
     gate_first,
     up_all,
     down_all,
-    up_late,
-    down_late,
     up_first,
     down_first,
     mixed_ref,
@@ -1029,7 +1003,7 @@
     tensor_at = lax.axis_index("tensor")
     z_at, y_at = expert_at // 2, expert_at % 2
     x_at, core_at = tensor_at // 2, tensor_at % 2
-    hidden = up_late.shape[1]
+    hidden = up_pair.shape[1]
     wide = ring.shape[2] // 2
     core_dev = (expert_at, tensor_at + 1 - 2 * core_at)
     x_dev = (expert_at, tensor_at + 2 - 4 * x_at)
@@ -1098,9 +1072,6 @@
         greet([(True, core_dev), (True, x_dev), (True, y_dev), (True, z_dev)])
         for copy in pair_copies:
             copy.start()
-        late_expert = jnp.where(z_at == 0, 1, 0)
-        late = late_expert * hidden
-        is_outer = (z_at == 0) | (z_at == 3)
         whole = [
             pltpu.make_async_copy(up_all.at[1], up_vm, load.at[0]),
             pltpu.make_async_copy(down_all.at[1], down_vm, load.at[1]),
@@ -1112,17 +1083,6 @@
         router_sum[...] = jnp.zeros_like(router_sum)
         for copy in whole:
             copy.wait()
-
-        @pl.when(is_outer)
-        def _():
-            parts = [
-                pltpu.make_async_copy(up_late, up_vm.at[:, lanes_at(late, hidden)], load.at[0]),
-                pltpu.make_async_copy(down_late, down_vm.at[aligned(late, hidden), :], load.at[1]),
-            ]
-            for copy in parts:
-                copy.start()
-            for copy in parts:
-                copy.wait()
 
     h_rows, cot_rows = h_ref[...], cot_ref[...]
     up, down, router = up_vm[...], down_vm[...], router_ref[...]
@@ -1192,8 +1152,6 @@
     gate_first,
     up,
     down,
-    up_late,
-    down_late,
     up_first,
     down_first,
     experts,
@@ -1233,7 +1191,7 @@
             by_step(features),
             by_step(128),
         ]
-        + [anywhere] * 6,
+        + [anywhere] * 4,
         out_specs=[by_step(features), whole(features, width), whole(features, width), whole(8, features)] + [anywhere] * 3,
         scratch_shapes=[
             pltpu.VMEM((features, width), bf16),
@@ -1253,23 +1211,23 @@
         compiler_params=pltpu.CompilerParams(
             collective_id=4, has_side_effects=True, vmem_limit_bytes=60 << 20
         ),
-    )(h_rows, cot_rows, kept, router, mixed_first, grad_h_first, gate_first, up, down, up_late, down_late, up_first, down_first)
+    )(h_rows, cot_rows, kept, router, mixed_first, grad_h_first, gate_first, up, down, up_first, down_first)
 
 
 def backward_kernel(
-    tok_ref,
     gain1_ref,
     shift1_ref,
     gain2_ref,
     qkv_ref,
     out_w_ref,
-    q_ref,
-    k_ref,
-    v_ref,
-    att_ref,
-    lse_ref,
-    grad_h_ref,
     grad_router_ref,
+    tok_hbm,
+    q_hbm,
+    k_hbm,
+    v_hbm,
+    att_hbm,
+    lse_hbm,
+    grad_h_hbm,
     resid_ref,
     cot_ref,
     mixed_ref,
@@ -1286,6 +1244,13 @@
     out_w_out,
     sums_out,
     mixed_out,
+    tok_ref,
+    q_ref,
+    k_ref,
+    v_ref,
+    att_ref,
+    lse_ref,
+    grad_h_ref,
     rows_kept,
     cot_rows,
     m_mine,
@@ -1314,6 +1279,9 @@
     late_mine,
     late_y,
     late_z,
+    up_total,
+    down_total,
+    sums_all,
     whole,
     mc_s,
     mc_r,
@@ -1345,6 +1313,7 @@
     late_s,
     late_r,
     load,
+    image_load,
     own_sem,
     weight_store,
     store,
@@ -1359,7 +1328,7 @@
     x_at, core_at = tensor_at // 2, tensor_at % 2
     other = 1 - core_at
     rows = images * PITCH
-    features = tok_ref.shape[2]
+    features = tok_hbm.shape[2]
     wide = features // 2
     share = out_w_ref.shape[0]
     hidden = line.shape[3]
@@ -1395,13 +1364,28 @@
         m_core_copy(1, part).start()
     for part in range(part_count):
         m_core_copy(0, part).start()
-    loads = [
-        pltpu.make_async_copy(resid_ref, rows_kept, load.at[0]),
-        pltpu.make_async_copy(cot_ref.at[pl.ds(0, rows), :], cot_rows, load.at[1]),
-        pltpu.make_async_copy(mixed_ref.at[:, my_cols], m_mine, load.at[2]),
+    m_loads = [
+        pltpu.make_async_copy(mixed_ref.at[pl.ds(side * rows, rows), my_cols], m_mine.at[pl.ds(side * rows, rows), :], load.at[side])
+        for side in range(2)
     ]
-    for copy in loads:
-        copy.start()
+
+    def image_loads(image):
+        at = at_image(image)
+        by_image = ((tok_hbm, tok_ref), (q_hbm, q_ref), (k_hbm, k_ref), (v_hbm, v_ref), (att_hbm, att_ref), (lse_hbm, lse_ref))
+        by_row = ((grad_h_hbm, grad_h_ref), (resid_ref, rows_kept), (cot_ref, cot_rows))
+        pairs = [(source.at[image], target.at[image]) for source, target in by_image]
+        pairs += [(source.at[at, :], target.at[at, :]) for source, target in by_row]
+        return [pltpu.make_async_copy(source, target, image_load.at[n, image]) for n, (source, target) in enumerate(pairs)]
+
+    def start_loads(image, _):
+        for copy in image_loads(image):
+            copy.start()
+        return 0
+
+    start_loads(0, 0)
+    m_loads[1].start()
+    lax.fori_loop(1, images, start_loads, 0)
+    m_loads[0].start()
     route_one = remote(grad_router_ref, route_core, r_s.at[0], r_r.at[0], core_dev)
     route_one.start()
 
@@ -1467,8 +1451,6 @@
             )
         )
     ]
-    for copy in loads:
-        copy.wait()
     for copy in later:
         copy.start()
     weight_sum[...] = jnp.zeros_like(weight_sum)
@@ -1502,6 +1484,8 @@
         m_y_copy(part).start()
 
     def run_m_x(part):
+        if isinstance(part, int) and part == 0:
+            m_loads[0].wait()
         m_core_copy(0, part).wait_recv()
         m_y_copy(part).wait_recv()
         at = m_rows(0, part)
@@ -1525,6 +1509,7 @@
             m_quarter_copy(part).start()
             m_store_copy(part).start()
 
+    m_loads[1].wait()
     for part in range(part_count):
         run_m_y(part)
     route_one.wait_recv()
@@ -1558,10 +1543,12 @@
         sums[row + 1 : row + 2, :] += jnp.sum(grad, axis=0, keepdims=True)
 
     def run_attention(image):
+        for copy in image_loads(image):
+            copy.wait()
         at = at_image(image)
         grad_h = grad_h_ref[at, :].astype(f32)
         normed, inverse = norm_stats(rows_kept[at, :])
-        add_sums(weight_sum, features, grad_h, normed)
+        add_sums(late_mine, 2, grad_h, normed)
         grad_resid = cot_rows[at, :].astype(f32) + norm_back(grad_h, gain2, normed, inverse)
         rows_kept[at, :] = grad_resid
         grad_branch = grad_resid.astype(bf16)
@@ -1640,39 +1627,33 @@
         def _():
             run(image)
 
-    def m_stage(tick, ticks, run):
-        part = sum(jnp.where(tick > when, 1, 0) for when in ticks)
-        falls = sum(jnp.where(tick == when, 1, 0) for when in ticks)
-
-        @pl.when(falls == 1)
+    def at_tick(tick, when, run):
+        @pl.when(tick == when)
         def _():
-            run(part)
+            run()
+
+    def line_first():
+        later[0].wait()
+        later[1].wait()
+        line_add(0)
+
+    def line_second():
+        line_add(1)
+        line_pass(0)
 
     def per_tick(tick, _):
         stage(tick, 0, run_attention)
         stage(tick, 1, run_one_x)
-        stage(tick, 2, run_one_total)
-        stage(tick, 3, run_tokens)
-        m_stage(tick, (2, 4, 5, 7), run_m_x)
-        m_stage(tick, (4, 5, 7), run_m_out)
-
-        @pl.when(tick == 2)
-        def _():
-            later[0].wait()
-            later[1].wait()
-            line_add(0)
-
-        @pl.when(tick == 5)
-        def _():
-            line_add(1)
-            line_pass(0)
-
+        stage(tick, 4, run_one_total)
+        stage(tick, 5, run_tokens)
+        at_tick(tick, 3, line_first)
+        at_tick(tick, 5, lambda: run_m_x(0))
+        at_tick(tick, 6, line_second)
+        at_tick(tick, 7, lambda: run_m_x(1))
         return 0
 
     lax.fori_loop(0, images, per_tick, 0)
 
-    route_two.wait_recv()
-    weight_sum[features + 8 : features + 16, :] = route_core[...] + route_x[...]
     part_rows = shared.shape[1]
     quarter = part_rows // (z_last + 1)
 
@@ -1706,8 +1687,9 @@
     for number in range(4):
         shared_y_copy(number).start()
     run_one_x(images - 1)
-    run_one_total(images - 2)
-    run_tokens(images - 3)
+    run_m_x(part_count - 2)
+    run_one_total(images - 4)
+    run_tokens(images - 5)
     line_pass(1)
     line_add(2)
 
@@ -1749,39 +1731,55 @@
                 small_copy(step, way).wait_recv()
 
         if step == 0:
+            run_m_x(part_count - 1)
+            run_one_total(images - 3)
+            run_tokens(images - 4)
+            run_m_out(0)
+        if step == 1:
+            run_one_total(images - 2)
+            run_tokens(images - 3)
+            run_m_out(1)
+            line_add(3)
+
+    own_rows = quarter_at(z_at)
+    from_below = jnp.where(z_at > 0, shared_line[0, 1, 2].astype(f32), 0.0)
+    from_above = jnp.where(z_at < z_last, shared_line[1, 1, 2].astype(f32), 0.0)
+
+    def final_rows(side, piece):
+        return shared_all.at[side, quarter_at(piece), :]
+
+    shared_all[y_at, own_rows, :] = (weight_half[own_rows, :] + from_below + from_above).astype(bf16)
+    for number in range(4):
+        shared_y_copy(number).wait_send()
+
+    def gather_z(step, way, piece):
+        ref = final_rows(y_at, piece)
+        return remote(ref, ref, sg_s.at[way, step], sg_r.at[way, step], z_devs[way])
+
+    def gather_y(step, way, piece, side):
+        ref = final_rows(side, piece)
+        return remote(ref, ref, sz_s.at[way, step], sz_r.at[way, step], y_dev)
+
+    gather_y(0, 0, z_at, y_at).start()
+
+    def between(step):
+        if step == 0:
             run_one_total(images - 1)
             run_tokens(images - 2)
         if step == 1:
             run_tokens(images - 1)
+            route_two.wait_recv()
+            late_mine[8:16, :] = route_core[...] + route_x[...]
             late_y_copy.start()
             store_copy.start()
+            run_m_out(part_count - 2)
+        if step == 2:
             run_m_out(part_count - 1)
-            line_add(3)
-
-    late_y_copy.wait_recv()
-    late_z[z_at] = late_mine[...] + late_y[...]
-    for number in range(planes - 1):
-        late_copy(number).start()
-    own_rows = quarter_at(z_at)
-    from_below = jnp.where(z_at > 0, shared_line[0, 1, 2].astype(f32), 0.0)
-    from_above = jnp.where(z_at < z_last, shared_line[1, 1, 2].astype(f32), 0.0)
-
-    def final_rows(side, piece):
-        return shared_all.at[side, quarter_at(piece), :]
-
-    shared_all[y_at, own_rows, :] = (weight_half[own_rows, :] + from_below + from_above).astype(bf16)
-    for number in range(4):
-        shared_y_copy(number).wait_send()
-
-    def gather_z(step, way, piece):
-        ref = final_rows(y_at, piece)
-        return remote(ref, ref, sg_s.at[way, step], sg_r.at[way, step], z_devs[way])
-
-    def gather_y(step, way, piece, side):
-        ref = final_rows(side, piece)
-        return remote(ref, ref, sz_s.at[way, step], sz_r.at[way, step], y_dev)
-
-    gather_y(0, 0, z_at, y_at).start()
+            late_y_copy.wait_recv()
+            late_z[z_at] = late_mine[...] + late_y[...]
+            for number in range(planes - 1):
+                late_copy(number).start()
+
     for step in range(3):
         for way in range(2):
             at = place(way)
@@ -1791,6 +1789,7 @@
             def _():
                 gather_z(step, way, piece).start()
 
+        between(step)
         for way in range(2):
             at = place(way)
             piece = z_at - 1 - step if way == 0 else z_at + 1 + step
@@ -1800,40 +1799,6 @@
                 gather_z(step, way, piece).wait_recv()
                 gather_y(step + 1, way, piece, y_at).start()
 
-    gather_y(0, 0, z_at, 1 - y_at).wait_recv()
-    for step in range(3):
-        for way in range(2):
-            at = place(way)
-            piece = z_at - 1 - step if way == 0 else z_at + 1 + step
-
-            @pl.when(at >= 1 + step)
-            def _():
-                gather_y(step + 1, way, piece, 1 - y_at).wait_recv()
-
-    def to_out(piece, _):
-        for side in range(2):
-            weight_sum[aligned(side * part_rows + piece * quarter, quarter), :] = shared_all[
-                side, quarter_at(piece), :
-            ].astype(f32)
-        return 0
-
-    lax.fori_loop(0, z_last + 1, to_out, 0)
-    for number in range(planes - 1):
-        late_copy(number).wait_recv()
-    late = late_z[0]
-    for plane in range(1, planes):
-        late += late_z[plane]
-    weight_sum[features + 2 : features + 4, :] = late[:2]
-    weight_copies = [
-        *[
-            pltpu.make_async_copy(weight_sum.at[pl.ds(n * share, share), :], qkv_out.at[n], weight_store.at[n])
-            for n in range(3)
-        ],
-        pltpu.make_async_copy(weight_sum.at[pl.ds(3 * share, share), :], out_w_out, weight_store.at[3]),
-        pltpu.make_async_copy(weight_sum.at[pl.ds(features, 16), :], sums_out, weight_store.at[4]),
-    ]
-    for copy in weight_copies:
-        copy.start()
     for copy in later[2:]:
         copy.wait()
     for way in range(2):
@@ -1859,12 +1824,52 @@
             + line[from_far, first_piece + n, at_rows, :].astype(f32)
             for n in range(2)
         ]
-        up_out[at_rows, :] = totals[0]
-        down_out[:, lanes_at(piece * 128, 128)] = totals[1].T
+        up_total[at_rows, :] = totals[0]
+        down_total[:, lanes_at(piece * 128, 128)] = totals[1].T
         return 0
 
     lax.fori_loop(0, features // 128, finish, 0)
-
+    expert_copies = [
+        pltpu.make_async_copy(up_total, up_out, weight_store.at[5]),
+        pltpu.make_async_copy(down_total, down_out, weight_store.at[6]),
+    ]
+    for copy in expert_copies:
+        copy.start()
+
+    gather_y(0, 0, z_at, 1 - y_at).wait_recv()
+    for step in range(3):
+        for way in range(2):
+            at = place(way)
+            piece = z_at - 1 - step if way == 0 else z_at + 1 + step
+
+            @pl.when(at >= 1 + step)
+            def _():
+                gather_y(step + 1, way, piece, 1 - y_at).wait_recv()
+
+    def to_out(piece, _):
+        for side in range(2):
+            weight_sum[aligned(side * part_rows + piece * quarter, quarter), :] = shared_all[
+                side, quarter_at(piece), :
+            ].astype(f32)
+        return 0
+
+    lax.fori_loop(0, z_last + 1, to_out, 0)
+    for number in range(planes - 1):
+        late_copy(number).wait_recv()
+    late = late_z[0]
+    for plane in range(1, planes):
+        late += late_z[plane]
+    sums_all[...] = late
+    weight_copies = [
+        *[
+            pltpu.make_async_copy(weight_sum.at[pl.ds(n * share, share), :], qkv_out.at[n], weight_store.at[n])
+            for n in range(3)
+        ],
+        pltpu.make_async_copy(weight_sum.at[pl.ds(3 * share, share), :], out_w_out, weight_store.at[3]),
+        pltpu.make_async_copy(sums_all, sums_out, weight_store.at[4]),
+    ]
+    for copy in weight_copies:
+        copy.start()
     route_one.wait_send()
     route_two.wait_send()
 
@@ -1889,7 +1894,7 @@
             m_x_copy(part).wait_send()
             m_quarter_copy(part).wait_recv()
 
-    for copy in (*weight_copies, store_copy):
+    for copy in (*weight_copies, *expert_copies, store_copy):
         copy.wait()
     late_y_copy.wait_send()
     for number in range(planes - 1):
@@ -1928,37 +1933,13 @@
                 gather_y(step + 1, way, piece, y_at).wait_send()
 
 
-def run_backward(
-    tok,
-    gain1,
-    shift1,
-    gain2,
-    qkv_w,
-    out_w,
-    q,
-    k,
-    v,
-    att,
-    lse,
-    grad_h,
-    grad_router,
-    resid,
-    cot,
-    mixed,
-    up_first,
-    down_first,
-    up_pair,
-    down_pair,
-    up_second,
-    down_second,
-):
+def run_backward(gain1, shift1, gain2, qkv_w, out_w, grad_router, tok, *streamed):
     images, _, features = tok.shape
     rows = images * PITCH
     share = out_w.shape[0]
     heads = share // HD
-    hidden = up_first.shape[1] // 2
+    hidden = streamed[-1].shape[1] // 2
     wide = features // 2
-    packed = features + 128
     parts = 4
     vmem = pl.BlockSpec(memory_space=pltpu.VMEM)
     anywhere = pl.BlockSpec(memory_space=pl.ANY)
@@ -1976,9 +1957,13 @@
             shape((16, features), f32),
             shape((rows, wide // 2), bf16),
         ],
-        in_specs=[vmem] * 13 + [anywhere] * 9,
-        out_specs=[vmem] * 2 + [anywhere] * 5,
+        in_specs=[vmem] * 6 + [anywhere] * (1 + len(streamed)),
+        out_specs=[anywhere] * 7,
         scratch_shapes=[
+            pltpu.VMEM((images, PITCH, features), bf16),
+            *[pltpu.VMEM((images, PITCH, share), bf16)] * 4,
+            pltpu.VMEM((images, PITCH, 128), f32),
+            pltpu.VMEM((rows, features), bf16),
             pltpu.VMEM((rows, features), f32),
             pltpu.VMEM((rows, features), bf16),
             pltpu.VMEM((2 * rows, wide), bf16),
@@ -1991,14 +1976,18 @@
             pltpu.VMEM((2, features, 2 * hidden), bf16),
             *[pltpu.VMEM(block, bf16)] * 5,
             pltpu.VMEM((2, 4, features, hidden), bf16),
-            pltpu.VMEM((packed, features), f32),
-            pltpu.VMEM((packed // 2, features), f32),
-            pltpu.VMEM((2, packed // 2, features), bf16),
-            pltpu.VMEM((packed // 2, features), bf16),
-            pltpu.VMEM((2, 2, 3, packed // 8, features), bf16),
-            pltpu.VMEM((2, packed // 2, features), bf16),
-            *[pltpu.VMEM((8, features), f32)] * 4,
-            pltpu.VMEM((4, 8, features), f32),
+            pltpu.VMEM((features, features), f32),
+            pltpu.VMEM((features // 2, features), f32),
+            pltpu.VMEM((2, features // 2, features), bf16),
+            pltpu.VMEM((features // 2, features), bf16),
+            pltpu.VMEM((2, 2, 3, features // 8, features), bf16),
+            pltpu.VMEM((2, features // 2, features), bf16),
+            *[pltpu.VMEM((8, features), f32)] * 2,
+            *[pltpu.VMEM((16, features), f32)] * 2,
+            pltpu.VMEM((4, 16, features), f32),
+            pltpu.VMEM((features, hidden), f32),
+            pltpu.VMEM((hidden, features), f32),
+            pltpu.VMEM((16, features), f32),
             pltpu.VMEM((PITCH, features), f32),
         ]
         + [dma((2, parts))] * 2
@@ -2010,34 +1999,11 @@
         + [dma((2, 4))] * 2
         + [dma((2,))] * 2
         + [dma((4,))] * 2
-        + [dma((4,)), dma((6,)), dma((5,)), dma((1,))],
+        + [dma((4,)), dma((9, images)), dma((6,)), dma((7,)), dma((1,))],
         compiler_params=pltpu.CompilerParams(
             collective_id=2, has_side_effects=True, vmem_limit_bytes=63 << 20
         ),
-    )(
-        tok,
-        gain1,
-        shift1,
-        gain2,
-        qkv_w,
-        out_w,
-        q,
-        k,
-        v,
-        att,
-        lse,
-        grad_h,
-        grad_router,
-        resid,
-        cot,
-        mixed,
-        up_first,
-        down_first,
-        up_pair,
-        down_pair,
-        up_second,
-        down_second,
-    )
+    )(gain1, shift1, gain2, qkv_w, out_w, grad_router, tok, *streamed)
 
 
 def per_image(rows_in):
@@ -2079,7 +2045,24 @@
     router_wide = jnp.pad(router_weight, ((0, 0), (0, 128 - experts_all)))
     tok = per_image(tokens)
     qkv_turned = jnp.swapaxes(qkv_weight, 1, 2)
-    queries, keys, values, attended, lse, resid, h_all, cot_all, kept_all, up_all, down_all = run_forward(
+    (
+        queries,
+        keys,
+        values,
+        attended,
+        lse,
+        resid,
+        h_all,
+        cot_all,
+        kept_all,
+        up_all,
+        down_all,
+        mixed_first,
+        grad_h_first,
+        gate_first,
+        up_first,
+        down_first,
+    ) = run_forward(
         tok,
         gain_attn,
         shift_attn,
@@ -2091,9 +2074,8 @@
         expert_down[0],
         per_image(cotangent).reshape(rows, quarter_width),
         kept,
-    )
-    mixed_first, grad_h_first, gate_first, up_first, down_first, up_late, down_late = run_first_pair(
-        h_all, cot_all, kept_all, router_wide, up_all, down_all, experts_all
+        router_wide,
+        experts_all,
     )
     mixed_part, up_second, down_second, grad_router, grad_h_two, up_pair, down_pair = run_second_pair(
         h_all,
@@ -2105,26 +2087,24 @@
         gate_first,
         up_all,
         down_all,
-        up_late,
-        down_late,
         up_first,
         down_first,
         experts_all,
     )
     grad_up, grad_down, tokens_grad, grad_qkv, grad_out, sums, mixed = run_backward(
-        tok,
         gain_attn,
         shift_attn,
         gain_moe,
         qkv_turned,
         out_weight,
+        grad_router,
+        tok,
         queries,
         keys,
         values,
         attended,
         lse,
         grad_h_two,
-        grad_router,
         resid,
         cot_all,
         mixed_part,
@@ -2138,12 +2118,12 @@
     return (
         unpad(mixed.reshape(images, PITCH, quarter_width)),
         tokens_grad,
+        sums[0],
+        sums[1],
+        jnp.swapaxes(grad_qkv, 1, 2),
+        grad_out,
         sums[2],
         sums[3],
-        jnp.swapaxes(grad_qkv, 1, 2),
-        grad_out,
-        sums[0],
-        sums[1],
         sums[8 : 8 + experts_all].T,
         grad_up[None],
         grad_down[None],

time: 317 us -> 294 us (0.927)
  Pallas kernels: 290 us -> 268 us
    pallas_call x2 -> x1, Pallas kernels: 110 us -> 99.1 us  [run_forward(): pl.pallas_call(partial(forward_kernel, images=images, heads=heads, expert...]
    pallas_call x1, Pallas kernels: 116 us -> 107 us  [run_backward(): pl.pallas_call(partial(backward_kernel, images=images, heads=heads), out_...]
where the time goes in v5:
time: 294 us
  Pallas kernels  268 us (91%)
  local copies, waits for them, and re-layouts  23.3 us (8%)
    pallas_call x1, Pallas kernels, run_backward(): pl.pallas_call(partial(backward_kernel, images=images, heads=heads), out_...  107 us
    pallas_call x1, Pallas kernels, run_forward(): pl.pallas_call(partial(forward_kernel, images=images, heads=heads, expert...  99.1 us
    pallas_call x1, Pallas kernels, run_second_pair(): pl.pallas_call(partial(second_pair_kernel, experts=experts, steps=steps),...  61.5 us
    unnamed x16, local copies, waits for them, and re-layouts  10.2 us

profile of v5, /device:TPU:0, one launch (start us, length us, event | category | flops | bytes accessed | tf_op | source)
XLA Modules:
  0.0 293.9 jit_solution(16450239581820095212)
XLA Ops:
  0.6 0.7 fusion.1
  1.4 0.1 reshape.51
  1.5 0.1 sub.7
  1.6 0.9 copy.33
  2.5 0.7 pad.19.router_ref
  3.2 0.8 fusion
  4.0 0.8 convert_element_type.9.kept_ref
  4.8 2.4 reshape.49
  7.2 0.8 copy.32
  8.0 1.0 pad.17
  9.1 2.4 reshape.48
  11.5 1.6 pad.16.tok_ref.tok_hbm
  13.1 99.1 %shard_map.212 = (bf16[8,208,192]{2,1,0:T(8,128)(2,1)}, bf16[8,208,192]{2,1,0:T(8,128)(2,1)}, bf16[8,208,192]{2,1,0:T(8,128)(2,1)}, bf16[8,208,192]{2,1,0:T(8,12...) custom-call(bf16[8,208,768]{2,1,0:T(8,128)(2,1)} %pad.16.tok_ref.tok, ...), custom_call_target="tpu_custom_call" | custom-call | tf_op jit(solution)/shard_map/pallas_call | solution.py:893
  112.2 61.5 %shard_map.213 = (bf16[3328,768]{1,0:T(8,128)(2,1)}, bf16[768,768]{1,0:T(8,128)(2,1)}, bf16[768,768]{1,0:T(8,128)(2,1)}, f32[8,768]{1,0:T(8,128)}, bf16[1664,768...) custom-call(bf16[3328,768]{1,0:T(8,128)(2,1)} %get-tuple-element.41.h_ref, ...), custom_call_target="tpu_custom_call" | custom-call | tf_op jit(solution)/shard_map/pallas_call | solution.py:1173
  173.7 106.9 %shard_map.214 = (f32[768,384]{1,0:T(8,128)}, f32[384,768]{1,0:T(8,128)}, f32[1576,768]{1,0:T(8,128)}, f32[3,192,768]{2,1,0:T(8,128)}, f32[192,768]{1,0:T(8,128)...) custom-call(f32[768]{0:T(1024)} %gain1_ref.3, f32[768]{0:T(1024)} %shift1_ref.3, f32[768]{0:T(1024)} %gain2_ref.3, ...), custom_call_target="tpu_custom_call" | custom-call | tf_op jit(solution)/shard_map/pallas_call | solution.py:1949
  280.6 0.0 copy-start.4
  280.7 1.2 slice.24
  281.9 0.4 reshape.54
  282.2 1.1 copy.35
  283.4 0.0 copy-done.4
  283.4 0.6 slice_bitcast_fusion
  284.0 0.6 slice_reduce_fusion
  284.6 0.0 copy-start
  284.6 5.0 %copy.41 = f32[1576,768]{1,0:T(8,128)} copy(f32[1576,768]{1,0:T(8,128)} %get-tuple-element.87) | data formatting | bytes 9682944
  289.6 0.0 copy-done
  289.6 1.2 copy.42
  290.9 0.2 copy-done.3
  291.1 0.8 copy.43
  291.9 0.0 copy-done.2
  291.9 1.0 copy.44
  292.9 0.0 copy-done.1
  292.9 1.0 copy.45
  (4 shorter events, 0.0 us)
Async XLA Ops:
  280.6 2.7 copy-start.4
  284.6 5.0 %copy-start = (f32[3,192,768]{2,1,0:T(8,128)S(1)}, f32[3,192,768]{2,1,0:T(8,128)}, u32[]{:S(2)}) copy-start(f32[3,192,768]{2,1,0:T(8,128)} %get-tuple-element.67) | copy-start | bytes 5308420
  289.6 1.4 copy-start.3
  289.6 2.3 copy-start.2
  291.1 1.8 copy-start.1

commit v6 on v5

--- a/solution.py
+++ b/solution.py
@@ -718,11 +718,6 @@
         relay_arriving(image).wait_recv()
         other_copy(image).start()
 
-    def at_tick(tick, when, run):
-        @pl.when(tick == when)
-        def _():
-            run()
-
     def cot_step_one():
         cot_x_in.wait_recv()
         cot_share[0].start()
@@ -756,6 +751,11 @@
         relay_in.wait_recv()
         cot_share[2].start()
 
+    outs = [
+        pltpu.make_async_copy(cot_all, cot_out, cot_sem.at[0]),
+        pltpu.make_async_copy(kept_all, kept_out, cot_sem.at[1]),
+    ]
+
     def ready_own():
         cot_share_in[0].wait_recv()
         for copy in (*own_copies, *near_copies):
@@ -764,6 +764,8 @@
     def ready_other():
         for copy in (cot_share_in[1], cot_share_in[2], kept_share_in):
             copy.wait_recv()
+        for copy in outs:
+            copy.start()
 
     def block_copies(number, place):
         at = aligned(number * BLOCK, BLOCK)
@@ -796,36 +798,51 @@
         up_sum[...] += dot(h_rows.T, grad_pre)
         down_sum[...] += dot(cot_rows.T, hidden_rows)
 
-    def choose(tick, table):
-        return sum(jnp.where(tick == when, value, 0) for when, value in table)
-
-    BLOCKS_AT = ((7, 0), (9, 1), (11, 2), (12, 4), (13, 3), (14, 5), (16, 6), (18, 7))
-    TURNS = tuple((when, turn) for turn, (when, _) in enumerate(BLOCKS_AT))
-
-    def per_tick(tick, _):
+    up_sum[...] = jnp.zeros_like(up_sum)
+    down_sum[...] = jnp.zeros_like(down_sum)
+
+    def first_ticks(tick, _):
         stage(tick, 0, run_attend)
         stage(tick, 1, run_x)
-        stage(tick, 4, run_total)
-        stage(tick, 5, run_norm)
-        stage(tick, 9, run_relay)
-        stage(tick, 10, run_end)
-        at_tick(tick, 5, cot_step_one)
-        at_tick(tick, 6, weights_step_one)
-        at_tick(tick, 6, cot_step_two)
-        at_tick(tick, 7, ready_own)
-        at_tick(tick, 9, cot_step_three)
-        at_tick(tick, 12, ready_other)
-        at_tick(tick, 13, weights_step_two)
-
-        @pl.when(choose(tick, tuple((when, 1) for when, _ in BLOCKS_AT)) == 1)
+        return 0
+
+    lax.fori_loop(0, images + 1, first_ticks, 0)
+    pairs = images // 2
+
+    def both(first, *runs):
+        for run in runs:
+            run(first)
+            run(first + 1)
+
+    cot_step_one()
+    both(0, run_total, run_norm)
+    cot_step_two()
+    weights_step_one()
+    ready_own()
+
+    def per_turn(turn, _):
+        @pl.when((turn <= 1) | (turn == 3))
         def _():
-            run_block(choose(tick, BLOCKS_AT), choose(tick, TURNS))
-
+            both(jnp.where(turn == 3, 6, 2 * turn + 2), run_total, run_norm)
+
+        @pl.when((turn >= 2) & (turn < pairs + 2))
+        def _():
+            both(2 * turn - 4, run_relay)
+
+        @pl.when(turn == pairs)
+        def _():
+            weights_step_two()
+            cot_step_three()
+            ready_other()
+
+        @pl.when(turn >= pairs)
+        def _():
+            both(2 * (turn - pairs), run_end)
+
+        run_block(turn, turn)
         return 0
 
-    up_sum[...] = jnp.zeros_like(up_sum)
-    down_sum[...] = jnp.zeros_like(down_sum)
-    lax.fori_loop(0, images + 11, per_tick, 0)
+    lax.fori_loop(0, 2 * pairs, per_turn, 0)
     grad_up_vm[...] = up_sum[...].astype(bf16)
     grad_down_vm[...] = down_sum[...].astype(bf16)
     grad_copies = [
@@ -833,12 +850,6 @@
         pltpu.make_async_copy(grad_down_vm, grad_down_out, grad_sem.at[1]),
     ]
     for copy in grad_copies:
-        copy.start()
-    outs = [
-        pltpu.make_async_copy(cot_all, cot_out, cot_sem.at[0]),
-        pltpu.make_async_copy(kept_all, kept_out, cot_sem.at[1]),
-    ]
-    for copy in outs:
         copy.start()
     for copy in (swap, kept_y, kept_share, cot_x, cot_y, *cot_share):
         copy.wait_send()
@@ -973,6 +984,7 @@
     grad_h_out,
     up_pair,
     down_pair,
+    line_first,
     up_vm,
     down_vm,
     up_sum,
@@ -994,6 +1006,8 @@
     store,
     pair_s,
     pair_r,
+    line_s,
+    line_r,
     *,
     experts,
     steps,
@@ -1067,6 +1081,10 @@
         for number, (source, target) in enumerate(((up_first, up_pair), (down_first, down_pair)))
     ]
 
+    far_lanes = lanes_at(jnp.where(z_at == 0, 1, 0) * hidden, hidden)
+    line_copy = remote(grad_up_ref.at[:, far_lanes], line_first, line_s.at[0], line_r.at[0], z_dev)
+    is_outer = (z_at == 0) | (z_at == lax.axis_size("expert") // 2 - 1)
+
     @pl.when(turn == 0)
     def _():
         greet([(True, core_dev), (True, x_dev), (True, y_dev), (True, z_dev)])
@@ -1107,7 +1125,6 @@
     def _():
         pass_own(before, (turn - 3) // 2)
 
-    mixed_ref[...] = (mixed_first[...].astype(f32) + dot(hidden_rows, down)).astype(bf16)
 
     @pl.when(turn >= 2)
     def _():
@@ -1117,6 +1134,7 @@
         grad_h_first[...].astype(f32) + dot(grad_pre, up, ((1,), (1,))) + dot(grad_logits, router, ((1,), (1,)))
     ).astype(bf16)
     core_copy(turn).start()
+    mixed_ref[...] = (mixed_first[...].astype(f32) + dot(hidden_rows, down)).astype(bf16)
     h_turned = h_rows.T
     up_sum[...] += dot(h_turned, grad_pre)
     router_sum[...] += dot(h_turned, grad_logits)
@@ -1124,14 +1142,28 @@
 
     @pl.when(turn == steps - 1)
     def _():
+        grad_up_ref[...] = up_sum[...].astype(bf16)
+
+        @pl.when(is_outer)
+        def _():
+            line_copy.start()
+
         pass_own(7, 3)
         pass_total(2)
-        grad_up_ref[...] = up_sum[...].astype(bf16)
         grad_down_ref[...] = down_sum[...].astype(bf16)
         grad_router_ref[...] = router_sum[...].T[:8]
         pass_total(3)
         for copy in pair_copies:
             copy.wait()
+
+        @pl.when(is_outer)
+        def _():
+            line_copy.wait_send()
+
+        @pl.when(jnp.logical_not(is_outer))
+        def _():
+            line_copy.wait_recv()
+
         for number in (6, 7):
             core_copy(number).wait_send()
         for place in range(4):
@@ -1181,6 +1213,7 @@
             shape((rows // 2, features), bf16),
             shape((features, width // 2), bf16),
             shape((features, width // 2), bf16),
+            shape((features, width // 2), bf16),
         ],
         in_specs=[
             by_step(features),
@@ -1192,7 +1225,7 @@
             by_step(128),
         ]
         + [anywhere] * 4,
-        out_specs=[by_step(features), whole(features, width), whole(features, width), whole(8, features)] + [anywhere] * 3,
+        out_specs=[by_step(features), whole(features, width), whole(features, width), whole(8, features)] + [anywhere] * 4,
         scratch_shapes=[
             pltpu.VMEM((features, width), bf16),
             pltpu.VMEM((width, features), bf16),
@@ -1207,7 +1240,8 @@
         ]
         + [dma((8,))] * 2
         + [dma((4,))] * 7
-        + [dma((2,))] * 2,
+        + [dma((2,))] * 2
+        + [dma((1,))] * 2,
         compiler_params=pltpu.CompilerParams(
             collective_id=4, has_side_effects=True, vmem_limit_bytes=60 << 20
         ),
@@ -1237,6 +1271,7 @@
     down_pair,
     up_second,
     down_second,
+    line_first,
     up_out,
     down_out,
     tokens_out,
@@ -1407,7 +1442,7 @@
 
             @pl.when(place(way) == 0)
             def _():
-                for piece in range(4):
+                for piece in range(1, 4):
                     source = (up_second, down_second)[piece % 2]
                     line_copy(source.at[:, far_lanes(way, piece)], way, piece).start()
 
@@ -1416,7 +1451,8 @@
 
             @pl.when(place(way) == 1)
             def _():
-                line_copy_on(way, piece).wait_recv()
+                if piece > 0:
+                    line_copy_on(way, piece).wait_recv()
                 lanes = far_lanes(way, piece)
 
                 def add(part, _):
@@ -1451,6 +1487,13 @@
             )
         )
     ]
+    is_inner = (z_at == 1) | (z_at == z_last - 1)
+    first_copy = pltpu.make_async_copy(line_first, line.at[jnp.where(z_at == 1, 0, 1), 0], own_sem.at[6])
+
+    @pl.when(is_inner)
+    def _():
+        first_copy.start()
+
     for copy in later:
         copy.start()
     weight_sum[...] = jnp.zeros_like(weight_sum)
@@ -1512,6 +1555,14 @@
     m_loads[1].wait()
     for part in range(part_count):
         run_m_y(part)
+    later[0].wait()
+    later[1].wait()
+
+    @pl.when(is_inner)
+    def _():
+        first_copy.wait()
+
+    line_add(0)
     route_one.wait_recv()
     route_core[...] += grad_router_ref[...]
     route_two = remote(route_core, route_x, r_s.at[1], r_r.at[1], x_dev)
@@ -1632,23 +1683,22 @@
         def _():
             run()
 
-    def line_first():
-        later[0].wait()
-        later[1].wait()
-        line_add(0)
-
     def line_second():
         line_add(1)
         line_pass(0)
+
+    def line_third():
+        line_add(2)
+        line_pass(1)
 
     def per_tick(tick, _):
         stage(tick, 0, run_attention)
         stage(tick, 1, run_one_x)
         stage(tick, 4, run_one_total)
         stage(tick, 5, run_tokens)
-        at_tick(tick, 3, line_first)
         at_tick(tick, 5, lambda: run_m_x(0))
-        at_tick(tick, 6, line_second)
+        at_tick(tick, 3, line_second)
+        at_tick(tick, 6, line_third)
         at_tick(tick, 7, lambda: run_m_x(1))
         return 0
 
@@ -1690,8 +1740,7 @@
     run_m_x(part_count - 2)
     run_one_total(images - 4)
     run_tokens(images - 5)
-    line_pass(1)
-    line_add(2)
+    line_add(3)
 
     def quarter_of(step, at, way):
         mirrored = z_last - step + at
@@ -1739,7 +1788,6 @@
             run_one_total(images - 2)
             run_tokens(images - 3)
             run_m_out(1)
-            line_add(3)
 
     own_rows = quarter_at(z_at)
     from_below = jnp.where(z_at > 0, shared_line[0, 1, 2].astype(f32), 0.0)
@@ -1904,8 +1952,12 @@
 
         @pl.when(place(way) <= 1)
         def _():
-            for piece in range(4):
+            for piece in range(1, 4):
                 line_copy_on(way, piece).wait_send()
+
+        @pl.when(place(way) == 1)
+        def _():
+            line_copy_on(way, 0).wait_send()
 
         @pl.when(place(way) == 2)
         def _():
@@ -1938,7 +1990,7 @@
     rows = images * PITCH
     share = out_w.shape[0]
     heads = share // HD
-    hidden = streamed[-1].shape[1] // 2
+    hidden = streamed[-1].shape[1]
     wide = features // 2
     parts = 4
     vmem = pl.BlockSpec(memory_space=pltpu.VMEM)
@@ -1999,7 +2051,7 @@
         + [dma((2, 4))] * 2
         + [dma((2,))] * 2
         + [dma((4,))] * 2
-        + [dma((4,)), dma((9, images)), dma((6,)), dma((7,)), dma((1,))],
+        + [dma((4,)), dma((9, images)), dma((7,)), dma((7,)), dma((1,))],
         compiler_params=pltpu.CompilerParams(
             collective_id=2, has_side_effects=True, vmem_limit_bytes=63 << 20
         ),
@@ -2077,7 +2129,7 @@
         router_wide,
         experts_all,
     )
-    mixed_part, up_second, down_second, grad_router, grad_h_two, up_pair, down_pair = run_second_pair(
+    mixed_part, up_second, down_second, grad_router, grad_h_two, up_pair, down_pair, line_first = run_second_pair(
         h_all,
         cot_all,
         kept_all,
@@ -2114,6 +2166,7 @@
         down_pair,
         up_second,
         down_second,
+        line_first,
     )
     return (
         unpad(mixed.reshape(images, PITCH, quarter_width)),

time: 294 us -> 275 us (0.935)
  Pallas kernels: 268 us -> 248 us
    pallas_call x1, Pallas kernels: 107 us -> 97.4 us  [run_backward(): pl.pallas_call(partial(backward_kernel, images=images, heads=heads), out_...]
    pallas_call x1, Pallas kernels: 99.1 us -> 91.1 us  [run_forward(): pl.pallas_call(partial(forward_kernel, images=images, heads=heads, expert...]
where the time goes in v6:
time: 275 us; the launch traced here: 274 us
  Pallas kernels  248 us (90%)
  local copies, waits for them, and re-layouts  23.3 us (8%)
    pallas_call x1, Pallas kernels, run_backward(): pl.pallas_call(partial(backward_kernel, images=images, heads=heads), out_...  97.4 us
    pallas_call x1, Pallas kernels, run_forward(): pl.pallas_call(partial(forward_kernel, images=images, heads=heads, expert...  91.1 us
    pallas_call x1, Pallas kernels, run_second_pair(): pl.pallas_call(partial(second_pair_kernel, experts=experts, steps=steps),...  59.5 us
    unnamed x16, local copies, waits for them, and re-layouts  10.2 us
    reshape x4, local copies, waits for them, and re-layouts, per_image(): blocks = rows_in.reshape(images, SEQ, rows_in.shape[1])  5.67 us

profile of v6, /device:TPU:0, one launch (start us, length us, event | category | flops | bytes accessed | tf_op | source)
XLA Modules:
  0.0 274.4 jit_solution(16858110170122061151)
XLA Ops:
  0.6 0.7 fusion.1
  1.4 0.1 reshape.51
  1.5 0.1 sub.7
  1.6 0.9 copy.33
  2.5 0.7 pad.19.router_ref
  3.2 0.8 fusion
  4.0 0.8 convert_element_type.9.kept_ref
  4.8 2.4 reshape.49
  7.2 0.8 copy.32
  8.0 1.0 pad.17
  9.1 2.4 reshape.48
  11.5 1.6 pad.16.tok_ref.tok_hbm
  13.1 91.1 %shard_map.212 = (bf16[8,208,192]{2,1,0:T(8,128)(2,1)}, bf16[8,208,192]{2,1,0:T(8,128)(2,1)}, bf16[8,208,192]{2,1,0:T(8,128)(2,1)}, bf16[8,208,192]{2,1,0:T(8,12...) custom-call(bf16[8,208,768]{2,1,0:T(8,128)(2,1)} %pad.16.tok_ref.tok, ...), custom_call_target="tpu_custom_call" | custom-call | tf_op jit(solution)/shard_map/pallas_call | solution.py:904
  104.2 59.5 %shard_map.213 = (bf16[3328,768]{1,0:T(8,128)(2,1)}, bf16[768,768]{1,0:T(8,128)(2,1)}, bf16[768,768]{1,0:T(8,128)(2,1)}, f32[8,768]{1,0:T(8,128)}, bf16[1664,768...) custom-call(bf16[3328,768]{1,0:T(8,128)(2,1)} %get-tuple-element.42.h_ref, ...), custom_call_target="tpu_custom_call" | custom-call | tf_op jit(solution)/shard_map/pallas_call | solution.py:1205
  163.7 97.4 %shard_map.214 = (f32[768,384]{1,0:T(8,128)}, f32[384,768]{1,0:T(8,128)}, f32[1576,768]{1,0:T(8,128)}, f32[3,192,768]{2,1,0:T(8,128)}, f32[192,768]{1,0:T(8,128)...) custom-call(f32[768]{0:T(1024)} %gain1_ref.3, f32[768]{0:T(1024)} %shift1_ref.3, f32[768]{0:T(1024)} %gain2_ref.3, ...), custom_call_target="tpu_custom_call" | custom-call | tf_op jit(solution)/shard_map/pallas_call | solution.py:2001
  261.1 0.0 copy-start.4
  261.1 1.2 slice.24
  262.3 0.4 reshape.54
  262.7 1.1 copy.35
  263.8 0.0 copy-done.4
  263.8 0.6 slice_bitcast_fusion
  264.4 0.6 slice_reduce_fusion
  265.0 0.0 copy-start
  265.0 5.0 %copy.41 = f32[1576,768]{1,0:T(8,128)} copy(f32[1576,768]{1,0:T(8,128)} %get-tuple-element.89) | data formatting | bytes 9682944
  270.1 0.0 copy-done
  270.1 1.2 copy.42
  271.3 0.2 copy-done.3
  271.5 0.8 copy.43
  272.3 0.0 copy-done.2
  272.3 1.0 copy.44
  273.4 0.0 copy-done.1
  273.4 1.0 copy.45
  (4 shorter events, 0.0 us)
Async XLA Ops:
  261.1 2.7 copy-start.4
  265.0 5.0 %copy-start = (f32[3,192,768]{2,1,0:T(8,128)S(1)}, f32[3,192,768]{2,1,0:T(8,128)}, u32[]{:S(2)}) copy-start(f32[3,192,768]{2,1,0:T(8,128)} %get-tuple-element.69) | copy-start | bytes 5308420
  270.1 1.4 copy-start.3
  270.1 2.3 copy-start.2
  271.5 1.8 copy-start.1

commit v7 on v6

--- a/solution.py
+++ b/solution.py
@@ -353,7 +353,7 @@
     block = h_rows.shape[0]
     hidden = up.shape[1] // 2
     lane = lax.broadcasted_iota(jnp.int32, (block, 128), 1)
-    logits = jnp.where(lane < experts, dot(h_rows, router), -1e30)
+    logits = jnp.where(lane < experts, dot(h_rows, router, ((1,), (1,))), -1e30)
     powers = jnp.exp(logits - jnp.max(logits, axis=1, keepdims=True))
     probs = powers / jnp.sum(powers, axis=1, keepdims=True)
     gates = kept * probs
@@ -381,7 +381,7 @@
 
 
 def forward_kernel(
-    tok_ref,
+    tok_raw,
     gain1_ref,
     shift1_ref,
     gain2_ref,
@@ -390,7 +390,7 @@
     out_w_ref,
     up_ref,
     down_ref,
-    cot_ref,
+    cot_turned,
     kept_ref,
     router_ref,
     q_ref,
@@ -409,6 +409,9 @@
     gate_out,
     grad_up_out,
     grad_down_out,
+    tok_out,
+    tok_ref,
+    cot_ref,
     up_vm,
     down_vm,
     up_sum,
@@ -543,6 +546,12 @@
     for copy in own_copies:
         copy.start()
 
+    for number in range(images):
+        first = number * SEQ // 128 * 128
+        skip = number * SEQ - first
+        turned = cot_turned[:, first : first + 384].T.astype(f32)[skip : skip + SEQ]
+        padded = jnp.concatenate([turned, jnp.zeros((PITCH - SEQ, turned.shape[1]), f32)], axis=0)
+        cot_ref[number * PITCH : (number + 1) * PITCH, :] = padded.astype(bf16)
     swap = remote(cot_ref, cot_core, c_s.at[0], c_r.at[0], core_dev)
     swap.start()
     kept_all[pl.ds(0, rows), :] = kept_ref[...]
@@ -658,7 +667,7 @@
         ref = h_block(1, image, other)
         return remote(ref, ref, rel_s.at[image], rel_r.at[image], core_dev)
 
-    attend_outs = ((q_all, q_ref), (k_all, k_ref), (v_all, v_ref), (att_all, att_ref), (lse_all, lse_ref))
+    attend_outs = ((tok_ref, tok_out), (q_all, q_ref), (k_all, k_ref), (v_all, v_ref), (att_all, att_ref), (lse_all, lse_ref))
 
     def out_copies(image):
         copies = [
@@ -667,13 +676,13 @@
         ]
         at = aligned(image * PITCH, PITCH)
         return copies, [
-            pltpu.make_async_copy(resid_all.at[image], resid_ref.at[at, :], out_sem.at[5, image]),
-            pltpu.make_async_copy(h_all.at[at, :], h_out.at[at, :], out_sem.at[6, image]),
+            pltpu.make_async_copy(resid_all.at[image], resid_ref.at[at, :], out_sem.at[6, image]),
+            pltpu.make_async_copy(h_all.at[at, :], h_out.at[at, :], out_sem.at[7, image]),
         ]
 
     def other_copy(image):
         at = aligned(rows + image * PITCH, PITCH)
-        return pltpu.make_async_copy(h_all.at[at, :], h_out.at[at, :], out_sem.at[7, image])
+        return pltpu.make_async_copy(h_all.at[at, :], h_out.at[at, :], out_sem.at[8, image])
 
     def stage(tick, lag, run):
         image = tick - lag
@@ -801,7 +810,18 @@
     up_sum[...] = jnp.zeros_like(up_sum)
     down_sum[...] = jnp.zeros_like(down_sum)
 
+    def take_tokens(number):
+        first = number * SEQ // 16 * 16
+        skip = number * SEQ - first
+        taken = min(224, images * SEQ - first)
+        rows_in = tok_raw[first : first + taken, :].astype(f32)[skip : skip + SEQ]
+        padded = jnp.concatenate([rows_in, jnp.zeros((PITCH - SEQ, rows_in.shape[1]), f32)], axis=0)
+        tok_ref[number] = padded.astype(bf16)
+
     def first_ticks(tick, _):
+        for number in range(images):
+            pl.when(tick == number)(partial(take_tokens, number))
+
         stage(tick, 0, run_attend)
         stage(tick, 1, run_x)
         return 0
@@ -888,10 +908,10 @@
         copy.wait()
 
 
-def run_forward(tok, gain1, shift1, gain2, shift2, qkv_w, out_w, up, down, cot, kept, router, experts):
-    images = tok.shape[0]
+def run_forward(tok_raw, gain1, shift1, gain2, shift2, qkv_w, out_w, up, down, cot, kept, router, experts):
+    images = tok_raw.shape[0] // SEQ
     rows = images * PITCH
-    features = tok.shape[2]
+    features = tok_raw.shape[1]
     share = out_w.shape[0]
     heads = share // HD
     hidden = up.shape[1]
@@ -920,10 +940,13 @@
             shape((2 * rows, 128), f32),
             shape((features, 2 * hidden), bf16),
             shape((features, 2 * hidden), bf16),
+            shape((images, PITCH, features), bf16),
         ],
         in_specs=[vmem] * 7 + [anywhere] * 2 + [vmem] * 3,
-        out_specs=[anywhere] * 16,
+        out_specs=[anywhere] * 17,
         scratch_shapes=[
+            pltpu.VMEM((images, PITCH, features), bf16),
+            pltpu.VMEM((rows, share), bf16),
             pltpu.VMEM((features, 2 * hidden), bf16),
             pltpu.VMEM((2 * hidden, features), bf16),
             *[pltpu.VMEM((features, 2 * hidden), f32)] * 2,
@@ -949,11 +972,11 @@
         + [dma((images,))] * 10
         + [dma((2, 3, 2))] * 2
         + [dma((9,))] * 2
-        + [dma((2,)), dma((2,)), dma((3, 2)), dma((2,)), dma((2,)), dma((8, images))],
+        + [dma((2,)), dma((2,)), dma((3, 2)), dma((2,)), dma((2,)), dma((9, images))],
         compiler_params=pltpu.CompilerParams(
             collective_id=1, has_side_effects=True, vmem_limit_bytes=63 << 20
         ),
-    )(tok, gain1, shift1, gain2, shift2, qkv_w, out_w, up, down, cot, kept, router)
+    )(tok_raw, gain1, shift1, gain2, shift2, qkv_w, out_w, up, down, cot, kept, router)
 
 
 def turn_is_other(turn):
@@ -1056,8 +1079,7 @@
 
     def pass_other(number):
         core_copy(number).wait_recv()
-        total = from_core[number].astype(f32) + ring[number % 2, :, my_cols].astype(f32)
-        from_core[number] = total.astype(bf16)
+        from_core[number] = from_core[number] + ring[number % 2, :, my_cols]
         y_copy(number, (number + 1) // 2).start()
 
     def pass_own(number, place):
@@ -1070,7 +1092,7 @@
     def pass_total(place):
         number = own_turn(place)
         x_copy(number, place).wait_recv()
-        from_x[place] = (from_core[number].astype(f32) + from_x[place].astype(f32)).astype(bf16)
+        from_x[place] = from_core[number] + from_x[place]
         total_copy(place).start()
         store_copy(place).start()
 
@@ -1131,7 +1153,7 @@
         core_copy(turn - 2).wait_send()
 
     ring[turn % 2] = (
-        grad_h_first[...].astype(f32) + dot(grad_pre, up, ((1,), (1,))) + dot(grad_logits, router, ((1,), (1,)))
+        grad_h_first[...].astype(f32) + dot(grad_pre, up, ((1,), (1,))) + dot(grad_logits, router)
     ).astype(bf16)
     core_copy(turn).start()
     mixed_ref[...] = (mixed_first[...].astype(f32) + dot(hidden_rows, down)).astype(bf16)
@@ -1219,7 +1241,7 @@
             by_step(features),
             by_step(features),
             by_step(128),
-            whole(features, 128),
+            whole(128, features),
             by_step(features),
             by_step(features),
             by_step(128),
@@ -1265,18 +1287,12 @@
     resid_ref,
     cot_ref,
     mixed_ref,
-    up_first,
-    down_first,
-    up_pair,
-    down_pair,
     up_second,
     down_second,
     line_first,
-    up_out,
-    down_out,
+    line_out,
     tokens_out,
-    qkv_out,
-    out_w_out,
+    weights_out,
     sums_out,
     mixed_out,
     tok_ref,
@@ -1294,8 +1310,6 @@
     m_x,
     m_out,
     m_resid,
-    own_vm,
-    pair_vm,
     far_vm,
     one_mine,
     one_to,
@@ -1314,9 +1328,8 @@
     late_mine,
     late_y,
     late_z,
-    up_total,
-    down_total,
     sums_all,
+    tokens_low,
     whole,
     mc_s,
     mc_r,
@@ -1473,22 +1486,12 @@
                 line_copy_on(way, piece).start()
 
     line_start()
-    own_lanes = lanes_at(z_at % 2 * hidden, hidden)
     later = [
-        pltpu.make_async_copy(source, target, own_sem.at[number])
-        for number, (source, target) in enumerate(
-            (
-                (up_second, far_vm.at[0]),
-                (down_second, far_vm.at[1]),
-                (up_first.at[:, own_lanes], own_vm.at[0]),
-                (down_first.at[:, own_lanes], own_vm.at[1]),
-                (up_pair, pair_vm.at[0]),
-                (down_pair, pair_vm.at[1]),
-            )
-        )
+        pltpu.make_async_copy((up_second, down_second)[number], far_vm.at[number], own_sem.at[number])
+        for number in range(2)
     ]
     is_inner = (z_at == 1) | (z_at == z_last - 1)
-    first_copy = pltpu.make_async_copy(line_first, line.at[jnp.where(z_at == 1, 0, 1), 0], own_sem.at[6])
+    first_copy = pltpu.make_async_copy(line_first, line.at[jnp.where(z_at == 1, 0, 1), 0], own_sem.at[2])
 
     @pl.when(is_inner)
     def _():
@@ -1577,7 +1580,7 @@
     def one_total_copy(image):
         return remote(one_x.at[image], one_total.at[image], ot_s.at[image], ot_r.at[image], core_dev)
 
-    store_copy = pltpu.make_async_copy(rows_kept.at[pl.ds(0, images * SEQ), :], tokens_out, store.at[0])
+    store_copy = pltpu.make_async_copy(tokens_low, tokens_out, store.at[0])
 
     lane = lax.broadcasted_iota(jnp.int32, (PITCH, 2 * HD), 1)
     key_mask = lax.broadcasted_iota(jnp.int32, (PITCH, PITCH), 1) < SEQ
@@ -1740,7 +1743,6 @@
     run_m_x(part_count - 2)
     run_one_total(images - 4)
     run_tokens(images - 5)
-    line_add(3)
 
     def quarter_of(step, at, way):
         mirrored = z_last - step + at
@@ -1816,9 +1818,11 @@
             run_tokens(images - 2)
         if step == 1:
             run_tokens(images - 1)
+            line_add(3)
             route_two.wait_recv()
             late_mine[8:16, :] = route_core[...] + route_x[...]
             late_y_copy.start()
+            tokens_low[...] = rows_kept[pl.ds(0, images * SEQ), :].astype(bf16)
             store_copy.start()
             run_m_out(part_count - 2)
         if step == 2:
@@ -1847,8 +1851,6 @@
                 gather_z(step, way, piece).wait_recv()
                 gather_y(step + 1, way, piece, y_at).start()
 
-    for copy in later[2:]:
-        copy.wait()
     for way in range(2):
 
         @pl.when(place(way) == 2)
@@ -1864,26 +1866,11 @@
     from_far = 1 - z_at // 2
     first_piece = jnp.where((z_at == 0) | (z_at == z_last), 0, 2)
 
-    def finish(piece, _):
-        at_rows = aligned(piece * 128, 128)
-        totals = [
-            own_vm[n, at_rows, :].astype(f32)
-            + pair_vm[n, at_rows, :].astype(f32)
-            + line[from_far, first_piece + n, at_rows, :].astype(f32)
-            for n in range(2)
-        ]
-        up_total[at_rows, :] = totals[0]
-        down_total[:, lanes_at(piece * 128, 128)] = totals[1].T
-        return 0
-
-    lax.fori_loop(0, features // 128, finish, 0)
-    expert_copies = [
-        pltpu.make_async_copy(up_total, up_out, weight_store.at[5]),
-        pltpu.make_async_copy(down_total, down_out, weight_store.at[6]),
+    line_out_copies = [
+        pltpu.make_async_copy(line.at[from_far, first_piece + n], line_out.at[n], weight_store.at[n]) for n in range(2)
     ]
-    for copy in expert_copies:
+    for copy in line_out_copies:
         copy.start()
-
     gather_y(0, 0, z_at, 1 - y_at).wait_recv()
     for step in range(3):
         for way in range(2):
@@ -1894,29 +1881,17 @@
             def _():
                 gather_y(step + 1, way, piece, 1 - y_at).wait_recv()
 
-    def to_out(piece, _):
-        for side in range(2):
-            weight_sum[aligned(side * part_rows + piece * quarter, quarter), :] = shared_all[
-                side, quarter_at(piece), :
-            ].astype(f32)
-        return 0
-
-    lax.fori_loop(0, z_last + 1, to_out, 0)
     for number in range(planes - 1):
         late_copy(number).wait_recv()
     late = late_z[0]
     for plane in range(1, planes):
         late += late_z[plane]
     sums_all[...] = late
-    weight_copies = [
-        *[
-            pltpu.make_async_copy(weight_sum.at[pl.ds(n * share, share), :], qkv_out.at[n], weight_store.at[n])
-            for n in range(3)
-        ],
-        pltpu.make_async_copy(weight_sum.at[pl.ds(3 * share, share), :], out_w_out, weight_store.at[3]),
-        pltpu.make_async_copy(sums_all, sums_out, weight_store.at[4]),
+    out_copies = [
+        pltpu.make_async_copy(shared_all, weights_out, weight_store.at[2]),
+        pltpu.make_async_copy(sums_all, sums_out, weight_store.at[3]),
     ]
-    for copy in weight_copies:
+    for copy in out_copies:
         copy.start()
     route_one.wait_send()
     route_two.wait_send()
@@ -1942,7 +1917,7 @@
             m_x_copy(part).wait_send()
             m_quarter_copy(part).wait_recv()
 
-    for copy in (*weight_copies, *expert_copies, store_copy):
+    for copy in (*line_out_copies, *out_copies, store_copy):
         copy.wait()
     late_y_copy.wait_send()
     for number in range(planes - 1):
@@ -2001,16 +1976,14 @@
     return pl.pallas_call(
         partial(backward_kernel, images=images, heads=heads),
         out_shape=[
-            shape((features, hidden), f32),
-            shape((hidden, features), f32),
-            shape((images * SEQ, features), f32),
-            shape((3, share, features), f32),
-            shape((share, features), f32),
+            shape((2, features, hidden), bf16),
+            shape((images * SEQ, features), bf16),
+            shape((2, features // 2, features), bf16),
             shape((16, features), f32),
             shape((rows, wide // 2), bf16),
         ],
         in_specs=[vmem] * 6 + [anywhere] * (1 + len(streamed)),
-        out_specs=[anywhere] * 7,
+        out_specs=[anywhere] * 5,
         scratch_shapes=[
             pltpu.VMEM((images, PITCH, features), bf16),
             *[pltpu.VMEM((images, PITCH, share), bf16)] * 4,
@@ -2023,8 +1996,6 @@
             *[pltpu.VMEM((parts, rows // parts, wide), bf16)] * 2,
             pltpu.VMEM((parts, 2, rows // parts, wide // 2), bf16),
             pltpu.VMEM((rows // parts, wide), f32),
-            pltpu.VMEM((2, features, hidden), bf16),
-            pltpu.VMEM((2, features, hidden), bf16),
             pltpu.VMEM((2, features, 2 * hidden), bf16),
             *[pltpu.VMEM(block, bf16)] * 5,
             pltpu.VMEM((2, 4, features, hidden), bf16),
@@ -2037,9 +2008,8 @@
             *[pltpu.VMEM((8, features), f32)] * 2,
             *[pltpu.VMEM((16, features), f32)] * 2,
             pltpu.VMEM((4, 16, features), f32),
-            pltpu.VMEM((features, hidden), f32),
-            pltpu.VMEM((hidden, features), f32),
             pltpu.VMEM((16, features), f32),
+            pltpu.VMEM((images * SEQ, features), bf16),
             pltpu.VMEM((PITCH, features), f32),
         ]
         + [dma((2, parts))] * 2
@@ -2051,7 +2021,7 @@
         + [dma((2, 4))] * 2
         + [dma((2,))] * 2
         + [dma((4,))] * 2
-        + [dma((4,)), dma((9, images)), dma((7,)), dma((7,)), dma((1,))],
+        + [dma((4,)), dma((9, images)), dma((3,)), dma((4,)), dma((1,))],
         compiler_params=pltpu.CompilerParams(
             collective_id=2, has_side_effects=True, vmem_limit_bytes=63 << 20
         ),
@@ -2094,8 +2064,8 @@
     kept_routes = per_image(jnp.where(keep_mask > 0, routes, -1) + 1).reshape(rows, 2) - 1
     chosen = kept_routes[:, :, None] == jnp.arange(128, dtype=jnp.int32)[None, None, :]
     kept = jnp.any(chosen, axis=1).astype(bf16)
-    router_wide = jnp.pad(router_weight, ((0, 0), (0, 128 - experts_all)))
-    tok = per_image(tokens)
+    router_wide = jnp.pad(router_weight.T, ((0, 128 - experts_all), (0, 0)))
+    cot_turned = jnp.pad(cotangent.T, ((0, 0), (0, -row_count % 128)))
     qkv_turned = jnp.swapaxes(qkv_weight, 1, 2)
     (
         queries,
@@ -2114,8 +2084,9 @@
         gate_first,
         up_first,
         down_first,
+        tok,
     ) = run_forward(
-        tok,
+        tokens,
         gain_attn,
         shift_attn,
         gain_moe,
@@ -2124,7 +2095,7 @@
         out_weight,
         expert_up[0],
         expert_down[0],
-        per_image(cotangent).reshape(rows, quarter_width),
+        cot_turned,
         kept,
         router_wide,
         experts_all,
@@ -2143,7 +2114,7 @@
         down_first,
         experts_all,
     )
-    grad_up, grad_down, tokens_grad, grad_qkv, grad_out, sums, mixed = run_backward(
+    line_sum, tokens_grad, weights_grad, sums, mixed = run_backward(
         gain_attn,
         shift_attn,
         gain_moe,
@@ -2160,26 +2131,31 @@
         resid,
         cot_all,
         mixed_part,
-        up_first,
-        down_first,
-        up_pair,
-        down_pair,
         up_second,
         down_second,
         line_first,
     )
+    own_lane = lax.axis_index("expert") // 2 % 2 * hidden
+
+    def expert_total(first, pair, line):
+        own = lax.dynamic_slice_in_dim(first, own_lane, hidden, 1)
+        return own.astype(f32) + pair.astype(f32) + line.astype(f32)
+
+    weights_grad = weights_grad.reshape(feature_count, feature_count)
+    share = qkv_weight.shape[2]
+    grad_qkv = weights_grad[: 3 * share].reshape(3, share, feature_count)
     return (
         unpad(mixed.reshape(images, PITCH, quarter_width)),
-        tokens_grad,
+        tokens_grad.astype(f32),
         sums[0],
         sums[1],
-        jnp.swapaxes(grad_qkv, 1, 2),
-        grad_out,
+        jnp.swapaxes(grad_qkv, 1, 2).astype(f32),
+        weights_grad[3 * share :].astype(f32),
         sums[2],
         sums[3],
         sums[8 : 8 + experts_all].T,
-        grad_up[None],
-        grad_down[None],
+        expert_total(up_first, up_pair, line_sum[0])[None],
+        expert_total(down_first, down_pair, line_sum[1]).T[None],
     )
 
 

time: 275 us -> 261 us (0.949)
  local copies, waits for them, and re-layouts: 23.3 us -> 6.75 us
  other arithmetic: 2.37 us -> 12.1 us
  Pallas kernels: 248 us -> 241 us
    unnamed x16 -> x11, local copies, waits for them, and re-layouts: 10.2 us -> 1.41 us
    pallas_call x1, Pallas kernels: 97.4 us -> 90 us  [run_backward(): pl.pallas_call(partial(backward_kernel, images=images, heads=heads), out_...]
    convert_element_type x0 -> x3, other arithmetic: none -> 6.58 us  [the longest x1 4.37 us: per_device_dense(): tokens_grad.astype(f32)]
    reshape x4 -> x1, local copies, waits for them, and re-layouts: 5.67 us -> 0.09 us  [per_image(): blocks = rows_in.reshape(images, SEQ, rows_in.shape[1])]
    broadcast_in_dim x0 -> x1, other arithmetic: none -> 3.18 us  [per_device_dense(): expert_total(down_first, down_pair, line_sum[1]).T[None]]
where the time goes in v7:
time: 261 us; the launch traced here: 260 us
  Pallas kernels  241 us (92%)
  other arithmetic  12.1 us (5%)
  local copies, waits for them, and re-layouts  6.75 us (3%)
    pallas_call x1, Pallas kernels, run_forward(): pl.pallas_call(partial(forward_kernel, images=images, heads=heads, expert...  91.4 us
    pallas_call x1, Pallas kernels, run_backward(): pl.pallas_call(partial(backward_kernel, images=images, heads=heads), out_...  90 us
    pallas_call x1, Pallas kernels, run_second_pair(): pl.pallas_call(partial(second_pair_kernel, experts=experts, steps=steps),...  59.2 us

profile of v7, /device:TPU:0, one launch (start us, length us, event | category | flops | bytes accessed | tf_op | source)
XLA Modules:
  0.0 260.2 jit_solution(12360032223168440828)
XLA Ops:
  0.6 0.0 copy-start.2
  0.7 1.4 pad.14.router_ref
  2.1 0.7 fusion.3
  2.8 0.1 reshape.49
  2.9 0.1 sub.11
  3.0 0.8 fusion
  3.8 0.8 convert_element_type.46.kept_ref
  4.7 0.0 copy-done.2
  4.7 0.9 pad.12.cot_turned
  5.6 91.4 %shard_map.212 = (bf16[8,208,192]{2,1,0:T(8,128)(2,1)}, bf16[8,208,192]{2,1,0:T(8,128)(2,1)}, bf16[8,208,192]{2,1,0:T(8,128)(2,1)}, bf16[8,208,192]{2,1,0:T(8,12...) custom-call(bf16[1576,768]{1,0:T(8,128)(2,1)} %tok_raw.1, ...), custom_call_target="tpu_custom_call" | custom-call | tf_op jit(solution)/shard_map/pallas_call | solution.py:924
  96.9 59.2 %shard_map.213 = (bf16[3328,768]{1,0:T(8,128)(2,1)}, bf16[768,768]{1,0:T(8,128)(2,1)}, bf16[768,768]{1,0:T(8,128)(2,1)}, f32[8,768]{1,0:T(8,128)}, bf16[1664,768...) custom-call(bf16[3328,768]{1,0:T(8,128)(2,1)} %get-tuple-element.41.h_ref, ...), custom_call_target="tpu_custom_call" | custom-call | tf_op jit(solution)/shard_map/pallas_call | solution.py:1227
  156.1 0.0 copy-start.3
  156.1 90.0 %shard_map.214 = (bf16[2,768,384]{2,1,0:T(8,128)(2,1)}, bf16[1576,768]{1,0:T(8,128)(2,1)}, bf16[2,384,768]{2,1,0:T(8,128)(2,1)}, f32[16,768]{1,0:T(8,128)}, bf16[1664,192]{1,0:T(8,128)(2,1)}) custom-call(f32[768]{0:T(1024)} %gain1_ref.3, f32[768]{0:T(1024)} %shift1_ref.3, f32[768]{0:T(1024)} %gain2_ref.3, bf16[3,192,768]{2,1,0:T(8,128)(2,1)} %bitcast.31, ...), custom_call_target="tpu_custom_call" | custom-call | tf_op jit(solution)/shard_map/pallas_call | solution.py:1976
  246.2 0.0 copy-done.3
  246.2 3.2 %fusion.1 = (f32[1,384,768]{1,2,0:T(8,128)S(1)}, f32[1,768,384]{2,1,0:T(8,128)}) fusion(bf16[768,384]{1,0:T(8,128)(2,1)} %get-tuple-element.70, bf16[2,768,384]{2,1,0:T(8,128)(2,1)} %get-tuple-element.69, bf16[768,768]{1,0:T(8,128)(2,1)} %get-tuple-element.50.down_first, s32[]{:T(128)S(6)} %select_n.22, bf16[768,384]{1,0:T(8,128)(2,1)S(1)} %copy-done.3, ...), kind=kLoop, calls=%fused_computation.4 | loop fusion | flops 2949120 | bytes 5898244 | tf_op jit(solution)/shard_map/broadcast_in_dim | solution.py:2158
  249.3 1.4 copy.28
  250.7 0.0 copy-start
  250.7 4.4 %convert_element_type.47 = f32[1576,768]{1,0:T(8,128)} convert(bf16[1576,768]{1,0:T(8,128)(2,1)} %get-tuple-element.65) | non-fusion elementwise | flops 1210368 | bytes 7262208 | tf_op jit(solution)/shard_map/convert_element_type | solution.py:2149
  255.1 0.0 copy-done
  255.1 0.1 slice.41
  255.2 0.0 copy-start.1
  255.2 1.4 convert_bitcast_fusion
  256.5 0.0 copy-done.1
  256.5 0.1 slice.40
  256.6 0.4 reshape.56
  257.0 0.0 copy-start.4
  257.0 1.1 copy.29
  258.1 0.9 slice_convert_fusion
  258.9 0.0 copy-done.4
  259.0 0.6 slice_reduce_fusion
  259.6 0.6 slice_bitcast_fusion
  (1 shorter events, 0.0 us)
Async XLA Ops:
  0.6 4.0 %copy-start.2 = (bf16[1576,192]{0,1:T(8,128)(2,1)S(1)}, bf16[1576,192]{0,1:T(8,128)(2,1)}, u32[]{:S(2)}) copy-start(bf16[1576,192]{0,1:T(8,128)(2,1)} %param.25) | copy-start | bytes 1815556
  156.1 90.0 %copy-start.3 = (bf16[768,384]{1,0:T(8,128)(2,1)S(1)}, bf16[768,384]{1,0:T(8,128)(2,1)}, u32[]{:S(2)}) copy-start(bf16[768,384]{1,0:T(8,128)(2,1)} %get-tuple-element.68) | copy-start | bytes 1769476
  250.7 4.4 %copy-start = (bf16[2,384,768]{2,1,0:T(8,128)(2,1)S(1)}, bf16[2,384,768]{2,1,0:T(8,128)(2,1)}, u32[]{:S(2)}) copy-start(bf16[2,384,768]{2,1,0:T(8,128)(2,1)} %get-tuple-element.67) | copy-start | bytes 3538948
  255.2 1.4 copy-start.1
  257.0 2.0 copy-start.4

commit v8 on v7

--- a/solution.py
+++ b/solution.py
@@ -381,18 +381,18 @@
 
 
 def forward_kernel(
-    tok_raw,
     gain1_ref,
     shift1_ref,
     gain2_ref,
     shift2_ref,
-    qkv_ref,
-    out_w_ref,
     up_ref,
     down_ref,
-    cot_turned,
-    kept_ref,
     router_ref,
+    cot_hbm,
+    kept_hbm,
+    tok_hbm,
+    qkv_hbm,
+    out_w_hbm,
     q_ref,
     k_ref,
     v_ref,
@@ -410,6 +410,11 @@
     grad_up_out,
     grad_down_out,
     tok_out,
+    cot_turned,
+    kept_ref,
+    tok_raw,
+    qkv_ref,
+    out_w_ref,
     tok_ref,
     cot_ref,
     up_vm,
@@ -453,6 +458,7 @@
     w_r,
     c_s,
     c_r,
+    load_sem,
     own_sem,
     pair_sem,
     block_sem,
@@ -473,6 +479,20 @@
     rows = images * PITCH
     half = rows // 2
     wide = out_w_ref.shape[1] // 2
+    loads = [
+        pltpu.make_async_copy(source, target, load_sem.at[number])
+        for number, (source, target) in enumerate(
+            (
+                (cot_hbm, cot_turned),
+                (kept_hbm, kept_ref),
+                (tok_hbm, tok_raw),
+                (qkv_hbm, qkv_ref),
+                (out_w_hbm, out_w_ref),
+            )
+        )
+    ]
+    for copy in loads:
+        copy.start()
     hidden = up_ref.shape[1]
     core_dev = (expert_at, tensor_at + 1 - 2 * core_at)
     x_dev = (expert_at, tensor_at + 2 - 4 * x_at)
@@ -546,6 +566,7 @@
     for copy in own_copies:
         copy.start()
 
+    loads[0].wait()
     for number in range(images):
         first = number * SEQ // 128 * 128
         skip = number * SEQ - first
@@ -554,6 +575,7 @@
         cot_ref[number * PITCH : (number + 1) * PITCH, :] = padded.astype(bf16)
     swap = remote(cot_ref, cot_core, c_s.at[0], c_r.at[0], core_dev)
     swap.start()
+    loads[1].wait()
     kept_all[pl.ds(0, rows), :] = kept_ref[...]
 
     def kept_half(side, core):
@@ -826,6 +848,8 @@
         stage(tick, 1, run_x)
         return 0
 
+    for copy in loads[2:]:
+        copy.wait()
     lax.fori_loop(0, images + 1, first_ticks, 0)
     pairs = images // 2
 
@@ -942,9 +966,14 @@
             shape((features, 2 * hidden), bf16),
             shape((images, PITCH, features), bf16),
         ],
-        in_specs=[vmem] * 7 + [anywhere] * 2 + [vmem] * 3,
+        in_specs=[vmem] * 4 + [anywhere] * 2 + [vmem] + [anywhere] * 5,
         out_specs=[anywhere] * 17,
         scratch_shapes=[
+            pltpu.VMEM(cot.shape, bf16),
+            pltpu.VMEM(kept.shape, bf16),
+            pltpu.VMEM(tok_raw.shape, bf16),
+            pltpu.VMEM(qkv_w.shape, bf16),
+            pltpu.VMEM(out_w.shape, bf16),
             pltpu.VMEM((images, PITCH, features), bf16),
             pltpu.VMEM((rows, share), bf16),
             pltpu.VMEM((features, 2 * hidden), bf16),
@@ -972,11 +1001,11 @@
         + [dma((images,))] * 10
         + [dma((2, 3, 2))] * 2
         + [dma((9,))] * 2
-        + [dma((2,)), dma((2,)), dma((3, 2)), dma((2,)), dma((2,)), dma((9, images))],
+        + [dma((5,)), dma((2,)), dma((2,)), dma((3, 2)), dma((2,)), dma((2,)), dma((9, images))],
         compiler_params=pltpu.CompilerParams(
             collective_id=1, has_side_effects=True, vmem_limit_bytes=63 << 20
         ),
-    )(tok_raw, gain1, shift1, gain2, shift2, qkv_w, out_w, up, down, cot, kept, router)
+    )(gain1, shift1, gain2, shift2, up, down, router, cot, kept, tok_raw, qkv_w, out_w)
 
 
 def turn_is_other(turn):
@@ -1274,9 +1303,9 @@
     gain1_ref,
     shift1_ref,
     gain2_ref,
-    qkv_ref,
-    out_w_ref,
     grad_router_ref,
+    qkv_hbm,
+    out_w_hbm,
     tok_hbm,
     q_hbm,
     k_hbm,
@@ -1295,6 +1324,8 @@
     weights_out,
     sums_out,
     mixed_out,
+    qkv_ref,
+    out_w_ref,
     tok_ref,
     q_ref,
     k_ref,
@@ -1398,6 +1429,69 @@
     def at_image(image):
         return aligned(image * PITCH, PITCH)
 
+    def place(way):
+        return z_at if way == 0 else z_last - z_at
+
+    def far_lanes(way, piece):
+        expert = z_last - piece // 2 if way == 0 else piece // 2
+        return pl.ds(expert % 2 * hidden, hidden)
+
+    def line_copy(source, way, piece):
+        return remote(source, line.at[way, piece], l_s.at[way, piece], l_r.at[way, piece], z_devs[way])
+
+    def line_copy_on(way, piece):
+        return line_copy(line.at[way, piece], way, piece)
+
+    def line_start():
+        for way in range(2):
+
+            @pl.when(place(way) == 0)
+            def _():
+                for piece in range(1, 4):
+                    source = (up_second, down_second)[piece % 2]
+                    line_copy(source.at[:, far_lanes(way, piece)], way, piece).start()
+
+    def line_add(piece):
+        for way in range(2):
+
+            @pl.when(place(way) == 1)
+            def _():
+                if piece > 0:
+                    line_copy_on(way, piece).wait_recv()
+                lanes = far_lanes(way, piece)
+
+                def add(part, _):
+                    at_rows = aligned(part * 96, 96)
+                    total = line[way, piece, at_rows, :].astype(f32) + far_vm[piece % 2, at_rows, lanes].astype(f32)
+                    line[way, piece, at_rows, :] = total.astype(bf16)
+                    return 0
+
+                lax.fori_loop(0, features // 96, add, 0)
+                line_copy_on(way, piece).start()
+
+    def line_pass(piece):
+        for way in range(2):
+
+            @pl.when(place(way) == 2)
+            def _():
+                line_copy_on(way, piece).wait_recv()
+                line_copy_on(way, piece).start()
+
+    line_start()
+    later = [
+        pltpu.make_async_copy((up_second, down_second)[number], far_vm.at[number], own_sem.at[number])
+        for number in range(2)
+    ]
+    is_inner = (z_at == 1) | (z_at == z_last - 1)
+    first_copy = pltpu.make_async_copy(line_first, line.at[jnp.where(z_at == 1, 0, 1), 0], own_sem.at[2])
+
+    @pl.when(is_inner)
+    def _():
+        first_copy.start()
+
+    for copy in later:
+        copy.start()
+
     part_count = m_y.shape[0]
     part_rows_m = rows // part_count
 
@@ -1430,6 +1524,12 @@
             copy.start()
         return 0
 
+    weight_loads = [
+        pltpu.make_async_copy(qkv_hbm, qkv_ref, own_sem.at[3]),
+        pltpu.make_async_copy(out_w_hbm, out_w_ref, own_sem.at[4]),
+    ]
+    for copy in weight_loads:
+        copy.start()
     start_loads(0, 0)
     m_loads[1].start()
     lax.fori_loop(1, images, start_loads, 0)
@@ -1437,68 +1537,6 @@
     route_one = remote(grad_router_ref, route_core, r_s.at[0], r_r.at[0], core_dev)
     route_one.start()
 
-    def place(way):
-        return z_at if way == 0 else z_last - z_at
-
-    def far_lanes(way, piece):
-        expert = z_last - piece // 2 if way == 0 else piece // 2
-        return pl.ds(expert % 2 * hidden, hidden)
-
-    def line_copy(source, way, piece):
-        return remote(source, line.at[way, piece], l_s.at[way, piece], l_r.at[way, piece], z_devs[way])
-
-    def line_copy_on(way, piece):
-        return line_copy(line.at[way, piece], way, piece)
-
-    def line_start():
-        for way in range(2):
-
-            @pl.when(place(way) == 0)
-            def _():
-                for piece in range(1, 4):
-                    source = (up_second, down_second)[piece % 2]
-                    line_copy(source.at[:, far_lanes(way, piece)], way, piece).start()
-
-    def line_add(piece):
-        for way in range(2):
-
-            @pl.when(place(way) == 1)
-            def _():
-                if piece > 0:
-                    line_copy_on(way, piece).wait_recv()
-                lanes = far_lanes(way, piece)
-
-                def add(part, _):
-                    at_rows = aligned(part * 96, 96)
-                    total = line[way, piece, at_rows, :].astype(f32) + far_vm[piece % 2, at_rows, lanes].astype(f32)
-                    line[way, piece, at_rows, :] = total.astype(bf16)
-                    return 0
-
-                lax.fori_loop(0, features // 96, add, 0)
-                line_copy_on(way, piece).start()
-
-    def line_pass(piece):
-        for way in range(2):
-
-            @pl.when(place(way) == 2)
-            def _():
-                line_copy_on(way, piece).wait_recv()
-                line_copy_on(way, piece).start()
-
-    line_start()
-    later = [
-        pltpu.make_async_copy((up_second, down_second)[number], far_vm.at[number], own_sem.at[number])
-        for number in range(2)
-    ]
-    is_inner = (z_at == 1) | (z_at == z_last - 1)
-    first_copy = pltpu.make_async_copy(line_first, line.at[jnp.where(z_at == 1, 0, 1), 0], own_sem.at[2])
-
-    @pl.when(is_inner)
-    def _():
-        first_copy.start()
-
-    for copy in later:
-        copy.start()
     weight_sum[...] = jnp.zeros_like(weight_sum)
     late_mine[...] = jnp.zeros_like(late_mine)
 
@@ -1555,17 +1593,17 @@
             m_quarter_copy(part).start()
             m_store_copy(part).start()
 
+    later[0].wait()
+    later[1].wait()
+
+    @pl.when(is_inner)
+    def _():
+        first_copy.wait()
+
+    line_add(0)
     m_loads[1].wait()
     for part in range(part_count):
         run_m_y(part)
-    later[0].wait()
-    later[1].wait()
-
-    @pl.when(is_inner)
-    def _():
-        first_copy.wait()
-
-    line_add(0)
     route_one.wait_recv()
     route_core[...] += grad_router_ref[...]
     route_two = remote(route_core, route_x, r_s.at[1], r_r.at[1], x_dev)
@@ -1705,118 +1743,143 @@
         at_tick(tick, 7, lambda: run_m_x(1))
         return 0
 
+    for copy in weight_loads:
+        copy.wait()
     lax.fori_loop(0, images, per_tick, 0)
 
     part_rows = shared.shape[1]
-    quarter = part_rows // (z_last + 1)
-
-    def to_half(side):
-        def cast(piece, _):
-            at_rows = aligned(piece * quarter, quarter)
-            shared[side, at_rows, :] = weight_sum[aligned(side * part_rows + piece * quarter, quarter), :].astype(bf16)
-            return 0
-
-        lax.fori_loop(0, z_last + 1, cast, 0)
-
-    to_half(0)
-    to_half(1)
+    chunks = 2
+    chunk_rows = part_rows // chunks
+    quarter = chunk_rows // planes
+
+    def cast(piece, _):
+        for side in range(2):
+            at_rows = aligned(piece * 96, 96)
+            shared[side, at_rows, :] = weight_sum[aligned(side * part_rows + piece * 96, 96), :].astype(bf16)
+        return 0
+
+    lax.fori_loop(0, part_rows // 96, cast, 0)
 
     def y_piece(number):
         inner = jnp.where(z_at == 1, jnp.where(number < 2, z_last - number, number - 2), jnp.where(number < 2, number, 5 - number))
         return jnp.where(z_at == 0, z_last - number, jnp.where(z_at == z_last, number, inner))
 
-    def quarter_at(piece):
-        return aligned(piece * quarter, quarter)
-
-    def shared_y_copy(number):
-        at_rows = quarter_at(y_piece(number))
-        return remote(shared.at[1 - y_at, at_rows, :], shared_y.at[at_rows, :], sy_s.at[number], sy_r.at[number], y_dev)
-
-    def take_y(number):
-        shared_y_copy(number).wait_recv()
-        at_rows = quarter_at(y_piece(number))
+    def quarter_at(chunk, piece):
+        return aligned(chunk * chunk_rows + piece * quarter, quarter)
+
+    def shared_y_copy(chunk, number):
+        at_rows = quarter_at(chunk, y_piece(number))
+        return remote(
+            shared.at[1 - y_at, at_rows, :], shared_y.at[at_rows, :], sy_s.at[chunk, number], sy_r.at[chunk, number], y_dev
+        )
+
+    def take_y(chunk, number):
+        shared_y_copy(chunk, number).wait_recv()
+        at_rows = quarter_at(chunk, y_piece(number))
         weight_half[at_rows, :] = shared[y_at, at_rows, :].astype(f32) + shared_y[at_rows, :].astype(f32)
-
-    for number in range(4):
-        shared_y_copy(number).start()
-    run_one_x(images - 1)
-    run_m_x(part_count - 2)
-    run_one_total(images - 4)
-    run_tokens(images - 5)
 
     def quarter_of(step, at, way):
         mirrored = z_last - step + at
         return mirrored if way == 0 else z_last - mirrored
 
+    def small_copy(chunk, step, way):
+        return remote(
+            shared_line.at[chunk, way, 0, step],
+            shared_line.at[chunk, way, 1, step],
+            sl_s.at[chunk, way, step],
+            sl_r.at[chunk, way, step],
+            z_devs[way],
+        )
+
+    def sum_wait(chunk, step):
+        for way in range(2):
+            at = place(way)
+
+            @pl.when((at > 0) & (at - 1 <= step))
+            def _():
+                small_copy(chunk, step, way).wait_recv()
+
+    def sum_send(chunk, step):
+        for way in range(2):
+            at = place(way)
+
+            @pl.when((at <= step) & (at < z_last))
+            def _():
+                at_rows = quarter_at(chunk, quarter_of(step, at, way))
+                if step == 0:
+                    shared_line[chunk, way, 0, step] = weight_half[at_rows, :].astype(bf16)
+                else:
+                    came = jnp.where(at > 0, shared_line[chunk, way, 1, step - 1].astype(f32), 0.0)
+                    shared_line[chunk, way, 0, step] = (weight_half[at_rows, :] + came).astype(bf16)
+                small_copy(chunk, step, way).start()
+
+    def final_rows(chunk, side, piece):
+        return shared_all.at[side, quarter_at(chunk, piece), :]
+
+    def gather_z(chunk, step, way, piece):
+        ref = final_rows(chunk, y_at, piece)
+        return remote(ref, ref, sg_s.at[chunk, way, step], sg_r.at[chunk, way, step], z_devs[way])
+
+    def gather_y(chunk, step, way, piece, side):
+        ref = final_rows(chunk, side, piece)
+        return remote(ref, ref, sz_s.at[chunk, way, step], sz_r.at[chunk, way, step], y_dev)
+
+    def piece_out(step, way):
+        return z_at - step if way == 0 else z_at + step
+
+    def piece_in(step, way):
+        return z_at - 1 - step if way == 0 else z_at + 1 + step
+
+    def gather_send(chunk, step):
+        for way in range(2):
+            at = place(way)
+
+            @pl.when((at >= step) & (at < z_last))
+            def _():
+                gather_z(chunk, step, way, piece_out(step, way)).start()
+
+    def gather_take(chunk, step):
+        for way in range(2):
+
+            @pl.when(place(way) >= 1 + step)
+            def _():
+                gather_z(chunk, step, way, piece_in(step, way)).wait_recv()
+                gather_y(chunk, step + 1, way, piece_in(step, way), y_at).start()
+
+    def finish_sum(chunk):
+        own_rows = quarter_at(chunk, z_at)
+        from_below = jnp.where(z_at > 0, shared_line[chunk, 0, 1, 2].astype(f32), 0.0)
+        from_above = jnp.where(z_at < z_last, shared_line[chunk, 1, 1, 2].astype(f32), 0.0)
+        shared_all[y_at, own_rows, :] = (weight_half[own_rows, :] + from_below + from_above).astype(bf16)
+        gather_y(chunk, 0, 0, z_at, y_at).start()
+
     late_y_copy = remote(late_mine, late_y, late_s.at[0], late_r.at[0], y_dev)
 
     def late_copy(number):
         ref = late_z.at[z_at]
         return remote(ref, ref, late_s.at[number + 1], late_r.at[number + 1], z_others[number])
 
-    def small_copy(step, way):
-        return remote(shared_line.at[way, 0, step], shared_line.at[way, 1, step], sl_s.at[way, step], sl_r.at[way, step], z_devs[way])
-
-    for step in range(3):
-        take_y(step)
-        if step == 2:
-            take_y(3)
-        for way in range(2):
-            at = place(way)
-
-            @pl.when((at <= step) & (at < z_last))
-            def _():
-                at_rows = quarter_at(quarter_of(step, at, way))
-                if step == 0:
-                    shared_line[way, 0, step] = weight_half[at_rows, :].astype(bf16)
-                else:
-                    came = jnp.where(at > 0, shared_line[way, 1, step - 1].astype(f32), 0.0)
-                    shared_line[way, 0, step] = (weight_half[at_rows, :] + came).astype(bf16)
-                small_copy(step, way).start()
-
-        for way in range(2):
-            at = place(way)
-
-            @pl.when((at > 0) & (at - 1 <= step))
-            def _():
-                small_copy(step, way).wait_recv()
-
-        if step == 0:
+    def meanwhile(place_in_order):
+        if place_in_order == 0:
+            run_one_x(images - 1)
+            run_tokens(images - 5)
+            run_one_total(images - 4)
+            run_m_x(part_count - 2)
+        if place_in_order == 1:
             run_m_x(part_count - 1)
+            run_tokens(images - 4)
             run_one_total(images - 3)
-            run_tokens(images - 4)
+        if place_in_order == 2:
             run_m_out(0)
-        if step == 1:
+            run_tokens(images - 3)
+        if place_in_order == 3:
             run_one_total(images - 2)
-            run_tokens(images - 3)
             run_m_out(1)
-
-    own_rows = quarter_at(z_at)
-    from_below = jnp.where(z_at > 0, shared_line[0, 1, 2].astype(f32), 0.0)
-    from_above = jnp.where(z_at < z_last, shared_line[1, 1, 2].astype(f32), 0.0)
-
-    def final_rows(side, piece):
-        return shared_all.at[side, quarter_at(piece), :]
-
-    shared_all[y_at, own_rows, :] = (weight_half[own_rows, :] + from_below + from_above).astype(bf16)
-    for number in range(4):
-        shared_y_copy(number).wait_send()
-
-    def gather_z(step, way, piece):
-        ref = final_rows(y_at, piece)
-        return remote(ref, ref, sg_s.at[way, step], sg_r.at[way, step], z_devs[way])
-
-    def gather_y(step, way, piece, side):
-        ref = final_rows(side, piece)
-        return remote(ref, ref, sz_s.at[way, step], sz_r.at[way, step], y_dev)
-
-    gather_y(0, 0, z_at, y_at).start()
-
-    def between(step):
-        if step == 0:
+            run_tokens(images - 2)
+        if place_in_order == 4:
             run_one_total(images - 1)
-            run_tokens(images - 2)
-        if step == 1:
+            run_m_out(2)
+        if place_in_order == 5:
             run_tokens(images - 1)
             line_add(3)
             route_two.wait_recv()
@@ -1824,32 +1887,37 @@
             late_y_copy.start()
             tokens_low[...] = rows_kept[pl.ds(0, images * SEQ), :].astype(bf16)
             store_copy.start()
-            run_m_out(part_count - 2)
-        if step == 2:
-            run_m_out(part_count - 1)
+        if place_in_order == 6:
+            run_m_out(3)
             late_y_copy.wait_recv()
             late_z[z_at] = late_mine[...] + late_y[...]
             for number in range(planes - 1):
                 late_copy(number).start()
 
+    for number in range(4):
+        for chunk in range(chunks):
+            shared_y_copy(chunk, number).start()
+    meanwhile(0)
     for step in range(3):
-        for way in range(2):
-            at = place(way)
-            piece = z_at - step if way == 0 else z_at + step
-
-            @pl.when((at >= step) & (at < z_last))
-            def _():
-                gather_z(step, way, piece).start()
-
-        between(step)
-        for way in range(2):
-            at = place(way)
-            piece = z_at - 1 - step if way == 0 else z_at + 1 + step
-
-            @pl.when(at >= 1 + step)
-            def _():
-                gather_z(step, way, piece).wait_recv()
-                gather_y(step + 1, way, piece, y_at).start()
+        for chunk in range(chunks):
+            if step > 0:
+                sum_wait(chunk, step - 1)
+            take_y(chunk, step)
+            sum_send(chunk, step)
+        if step == 2:
+            for chunk in range(chunks):
+                take_y(chunk, 3)
+        meanwhile(1 + step)
+    for chunk in range(chunks):
+        sum_wait(chunk, 2)
+        finish_sum(chunk)
+        gather_send(chunk, 0)
+    for step in range(3):
+        meanwhile(4 + step)
+        for chunk in range(chunks):
+            gather_take(chunk, step)
+            if step < 2:
+                gather_send(chunk, step + 1)
 
     for way in range(2):
 
@@ -1871,15 +1939,14 @@
     ]
     for copy in line_out_copies:
         copy.start()
-    gather_y(0, 0, z_at, 1 - y_at).wait_recv()
-    for step in range(3):
-        for way in range(2):
-            at = place(way)
-            piece = z_at - 1 - step if way == 0 else z_at + 1 + step
-
-            @pl.when(at >= 1 + step)
-            def _():
-                gather_y(step + 1, way, piece, 1 - y_at).wait_recv()
+    for chunk in range(chunks):
+        gather_y(chunk, 0, 0, z_at, 1 - y_at).wait_recv()
+        for step in range(3):
+            for way in range(2):
+
+                @pl.when(place(way) >= 1 + step)
+                def _():
+                    gather_y(chunk, step + 1, way, piece_in(step, way), 1 - y_at).wait_recv()
 
     for number in range(planes - 1):
         late_copy(number).wait_recv()
@@ -1922,7 +1989,6 @@
     late_y_copy.wait_send()
     for number in range(planes - 1):
         late_copy(number).wait_send()
-    gather_y(0, 0, z_at, y_at).wait_send()
     for way in range(2):
 
         @pl.when(place(way) <= 1)
@@ -1939,28 +2005,28 @@
             for piece in range(2):
                 line_copy_on(way, piece).wait_send()
 
-    for step in range(3):
-        for way in range(2):
-            at = place(way)
-
-            @pl.when((at <= step) & (at < z_last))
-            def _():
-                small_copy(step, way).wait_send()
-
-            piece = z_at - step if way == 0 else z_at + step
-
-            @pl.when((at >= step) & (at < z_last))
-            def _():
-                gather_z(step, way, piece).wait_send()
-
-            piece = z_at - 1 - step if way == 0 else z_at + 1 + step
-
-            @pl.when(at >= 1 + step)
-            def _():
-                gather_y(step + 1, way, piece, y_at).wait_send()
-
-
-def run_backward(gain1, shift1, gain2, qkv_w, out_w, grad_router, tok, *streamed):
+    for chunk in range(chunks):
+        gather_y(chunk, 0, 0, z_at, y_at).wait_send()
+        for number in range(4):
+            shared_y_copy(chunk, number).wait_send()
+        for step in range(3):
+            for way in range(2):
+                at = place(way)
+
+                @pl.when((at <= step) & (at < z_last))
+                def _():
+                    small_copy(chunk, step, way).wait_send()
+
+                @pl.when((at >= step) & (at < z_last))
+                def _():
+                    gather_z(chunk, step, way, piece_out(step, way)).wait_send()
+
+                @pl.when(at >= 1 + step)
+                def _():
+                    gather_y(chunk, step + 1, way, piece_in(step, way), y_at).wait_send()
+
+
+def run_backward(gain1, shift1, gain2, grad_router, qkv_w, out_w, tok, *streamed):
     images, _, features = tok.shape
     rows = images * PITCH
     share = out_w.shape[0]
@@ -1982,9 +2048,11 @@
             shape((16, features), f32),
             shape((rows, wide // 2), bf16),
         ],
-        in_specs=[vmem] * 6 + [anywhere] * (1 + len(streamed)),
+        in_specs=[vmem] * 4 + [anywhere] * (3 + len(streamed)),
         out_specs=[anywhere] * 5,
         scratch_shapes=[
+            pltpu.VMEM(qkv_w.shape, bf16),
+            pltpu.VMEM(out_w.shape, bf16),
             pltpu.VMEM((images, PITCH, features), bf16),
             *[pltpu.VMEM((images, PITCH, share), bf16)] * 4,
             pltpu.VMEM((images, PITCH, 128), f32),
@@ -2003,7 +2071,7 @@
             pltpu.VMEM((features // 2, features), f32),
             pltpu.VMEM((2, features // 2, features), bf16),
             pltpu.VMEM((features // 2, features), bf16),
-            pltpu.VMEM((2, 2, 3, features // 8, features), bf16),
+            pltpu.VMEM((2, 2, 2, 3, features // 16, features), bf16),
             pltpu.VMEM((2, features // 2, features), bf16),
             *[pltpu.VMEM((8, features), f32)] * 2,
             *[pltpu.VMEM((16, features), f32)] * 2,
@@ -2016,16 +2084,70 @@
         + [dma((parts,))] * 7
         + [dma((images,))] * 6
         + [dma((2, 4))] * 2
-        + [dma((4,))] * 2
-        + [dma((2, 3))] * 4
         + [dma((2, 4))] * 2
+        + [dma((2, 2, 3))] * 4
+        + [dma((2, 2, 4))] * 2
         + [dma((2,))] * 2
         + [dma((4,))] * 2
-        + [dma((4,)), dma((9, images)), dma((3,)), dma((4,)), dma((1,))],
+        + [dma((4,)), dma((9, images)), dma((5,)), dma((4,)), dma((1,))],
         compiler_params=pltpu.CompilerParams(
             collective_id=2, has_side_effects=True, vmem_limit_bytes=63 << 20
         ),
-    )(gain1, shift1, gain2, qkv_w, out_w, grad_router, tok, *streamed)
+    )(gain1, shift1, gain2, grad_router, qkv_w, out_w, tok, *streamed)
+
+
+def last_kernel(
+    side_ref, tokens_ref, weights_ref, up_first, up_pair, down_first, down_pair, line_ref, tokens_out, qkv_out, out_w_out, up_out, down_out
+):
+    share = out_w_out.shape[0]
+    tokens_out[...] = tokens_ref[...].astype(f32)
+    for which in range(3):
+        qkv_out[which] = weights_ref[which * share : (which + 1) * share, :].astype(f32)
+    out_w_out[...] = weights_ref[3 * share :, :].astype(f32)
+    up_out[...] = up_first[...].astype(f32) + up_pair[...].astype(f32) + line_ref[0].astype(f32)
+    down_out[...] = (down_first[...].astype(f32) + down_pair[...].astype(f32) + line_ref[1].astype(f32)).T
+
+
+def run_last(side, tokens, weights, up_first, up_pair, down_first, down_pair, line, share):
+    rows, features = tokens.shape
+    hidden = up_pair.shape[1]
+    shape = jax.ShapeDtypeStruct
+
+    def lanes(height):
+        return pl.BlockSpec((height, 128), lambda n, side: (0, n))
+
+    own = pl.BlockSpec((128, hidden), lambda n, side: (n, side[0]))
+    plain = pl.BlockSpec((128, hidden), lambda n, side: (n, 0))
+    return pl.pallas_call(
+        last_kernel,
+        grid_spec=pltpu.PrefetchScalarGridSpec(
+            num_scalar_prefetch=1,
+            grid=(features // 128,),
+            in_specs=[
+                lanes(rows),
+                lanes(features),
+                own,
+                plain,
+                own,
+                plain,
+                pl.BlockSpec((2, 128, hidden), lambda n, side: (0, n, 0)),
+            ],
+            out_specs=[
+                lanes(rows),
+                pl.BlockSpec((3, share, 128), lambda n, side: (0, 0, n)),
+                lanes(share),
+                plain,
+                lanes(hidden),
+            ],
+        ),
+        out_shape=[
+            shape((rows, features), f32),
+            shape((3, share, features), f32),
+            shape((share, features), f32),
+            shape((features, hidden), f32),
+            shape((hidden, features), f32),
+        ],
+    )(side, tokens, weights, up_first, up_pair, down_first, down_pair, line)
 
 
 def per_image(rows_in):
@@ -2118,9 +2240,9 @@
         gain_attn,
         shift_attn,
         gain_moe,
+        grad_router,
         qkv_turned,
         out_weight,
-        grad_router,
         tok,
         queries,
         keys,
@@ -2135,27 +2257,30 @@
         down_second,
         line_first,
     )
-    own_lane = lax.axis_index("expert") // 2 % 2 * hidden
-
-    def expert_total(first, pair, line):
-        own = lax.dynamic_slice_in_dim(first, own_lane, hidden, 1)
-        return own.astype(f32) + pair.astype(f32) + line.astype(f32)
-
-    weights_grad = weights_grad.reshape(feature_count, feature_count)
-    share = qkv_weight.shape[2]
-    grad_qkv = weights_grad[: 3 * share].reshape(3, share, feature_count)
+    side = (lax.axis_index("expert") // 2 % 2).astype(jnp.int32)[None]
+    grad_tokens, grad_qkv, grad_out, grad_up, grad_down = run_last(
+        side,
+        tokens_grad,
+        weights_grad.reshape(feature_count, feature_count),
+        up_first,
+        up_pair,
+        down_first,
+        down_pair,
+        line_sum,
+        qkv_weight.shape[2],
+    )
     return (
         unpad(mixed.reshape(images, PITCH, quarter_width)),
-        tokens_grad.astype(f32),
+        grad_tokens,
         sums[0],
         sums[1],
-        jnp.swapaxes(grad_qkv, 1, 2).astype(f32),
-        weights_grad[3 * share :].astype(f32),
+        jnp.swapaxes(grad_qkv, 1, 2),
+        grad_out,
         sums[2],
         sums[3],
         sums[8 : 8 + experts_all].T,
-        expert_total(up_first, up_pair, line_sum[0])[None],
-        expert_total(down_first, down_pair, line_sum[1]).T[None],
+        grad_up[None],
+        grad_down[None],
     )
 
 

time: 261 us -> 250 us (0.958)
  other arithmetic: 12.1 us -> 2.37 us
    pallas_call x0 -> x1, Pallas kernels: none -> 8.03 us  [run_last(): pl.pallas_call(last_kernel, grid_spec=pltpu.PrefetchScalarGridSpec(num_sc...]
    pallas_call x1, Pallas kernels: 90 us -> 82.9 us  [run_backward(): pl.pallas_call(partial(backward_kernel, images=images, heads=heads), out_...]
    convert_element_type x3 -> x0, other arithmetic: 6.58 us -> none  [the longest x1 4.37 us: per_device_dense(): tokens_grad.astype(f32)]
    broadcast_in_dim x1 -> x0, other arithmetic: 3.18 us -> none  [per_device_dense(): expert_total(down_first, down_pair, line_sum[1]).T[None]]
where the time goes in v8:
time: 250 us
  Pallas kernels  240 us (96%)
  local copies, waits for them, and re-layouts  6.31 us (3%)
    pallas_call x1, Pallas kernels, run_forward(): pl.pallas_call(partial(forward_kernel, images=images, heads=heads, expert...  90.2 us
    pallas_call x1, Pallas kernels, run_backward(): pl.pallas_call(partial(backward_kernel, images=images, heads=heads), out_...  82.9 us
    pallas_call x1, Pallas kernels, run_second_pair(): pl.pallas_call(partial(second_pair_kernel, experts=experts, steps=steps),...  59.2 us
    pallas_call x1, Pallas kernels, run_last(): pl.pallas_call(last_kernel, grid_spec=pltpu.PrefetchScalarGridSpec(num_sc...  8.03 us

profile of v8, /device:TPU:0, one launch (start us, length us, event | category | flops | bytes accessed | tf_op | source)
XLA Modules:
  0.0 249.7 jit_solution(6319043539532757574)
XLA Ops:
  0.6 1.4 pad.12.router_ref
  2.0 0.7 fusion.1
  2.8 0.1 reshape.42
  2.9 0.1 sub.11
  3.0 0.8 fusion
  3.8 0.8 convert_element_type.7.kept_hbm
  4.6 2.0 pad.13.cot_hbm
  6.6 90.2 %shard_map.212 = (bf16[8,208,192]{2,1,0:T(8,128)(2,1)}, bf16[8,208,192]{2,1,0:T(8,128)(2,1)}, bf16[8,208,192]{2,1,0:T(8,128)(2,1)}, bf16[8,208,192]{2,1,0:T(8,12...) custom-call(f32[768]{0:T(1024)} %gain1_ref.3, ...), custom_call_target="tpu_custom_call" | custom-call | tf_op jit(solution)/shard_map/pallas_call | solution.py:948
  96.7 59.2 %shard_map.213 = (bf16[3328,768]{1,0:T(8,128)(2,1)}, bf16[768,768]{1,0:T(8,128)(2,1)}, bf16[768,768]{1,0:T(8,128)(2,1)}, f32[8,768]{1,0:T(8,128)}, bf16[1664,768...) custom-call(bf16[3328,768]{1,0:T(8,128)(2,1)} %get-tuple-element.46.h_ref, ...), custom_call_target="tpu_custom_call" | custom-call | tf_op jit(solution)/shard_map/pallas_call | solution.py:1256
  156.0 82.9 %shard_map.214 = (bf16[2,768,384]{2,1,0:T(8,128)(2,1)}, bf16[1576,768]{1,0:T(8,128)(2,1)}, bf16[2,384,768]{2,1,0:T(8,128)(2,1)}, f32[16,768]{1,0:T(8,128)}, bf16[1664,192]{1,0:T(8,128)(2,1)}) custom-call(f32[768]{0:T(1024)} %gain1_ref.3, f32[768]{0:T(1024)} %shift1_ref.3, f32[768]{0:T(1024)} %gain2_ref.3, f32[8,768]{1,0:T(8,128)} %get-tuple-element.56.grad_router_ref, ...), custom_call_target="tpu_custom_call" | custom-call | tf_op jit(solution)/shard_map/pallas_call | solution.py:2042
  238.9 0.0 copy-start
  238.9 8.0 %shard_map.215 = (f32[1576,768]{1,0:T(8,128)}, f32[3,192,768]{2,1,0:T(8,128)}, f32[192,768]{1,0:T(8,128)}, f32[768,384]{1,0:T(8,128)}, f32[384,768]{1,0:T(8,128)}) custom-call(s32[1]{0:T(128)} %bitcast.6.side_ref, bf16[1576,768]{1,0:T(8,128)(2,1)} %get-tuple-element.70.tokens_ref, bf16[768,768]{1,0:T(8,128)(2,1)} %bitcast.19, ...), custom_call_target="tpu_custom_call" | custom-call | tf_op jit(solution)/shard_map/pallas_call | solution.py:2121
  246.9 0.0 copy-start.1
  246.9 0.0 copy-done
  247.0 0.1 slice.24
  247.0 0.4 reshape.46
  247.4 1.1 copy.27
  248.5 0.0 copy-done.1
  248.5 0.6 slice_reduce_fusion
  249.1 0.6 slice_bitcast_fusion
  (1 shorter events, 0.0 us)
Async XLA Ops:
  238.9 8.0 %copy-start = (bf16[1664,192]{1,0:T(8,128)(2,1)S(1)}, bf16[1664,192]{1,0:T(8,128)(2,1)}, u32[]{:S(2)}) copy-start(bf16[1664,192]{1,0:T(8,128)(2,1)} %get-tuple-element.69) | copy-start | bytes 1916932
  246.9 1.6 copy-start.1

commit v9 on v8

--- a/solution.py
+++ b/solution.py
@@ -535,23 +535,26 @@
         target = slot(expert, z_at)
         return [remote(target[n], target[n], w_s.at[way, step, n], w_r.at[way, step, n], core_dev) for n in range(2)]
 
-    def start_hops(step):
+    def start_hops(step, which):
         for way in range(2):
 
             @pl.when(hop_goes(step, way))
             def _():
-                for copy in hop(step, way):
-                    copy.start()
-
-    def await_hops(step):
+                hop(step, way)[which].start()
+
+    def await_hops(step, which):
         for way in range(2):
 
             @pl.when(hop_comes(step, way))
             def _():
-                for copy in hop_arriving(step, way):
-                    copy.wait_recv()
-
-    start_hops(0)
+                hop_arriving(step, way)[which].wait_recv()
+
+    def pass_hops(step, which):
+        await_hops(step, which)
+        start_hops(step + 1, which)
+
+    start_hops(0, 0)
+    start_hops(0, 1)
 
     def pair_place(expert):
         return up_vm.at[:, lanes_at(expert % 2 * hidden, hidden)], down_vm.at[aligned(expert % 2 * hidden, hidden), :]
@@ -612,7 +615,6 @@
     cot_x_in = cot_copy(1, across_x, across_x, x_dev)
     cot_y_in = cot_copy(2, across_y, across_y, y_dev)
     relay_y = cot_copy(3, across_x, across_both, y_dev)
-    relay_x = cot_copy(3, across_y, across_y, x_dev)
     relay_in = cot_copy(3, across_both, across_both, y_dev)
     cot_share = [
         cot_copy(4, across_x, across_x, core_dev),
@@ -753,9 +755,7 @@
         cot_x_in.wait_recv()
         cot_share[0].start()
 
-        @pl.when(core_at == 0)
-        def _():
-            relay_y.start()
+        relay_y.start()
 
         kept_y.wait_recv()
         kept_share.start()
@@ -764,19 +764,10 @@
         cot_y_in.wait_recv()
         cot_share[1].start()
 
-        @pl.when(core_at == 1)
-        def _():
-            relay_x.start()
-
     def weights_step_one():
-        await_hops(0)
-        start_hops(1)
+        pass_hops(0, 1)
         for copy in near_copies:
             copy.start()
-
-    def weights_step_two():
-        await_hops(1)
-        start_hops(2)
 
     def cot_step_three():
         relay_in.wait_recv()
@@ -858,6 +849,7 @@
             run(first)
             run(first + 1)
 
+    pass_hops(0, 0)
     cot_step_one()
     both(0, run_total, run_norm)
     cot_step_two()
@@ -873,10 +865,14 @@
         def _():
             both(2 * turn - 4, run_relay)
 
+        @pl.when(turn == 2)
+        def _():
+            pass_hops(1, 0)
+            cot_step_three()
+
         @pl.when(turn == pairs)
         def _():
-            weights_step_two()
-            cot_step_three()
+            pass_hops(1, 1)
             ready_other()
 
         @pl.when(turn >= pairs)
@@ -898,13 +894,7 @@
     for copy in (swap, kept_y, kept_share, cot_x, cot_y, *cot_share):
         copy.wait_send()
 
-    @pl.when(core_at == 0)
-    def _():
-        relay_y.wait_send()
-
-    @pl.when(core_at == 1)
-    def _():
-        relay_x.wait_send()
+    relay_y.wait_send()
 
     def drain(image, _):
         for copy in (core_copy, x_copy, total_copy, y_copy, relay_copy):
@@ -919,7 +909,8 @@
         for copy in block_copies(0, place):
             copy.wait()
 
-    await_hops(2)
+    await_hops(2, 0)
+    await_hops(2, 1)
     for step in range(3):
         for way in range(2):
 
@@ -1030,15 +1021,17 @@
     up_first,
     down_first,
     mixed_ref,
-    grad_up_ref,
-    grad_down_ref,
     grad_router_ref,
+    grad_up_out,
+    grad_down_out,
     grad_h_out,
     up_pair,
     down_pair,
     line_first,
     up_vm,
     down_vm,
+    grad_up_ref,
+    grad_down_ref,
     up_sum,
     down_sum,
     router_sum,
@@ -1136,16 +1129,21 @@
     line_copy = remote(grad_up_ref.at[:, far_lanes], line_first, line_s.at[0], line_r.at[0], z_dev)
     is_outer = (z_at == 0) | (z_at == lax.axis_size("expert") // 2 - 1)
 
+    grad_copies = [
+        pltpu.make_async_copy(grad_up_ref, grad_up_out, load.at[2]),
+        pltpu.make_async_copy(grad_down_ref, grad_down_out, load.at[3]),
+    ]
+
     @pl.when(turn == 0)
     def _():
-        greet([(True, core_dev), (True, x_dev), (True, y_dev), (True, z_dev)])
-        for copy in pair_copies:
-            copy.start()
         whole = [
             pltpu.make_async_copy(up_all.at[1], up_vm, load.at[0]),
             pltpu.make_async_copy(down_all.at[1], down_vm, load.at[1]),
         ]
         for copy in whole:
+            copy.start()
+        greet([(True, core_dev), (True, x_dev), (True, y_dev), (True, z_dev)])
+        for copy in pair_copies:
             copy.start()
         up_sum[...] = jnp.zeros_like(up_sum)
         down_sum[...] = jnp.zeros_like(down_sum)
@@ -1194,6 +1192,7 @@
     @pl.when(turn == steps - 1)
     def _():
         grad_up_ref[...] = up_sum[...].astype(bf16)
+        grad_copies[0].start()
 
         @pl.when(is_outer)
         def _():
@@ -1202,9 +1201,10 @@
         pass_own(7, 3)
         pass_total(2)
         grad_down_ref[...] = down_sum[...].astype(bf16)
+        grad_copies[1].start()
         grad_router_ref[...] = router_sum[...].T[:8]
         pass_total(3)
-        for copy in pair_copies:
+        for copy in (*pair_copies, *grad_copies):
             copy.wait()
 
         @pl.when(is_outer)
@@ -1258,9 +1258,9 @@
         grid=(steps,),
         out_shape=[
             shape((rows, features), bf16),
+            shape((8, features), f32),
             shape((features, width), bf16),
             shape((features, width), bf16),
-            shape((8, features), f32),
             shape((rows // 2, features), bf16),
             shape((features, width // 2), bf16),
             shape((features, width // 2), bf16),
@@ -1276,10 +1276,11 @@
             by_step(128),
         ]
         + [anywhere] * 4,
-        out_specs=[by_step(features), whole(features, width), whole(features, width), whole(8, features)] + [anywhere] * 4,
+        out_specs=[by_step(features), whole(8, features)] + [anywhere] * 6,
         scratch_shapes=[
             pltpu.VMEM((features, width), bf16),
             pltpu.VMEM((width, features), bf16),
+            *[pltpu.VMEM((features, width), bf16)] * 2,
             pltpu.VMEM((features, width), f32),
             pltpu.VMEM((features, width), f32),
             pltpu.VMEM((features, 128), f32),
@@ -1287,7 +1288,7 @@
             pltpu.VMEM((8, *half), bf16),
             pltpu.VMEM((4, *half), bf16),
             pltpu.VMEM((4, *half), bf16),
-            dma((2,)),
+            dma((4,)),
         ]
         + [dma((8,))] * 2
         + [dma((4,))] * 7
@@ -2222,7 +2223,7 @@
         router_wide,
         experts_all,
     )
-    mixed_part, up_second, down_second, grad_router, grad_h_two, up_pair, down_pair, line_first = run_second_pair(
+    mixed_part, grad_router, up_second, down_second, grad_h_two, up_pair, down_pair, line_first = run_second_pair(
         h_all,
         cot_all,
         kept_all,

time: 250 us -> 242 us (0.968)
  Pallas kernels: 240 us -> 232 us
    pallas_call x1, Pallas kernels: 90.2 us -> 84.1 us  [run_forward(): pl.pallas_call(partial(forward_kernel, images=images, heads=heads, expert...]
where the time goes in v9:
time: 242 us; the launch traced here: 241 us
  Pallas kernels  232 us (96%)
  local copies, waits for them, and re-layouts  6.31 us (3%)
    pallas_call x1, Pallas kernels, run_forward(): pl.pallas_call(partial(forward_kernel, images=images, heads=heads, expert...  84.1 us
    pallas_call x1, Pallas kernels, run_backward(): pl.pallas_call(partial(backward_kernel, images=images, heads=heads), out_...  82.3 us
    pallas_call x1, Pallas kernels, run_second_pair(): pl.pallas_call(partial(second_pair_kernel, experts=experts, steps=steps),...  57.3 us
    pallas_call x1, Pallas kernels, run_last(): pl.pallas_call(last_kernel, grid_spec=pltpu.PrefetchScalarGridSpec(num_sc...  8.03 us

profile of v9, /device:TPU:0, one launch (start us, length us, event | category | flops | bytes accessed | tf_op | source)
XLA Modules:
  0.0 241.1 jit_solution(8398090913424256943)
XLA Ops:
  0.6 1.4 pad.12.router_ref
  2.0 0.7 fusion.1
  2.8 0.1 reshape.42
  2.9 0.1 sub.11
  3.0 0.8 fusion
  3.8 0.8 convert_element_type.7.kept_hbm
  4.6 2.0 pad.13.cot_hbm
  6.6 84.1 %shard_map.212 = (bf16[8,208,192]{2,1,0:T(8,128)(2,1)}, bf16[8,208,192]{2,1,0:T(8,128)(2,1)}, bf16[8,208,192]{2,1,0:T(8,128)(2,1)}, bf16[8,208,192]{2,1,0:T(8,12...) custom-call(f32[768]{0:T(1024)} %gain1_ref.3, ...), custom_call_target="tpu_custom_call" | custom-call | tf_op jit(solution)/shard_map/pallas_call | solution.py:939
  90.7 57.3 %shard_map.213 = (bf16[3328,768]{1,0:T(8,128)(2,1)}, f32[8,768]{1,0:T(8,128)}, bf16[768,768]{1,0:T(8,128)(2,1)}, bf16[768,768]{1,0:T(8,128)(2,1)}, bf16[1664,768...) custom-call(bf16[3328,768]{1,0:T(8,128)(2,1)} %get-tuple-element.46.h_ref, ...), custom_call_target="tpu_custom_call" | custom-call | tf_op jit(solution)/shard_map/pallas_call | solution.py:1256
  147.9 82.3 %shard_map.214 = (bf16[2,768,384]{2,1,0:T(8,128)(2,1)}, bf16[1576,768]{1,0:T(8,128)(2,1)}, bf16[2,384,768]{2,1,0:T(8,128)(2,1)}, f32[16,768]{1,0:T(8,128)}, bf16[1664,192]{1,0:T(8,128)(2,1)}) custom-call(f32[768]{0:T(1024)} %gain1_ref.3, f32[768]{0:T(1024)} %shift1_ref.3, f32[768]{0:T(1024)} %gain2_ref.3, f32[8,768]{1,0:T(8,128)} %get-tuple-element.56.grad_router_ref, ...), custom_call_target="tpu_custom_call" | custom-call | tf_op jit(solution)/shard_map/pallas_call | solution.py:2043
  230.3 0.0 copy-start
  230.3 8.0 %shard_map.215 = (f32[1576,768]{1,0:T(8,128)}, f32[3,192,768]{2,1,0:T(8,128)}, f32[192,768]{1,0:T(8,128)}, f32[768,384]{1,0:T(8,128)}, f32[384,768]{1,0:T(8,128)}) custom-call(s32[1]{0:T(128)} %bitcast.6.side_ref, bf16[1576,768]{1,0:T(8,128)(2,1)} %get-tuple-element.70.tokens_ref, bf16[768,768]{1,0:T(8,128)(2,1)} %bitcast.19, ...), custom_call_target="tpu_custom_call" | custom-call | tf_op jit(solution)/shard_map/pallas_call | solution.py:2122
  238.3 0.0 copy-start.1
  238.3 0.0 copy-done
  238.4 0.1 slice.24
  238.4 0.4 reshape.46
  238.8 1.1 copy.27
  239.9 0.0 copy-done.1
  239.9 0.6 slice_reduce_fusion
  240.5 0.6 slice_bitcast_fusion
  (1 shorter events, 0.0 us)
Async XLA Ops:
  230.3 8.0 %copy-start = (bf16[1664,192]{1,0:T(8,128)(2,1)S(1)}, bf16[1664,192]{1,0:T(8,128)(2,1)}, u32[]{:S(2)}) copy-start(bf16[1664,192]{1,0:T(8,128)(2,1)} %get-tuple-element.69) | copy-start | bytes 1916932
  238.3 1.6 copy-start.1

commit v10 on v9

--- a/solution.py
+++ b/solution.py
@@ -387,7 +387,7 @@
     shift2_ref,
     up_ref,
     down_ref,
-    router_ref,
+    router_raw,
     cot_hbm,
     kept_hbm,
     tok_hbm,
@@ -410,6 +410,8 @@
     grad_up_out,
     grad_down_out,
     tok_out,
+    router_out,
+    router_ref,
     cot_turned,
     kept_ref,
     tok_raw,
@@ -578,8 +580,10 @@
         cot_ref[number * PITCH : (number + 1) * PITCH, :] = padded.astype(bf16)
     swap = remote(cot_ref, cot_core, c_s.at[0], c_r.at[0], core_dev)
     swap.start()
-    loads[1].wait()
-    kept_all[pl.ds(0, rows), :] = kept_ref[...]
+
+    narrow = router_raw[...].astype(f32)
+    router_ref[0:16, :] = jnp.concatenate([narrow, jnp.zeros((16 - experts, narrow.shape[1]), f32)], axis=0).astype(bf16)
+    router_ref[16:128, :] = jnp.zeros((112, narrow.shape[1]), bf16)
 
     def kept_half(side, core):
         return kept_all.at[aligned(side * rows + core * half, half), :]
@@ -587,6 +591,8 @@
     kept_y = remote(kept_half(0, core_at), kept_half(1, core_at), c_s.at[7], c_r.at[7], y_dev)
     kept_share = remote(kept_half(1, core_at), kept_half(1, core_at), c_s.at[6], c_r.at[6], core_dev)
     kept_share_in = remote(kept_half(1, other), kept_half(1, other), c_s.at[6], c_r.at[6], core_dev)
+    loads[1].wait()
+    kept_all[pl.ds(0, rows), :] = kept_ref[...]
     kept_y.start()
     swap.wait_recv()
 
@@ -757,9 +763,6 @@
 
         relay_y.start()
 
-        kept_y.wait_recv()
-        kept_share.start()
-
     def cot_step_two():
         cot_y_in.wait_recv()
         cot_share[1].start()
@@ -770,12 +773,15 @@
             copy.start()
 
     def cot_step_three():
+        kept_y.wait_recv()
+        kept_share.start()
         relay_in.wait_recv()
         cot_share[2].start()
 
     outs = [
         pltpu.make_async_copy(cot_all, cot_out, cot_sem.at[0]),
         pltpu.make_async_copy(kept_all, kept_out, cot_sem.at[1]),
+        pltpu.make_async_copy(router_ref, router_out, cot_sem.at[2]),
     ]
 
     def ready_own():
@@ -923,7 +929,7 @@
         copy.wait()
 
 
-def run_forward(tok_raw, gain1, shift1, gain2, shift2, qkv_w, out_w, up, down, cot, kept, router, experts):
+def run_forward(tok_raw, gain1, shift1, gain2, shift2, qkv_w, out_w, up, down, router, cot, kept, experts):
     images = tok_raw.shape[0] // SEQ
     rows = images * PITCH
     features = tok_raw.shape[1]
@@ -956,10 +962,12 @@
             shape((features, 2 * hidden), bf16),
             shape((features, 2 * hidden), bf16),
             shape((images, PITCH, features), bf16),
+            shape((128, features), bf16),
         ],
         in_specs=[vmem] * 4 + [anywhere] * 2 + [vmem] + [anywhere] * 5,
-        out_specs=[anywhere] * 17,
+        out_specs=[anywhere] * 18,
         scratch_shapes=[
+            pltpu.VMEM((128, features), bf16),
             pltpu.VMEM(cot.shape, bf16),
             pltpu.VMEM(kept.shape, bf16),
             pltpu.VMEM(tok_raw.shape, bf16),
@@ -992,7 +1000,7 @@
         + [dma((images,))] * 10
         + [dma((2, 3, 2))] * 2
         + [dma((9,))] * 2
-        + [dma((5,)), dma((2,)), dma((2,)), dma((3, 2)), dma((2,)), dma((2,)), dma((9, images))],
+        + [dma((5,)), dma((2,)), dma((2,)), dma((3, 2)), dma((2,)), dma((3,)), dma((9, images))],
         compiler_params=pltpu.CompilerParams(
             collective_id=1, has_side_effects=True, vmem_limit_bytes=63 << 20
         ),
@@ -1063,12 +1071,11 @@
     z_at, y_at = expert_at // 2, expert_at % 2
     x_at, core_at = tensor_at // 2, tensor_at % 2
     hidden = up_pair.shape[1]
-    wide = ring.shape[2] // 2
+    wide = ring.shape[3]
     core_dev = (expert_at, tensor_at + 1 - 2 * core_at)
     x_dev = (expert_at, tensor_at + 2 - 4 * x_at)
     y_dev = (expert_at + 1 - 2 * y_at, tensor_at)
     my_cols = lanes_at(core_at * wide, wide)
-    their_cols = lanes_at((1 - core_at) * wide, wide)
 
     def remote(src, dst, send, recv, device):
         return pltpu.make_async_remote_copy(
@@ -1076,7 +1083,7 @@
         )
 
     def core_copy(number):
-        return remote(ring.at[number % 2, :, their_cols], from_core.at[number], core_s.at[number], core_r.at[number], core_dev)
+        return remote(ring.at[number % 2, 1 - core_at], from_core.at[number], core_s.at[number], core_r.at[number], core_dev)
 
     def y_copy(number, place):
         return remote(from_core.at[number], from_y.at[place], y_s.at[place], y_r.at[place], y_dev)
@@ -1101,13 +1108,13 @@
 
     def pass_other(number):
         core_copy(number).wait_recv()
-        from_core[number] = from_core[number] + ring[number % 2, :, my_cols]
+        from_core[number] = from_core[number] + ring[number % 2, core_at]
         y_copy(number, (number + 1) // 2).start()
 
     def pass_own(number, place):
         core_copy(number).wait_recv()
         y_copy(number, place).wait_recv()
-        total = from_core[number].astype(f32) + ring[number % 2, :, my_cols].astype(f32) + from_y[place].astype(f32)
+        total = from_core[number].astype(f32) + ring[number % 2, core_at].astype(f32) + from_y[place].astype(f32)
         from_core[number] = total.astype(bf16)
         x_copy(number, place).start()
 
@@ -1179,9 +1186,11 @@
     def _():
         core_copy(turn - 2).wait_send()
 
-    ring[turn % 2] = (
+    grad_h = (
         grad_h_first[...].astype(f32) + dot(grad_pre, up, ((1,), (1,))) + dot(grad_logits, router)
     ).astype(bf16)
+    ring[turn % 2, 0] = grad_h[:, :wide]
+    ring[turn % 2, 1] = grad_h[:, wide:]
     core_copy(turn).start()
     mixed_ref[...] = (mixed_first[...].astype(f32) + dot(hidden_rows, down)).astype(bf16)
     h_turned = h_rows.T
@@ -1284,7 +1293,7 @@
             pltpu.VMEM((features, width), f32),
             pltpu.VMEM((features, width), f32),
             pltpu.VMEM((features, 128), f32),
-            pltpu.VMEM((2, BLOCK, features), bf16),
+            pltpu.VMEM((2, 2, *half), bf16),
             pltpu.VMEM((8, *half), bf16),
             pltpu.VMEM((4, *half), bf16),
             pltpu.VMEM((4, *half), bf16),
@@ -1470,6 +1479,26 @@
                 lax.fori_loop(0, features // 96, add, 0)
                 line_copy_on(way, piece).start()
 
+    part_height = line.shape[2] // 4
+
+    def line_part_copy(way, part):
+        ref = line.at[way, 3, pl.ds(part * part_height, part_height)]
+        return remote(ref, ref, l_s.at[way, 3 + part], l_r.at[way, 3 + part], z_devs[way])
+
+    def line_part(part):
+        for way in range(2):
+
+            @pl.when(place(way) == 1)
+            def _():
+                if part == 0:
+                    line_copy_on(way, 3).wait_recv()
+                lanes = far_lanes(way, 3)
+                for piece in range(2):
+                    at_rows = pl.ds(part * part_height + piece * part_height // 2, part_height // 2)
+                    total = line[way, 3, at_rows, :].astype(f32) + far_vm[1, at_rows, lanes].astype(f32)
+                    line[way, 3, at_rows, :] = total.astype(bf16)
+                line_part_copy(way, part).start()
+
     def line_pass(piece):
         for way in range(2):
 
@@ -1874,21 +1903,24 @@
             run_m_out(0)
             run_tokens(images - 3)
         if place_in_order == 3:
+            line_part(0)
             run_one_total(images - 2)
             run_m_out(1)
             run_tokens(images - 2)
         if place_in_order == 4:
+            line_part(1)
             run_one_total(images - 1)
             run_m_out(2)
         if place_in_order == 5:
+            line_part(2)
             run_tokens(images - 1)
-            line_add(3)
             route_two.wait_recv()
             late_mine[8:16, :] = route_core[...] + route_x[...]
             late_y_copy.start()
             tokens_low[...] = rows_kept[pl.ds(0, images * SEQ), :].astype(bf16)
             store_copy.start()
         if place_in_order == 6:
+            line_part(3)
             run_m_out(3)
             late_y_copy.wait_recv()
             late_z[z_at] = late_mine[...] + late_y[...]
@@ -1925,7 +1957,8 @@
         @pl.when(place(way) == 2)
         def _():
             line_copy_on(way, 2).wait_recv()
-            line_copy_on(way, 3).wait_recv()
+            for part in range(4):
+                line_part_copy(way, part).wait_recv()
 
         @pl.when(place(way) == z_last)
         def _():
@@ -1992,14 +2025,17 @@
         late_copy(number).wait_send()
     for way in range(2):
 
-        @pl.when(place(way) <= 1)
+        @pl.when(place(way) == 0)
         def _():
             for piece in range(1, 4):
                 line_copy_on(way, piece).wait_send()
 
         @pl.when(place(way) == 1)
         def _():
-            line_copy_on(way, 0).wait_send()
+            for piece in range(3):
+                line_copy_on(way, piece).wait_send()
+            for part in range(4):
+                line_part_copy(way, part).wait_send()
 
         @pl.when(place(way) == 2)
         def _():
@@ -2084,7 +2120,7 @@
         + [dma((2, parts))] * 2
         + [dma((parts,))] * 7
         + [dma((images,))] * 6
-        + [dma((2, 4))] * 2
+        + [dma((2, 7))] * 2
         + [dma((2, 4))] * 2
         + [dma((2, 2, 3))] * 4
         + [dma((2, 2, 4))] * 2
@@ -2114,6 +2150,10 @@
     hidden = up_pair.shape[1]
     shape = jax.ShapeDtypeStruct
 
+    steps = features // 128
+    height = -(-rows // (16 * steps)) * 16
+    by_rows = pl.BlockSpec((height, features), lambda n, side: (n, 0))
+
     def lanes(height):
         return pl.BlockSpec((height, 128), lambda n, side: (0, n))
 
@@ -2125,7 +2165,7 @@
             num_scalar_prefetch=1,
             grid=(features // 128,),
             in_specs=[
-                lanes(rows),
+                by_rows,
                 lanes(features),
                 own,
                 plain,
@@ -2134,7 +2174,7 @@
                 pl.BlockSpec((2, 128, hidden), lambda n, side: (0, n, 0)),
             ],
             out_specs=[
-                lanes(rows),
+                by_rows,
                 pl.BlockSpec((3, share, 128), lambda n, side: (0, 0, n)),
                 lanes(share),
                 plain,
@@ -2187,7 +2227,6 @@
     kept_routes = per_image(jnp.where(keep_mask > 0, routes, -1) + 1).reshape(rows, 2) - 1
     chosen = kept_routes[:, :, None] == jnp.arange(128, dtype=jnp.int32)[None, None, :]
     kept = jnp.any(chosen, axis=1).astype(bf16)
-    router_wide = jnp.pad(router_weight.T, ((0, 128 - experts_all), (0, 0)))
     cot_turned = jnp.pad(cotangent.T, ((0, 0), (0, -row_count % 128)))
     qkv_turned = jnp.swapaxes(qkv_weight, 1, 2)
     (
@@ -2208,6 +2247,7 @@
         up_first,
         down_first,
         tok,
+        router_wide,
     ) = run_forward(
         tokens,
         gain_attn,
@@ -2218,9 +2258,9 @@
         out_weight,
         expert_up[0],
         expert_down[0],
+        router_weight.T,
         cot_turned,
         kept,
-        router_wide,
         experts_all,
     )
     mixed_part, grad_router, up_second, down_second, grad_h_two, up_pair, down_pair, line_first = run_second_pair(

time: 242 us -> 239 us (0.988)
  no operation moved by 1% of the time
where the time goes in v10:
time: 239 us
  Pallas kernels  231 us (97%)
  local copies, waits for them, and re-layouts  4.92 us (2%)
    pallas_call x1, Pallas kernels, run_forward(): pl.pallas_call(partial(forward_kernel, images=images, heads=heads, expert...  83.9 us
    pallas_call x1, Pallas kernels, run_backward(): pl.pallas_call(partial(backward_kernel, images=images, heads=heads), out_...  81.3 us
    pallas_call x1, Pallas kernels, run_second_pair(): pl.pallas_call(partial(second_pair_kernel, experts=experts, steps=steps),...  57.3 us
    pallas_call x1, Pallas kernels, run_last(): pl.pallas_call(last_kernel, grid_spec=pltpu.PrefetchScalarGridSpec(num_sc...  8.27 us

profile of v10, /device:TPU:0, one launch (start us, length us, event | category | flops | bytes accessed | tf_op | source)
XLA Modules:
  0.0 238.8 jit_solution(12929895899334707453)
XLA Ops:
  0.6 0.7 fusion.1
  1.4 0.1 reshape.42
  1.5 0.1 sub.11
  1.6 0.8 fusion
  2.4 0.8 convert_element_type.5.kept_hbm
  3.2 2.0 pad.8.cot_hbm
  5.2 83.9 %shard_map.212 = (bf16[8,208,192]{2,1,0:T(8,128)(2,1)}, bf16[8,208,192]{2,1,0:T(8,128)(2,1)}, bf16[8,208,192]{2,1,0:T(8,128)(2,1)}, bf16[8,208,192]{2,1,0:T(8,12...) custom-call(f32[768]{0:T(1024)} %gain1_ref.3, ...), custom_call_target="tpu_custom_call" | custom-call | tf_op jit(solution)/shard_map/pallas_call | solution.py:945
  89.1 57.3 %shard_map.213 = (bf16[3328,768]{1,0:T(8,128)(2,1)}, f32[8,768]{1,0:T(8,128)}, bf16[768,768]{1,0:T(8,128)(2,1)}, bf16[768,768]{1,0:T(8,128)(2,1)}, bf16[1664,768...) custom-call(bf16[3328,768]{1,0:T(8,128)(2,1)} %get-tuple-element.47.h_ref, ...), custom_call_target="tpu_custom_call" | custom-call | tf_op jit(solution)/shard_map/pallas_call | solution.py:1265
  146.4 81.3 %shard_map.214 = (bf16[2,768,384]{2,1,0:T(8,128)(2,1)}, bf16[1576,768]{1,0:T(8,128)(2,1)}, bf16[2,384,768]{2,1,0:T(8,128)(2,1)}, f32[16,768]{1,0:T(8,128)}, bf16[1664,192]{1,0:T(8,128)(2,1)}) custom-call(f32[768]{0:T(1024)} %gain1_ref.3, f32[768]{0:T(1024)} %shift1_ref.3, f32[768]{0:T(1024)} %gain2_ref.3, f32[8,768]{1,0:T(8,128)} %get-tuple-element.58.grad_router_ref, ...), custom_call_target="tpu_custom_call" | custom-call | tf_op jit(solution)/shard_map/pallas_call | solution.py:2079
  227.7 0.0 copy-start
  227.7 8.3 %shard_map.215 = (f32[1576,768]{1,0:T(8,128)}, f32[3,192,768]{2,1,0:T(8,128)}, f32[192,768]{1,0:T(8,128)}, f32[768,384]{1,0:T(8,128)}, f32[384,768]{1,0:T(8,128)}) custom-call(s32[1]{0:T(128)} %bitcast.6.side_ref, bf16[1576,768]{1,0:T(8,128)(2,1)} %get-tuple-element.72.tokens_ref, bf16[768,768]{1,0:T(8,128)(2,1)} %bitcast.19, ...), custom_call_target="tpu_custom_call" | custom-call | tf_op jit(solution)/shard_map/pallas_call | solution.py:2162
  236.0 0.0 copy-start.1
  236.0 0.0 copy-done
  236.0 0.1 slice.24
  236.1 0.4 reshape.46
  236.4 1.1 copy.27
  237.6 0.0 copy-done.1
  237.6 0.6 slice_reduce_fusion
  238.2 0.6 slice_bitcast_fusion
  (1 shorter events, 0.0 us)
Async XLA Ops:
  227.7 8.3 %copy-start = (bf16[1664,192]{1,0:T(8,128)(2,1)S(1)}, bf16[1664,192]{1,0:T(8,128)(2,1)}, u32[]{:S(2)}) copy-start(bf16[1664,192]{1,0:T(8,128)(2,1)} %get-tuple-element.71) | copy-start | bytes 1916932
  236.0 1.6 copy-start.1

commit v11 on v10

--- a/solution.py
+++ b/solution.py
@@ -575,7 +575,10 @@
     for number in range(images):
         first = number * SEQ // 128 * 128
         skip = number * SEQ - first
-        turned = cot_turned[:, first : first + 384].T.astype(f32)[skip : skip + SEQ]
+        lanes_in = cot_turned[:, first : min(first + 384, images * SEQ)].astype(f32)
+        if lanes_in.shape[1] < 384:
+            lanes_in = jnp.concatenate([lanes_in, jnp.zeros((lanes_in.shape[0], 384 - lanes_in.shape[1]), f32)], axis=1)
+        turned = lanes_in.T[skip : skip + SEQ]
         padded = jnp.concatenate([turned, jnp.zeros((PITCH - SEQ, turned.shape[1]), f32)], axis=0)
         cot_ref[number * PITCH : (number + 1) * PITCH, :] = padded.astype(bf16)
     swap = remote(cot_ref, cot_core, c_s.at[0], c_r.at[0], core_dev)
@@ -2225,9 +2228,9 @@
     experts_all = router_weight.shape[1]
     hidden = expert_up.shape[2]
     kept_routes = per_image(jnp.where(keep_mask > 0, routes, -1) + 1).reshape(rows, 2) - 1
-    chosen = kept_routes[:, :, None] == jnp.arange(128, dtype=jnp.int32)[None, None, :]
-    kept = jnp.any(chosen, axis=1).astype(bf16)
-    cot_turned = jnp.pad(cotangent.T, ((0, 0), (0, -row_count % 128)))
+    expert_lane = jnp.arange(128, dtype=jnp.int32)[None, :]
+    kept = ((kept_routes[:, 0:1] == expert_lane) | (kept_routes[:, 1:2] == expert_lane)).astype(bf16)
+    cot_turned = cotangent.T
     qkv_turned = jnp.swapaxes(qkv_weight, 1, 2)
     (
         queries,

time: 239 us -> 237 us (level)
  no operation moved by 1% of the time
where the time goes in v11:
time: 237 us
  Pallas kernels  231 us (97%)
  local copies, waits for them, and re-layouts  3 us (1%)
  other arithmetic  2.37 us (1%)
    pallas_call x1, Pallas kernels, run_forward(): pl.pallas_call(partial(forward_kernel, images=images, heads=heads, expert...  83.9 us
    pallas_call x1, Pallas kernels, run_backward(): pl.pallas_call(partial(backward_kernel, images=images, heads=heads), out_...  81.3 us
    pallas_call x1, Pallas kernels, run_second_pair(): pl.pallas_call(partial(second_pair_kernel, experts=experts, steps=steps),...  57.3 us
    pallas_call x1, Pallas kernels, run_last(): pl.pallas_call(last_kernel, grid_spec=pltpu.PrefetchScalarGridSpec(num_sc...  8.27 us

profile of v11, /device:TPU:0, one launch (start us, length us, event | category | flops | bytes accessed | tf_op | source)
XLA Modules:
  0.0 236.9 jit_solution(11580628531031595092)
XLA Ops:
  0.6 0.7 fusion.2
  1.4 0.1 reshape.37
  1.5 0.1 sub.11
  1.6 1.6 fusion.1.kept_hbm
  3.3 83.9 %shard_map.212 = (bf16[8,208,192]{2,1,0:T(8,128)(2,1)}, bf16[8,208,192]{2,1,0:T(8,128)(2,1)}, bf16[8,208,192]{2,1,0:T(8,128)(2,1)}, bf16[8,208,192]{2,1,0:T(8,12...) custom-call(f32[768]{0:T(1024)} %gain1_ref.3, ...), custom_call_target="tpu_custom_call" | custom-call | tf_op jit(solution)/shard_map/pallas_call | solution.py:948
  87.1 57.3 %shard_map.213 = (bf16[3328,768]{1,0:T(8,128)(2,1)}, f32[8,768]{1,0:T(8,128)}, bf16[768,768]{1,0:T(8,128)(2,1)}, bf16[768,768]{1,0:T(8,128)(2,1)}, bf16[1664,768...) custom-call(bf16[3328,768]{1,0:T(8,128)(2,1)} %get-tuple-element.47.h_ref, ...), custom_call_target="tpu_custom_call" | custom-call | tf_op jit(solution)/shard_map/pallas_call | solution.py:1268
  144.4 81.3 %shard_map.214 = (bf16[2,768,384]{2,1,0:T(8,128)(2,1)}, bf16[1576,768]{1,0:T(8,128)(2,1)}, bf16[2,384,768]{2,1,0:T(8,128)(2,1)}, f32[16,768]{1,0:T(8,128)}, bf16[1664,192]{1,0:T(8,128)(2,1)}) custom-call(f32[768]{0:T(1024)} %gain1_ref.3, f32[768]{0:T(1024)} %shift1_ref.3, f32[768]{0:T(1024)} %gain2_ref.3, f32[8,768]{1,0:T(8,128)} %get-tuple-element.58.grad_router_ref, ...), custom_call_target="tpu_custom_call" | custom-call | tf_op jit(solution)/shard_map/pallas_call | solution.py:2082
  225.8 0.0 copy-start
  225.8 8.3 %shard_map.215 = (f32[1576,768]{1,0:T(8,128)}, f32[3,192,768]{2,1,0:T(8,128)}, f32[192,768]{1,0:T(8,128)}, f32[768,384]{1,0:T(8,128)}, f32[384,768]{1,0:T(8,128)}) custom-call(s32[1]{0:T(128)} %bitcast.6.side_ref, bf16[1576,768]{1,0:T(8,128)(2,1)} %get-tuple-element.72.tokens_ref, bf16[768,768]{1,0:T(8,128)(2,1)} %bitcast.19, ...), custom_call_target="tpu_custom_call" | custom-call | tf_op jit(solution)/shard_map/pallas_call | solution.py:2165
  234.1 0.0 copy-start.1
  234.1 0.0 copy-done
  234.1 0.1 slice.34
  234.1 0.4 reshape.41
  234.5 1.1 copy.25
  235.6 0.0 copy-done.1
  235.6 0.6 slice_reduce_fusion.2
  236.3 0.6 slice_bitcast_fusion
  (2 shorter events, 0.0 us)
Async XLA Ops:
  225.8 8.3 %copy-start = (bf16[1664,192]{1,0:T(8,128)(2,1)S(1)}, bf16[1664,192]{1,0:T(8,128)(2,1)}, u32[]{:S(2)}) copy-start(bf16[1664,192]{1,0:T(8,128)(2,1)} %get-tuple-element.71) | copy-start | bytes 1916932
  234.1 1.6 copy-start.1

commit v12 on v11

--- a/solution.py
+++ b/solution.py
@@ -2153,10 +2153,6 @@
     hidden = up_pair.shape[1]
     shape = jax.ShapeDtypeStruct
 
-    steps = features // 128
-    height = -(-rows // (16 * steps)) * 16
-    by_rows = pl.BlockSpec((height, features), lambda n, side: (n, 0))
-
     def lanes(height):
         return pl.BlockSpec((height, 128), lambda n, side: (0, n))
 
@@ -2168,7 +2164,7 @@
             num_scalar_prefetch=1,
             grid=(features // 128,),
             in_specs=[
-                by_rows,
+                lanes(rows),
                 lanes(features),
                 own,
                 plain,
@@ -2177,7 +2173,7 @@
                 pl.BlockSpec((2, 128, hidden), lambda n, side: (0, n, 0)),
             ],
             out_specs=[
-                by_rows,
+                lanes(rows),
                 pl.BlockSpec((3, share, 128), lambda n, side: (0, 0, n)),
                 lanes(share),
                 plain,

time: 237 us -> 237 us (level)
  no operation moved by 1% of the time
where the time goes in v12:
time: 237 us
  Pallas kernels  231 us (97%)
  local copies, waits for them, and re-layouts  3 us (1%)
  other arithmetic  2.37 us (1%)
    pallas_call x1, Pallas kernels, run_forward(): pl.pallas_call(partial(forward_kernel, images=images, heads=heads, expert...  83.9 us
    pallas_call x1, Pallas kernels, run_backward(): pl.pallas_call(partial(backward_kernel, images=images, heads=heads), out_...  81.3 us
    pallas_call x1, Pallas kernels, run_second_pair(): pl.pallas_call(partial(second_pair_kernel, experts=experts, steps=steps),...  57.3 us
    pallas_call x1, Pallas kernels, run_last(): pl.pallas_call(last_kernel, grid_spec=pltpu.PrefetchScalarGridSpec(num_sc...  8.03 us

profile of v12, /device:TPU:0, one launch (start us, length us, event | category | flops | bytes accessed | tf_op | source)
XLA Modules:
  0.0 236.6 jit_solution(637621513412530968)
XLA Ops:
  0.6 0.7 fusion.2
  1.4 0.1 reshape.37
  1.5 0.1 sub.11
  1.6 1.6 fusion.1.kept_hbm
  3.3 83.9 %shard_map.212 = (bf16[8,208,192]{2,1,0:T(8,128)(2,1)}, bf16[8,208,192]{2,1,0:T(8,128)(2,1)}, bf16[8,208,192]{2,1,0:T(8,128)(2,1)}, bf16[8,208,192]{2,1,0:T(8,12...) custom-call(f32[768]{0:T(1024)} %gain1_ref.3, ...), custom_call_target="tpu_custom_call" | custom-call | tf_op jit(solution)/shard_map/pallas_call | solution.py:948
  87.1 57.3 %shard_map.213 = (bf16[3328,768]{1,0:T(8,128)(2,1)}, f32[8,768]{1,0:T(8,128)}, bf16[768,768]{1,0:T(8,128)(2,1)}, bf16[768,768]{1,0:T(8,128)(2,1)}, bf16[1664,768...) custom-call(bf16[3328,768]{1,0:T(8,128)(2,1)} %get-tuple-element.47.h_ref, ...), custom_call_target="tpu_custom_call" | custom-call | tf_op jit(solution)/shard_map/pallas_call | solution.py:1268
  144.4 81.3 %shard_map.214 = (bf16[2,768,384]{2,1,0:T(8,128)(2,1)}, bf16[1576,768]{1,0:T(8,128)(2,1)}, bf16[2,384,768]{2,1,0:T(8,128)(2,1)}, f32[16,768]{1,0:T(8,128)}, bf16[1664,192]{1,0:T(8,128)(2,1)}) custom-call(f32[768]{0:T(1024)} %gain1_ref.3, f32[768]{0:T(1024)} %shift1_ref.3, f32[768]{0:T(1024)} %gain2_ref.3, f32[8,768]{1,0:T(8,128)} %get-tuple-element.58.grad_router_ref, ...), custom_call_target="tpu_custom_call" | custom-call | tf_op jit(solution)/shard_map/pallas_call | solution.py:2082
  225.8 0.0 copy-start
  225.8 8.0 %shard_map.215 = (f32[1576,768]{1,0:T(8,128)}, f32[3,192,768]{2,1,0:T(8,128)}, f32[192,768]{1,0:T(8,128)}, f32[768,384]{1,0:T(8,128)}, f32[384,768]{1,0:T(8,128)}) custom-call(s32[1]{0:T(128)} %bitcast.6.side_ref, bf16[1576,768]{1,0:T(8,128)(2,1)} %get-tuple-element.72.tokens_ref, bf16[768,768]{1,0:T(8,128)(2,1)} %bitcast.19, ...), custom_call_target="tpu_custom_call" | custom-call | tf_op jit(solution)/shard_map/pallas_call | solution.py:2161
  233.8 0.0 copy-start.1
  233.8 0.0 copy-done
  233.8 0.1 slice.34
  233.9 0.4 reshape.41
  234.3 1.1 copy.25
  235.4 0.0 copy-done.1
  235.4 0.6 slice_reduce_fusion.2
  236.0 0.6 slice_bitcast_fusion
  (2 shorter events, 0.0 us)
Async XLA Ops:
  225.8 8.0 %copy-start = (bf16[1664,192]{1,0:T(8,128)(2,1)S(1)}, bf16[1664,192]{1,0:T(8,128)(2,1)}, u32[]{:S(2)}) copy-start(bf16[1664,192]{1,0:T(8,128)(2,1)} %get-tuple-element.71) | copy-start | bytes 1916932
  233.8 1.6 copy-start.1

commit v13 on v12

--- a/solution.py
+++ b/solution.py
@@ -1195,11 +1195,8 @@
     ring[turn % 2, 0] = grad_h[:, :wide]
     ring[turn % 2, 1] = grad_h[:, wide:]
     core_copy(turn).start()
-    mixed_ref[...] = (mixed_first[...].astype(f32) + dot(hidden_rows, down)).astype(bf16)
     h_turned = h_rows.T
     up_sum[...] += dot(h_turned, grad_pre)
-    router_sum[...] += dot(h_turned, grad_logits)
-    down_sum[...] += dot(cot_rows.T, hidden_rows)
 
     @pl.when(turn == steps - 1)
     def _():
@@ -1211,6 +1208,13 @@
             line_copy.start()
 
         pass_own(7, 3)
+
+    mixed_ref[...] = (mixed_first[...].astype(f32) + dot(hidden_rows, down)).astype(bf16)
+    router_sum[...] += dot(h_turned, grad_logits)
+    down_sum[...] += dot(cot_rows.T, hidden_rows)
+
+    @pl.when(turn == steps - 1)
+    def _():
         pass_total(2)
         grad_down_ref[...] = down_sum[...].astype(bf16)
         grad_copies[1].start()
@@ -1771,7 +1775,7 @@
         stage(tick, 4, run_one_total)
         stage(tick, 5, run_tokens)
         at_tick(tick, 5, lambda: run_m_x(0))
-        at_tick(tick, 3, line_second)
+        at_tick(tick, 2, line_second)
         at_tick(tick, 6, line_third)
         at_tick(tick, 7, lambda: run_m_x(1))
         return 0

time: 237 us -> 240 us (1.013)
    pallas_call x1, Pallas kernels: 57.3 us -> 60.3 us  [run_second_pair(): pl.pallas_call(partial(second_pair_kernel, experts=experts, steps=steps),...]
where the time goes in v13:
time: 240 us
  Pallas kernels  233 us (97%)
  local copies, waits for them, and re-layouts  3 us (1%)
    pallas_call x1, Pallas kernels, run_forward(): pl.pallas_call(partial(forward_kernel, images=images, heads=heads, expert...  83.9 us
    pallas_call x1, Pallas kernels, run_backward(): pl.pallas_call(partial(backward_kernel, images=images, heads=heads), out_...  81.3 us
    pallas_call x1, Pallas kernels, run_second_pair(): pl.pallas_call(partial(second_pair_kernel, experts=experts, steps=steps),...  60.3 us
    pallas_call x1, Pallas kernels, run_last(): pl.pallas_call(last_kernel, grid_spec=pltpu.PrefetchScalarGridSpec(num_sc...  8.03 us

profile of v13, /device:TPU:0, one launch (start us, length us, event | category | flops | bytes accessed | tf_op | source)
XLA Modules:
  0.0 239.6 jit_solution(8851843278405531723)
XLA Ops:
  0.6 0.7 fusion.2
  1.4 0.1 reshape.37
  1.5 0.1 sub.11
  1.6 1.6 fusion.1.kept_hbm
  3.3 83.9 %shard_map.212 = (bf16[8,208,192]{2,1,0:T(8,128)(2,1)}, bf16[8,208,192]{2,1,0:T(8,128)(2,1)}, bf16[8,208,192]{2,1,0:T(8,128)(2,1)}, bf16[8,208,192]{2,1,0:T(8,12...) custom-call(f32[768]{0:T(1024)} %gain1_ref.3, ...), custom_call_target="tpu_custom_call" | custom-call | tf_op jit(solution)/shard_map/pallas_call | solution.py:948
  87.1 60.3 %shard_map.213 = (bf16[3328,768]{1,0:T(8,128)(2,1)}, f32[8,768]{1,0:T(8,128)}, bf16[768,768]{1,0:T(8,128)(2,1)}, bf16[768,768]{1,0:T(8,128)(2,1)}, bf16[1664,768...) custom-call(bf16[3328,768]{1,0:T(8,128)(2,1)} %get-tuple-element.47.h_ref, ...), custom_call_target="tpu_custom_call" | custom-call | tf_op jit(solution)/shard_map/pallas_call | solution.py:1272
  147.4 81.3 %shard_map.214 = (bf16[2,768,384]{2,1,0:T(8,128)(2,1)}, bf16[1576,768]{1,0:T(8,128)(2,1)}, bf16[2,384,768]{2,1,0:T(8,128)(2,1)}, f32[16,768]{1,0:T(8,128)}, bf16[1664,192]{1,0:T(8,128)(2,1)}) custom-call(f32[768]{0:T(1024)} %gain1_ref.3, f32[768]{0:T(1024)} %shift1_ref.3, f32[768]{0:T(1024)} %gain2_ref.3, f32[8,768]{1,0:T(8,128)} %get-tuple-element.58.grad_router_ref, ...), custom_call_target="tpu_custom_call" | custom-call | tf_op jit(solution)/shard_map/pallas_call | solution.py:2086
  228.7 0.0 copy-start
  228.7 8.0 %shard_map.215 = (f32[1576,768]{1,0:T(8,128)}, f32[3,192,768]{2,1,0:T(8,128)}, f32[192,768]{1,0:T(8,128)}, f32[768,384]{1,0:T(8,128)}, f32[384,768]{1,0:T(8,128)}) custom-call(s32[1]{0:T(128)} %bitcast.6.side_ref, bf16[1576,768]{1,0:T(8,128)(2,1)} %get-tuple-element.72.tokens_ref, bf16[768,768]{1,0:T(8,128)(2,1)} %bitcast.19, ...), custom_call_target="tpu_custom_call" | custom-call | tf_op jit(solution)/shard_map/pallas_call | solution.py:2165
  236.8 0.0 copy-start.1
  236.8 0.0 copy-done
  236.8 0.1 slice.34
  236.8 0.4 reshape.41
  237.2 1.1 copy.25
  238.3 0.0 copy-done.1
  238.3 0.6 slice_reduce_fusion.2
  239.0 0.6 slice_bitcast_fusion
  (2 shorter events, 0.0 us)
Async XLA Ops:
  228.7 8.0 %copy-start = (bf16[1664,192]{1,0:T(8,128)(2,1)S(1)}, bf16[1664,192]{1,0:T(8,128)(2,1)}, u32[]{:S(2)}) copy-start(bf16[1664,192]{1,0:T(8,128)(2,1)} %get-tuple-element.71) | copy-start | bytes 1916932
  236.8 1.6 copy-start.1

commit v14 on v12

--- a/solution.py
+++ b/solution.py
@@ -1161,6 +1161,21 @@
         for copy in whole:
             copy.wait()
 
+    before = turn - 1
+
+    @pl.when((turn >= 1) & turn_is_other(before))
+    def _():
+        pass_other(before)
+
+    @pl.when((turn == 5) | (turn == 7))
+    def _():
+        pass_total((turn - 5) // 2)
+
+    @pl.when((turn == 3) | (turn == 5) | (turn == 7))
+    def _():
+        pass_own(before, (turn - 3) // 2)
+
+
     h_rows, cot_rows = h_ref[...], cot_ref[...]
     up, down, router = up_vm[...], down_vm[...], router_ref[...]
     kept = kept_ref[...].astype(f32)
@@ -1169,21 +1184,6 @@
     )
     grad_gate = kept * (grad_gate + gate_first[...])
     grad_logits = (probs * (grad_gate - jnp.sum(probs * grad_gate, axis=1, keepdims=True))).astype(bf16)
-
-    before = turn - 1
-
-    @pl.when((turn >= 1) & turn_is_other(before))
-    def _():
-        pass_other(before)
-
-    @pl.when((turn == 5) | (turn == 7))
-    def _():
-        pass_total((turn - 5) // 2)
-
-    @pl.when((turn == 3) | (turn == 5) | (turn == 7))
-    def _():
-        pass_own(before, (turn - 3) // 2)
-
 
     @pl.when(turn >= 2)
     def _():

time: 237 us -> 237 us (level)
  no operation moved by 1% of the time
where the time goes in v14:
time: 237 us
  Pallas kernels  230 us (97%)
  local copies, waits for them, and re-layouts  3 us (1%)
  other arithmetic  2.37 us (1%)
    pallas_call x1, Pallas kernels, run_forward(): pl.pallas_call(partial(forward_kernel, images=images, heads=heads, expert...  83.9 us
    pallas_call x1, Pallas kernels, run_backward(): pl.pallas_call(partial(backward_kernel, images=images, heads=heads), out_...  81.4 us
    pallas_call x1, Pallas kernels, run_second_pair(): pl.pallas_call(partial(second_pair_kernel, experts=experts, steps=steps),...  57.2 us
    pallas_call x1, Pallas kernels, run_last(): pl.pallas_call(last_kernel, grid_spec=pltpu.PrefetchScalarGridSpec(num_sc...  8.03 us

profile of v14, /device:TPU:0, one launch (start us, length us, event | category | flops | bytes accessed | tf_op | source)
XLA Modules:
  0.0 236.6 jit_solution(3552335051796234841)
XLA Ops:
  0.6 0.7 fusion.2
  1.4 0.1 reshape.37
  1.5 0.1 sub.11
  1.6 1.6 fusion.1.kept_hbm
  3.3 83.9 %shard_map.212 = (bf16[8,208,192]{2,1,0:T(8,128)(2,1)}, bf16[8,208,192]{2,1,0:T(8,128)(2,1)}, bf16[8,208,192]{2,1,0:T(8,128)(2,1)}, bf16[8,208,192]{2,1,0:T(8,12...) custom-call(f32[768]{0:T(1024)} %gain1_ref.3, ...), custom_call_target="tpu_custom_call" | custom-call | tf_op jit(solution)/shard_map/pallas_call | solution.py:948
  87.1 57.2 %shard_map.213 = (bf16[3328,768]{1,0:T(8,128)(2,1)}, f32[8,768]{1,0:T(8,128)}, bf16[768,768]{1,0:T(8,128)(2,1)}, bf16[768,768]{1,0:T(8,128)(2,1)}, bf16[1664,768...) custom-call(bf16[3328,768]{1,0:T(8,128)(2,1)} %get-tuple-element.47.h_ref, ...), custom_call_target="tpu_custom_call" | custom-call | tf_op jit(solution)/shard_map/pallas_call | solution.py:1268
  144.3 81.4 %shard_map.214 = (bf16[2,768,384]{2,1,0:T(8,128)(2,1)}, bf16[1576,768]{1,0:T(8,128)(2,1)}, bf16[2,384,768]{2,1,0:T(8,128)(2,1)}, f32[16,768]{1,0:T(8,128)}, bf16[1664,192]{1,0:T(8,128)(2,1)}) custom-call(f32[768]{0:T(1024)} %gain1_ref.3, f32[768]{0:T(1024)} %shift1_ref.3, f32[768]{0:T(1024)} %gain2_ref.3, f32[8,768]{1,0:T(8,128)} %get-tuple-element.58.grad_router_ref, ...), custom_call_target="tpu_custom_call" | custom-call | tf_op jit(solution)/shard_map/pallas_call | solution.py:2082
  225.7 0.0 copy-start
  225.7 8.0 %shard_map.215 = (f32[1576,768]{1,0:T(8,128)}, f32[3,192,768]{2,1,0:T(8,128)}, f32[192,768]{1,0:T(8,128)}, f32[768,384]{1,0:T(8,128)}, f32[384,768]{1,0:T(8,128)}) custom-call(s32[1]{0:T(128)} %bitcast.6.side_ref, bf16[1576,768]{1,0:T(8,128)(2,1)} %get-tuple-element.72.tokens_ref, bf16[768,768]{1,0:T(8,128)(2,1)} %bitcast.19, ...), custom_call_target="tpu_custom_call" | custom-call | tf_op jit(solution)/shard_map/pallas_call | solution.py:2161
  233.8 0.0 copy-start.1
  233.8 0.0 copy-done
  233.8 0.1 slice.34
  233.8 0.4 reshape.41
  234.2 1.1 copy.25
  235.3 0.0 copy-done.1
  235.3 0.6 slice_reduce_fusion.2
  236.0 0.6 slice_bitcast_fusion
  (2 shorter events, 0.0 us)
Async XLA Ops:
  225.7 8.0 %copy-start = (bf16[1664,192]{1,0:T(8,128)(2,1)S(1)}, bf16[1664,192]{1,0:T(8,128)(2,1)}, u32[]{:S(2)}) copy-start(bf16[1664,192]{1,0:T(8,128)(2,1)} %get-tuple-element.71) | copy-start | bytes 1916932
  233.8 1.6 copy-start.1
